TPU v7x, 128 devices: a whole 4x4x4 slice. The times are simulated.
128 devices in a mesh: fsdp: 8 (over y, core), tp: 16 (over z, x).
Axes of the slice: x: 4, y: 4, z: 4, core: 2. Of those that a mesh axis runs over, the one named last changes fastest.
Arguments:
- qkv_weight: bfloat16 [16384, 18432], P('fsdp', 'tp'), may hold values from -5 to 5
- placement: int32 [144], replicated, may hold values from 0 to 15, as said below
Outputs:
- packed_codes: bfloat16 [16, 16, 128, 16384], P('tp', None, None, 'fsdp')
- packed_peaks: float32 [16, 16, 128], P('tp')
Inputs may be any that keep to these rules, and one draw needn't show every extreme that they name: `placement`: heads t * 9 to (t + 1) * 9 - 1 form block t. No owner takes more than 1 head of one block, and one owner takes exactly 1 head of every block, so 16 heads in all.
All inputs are finite; a program needn't handle non-finite values. Where the computation divides by a largest or mean magnitude, that divisor is 1e-20 or more.
Results may differ from a plain program's by a relative error of at most 0.0075.
Values may be sent and summed in bfloat16 or wider, within the bound.
No kernel may reach another device: no remote copies, remote signals or barrier semaphores. Data moves between devices by JAX's collectives and lax.ppermute only.
A program may use at most 192 MiB of HBM per device.

v0:
```python
import jax
import jax.numpy as jnp
from jax import lax
from jax.sharding import PartitionSpec as P

HEAD_DIM = 128
HAD = 128


def hadamard_table(order):
    matrix = jnp.ones((1, 1), jnp.float32)
    while matrix.shape[0] < order:
        upper = jnp.concatenate([matrix, matrix], axis=1)
        lower = jnp.concatenate([matrix, -matrix], axis=1)
        matrix = jnp.concatenate([upper, lower], axis=0)
    return matrix


def rotate_items(received):
    item_count, chan_count, dim_total = received.shape
    signs_f = hadamard_table(HAD)
    signs_b = signs_f.astype(jnp.bfloat16)
    flat_rows = received.reshape(item_count * chan_count * HAD, HAD)
    right_turn = jnp.dot(flat_rows, signs_b.T, preferred_element_type=jnp.float32)
    right_turn = right_turn.reshape(item_count * chan_count, HAD, HAD)
    second = jnp.einsum("ia,caj->cij", signs_f, right_turn, precision=lax.Precision.HIGHEST)
    rotated = second * (1.0 / HAD)
    peak_vals = jnp.max(jnp.abs(rotated), axis=(1, 2))
    code_rows = (rotated / (peak_vals + 1e-06)[:, None, None]).astype(jnp.bfloat16)
    return (
        code_rows.reshape(item_count, chan_count, dim_total),
        peak_vals.reshape(item_count, chan_count),
    )


def per_device(qkv_weight, placement):
    rows_local, cols_local = qkv_weight.shape
    heads_here = cols_local // HEAD_DIM
    owners_n = lax.axis_size("tp")
    groups_n = lax.axis_size("fsdp")
    chan_count = HEAD_DIM // groups_n
    slot_count = (heads_here + owners_n - 1) // owners_n
    capacity = owners_n * slot_count
    shaped = jnp.transpose(qkv_weight.reshape(rows_local, heads_here, HEAD_DIM), (1, 2, 0))
    code_rows, peak_vals = rotate_items(
        lax.all_to_all(shaped, "fsdp", split_axis=1, concat_axis=2, tiled=True)
    )
    own_index = lax.axis_index("tp")
    my_owners = lax.dynamic_slice_in_dim(placement, own_index * heads_here, heads_here)
    head_order = jnp.arange(heads_here, dtype=jnp.int32)
    same_owner = my_owners[None, :] == my_owners[:, None]
    head_rank = jnp.sum(
        (same_owner & (head_order[None, :] < head_order[:, None])).astype(jnp.int32), axis=1
    )
    owner_ids = jnp.arange(owners_n, dtype=jnp.int32)
    slot_ids = jnp.arange(slot_count, dtype=jnp.int32)
    select = (my_owners[None, None, :] == owner_ids[:, None, None]) & (
        head_rank[None, None, :] == slot_ids[None, :, None]
    )
    select_b = select.astype(jnp.bfloat16)
    select_f = select.astype(jnp.float32)
    peak_buf = jnp.einsum("tsj,jc->tsc", select_f, peak_vals, precision=lax.Precision.HIGHEST)
    everyone = placement.reshape(owners_n, heads_here)
    counts = jnp.sum((everyone == own_index).astype(jnp.int32), axis=1)
    starts = jnp.cumsum(counts) - counts
    target = jnp.arange(capacity, dtype=jnp.int32)
    packing = (slot_ids[None, None, :] < counts[None, :, None]) & (
        starts[None, :, None] + slot_ids[None, None, :] == target[:, None, None]
    )
    packing_b = packing.astype(jnp.bfloat16)
    packing_f = packing.astype(jnp.float32)
    outgoing = jnp.einsum(
        "tsj,jcd->tscd", select_b, code_rows, preferred_element_type=jnp.float32
    ).astype(jnp.bfloat16)
    peak_out = jnp.broadcast_to(peak_buf[..., None], (owners_n, slot_count, chan_count, groups_n))
    arrived, arrived_peak = (
        lax.all_to_all(
            lax.all_to_all(outgoing, "fsdp", split_axis=3, concat_axis=2, tiled=True),
            "tp",
            split_axis=0,
            concat_axis=0,
            tiled=True,
        ),
        lax.all_to_all(
            lax.all_to_all(
                peak_out.astype(jnp.bfloat16), "fsdp", split_axis=3, concat_axis=2, tiled=True
            ),
            "tp",
            split_axis=0,
            concat_axis=0,
            tiled=True,
        ).astype(peak_out.dtype),
    )
    packed = jnp.einsum(
        "kts,tscd->kcd", packing_b, arrived, preferred_element_type=jnp.float32
    ).astype(jnp.bfloat16)
    packed_peak = jnp.einsum(
        "kts,tsc->kc", packing_f, arrived_peak[..., 0], precision=lax.Precision.HIGHEST
    )
    packed = packed.reshape(1, capacity, HEAD_DIM, rows_local)
    packed_peak = packed_peak.reshape(1, capacity, HEAD_DIM)
    return (packed, packed_peak)


def solution(mesh):
    in_specs = (P("fsdp", "tp"), P())
    out_specs = (P("tp", None, None, "fsdp"), P("tp", None, None))
    return jax.shard_map(
        per_device, mesh=mesh, in_specs=in_specs, out_specs=out_specs, check_vma=False
    )
```

profile of v0, /device:TPU:0, one launch (start us, length us, event | category | flops | bytes accessed | tf_op | source)
XLA Modules:
  0.0 758.5 jit_solution(14414768802258490881)
XLA Ops:
  0.6 6.7 copy.31
  7.3 8.8 %copy.32 = bf16[9,128,2048]{2,0,1:T(8,128)(2,1)} copy(bf16[9,128,2048]{2,1,0:T(8,128)(2,1)} %bitcast.71) | data formatting | bytes 9437184 | tf_op jit(solution)/shard_map/transpose | solution.py:44
  16.2 0.0 copy-start.2
  16.2 5.7 all-to-all-start
  21.9 0.0 copy-done.2
  21.9 0.1 dynamic_slice.3
  21.9 0.2 convert_reduce_fusion
  22.1 94.3 %all-to-all-done = bf16[9,128,2048]{2,0,1:T(8,128)(2,1)} async-done(((bf16[9,128,2048]{2,0,1:T(8,128)(2,1)}), bf16[9,128,2048]{2,0,1:T(8,128)(2,1)}, u32[]{:S(2)}, u32[]{:S(2)}) %all-to-all-start) | async-done | bytes 4718624 | tf_op jit(solution)/shard_map/all_to_all | solution.py:46
  116.5 0.0 copy-start.1
  116.5 8.4 %copy.34 = bf16[9,16,8,2048]{3,2,1,0:T(8,128)(2,1)} copy(bf16[9,16,8,2048]{3,0,1,2:T(8,128)(2,1)} %bitcast.9) | data formatting | bytes 9437184 | tf_op jit(solution)/shard_map/all_to_all | solution.py:46
  124.9 8.3 %reshape.267 = bf16[18432,128]{1,0:T(8,128)(2,1)} reshape(bf16[9,16,8,2048]{3,2,1,0:T(8,128)(2,1)} %copy.34) | data formatting | bytes 9437184 | tf_op jit(solution)/shard_map/reshape | solution.py:23
  133.2 0.0 copy-done.1
  133.2 0.0 copy-start
  133.2 3.8 convolution_bitcast_fusion
  137.0 0.0 copy-done
  137.0 10.1 %abs_reduce_fusion = (f32[144]{0:T(256)S(1)}, f32[144,128,128]{2,1,0:T(8,128)}) fusion(f32[128,128,1]{1,0,2:T(8,128)S(1)} %copy-done, f32[16,144,8,128]{3,2,1,0:T(8,128)S(1)} %convolution_bitcast_fusion), kind=kOutput, calls=%fused_computation.6 | convolution fusion | flops 3630956544 | bytes 18940480 | tf_op jit(solution)/shard_map/ia,caj->cij/dot_general | solution.py:26
  147.1 0.1 reshape.272
  147.1 7.5 fusion.10
  154.7 6.6 copy.36
  161.3 8.2 %reshape.269 = bf16[9,16,16384]{2,1,0:T(8,128)(2,1)} reshape(bf16[144,128,128]{2,1,0:T(8,128)(2,1)} %copy.36) | data formatting | bytes 9437184 | tf_op jit(solution)/shard_map/reshape | solution.py:31
  169.5 0.1 convolution_convert_fusion.1
  169.7 0.7 reshape.282
  170.4 3.5 all-to-all-start.3
  173.9 11.6 %fusion = bf16[16,1,16,16384]{3,0,2,1:T(8,128)(2,1)} fusion(bf16[9,16,16384]{2,1,0:T(8,128)(2,1)} %reshape.269, s32[9]{0:T(128)S(1)} %dynamic_slice.3, pred[9]{0:T(512)(128)(4,1)S(1)} %broadcast_compare_fusion), kind=kOutput, calls=%fused_computation.1 | convolution fusion | flops 79692064 | bytes 13107245 | tf_op jit(solution)/shard_map/tsj,jcd->tscd/dot_general | solution.py:72
  185.4 53.5 %copy.38 = bf16[16,1,16,16384]{0,2,1,3:T(8,128)(2,1)} copy(bf16[16,1,16,16384]{3,0,2,1:T(8,128)(2,1)} %fusion) | data formatting | bytes 16777216 | tf_op jit(solution)/shard_map/convert_element_type | solution.py:74
  238.9 104.1 %reshape.280 = bf16[8,2,262144]{2,1,0:T(2,128)(2,1)} reshape(bf16[16384,1,16,16]{3,2,1,0:T(8,128)(2,1)} %bitcast.57) | data formatting | bytes 16777216
  343.1 0.0 all-to-all-done.3
  343.1 5.0 all-to-all-start.1
  348.0 0.1 reshape.283
  348.1 0.7 all_to_all.56
  348.8 93.8 %all-to-all-done.1 = bf16[8,2,262144]{2,1,0:T(2,128)(2,1)} async-done(((bf16[8,2,262144]{2,1,0:T(2,128)(2,1)}), bf16[8,2,262144]{2,1,0:T(2,128)(2,1)}, u32[]{:S(2)}, u32[]{:S(2)}) %all-to-all-start.1) | async-done | bytes 8388640 | tf_op jit(solution)/shard_map/all_to_all | solution.py:78
  442.6 8.2 %all-to-all-start.4 = ((bf16[16,1,128,1]{2,3,1,0:T(2,128)(2,1)}), bf16[16,1,128,1]{2,3,1,0:T(2,128)(2,1)S(1)}, u32[]{:S(2)}, u32[]{:S(2)}) async-start(bf16[16,1,128,1]{2,3,1,0:T(2,128)(2,1)} %all_to_all.56), calls=%async_computation.4 | async-start | bytes 16384 | tf_op jit(solution)/shard_map/all_to_all | solution.py:84
  450.9 80.3 %reshape.281 = bf16[16384,1,16,16]{3,2,1,0:T(8,128)(2,1)} reshape(bf16[8,2,262144]{2,1,0:T(2,128)(2,1)} %all-to-all-done.1) | data formatting | bytes 16777216
  531.1 69.9 %copy.39 = bf16[16,1,8,16,2048]{4,3,2,0,1:T(8,128)(2,1)} copy(bf16[16,1,8,16,2048]{0,3,4,2,1:T(8,128)(2,1)} %bitcast.15) | data formatting | bytes 16777216 | tf_op jit(solution)/shard_map/all_to_all | solution.py:78
  601.0 0.0 all-to-all-done.4
  601.0 7.8 %all-to-all-start.2 = ((bf16[16,1,128,2048]{3,2,1,0:T(8,128)(2,1)}), bf16[16,1,128,2048]{3,2,1,0:T(8,128)(2,1)}, u32[]{:S(2)}, u32[]{:S(2)}) async-start(bf16[16,1,128,2048]{3,2,1,0:T(8,128)(2,1)} %bitcast.70), calls=%async_computation.2 | async-start | bytes 16777216 | tf_op jit(solution)/shard_map/all_to_all | solution.py:77
  608.9 0.1 reshape.275
  609.0 0.1 reduce_sum.18
  609.1 0.1 copy.30
  609.2 0.1 reduce.1
  609.4 0.7 convolution_bitcast_fusion.1
  610.1 120.6 %all-to-all-done.2 = bf16[16,1,128,2048]{3,2,1,0:T(8,128)(2,1)} async-done(((bf16[16,1,128,2048]{3,2,1,0:T(8,128)(2,1)}), bf16[16,1,128,2048]{3,2,1,0:T(8,128)(2,1)}, u32[]{:S(2)}, u32[]{:S(2)}) %all-to-all-start.2) | async-done | bytes 8388640 | tf_op jit(solution)/shard_map/all_to_all | solution.py:77
  730.7 16.0 %convert_bitcast_fusion = bf16[1,16,128,2048]{3,1,2,0:T(8,128)(2,1)} fusion(bf16[16,1,128,2048]{3,2,1,0:T(8,128)(2,1)} %all-to-all-done.2, s32[16]{0:T(128)S(1)} %sub.7, pred[16]{0:T(512)(128)(4,1)S(1)} %broadcast_compare_fusion.1), kind=kOutput, calls=%fused_computation.11 | convolution fusion | flops 138412544 | bytes 16777296 | tf_op jit(solution)/shard_map/kts,tscd->kcd/dot_general | solution.py:94
  746.7 11.6 %copy.43 = bf16[1,16,128,2048]{3,2,1,0:T(8,128)(2,1)} copy(bf16[1,16,128,2048]{3,1,2,0:T(8,128)(2,1)} %convert_bitcast_fusion) | data formatting | bytes 16777216
  (9 shorter events, 0.1 us)
Async XLA Ops:
  16.2 5.7 copy-start.2
  16.2 100.3 %all-to-all-start = ((bf16[9,128,2048]{2,0,1:T(8,128)(2,1)}), bf16[9,128,2048]{2,0,1:T(8,128)(2,1)}, u32[]{:S(2)}, u32[]{:S(2)}) async-start(bf16[9,128,2048]{2,0,1:T(8,128)(2,1)} %copy.32), calls=%async_computation | async-start | bytes 16777216 | tf_op jit(solution)/shard_map/all_to_all | solution.py:46
  116.5 16.7 %copy-start.1 = (bf16[128,128]{1,0:T(8,128)(2,1)S(1)}, bf16[128,128]{1,0:T(8,128)(2,1)}, u32[]{:S(2)}) copy-start(bf16[128,128]{1,0:T(8,128)(2,1)} %constant.3.clone.1) | copy-start | bytes 98308
  133.2 3.8 copy-start
  170.4 172.7 %all-to-all-start.3 = ((bf16[8,2,128]{2,1,0:T(2,128)(2,1)}), bf16[8,2,128]{2,1,0:T(2,128)(2,1)S(1)}, u32[]{:S(2)}, u32[]{:S(2)}) async-start(bf16[8,2,128]{2,1,0:T(2,128)(2,1)} %reshape.282), calls=%async_computation.3 | async-start | bytes 8192 | tf_op jit(solution)/shard_map/all_to_all | solution.py:85
  343.1 99.6 %all-to-all-start.1 = ((bf16[8,2,262144]{2,1,0:T(2,128)(2,1)}), bf16[8,2,262144]{2,1,0:T(2,128)(2,1)}, u32[]{:S(2)}, u32[]{:S(2)}) async-start(bf16[8,2,262144]{2,1,0:T(2,128)(2,1)} %reshape.280), calls=%async_computation.1 | async-start | bytes 16777216 | tf_op jit(solution)/shard_map/all_to_all | solution.py:78
  442.6 158.4 %all-to-all-start.4 = ((bf16[16,1,128,1]{2,3,1,0:T(2,128)(2,1)}), bf16[16,1,128,1]{2,3,1,0:T(2,128)(2,1)S(1)}, u32[]{:S(2)}, u32[]{:S(2)}) async-start(bf16[16,1,128,1]{2,3,1,0:T(2,128)(2,1)} %all_to_all.56), calls=%async_computation.4 | async-start | bytes 16384 | tf_op jit(solution)/shard_map/all_to_all | solution.py:84
  601.0 129.7 %all-to-all-start.2 = ((bf16[16,1,128,2048]{3,2,1,0:T(8,128)(2,1)}), bf16[16,1,128,2048]{3,2,1,0:T(8,128)(2,1)}, u32[]{:S(2)}, u32[]{:S(2)}) async-start(bf16[16,1,128,2048]{3,2,1,0:T(8,128)(2,1)} %bitcast.70), calls=%async_computation.2 | async-start | bytes 16777216 | tf_op jit(solution)/shard_map/all_to_all | solution.py:77
where the time goes:
time: 767 us; the launch traced here: 758 us
  local copies, waits for them, and re-layouts  368 us (48%)
  waiting for transfers between devices  309 us (40%)
  matrix products  42.2 us (6%)
  starting transfers between devices  30.2 us (4%)
  other arithmetic  8.02 us (1%)
    unnamed x13, local copies, waits for them, and re-layouts  203 us
    all_to_all x1, waiting for transfers between devices, per_device(): lax.all_to_all(lax.all_to_all(outgoing, 'fsdp', split_axis=3, concat_axis...  121 us
    all_to_all x1, waiting for transfers between devices, per_device(): lax.all_to_all(shaped, 'fsdp', split_axis=1, concat_axis=2, tiled=True)  94.3 us
    all_to_all x1, waiting for transfers between devices, per_device(): lax.all_to_all(outgoing, 'fsdp', split_axis=3, concat_axis=2, tiled=True)  93.8 us
    all_to_all x1, local copies, waits for them, and re-layouts, per_device(): lax.all_to_all(outgoing, 'fsdp', split_axis=3, concat_axis=2, tiled=True)  69.9 us
    convert_element_type x1, local copies, waits for them, and re-layouts, per_device(): outgoing = jnp.einsum('tsj,jcd->tscd', select_b, code_rows, preferred_ele...  53.5 us
    dot_general x1, matrix products, per_device(): jnp.einsum('kts,tscd->kcd', packing_b, arrived, preferred_element_type=jn...  16 us
  transfers between devices with their start and end apart: 5, of which 3 were waited for; matrix products, arithmetic and copies ran while one was open for 42% of the time, Pallas kernels for 0%

commit v1 on v0

v1 whole, which is shorter than its diff:
```python
import functools

import numpy as np
import jax
import jax.numpy as jnp
from jax import lax
from jax.experimental import pallas as pl
from jax.experimental.pallas import tpu as pltpu
from jax.sharding import PartitionSpec as P

HEAD_DIM = 128
HAD = 128
CHUNKS = 2
VMEM_BYTES = 48 * 1024 * 1024


def hadamard_table(order):
    matrix = np.ones((1, 1), np.float32)
    while matrix.shape[0] < order:
        matrix = np.block([[matrix, matrix], [matrix, -matrix]])
    return matrix


def butterfly(values):
    values = list(values)
    half = 1
    while half < len(values):
        for low in range(len(values)):
            if not low & half:
                first, second = values[low], values[low + half]
                values[low], values[low + half] = first + second, first - second
        half *= 2
    return values


def local_turn_kernel(rows_a, groups, weight_ref, signs_ref, *refs):
    out_refs, turned = refs[:-1], refs[-1]
    for a in range(rows_a):
        block = weight_ref[a * HAD : (a + 1) * HAD, :]
        turned[a] = lax.dot_general(
            block, signs_ref[...], (((0,), (0,)), ((), ())), preferred_element_type=jnp.float32
        )
    chans = HEAD_DIM // len(out_refs)
    each = rows_a // groups
    for chunk, out_ref in enumerate(out_refs):
        for low in range(0, chans, 16):
            start = chunk * chans + low
            outs = butterfly([turned[a, start : start + 16, :] for a in range(rows_a)])
            for a in range(rows_a):
                out_ref[a // each, 0, a % each, low : low + 16, :] = (outs[a] * (1.0 / HAD)).astype(jnp.bfloat16)


def cross_turn_kernel(in_ref, out_ref, peak_ref):
    groups, heads, each, chans, _ = in_ref.shape
    for head in range(heads):
        for low in range(0, chans, 16):
            rows = slice(low, low + 16)
            largest = None
            for e in range(each):
                outs = butterfly([in_ref[g, head, e, rows, :].astype(jnp.float32) for g in range(groups)])
                for g in range(groups):
                    out_ref[g, head, e, rows, :] = outs[g].astype(jnp.bfloat16)
                    magnitude = jnp.abs(outs[g])
                    largest = magnitude if largest is None else jnp.maximum(largest, magnitude)
            peak_ref[head, rows, :] = largest


def spread_kernel(head_ref, in_ref, out_ref, sems):
    copies = []
    for owner in range(out_ref.shape[0]):
        copies.append(pltpu.make_async_copy(in_ref.at[:, head_ref[owner]], out_ref.at[owner], sems.at[owner]))
    for copy in copies:
        copy.start()
    for copy in copies:
        copy.wait()


def pack_kernel(source_ref, live_ref, scale_ref, *refs):
    in_refs, out_ref = refs[:-1], refs[-1]
    slot = pl.program_id(0)
    _, groups, each, chans, _ = in_refs[0].shape

    @pl.when(live_ref[slot] != 0)
    def _():
        for chunk, in_ref in enumerate(in_refs):
            rows = slice(chunk * chans, (chunk + 1) * chans)
            scale = scale_ref[0, rows, :]
            for g in range(groups):
                for e in range(each):
                    lane = (g * each + e) * HAD
                    out_ref[0, 0, rows, lane : lane + HAD] = (
                        in_ref[0, g, e].astype(jnp.float32) * scale
                    ).astype(jnp.bfloat16)

    @pl.when(live_ref[slot] == 0)
    def _():
        out_ref[...] = jnp.zeros_like(out_ref)


def per_device(qkv_weight, placement):
    rows_local, cols_local = qkv_weight.shape
    heads = cols_local // HEAD_DIM
    owners = lax.axis_size("tp")
    groups = lax.axis_size("fsdp")
    rows_a = rows_local // HAD
    each = rows_a // groups
    chans = HEAD_DIM // CHUNKS
    params = pltpu.CompilerParams(vmem_limit_bytes=VMEM_BYTES)
    any_spec = pl.BlockSpec(memory_space=pl.ANY)

    me = lax.axis_index("tp")
    table = placement.reshape(owners, heads)
    my_owners = lax.dynamic_slice_in_dim(table, me, 1, axis=0)[0]
    head_ids = jnp.arange(heads, dtype=jnp.int32)
    owner_ids = jnp.arange(owners, dtype=jnp.int32)
    head_for = jnp.sum(jnp.where(my_owners[None, :] == owner_ids[:, None], head_ids[None, :], 0), axis=1)
    mine = table == me
    has = jnp.any(mine, axis=1)
    rank = jnp.cumsum(has.astype(jnp.int32)) - 1
    count = jnp.sum(has.astype(jnp.int32))
    takes = has[None, :] & (rank[None, :] == owner_ids[:, None])
    source = jnp.sum(jnp.where(takes, owner_ids[None, :], 0), axis=1)
    live = (owner_ids < count).astype(jnp.int32)
    picked = (takes[:, :, None] & mine[None]).reshape(owners, owners * heads)

    signs = jnp.asarray(hadamard_table(HAD), jnp.bfloat16)
    piece = (groups, heads, each, chans, HAD)
    sent = pl.pallas_call(
        functools.partial(local_turn_kernel, rows_a, groups),
        grid=(heads,),
        in_specs=[
            pl.BlockSpec((rows_local, HEAD_DIM), lambda h: (0, h)),
            pl.BlockSpec((HAD, HAD), lambda h: (0, 0)),
        ],
        out_specs=[pl.BlockSpec((groups, 1, each, chans, HAD), lambda h: (0, h, 0, 0, 0))] * CHUNKS,
        out_shape=[jax.ShapeDtypeStruct(piece, jnp.bfloat16)] * CHUNKS,
        scratch_shapes=[pltpu.VMEM((rows_a, HEAD_DIM, HAD), jnp.float32)],
        compiler_params=params,
        name="local_turn",
    )(qkv_weight, signs)

    step = 3 if heads % 3 == 0 else 1
    arrived, peaks = [], []
    previous = None
    for chunk in range(CHUNKS):
        block = sent[chunk]
        if previous is not None:
            block, previous = lax.optimization_barrier((block, previous))
        received = lax.all_to_all(block, "fsdp", split_axis=0, concat_axis=0, tiled=True)
        previous = received
        turned, partial_peak = pl.pallas_call(
            cross_turn_kernel,
            grid=(heads // step,),
            in_specs=[pl.BlockSpec((groups, step, each, chans, HAD), lambda h: (0, h, 0, 0, 0))],
            out_specs=[
                pl.BlockSpec((groups, step, each, chans, HAD), lambda h: (0, h, 0, 0, 0)),
                pl.BlockSpec((step, chans, HAD), lambda h: (h, 0, 0)),
            ],
            out_shape=[
                jax.ShapeDtypeStruct(piece, jnp.bfloat16),
                jax.ShapeDtypeStruct((heads, chans, HAD), jnp.float32),
            ],
            compiler_params=params,
            name="cross_turn",
        )(received)
        peaks.append(jnp.max(partial_peak, axis=2))
        returned = lax.all_to_all(turned, "fsdp", split_axis=0, concat_axis=0, tiled=True)
        spread = pl.pallas_call(
            spread_kernel,
            grid_spec=pltpu.PrefetchScalarGridSpec(
                num_scalar_prefetch=1,
                grid=(1,),
                in_specs=[any_spec],
                out_specs=any_spec,
                scratch_shapes=[pltpu.SemaphoreType.DMA((owners,))],
            ),
            out_shape=jax.ShapeDtypeStruct((owners, groups, each, chans, HAD), jnp.bfloat16),
            compiler_params=params,
            name="spread",
        )(head_for, returned)
        arrived.append(lax.all_to_all(spread, "tp", split_axis=0, concat_axis=0, tiled=True))

    local_peak = jnp.concatenate(peaks, axis=1)
    all_peaks = lax.all_gather(local_peak, ("fsdp", "tp"), axis=0, tiled=False)
    all_peaks = jnp.max(all_peaks.reshape(groups, owners * heads, HEAD_DIM), axis=0)
    slot_peaks = jnp.max(jnp.where(picked[:, :, None], all_peaks[None], 0.0), axis=1)
    scale = jnp.broadcast_to((1.0 / (slot_peaks + 1e-06))[:, :, None], (owners, HEAD_DIM, HAD))

    packed = pl.pallas_call(
        pack_kernel,
        grid_spec=pltpu.PrefetchScalarGridSpec(
            num_scalar_prefetch=2,
            grid=(owners,),
            in_specs=[pl.BlockSpec((1, HEAD_DIM, HAD), lambda k, source, live: (k, 0, 0))]
            + [
                pl.BlockSpec((1, groups, each, chans, HAD), lambda k, source, live: (source[k], 0, 0, 0, 0))
            ]
            * CHUNKS,
            out_specs=pl.BlockSpec((1, 1, HEAD_DIM, rows_local), lambda k, source, live: (0, k, 0, 0)),
        ),
        out_shape=jax.ShapeDtypeStruct((1, owners, HEAD_DIM, rows_local), jnp.bfloat16),
        compiler_params=params,
        name="pack",
    )(source, live, scale, *arrived)
    return packed, slot_peaks[None]


def solution(mesh):
    in_specs = (P("fsdp", "tp"), P())
    out_specs = (P("tp", None, None, "fsdp"), P("tp", None, None))
    return jax.shard_map(
        per_device, mesh=mesh, in_specs=in_specs, out_specs=out_specs, check_vma=False
    )
```

time: 767 us -> 416 us (0.54)
  local copies, waits for them, and re-layouts: 368 us -> 9.08 us
  waiting for transfers between devices: 309 us -> 78.5 us
  Pallas kernels: 0 us -> 151 us
  blocking collectives: 0 us -> 144 us
  matrix products: 42.2 us -> 0 us
    all_to_all x5, waiting for transfers between devices: 309 us -> 78.5 us  [the longest x2 52.8 us: per_device(): lax.all_to_all(turned, 'fsdp', split_axis=0, concat_axis=0, tiled=True)]
    unnamed x13 -> x18, local copies, waits for them, and re-layouts: 203 us -> 8.28 us
    pallas_call x0 -> x6, Pallas kernels: none -> 151 us  [the longest x2 132 us: per_device(): pl.pallas_call(spread_kernel, grid_spec=pltpu.PrefetchScalarGridSpec(num_...]
    all_gather x0 -> x1, blocking collectives: none -> 109 us  [per_device(): all_peaks = lax.all_gather(local_peak, ('fsdp', 'tp'), axis=0, tiled=False)]
    all_to_all x5 -> x0, local copies, waits for them, and re-layouts: 79.1 us -> none  [the longest x1 69.9 us: per_device(): lax.all_to_all(outgoing, 'fsdp', split_axis=3, concat_axis=2, tiled=True)]
    convert_element_type x3 -> x1, local copies, waits for them, and re-layouts: 60.2 us -> 0.09 us  [per_device(): rank = jnp.cumsum(has.astype(jnp.int32)) - 1]
    dot_general x6 -> x0, matrix products: 42.2 us -> none  [the longest x1 16 us: per_device(): jnp.einsum('kts,tscd->kcd', packing_b, arrived, preferred_element_type=jn...]
    all_to_all x0 -> x1, blocking collectives: none -> 34.8 us  [per_device(): lax.all_to_all(block, 'fsdp', split_axis=0, concat_axis=0, tiled=True)]
  transfers between devices with their start and end apart: 5 -> 5, of which waited for: 3 -> 3; matrix products, arithmetic and copies ran while one was open for 42% -> 1% of each run, Pallas kernels for 0% -> 32%
where the time goes in v1:
time: 416 us; the launch traced here: 413 us
  Pallas kernels  151 us (36%)
  blocking collectives  144 us (35%)
  waiting for transfers between devices  78.5 us (19%)
  starting transfers between devices  26.9 us (6%)
  local copies, waits for them, and re-layouts  9.08 us (2%)
    pallas_call x2, Pallas kernels, per_device(): pl.pallas_call(spread_kernel, grid_spec=pltpu.PrefetchScalarGridSpec(num_...  132 us
    all_gather x1, blocking collectives, per_device(): all_peaks = lax.all_gather(local_peak, ('fsdp', 'tp'), axis=0, tiled=False)  109 us
    all_to_all x2, waiting for transfers between devices, per_device(): lax.all_to_all(turned, 'fsdp', split_axis=0, concat_axis=0, tiled=True)  52.8 us
    all_to_all x1, blocking collectives, per_device(): lax.all_to_all(block, 'fsdp', split_axis=0, concat_axis=0, tiled=True)  34.8 us
    all_to_all x1, waiting for transfers between devices, per_device(): lax.all_to_all(block, 'fsdp', split_axis=0, concat_axis=0, tiled=True)  25.7 us
    all_to_all x2, starting transfers between devices, per_device(): lax.all_to_all(spread, 'tp', split_axis=0, concat_axis=0, tiled=True)  15.2 us
    pallas_call x1, Pallas kernels, per_device(): pl.pallas_call(pack_kernel, grid_spec=pltpu.PrefetchScalarGridSpec(num_sc...  9.65 us
  transfers between devices with their start and end apart: 5, of which 3 were waited for; matrix products, arithmetic and copies ran while one was open for 1% of the time, Pallas kernels for 32%

profile of v1, /device:TPU:0, one launch (start us, length us, event | category | flops | bytes accessed | tf_op | source)
XLA Modules:
  0.0 413.2 jit_solution(11079752838041617849)
XLA Ops:
  0.6 0.0 copy-start.6
  0.6 0.7 copy-done.6
  1.4 7.8 %local_turn.1 = (bf16[8,9,2,64,128]{4,3,2,1,0:T(8,128)(2,1)S(1)}, bf16[8,9,2,64,128]{4,3,2,1,0:T(8,128)(2,1)S(1)}) custom-call(bf16[2048,1152]{1,0:T(8,128)(2,1)} %weight_ref.1, bf16[128,128]{1,0:T(8,128)(2,1)S(1)} %copy-done.6), custom_call_target="tpu_custom_call" | custom-call | tf_op jit(solution)/shard_map/local_turn/pallas_call | solution.py:128
  9.2 0.0 copy-start.5
  9.2 34.8 %all_to_all.30.in_ref = bf16[8,9,2,64,128]{4,3,2,1,0:T(8,128)(2,1)} all-to-all(bf16[8,9,2,64,128]{4,3,2,1,0:T(8,128)(2,1)S(1)} %get-tuple-element.9), channel_id=1, replica_groups=mesh['fsdp'=8,'tp'=16] {'fsdp'}, dimensions={0} | all-to-all | bytes 4718592 | tf_op jit(solution)/shard_map/all_to_all | solution.py:149
  44.0 0.0 copy-done.5
  44.0 3.6 all-to-all-start.1
  47.6 0.0 copy-start.2
  47.6 1.7 copy-done.2
  49.3 1.2 cross_turn.2
  50.5 0.0 copy-start.4
  50.5 1.4 copy-done.4
  51.8 25.7 %all-to-all-done.1.in_ref = bf16[8,9,2,64,128]{4,3,2,1,0:T(8,128)(2,1)S(1)} async-done(((bf16[8,9,2,64,128]{4,3,2,1,0:T(8,128)(2,1)}), bf16[8,9,2,64,128]{4,3,2,1,0:T(8,128)(2,1)S(1)}, u32[]{:S(2)}, u32[]{:S(2)}) %all-to-all-start.1) | async-done | bytes 2359328 | tf_op jit(solution)/shard_map/all_to_all | solution.py:149
  77.6 0.0 copy-start
  77.6 1.4 copy-done
  79.0 3.6 all-to-all-start.2
  82.6 0.0 copy-start.1
  82.6 1.7 copy-done.1
  84.2 1.2 cross_turn.3
  85.4 0.0 copy-start.3
  85.4 1.4 copy-done.3
  86.8 25.7 %all-to-all-done.2.in_ref = bf16[8,9,2,64,128]{4,3,2,1,0:T(8,128)(2,1)S(1)} async-done(((bf16[8,9,2,64,128]{4,3,2,1,0:T(8,128)(2,1)}), bf16[8,9,2,64,128]{4,3,2,1,0:T(8,128)(2,1)S(1)}, u32[]{:S(2)}, u32[]{:S(2)}) %all-to-all-start.2) | async-done | bytes 2359328 | tf_op jit(solution)/shard_map/all_to_all | solution.py:167
  112.5 0.0 copy-start.8
  112.5 4.5 %all-to-all-start.4 = ((bf16[8,9,2,64,128]{4,3,2,1,0:T(8,128)(2,1)}), bf16[8,9,2,64,128]{4,3,2,1,0:T(8,128)(2,1)}, u32[]{:S(2)}, u32[]{:S(2)}) async-start(bf16[8,9,2,64,128]{4,3,2,1,0:T(8,128)(2,1)} %copy-done.3), calls=%async_computation.4 | async-start | bytes 4718592 | tf_op jit(solution)/shard_map/all_to_all | solution.py:167
  117.0 0.0 copy-done.8
  117.0 0.1 reshape.95
  117.1 0.1 select_reduce_fusion.1.head_ref
  117.2 2.7 spread.2
  119.9 27.1 %all-to-all-done.4.in_ref = bf16[8,9,2,64,128]{4,3,2,1,0:T(8,128)(2,1)} async-done(((bf16[8,9,2,64,128]{4,3,2,1,0:T(8,128)(2,1)}), bf16[8,9,2,64,128]{4,3,2,1,0:T(8,128)(2,1)}, u32[]{:S(2)}, u32[]{:S(2)}) %all-to-all-start.4) | async-done | bytes 2359328 | tf_op jit(solution)/shard_map/all_to_all | solution.py:167
  147.0 7.9 %all-to-all-start.3 = ((bf16[16,8,2,64,128]{4,3,2,1,0:T(8,128)(2,1)}), bf16[16,8,2,64,128]{4,3,2,1,0:T(8,128)(2,1)}, u32[]{:S(2)}, u32[]{:S(2)}) async-start(bf16[16,8,2,64,128]{4,3,2,1,0:T(8,128)(2,1)} %spread.2), calls=%async_computation.3 | async-start | bytes 8388608 | tf_op jit(solution)/shard_map/all_to_all | solution.py:181
  155.0 128.8 %spread.3 = bf16[16,8,2,64,128]{4,3,2,1,0:T(8,128)(2,1)} custom-call(s32[16]{0:T(128)S(1)} %select_reduce_fusion.1.head_ref, bf16[8,9,2,64,128]{4,3,2,1,0:T(8,128)(2,1)} %all-to-all-done.4.in_ref), custom_call_target="tpu_custom_call" | custom-call | tf_op jit(solution)/shard_map/spread/pallas_call | solution.py:168
  283.8 0.0 all-to-all-done.3.refs_0_
  283.8 7.2 %all-to-all-start.5 = ((bf16[16,8,2,64,128]{4,3,2,1,0:T(8,128)(2,1)}), bf16[16,8,2,64,128]{4,3,2,1,0:T(8,128)(2,1)}, u32[]{:S(2)}, u32[]{:S(2)}) async-start(bf16[16,8,2,64,128]{4,3,2,1,0:T(8,128)(2,1)} %spread.3), calls=%async_computation.5 | async-start | bytes 8388608 | tf_op jit(solution)/shard_map/all_to_all | solution.py:181
  291.1 0.1 compare_reduce_fusion
  291.2 0.1 copy.8
  291.3 0.1 add_reduce_fusion
  291.5 0.1 and.34
  291.6 0.1 and.35
  291.7 0.6 convert_reduce_fusion
  292.3 0.6 compare_convert_fusion.live_ref
  293.0 0.1 select_reduce_fusion.2.source_ref
  293.1 0.1 reduce_max.36
  293.3 0.1 reduce_max.37
  293.4 0.1 maximum_bitcast_fusion
  293.5 109.1 %all-gather.1 = f32[128,9,128]{2,1,0:T(8,128)S(1)} all-gather(f32[1,9,128]{2,1,0:T(8,128)S(1)} %maximum_bitcast_fusion), channel_id=2, replica_groups=mesh['fsdp'=8,'tp'=16] {'fsdp','tp'}, dimensions={0}, use_global_device_ids=true | all-gather | bytes 594432 | tf_op jit(solution)/shard_map/all_gather | solution.py:184
  402.6 0.1 reshape.96
  402.7 0.5 select_reduce_fusion
  403.2 0.0 copy-start.7
  403.2 0.0 all-to-all-done.5.refs_1_
  403.2 0.3 broadcast_in_dim.67.scale_ref
  403.6 9.6 %pack.1 = bf16[1,16,128,2048]{3,2,1,0:T(8,128)(2,1)} custom-call(s32[16]{0:T(128)S(1)} %select_reduce_fusion.2.source_ref, s32[16]{0:T(128)S(1)} %compare_convert_fusion.live_ref, f32[16,128,128]{2,1,0:T(8,128)S(1)} %broadcast_in_dim.67.scale_ref, bf16[16,8,2,64,128]{4,3,2,1,0:T(8,128)(2,1)} %all-to-all-done.3.refs_0_, ...), custom_call_target="tpu_custom_call" | custom-call | tf_op jit(solution)/shard_map/pack/pallas_call | solution.py:189
  413.2 0.0 copy-done.7
  (8 shorter events, 0.1 us)
Async XLA Ops:
  0.6 0.8 copy-start.6
  9.2 34.8 %copy-start.5 = (bf16[8,9,2,64,128]{4,3,2,1,0:T(8,128)(2,1)}, bf16[8,9,2,64,128]{4,3,2,1,0:T(8,128)(2,1)S(1)}, u32[]{:S(2)}) copy-start(bf16[8,9,2,64,128]{4,3,2,1,0:T(8,128)(2,1)S(1)} %get-tuple-element.12) | copy-start | bytes 7077892
  44.0 33.6 %all-to-all-start.1 = ((bf16[8,9,2,64,128]{4,3,2,1,0:T(8,128)(2,1)}), bf16[8,9,2,64,128]{4,3,2,1,0:T(8,128)(2,1)S(1)}, u32[]{:S(2)}, u32[]{:S(2)}) async-start(bf16[8,9,2,64,128]{4,3,2,1,0:T(8,128)(2,1)} %copy-done.5), calls=%async_computation.1 | async-start | bytes 4718592 | tf_op jit(solution)/shard_map/all_to_all | solution.py:149
  47.6 1.7 copy-start.2
  50.5 1.4 copy-start.4
  77.6 1.4 copy-start
  79.0 33.6 %all-to-all-start.2 = ((bf16[8,9,2,64,128]{4,3,2,1,0:T(8,128)(2,1)}), bf16[8,9,2,64,128]{4,3,2,1,0:T(8,128)(2,1)S(1)}, u32[]{:S(2)}, u32[]{:S(2)}) async-start(bf16[8,9,2,64,128]{4,3,2,1,0:T(8,128)(2,1)} %copy-done.4), calls=%async_computation.2 | async-start | bytes 4718592 | tf_op jit(solution)/shard_map/all_to_all | solution.py:167
  82.6 1.7 copy-start.1
  85.4 1.4 copy-start.3
  112.5 4.5 %copy-start.8 = (s32[144]{0:T(256)S(1)}, s32[144]{0:T(256)}, u32[]{:S(2)}) copy-start(s32[144]{0:T(256)} %param.4) | copy-start | bytes 1732
  112.5 34.5 %all-to-all-start.4 = ((bf16[8,9,2,64,128]{4,3,2,1,0:T(8,128)(2,1)}), bf16[8,9,2,64,128]{4,3,2,1,0:T(8,128)(2,1)}, u32[]{:S(2)}, u32[]{:S(2)}) async-start(bf16[8,9,2,64,128]{4,3,2,1,0:T(8,128)(2,1)} %copy-done.3), calls=%async_computation.4 | async-start | bytes 4718592 | tf_op jit(solution)/shard_map/all_to_all | solution.py:167
  147.0 136.8 %all-to-all-start.3 = ((bf16[16,8,2,64,128]{4,3,2,1,0:T(8,128)(2,1)}), bf16[16,8,2,64,128]{4,3,2,1,0:T(8,128)(2,1)}, u32[]{:S(2)}, u32[]{:S(2)}) async-start(bf16[16,8,2,64,128]{4,3,2,1,0:T(8,128)(2,1)} %spread.2), calls=%async_computation.3 | async-start | bytes 8388608 | tf_op jit(solution)/shard_map/all_to_all | solution.py:181
  283.8 119.4 %all-to-all-start.5 = ((bf16[16,8,2,64,128]{4,3,2,1,0:T(8,128)(2,1)}), bf16[16,8,2,64,128]{4,3,2,1,0:T(8,128)(2,1)}, u32[]{:S(2)}, u32[]{:S(2)}) async-start(bf16[16,8,2,64,128]{4,3,2,1,0:T(8,128)(2,1)} %spread.3), calls=%async_computation.5 | async-start | bytes 8388608 | tf_op jit(solution)/shard_map/all_to_all | solution.py:181
  403.2 10.0 %copy-start.7 = (f32[16,128]{1,0:T(8,128)}, f32[16,128]{1,0:T(8,128)S(1)}, u32[]{:S(2)}) copy-start(f32[16,128]{1,0:T(8,128)S(1)} %select_reduce_fusion) | copy-start | bytes 24580

commit v2 on v0

v2 whole, which is shorter than its diff:
```python
import functools

import numpy as np
import jax
import jax.numpy as jnp
from jax import lax
from jax.experimental import pallas as pl
from jax.experimental.pallas import tpu as pltpu
from jax.sharding import PartitionSpec as P

HEAD_DIM = 128
HAD = 128
CHUNKS = ((0, 32), (32, 48), (80, 48))
ORDER = (
    ("start", 0),
    ("start", 1),
    ("y_turn", 0),
    ("core_turn", 0),
    ("y_turn", 1),
    ("start", 2),
    ("core_turn", 1),
    ("spread", 0),
    ("regroup", 0),
    ("y_turn", 2),
    ("spread", 1),
    ("core_turn", 2),
    ("pack", 0),
    ("regroup", 1),
    ("spread", 2),
    ("pack", 1),
    ("regroup", 2),
    ("pack", 2),
)
TAIL = 16
VMEM_BYTES = 24 * 1024 * 1024
BOTH = ("fsdp", "tp")


def hadamard_table(order):
    matrix = np.ones((1, 1), np.float32)
    while matrix.shape[0] < order:
        matrix = np.block([[matrix, matrix], [matrix, -matrix]])
    return matrix


def butterfly(values):
    values = list(values)
    half = 1
    while half < len(values):
        for low in range(len(values)):
            if not low & half:
                first, second = values[low], values[low + half]
                values[low], values[low + half] = first + second, first - second
        half *= 2
    return values


def hop(array, flip):
    size = lax.axis_size("fsdp")
    return lax.ppermute(array, "fsdp", [(i, i ^ flip) for i in range(size)])


def ring_exchange(blocks):
    own, one, three, two_a, two_b = blocks
    two_a, two_b = hop(two_a, 2), hop(two_b, 6)
    one, three = hop(one, 2), hop(three, 6)
    return own, one, three, hop(two_a, 6), hop(two_b, 2)


def owner_table(core):
    one, two = ((1, 3), (3, 1))[core]
    table = np.zeros((4, 4), np.int32)
    for i in range(4):
        for j in range(4):
            x = (i & 1) * one ^ (j & 1) * two
            z = (i >> 1) * one ^ (j >> 1) * two
            table[i, j] = 4 * z + x
    return table


def pair_exchange(array, second):
    groups, owners = lax.axis_size("fsdp"), lax.axis_size("tp")
    members = []
    for f in range(groups):
        table = owner_table(f & 1)
        table = table if second else table.T
        members += [[f * owners + int(t) for t in row] for row in table]
    return lax.all_to_all(array, BOTH, split_axis=0, concat_axis=0, tiled=True, axis_index_groups=members)


def local_turn_kernel(rows_a, flip_ref, weight_ref, signs_ref, *refs):
    out_refs, turned = refs[:-1], refs[-1]
    columns = jnp.concatenate([weight_ref[a * HAD : (a + 1) * HAD, :].T for a in range(rows_a)], axis=0)
    turned[...] = jnp.dot(columns, signs_ref[...], preferred_element_type=jnp.float32)
    for index, (first, chans) in enumerate(CHUNKS):
        own, one, three, two_a, two_b = out_refs[5 * index : 5 * index + 5]
        for low in range(0, chans, 16):
            outs = []
            for a in range(rows_a):
                start = a * HEAD_DIM + first + low
                outs.append(turned[start : start + 16, :] * (flip_ref[a] * (1.0 / HAD)))
            outs = butterfly(outs)
            for a in range(rows_a):
                offset, e = a // 4, a % 4
                if offset == 2:
                    out_ref, e = (two_a, two_b)[e // 2], e % 2
                else:
                    out_ref = {0: own, 1: one, 3: three}[offset]
                out_ref[e * chans + low : e * chans + low + 16, :] = outs[a].astype(jnp.bfloat16)


def pieces(head, e, chans, low):
    whole = (head * 4 + e) * chans + low
    half = (head * 2 + e % 2) * chans + low
    return (0, whole), (1, whole), (3 + e // 2, half), (2, whole)


def y_turn_kernel(heads, chans, flip_in_ref, flip_out_ref, *refs):
    in_refs, out_ref = refs[:-1], refs[-1]
    for head in range(heads):
        for e in range(4):
            for low in range(0, chans, 16):
                parts = [
                    in_refs[array][row : row + 16, :].astype(jnp.float32) * flip_in_ref[o]
                    for o, (array, row) in enumerate(pieces(head, e, chans, low))
                ]
                row = (head * 4 + e) * chans + low
                for o, value in enumerate(butterfly(parts)):
                    out_ref[o, row : row + 16, :] = (value * flip_out_ref[o]).astype(jnp.bfloat16)


def join_parts(value, chans):
    return value + pltpu.roll(value, HAD - chans, 1)


def split_parts(value, chans):
    high = value.astype(jnp.bfloat16).astype(jnp.float32)
    lane = lax.broadcasted_iota(jnp.int32, value.shape, 1)
    both = jnp.where(lane < chans, high, pltpu.roll(value - high, chans, 1))
    return jnp.where(lane < 2 * chans, both, 0.0).astype(jnp.bfloat16)


def core_turn_kernel(heads, chans, sign_ref, mine_ref, other_ref, *out_refs):
    row_id = lax.broadcasted_iota(jnp.int32, (TAIL, HAD), 0)
    tail = jnp.zeros((TAIL, HAD), jnp.float32)
    sign = sign_ref[0]
    for head in range(heads):
        columns = []
        for low in range(0, chans, 16):
            largest = None
            for e in range(4):
                row = (head * 4 + e) * chans + low
                for o, (array, out_row) in enumerate(pieces(head, e, chans, low)):
                    mine = mine_ref[o, row : row + 16, :].astype(jnp.float32)
                    other = other_ref[o, row : row + 16, :].astype(jnp.float32)
                    out_refs[array][out_row : out_row + 16, :] = (other + mine * sign).astype(jnp.bfloat16)
                    magnitude = jnp.abs(mine) + jnp.abs(other)
                    largest = magnitude if largest is None else jnp.maximum(largest, magnitude)
            columns.append(largest)
        columns.append(jnp.zeros((HAD - chans, HAD), jnp.float32))
        peak = jnp.max(jnp.concatenate(columns, axis=0).T, axis=0, keepdims=True)
        tail = jnp.where(row_id == head, peak, tail)
    tail = split_parts(tail, chans)
    for out_ref in out_refs[:4]:
        out_ref[out_ref.shape[0] - TAIL :, :] = tail


def spread_kernel(heads, chans, head_ref, *refs):
    in_refs, out_ref = refs[:-1], refs[-1]
    peaks = None
    for in_ref in in_refs[:4]:
        part = join_parts(in_ref[in_ref.shape[0] - TAIL :, :].astype(jnp.float32), chans)
        peaks = part if peaks is None else jnp.maximum(peaks, part)
    row_id = lax.broadcasted_iota(jnp.int32, (TAIL, HAD), 0)
    span = 4 * chans
    half = 2 * chans
    own, one, three, two_a, two_b = in_refs
    for slot in range(16):
        head = head_ref[slot]
        whole = pl.ds(pl.multiple_of(head * span, 16), span)
        part = pl.ds(pl.multiple_of(head * half, 16), half)
        i, j = slot // 4, slot % 4
        out_ref[i, j, 0:span, :] = own[whole, :]
        out_ref[i, j, span : 2 * span, :] = one[whole, :]
        out_ref[i, j, 2 * span : 2 * span + half, :] = two_a[part, :]
        out_ref[i, j, 2 * span + half : 3 * span, :] = two_b[part, :]
        out_ref[i, j, 3 * span : 4 * span, :] = three[whole, :]
        peak = jnp.sum(jnp.where(row_id == head, peaks, 0.0), axis=0, keepdims=True)
        out_ref[i, j, 4 * span :, :] = split_parts(jnp.broadcast_to(peak, (TAIL, HAD)), chans)


def regroup_kernel(in_ref, out_ref):
    for i in range(4):
        for j in range(4):
            out_ref[j, i] = in_ref[i, j]


def pack_kernel(owners, chunk, has_past, from_ref, live_ref, place_ref, in_ref, *refs):
    first, chans = chunk
    past_ref = refs[0] if has_past else None
    peak_ref, out_ref, buffer, sems = refs[-4:]
    lane = lax.broadcasted_iota(jnp.int32, (TAIL, HAD), 1)
    depth = buffer.shape[0]
    copies = [None] * depth
    for slot in range(owners):
        part = slot % depth
        if copies[part] is not None:
            copies[part].wait()
        live = live_ref[slot] != 0
        origin = from_ref[slot]
        i, j = origin // 4, origin % 4
        tail = in_ref[i, j, 16 * chans :, :].astype(jnp.float32)
        row = jnp.where((lane < chans) & live, join_parts(tail, chans), 0.0)[:1, :]
        scale = jnp.where(live, 1.0 / (row + 1e-06), 0.0)
        scale = jnp.broadcast_to(scale, (HEAD_DIM, HAD)).T[:chans, :]
        row = pltpu.roll(jnp.broadcast_to(row, (8, HAD)), first, 1)[:1, :] if first else row
        if has_past:
            row = row + past_ref[slot : slot + 1, :]
        peak_ref[slot : slot + 1, :] = row
        for o in range(4):
            for e in range(4):
                start = (o * 4 + e) * chans
                lanes = pl.ds(pl.multiple_of(place_ref[o] + e * HAD, HAD), HAD)
                block = in_ref[i, j, start : start + chans, :]
                buffer[part, :, lanes] = (block.astype(jnp.float32) * scale).astype(jnp.bfloat16)
        copies[part] = pltpu.make_async_copy(
            buffer.at[part], out_ref.at[0, slot, first : first + chans, :], sems.at[part]
        )
        copies[part].start()
    for copy in copies:
        copy.wait()


def per_device(qkv_weight, placement):
    rows_local, cols_local = qkv_weight.shape
    heads = cols_local // HEAD_DIM
    owners = lax.axis_size("tp")
    rows_a = rows_local // HAD
    params = pltpu.CompilerParams(vmem_limit_bytes=VMEM_BYTES)
    any_spec = pl.BlockSpec(memory_space=pl.ANY)
    smem_spec = pl.BlockSpec(memory_space=pltpu.SMEM)
    vmem_spec = pl.BlockSpec(memory_space=pltpu.VMEM)

    def block_of(rows):
        return jax.ShapeDtypeStruct((rows, HAD), jnp.bfloat16)

    def blocks_of(chans, tail):
        whole, half = heads * 4 * chans, heads * 2 * chans
        return [block_of(rows) for rows in (whole + tail, whole + tail, whole + tail, half + tail, half)]

    me = lax.axis_index("tp")
    group = lax.axis_index("fsdp")
    y, core = group // 2, group % 2
    table_y = jnp.asarray(hadamard_table(4))
    flip_a = jnp.asarray(hadamard_table(rows_a))[4 * y]
    flip_in = table_y[y]
    flip_out = flip_in * flip_in[y]
    sign = (1 - 2 * core).astype(jnp.float32).reshape(1)
    place = (jnp.arange(4, dtype=jnp.int32) ^ y) * (4 * HAD)

    blocks = placement.reshape(owners, heads)
    head_ids = jnp.arange(heads, dtype=jnp.int32)
    owner_ids = jnp.arange(owners, dtype=jnp.int32)
    by_core = [owner_table(c) for c in range(2)]
    send_to = jnp.where(core == 0, jnp.asarray(by_core[0].reshape(-1)), jnp.asarray(by_core[1].reshape(-1)))
    source = jnp.where(core == 0, jnp.asarray(by_core[0].T.reshape(-1)), jnp.asarray(by_core[1].T.reshape(-1)))
    my_owners = lax.dynamic_slice_in_dim(blocks, me, 1, axis=0)
    head_for = jnp.sum(jnp.where(my_owners == send_to[:, None], head_ids[None, :], 0), axis=1)
    has = jnp.any(blocks == me, axis=1)
    present = jnp.any(has[None, :] & (source[:, None] == owner_ids[None, :]), axis=1)
    rank = jnp.sum(((source[None, :] < source[:, None]) & present[None, :]).astype(jnp.int32), axis=1)
    taken = present[None, :] & (rank[None, :] == owner_ids[:, None])
    come_from = jnp.sum(jnp.where(taken, owner_ids[None, :], 0), axis=1)
    live = jnp.any(taken, axis=1).astype(jnp.int32)

    signs = jnp.asarray(hadamard_table(HAD), jnp.bfloat16)
    first_blocks = [shape for _, chans in CHUNKS for shape in blocks_of(chans, 0)]
    turned = pl.pallas_call(
        functools.partial(local_turn_kernel, rows_a),
        grid=(heads,),
        in_specs=[
            smem_spec,
            pl.BlockSpec((rows_local, HEAD_DIM), lambda h: (0, h)),
            pl.BlockSpec((HAD, HAD), lambda h: (0, 0)),
        ],
        out_specs=[pl.BlockSpec((shape.shape[0] // heads, HAD), lambda h: (h, 0)) for shape in first_blocks],
        out_shape=first_blocks,
        scratch_shapes=[pltpu.VMEM((rows_local, HAD), jnp.float32)],
        compiler_params=params,
        name="local_turn",
    )(flip_a, qkv_weight, signs)

    state = [turned[5 * index : 5 * index + 5] for index in range(len(CHUNKS))]
    token = None
    past = []

    def tie(arrays):
        if token is None:
            return list(arrays)
        return list(lax.optimization_barrier((list(arrays), token))[0])

    for stage, index in ORDER:
        first, chans = chunk = CHUNKS[index]
        arrays = tie(state[index])
        if stage == "start":
            state[index] = ring_exchange(arrays)
        elif stage == "y_turn":
            token = pl.pallas_call(
                functools.partial(y_turn_kernel, heads, chans),
                in_specs=[smem_spec] * 2 + [vmem_spec] * 5,
                out_specs=vmem_spec,
                out_shape=jax.ShapeDtypeStruct((4, heads * 4 * chans, HAD), jnp.bfloat16),
                compiler_params=params,
                name="y_turn",
            )(flip_in, flip_out, *arrays)
            state[index] = [token, hop(token, 1)]
        elif stage == "core_turn":
            outs = pl.pallas_call(
                functools.partial(core_turn_kernel, heads, chans),
                in_specs=[smem_spec] + [vmem_spec] * 2,
                out_specs=[vmem_spec] * 5,
                out_shape=blocks_of(chans, TAIL)[:4] + blocks_of(chans, 0)[4:],
                compiler_params=params,
                name="core_turn",
            )(sign, *arrays)
            token = outs[0]
            state[index] = ring_exchange(outs)
        elif stage == "spread":
            token = pl.pallas_call(
                functools.partial(spread_kernel, heads, chans),
                in_specs=[smem_spec] + [vmem_spec] * 5,
                out_specs=vmem_spec,
                out_shape=jax.ShapeDtypeStruct((4, 4, 16 * chans + TAIL, HAD), jnp.bfloat16),
                compiler_params=params,
                name="spread",
            )(head_for, *arrays)
            state[index] = [pair_exchange(token, False)]
        elif stage == "regroup":
            token = pl.pallas_call(
                regroup_kernel,
                in_specs=[vmem_spec],
                out_specs=vmem_spec,
                out_shape=jax.ShapeDtypeStruct(arrays[0].shape, jnp.bfloat16),
                compiler_params=params,
                name="regroup",
            )(*arrays)
            state[index] = [pair_exchange(token, True)]
        else:
            past = pl.pallas_call(
                functools.partial(pack_kernel, owners, chunk, bool(past)),
                in_specs=[smem_spec] * 3 + [vmem_spec] + ([vmem_spec, any_spec] if past else []),
                out_specs=[vmem_spec, any_spec],
                out_shape=[
                    jax.ShapeDtypeStruct((owners, HEAD_DIM), jnp.float32),
                    jax.ShapeDtypeStruct((1, owners, HEAD_DIM, rows_local), jnp.bfloat16),
                ],
                scratch_shapes=[pltpu.VMEM((3, chans, rows_local), jnp.bfloat16), pltpu.SemaphoreType.DMA((3,))],
                input_output_aliases={5: 1} if past else {},
                compiler_params=params,
                name="pack",
            )(come_from, live, place, *arrays, *past)
            token = past[0]
    peaks, packed = past
    return packed, peaks[None]


def solution(mesh):
    in_specs = (P("fsdp", "tp"), P())
    out_specs = (P("tp", None, None, "fsdp"), P("tp", None, None))
    return jax.shard_map(
        per_device, mesh=mesh, in_specs=in_specs, out_specs=out_specs, check_vma=False
    )
```

time: 767 us -> 286 us (0.37); the launches traced: 758 us -> 285 us
  local copies, waits for them, and re-layouts: 368 us -> 25.8 us
  waiting for transfers between devices: 309 us -> 108 us
  blocking collectives: 0 us -> 47.9 us
  matrix products: 42.2 us -> 0 us
  Pallas kernels: 0 us -> 39.8 us
  starting transfers between devices: 30.2 us -> 59.8 us
    all_to_all x5 -> x4, waiting for transfers between devices: 309 us -> 20.8 us  [pair_exchange(): lax.all_to_all(array, BOTH, split_axis=0, concat_axis=0, tiled=True, axis...]
    unnamed x13 -> x84, local copies, waits for them, and re-layouts: 203 us -> 23.8 us
    ppermute x0 -> x39, waiting for transfers between devices: none -> 87.1 us  [hop(): return lax.ppermute(array, 'fsdp', [(i, i ^ flip) for i in range(size)])]
    all_to_all x5 -> x0, local copies, waits for them, and re-layouts: 79.1 us -> none  [the longest x1 69.9 us: per_device(): lax.all_to_all(outgoing, 'fsdp', split_axis=3, concat_axis=2, tiled=True)]
    convert_element_type x3 -> x0, local copies, waits for them, and re-layouts: 60.2 us -> none  [the longest x1 53.5 us: per_device(): outgoing = jnp.einsum('tsj,jcd->tscd', select_b, code_rows, preferred_ele...]
    all_to_all x0 -> x2, blocking collectives: none -> 47.9 us  [pair_exchange(): lax.all_to_all(array, BOTH, split_axis=0, concat_axis=0, tiled=True, axis...]
    dot_general x6 -> x0, matrix products: 42.2 us -> none  [the longest x1 16 us: per_device(): jnp.einsum('kts,tscd->kcd', packing_b, arrived, preferred_element_type=jn...]
    ppermute x0 -> x39, starting transfers between devices: none -> 41.5 us  [hop(): return lax.ppermute(array, 'fsdp', [(i, i ^ flip) for i in range(size)])]
  transfers between devices with their start and end apart: 5 -> 43, of which waited for: 3 -> 20; matrix products, arithmetic and copies ran while one was open for 42% -> 1% of each run, Pallas kernels for 0% -> 7%
where the time goes in v2:
time: 286 us; the launch traced here: 285 us
  waiting for transfers between devices  108 us (38%)
  starting transfers between devices  59.8 us (21%)
  blocking collectives  47.9 us (17%)
  Pallas kernels  39.8 us (14%)
  local copies, waits for them, and re-layouts  25.8 us (9%)
    ppermute x39, waiting for transfers between devices, hop(): return lax.ppermute(array, 'fsdp', [(i, i ^ flip) for i in range(size)])  87.1 us
    all_to_all x2, blocking collectives, pair_exchange(): lax.all_to_all(array, BOTH, split_axis=0, concat_axis=0, tiled=True, axis...  47.9 us
    ppermute x39, starting transfers between devices, hop(): return lax.ppermute(array, 'fsdp', [(i, i ^ flip) for i in range(size)])  41.5 us
    unnamed x84, local copies, waits for them, and re-layouts  23.8 us
    all_to_all x4, waiting for transfers between devices, pair_exchange(): lax.all_to_all(array, BOTH, split_axis=0, concat_axis=0, tiled=True, axis...  20.8 us
    all_to_all x4, starting transfers between devices, pair_exchange(): lax.all_to_all(array, BOTH, split_axis=0, concat_axis=0, tiled=True, axis...  18.3 us
    pallas_call x3, Pallas kernels, per_device(): pl.pallas_call(functools.partial(pack_kernel, owners, chunk, bool(past)),...  17.8 us
    pallas_call x3, Pallas kernels, per_device(): pl.pallas_call(functools.partial(spread_kernel, heads, chans), in_specs=[...  6.39 us
  transfers between devices with their start and end apart: 43, of which 20 were waited for; matrix products, arithmetic and copies ran while one was open for 1% of the time, Pallas kernels for 7%

profile of v2, /device:TPU:0, one launch (start us, length us, event | category | flops | bytes accessed | tf_op | source)
XLA Modules:
  0.0 285.2 jit_solution(10704487338968409107)
XLA Ops:
  1.4 2.3 copy-done.6
  4.5 5.6 %local_turn.1 = (bf16[1152,128]{1,0:T(8,128)(2,1)S(1)}, bf16[1152,128]{1,0:T(8,128)(2,1)S(1)}, bf16[1152,128]{1,0:T(8,128)(2,1)S(1)}, bf16[576,128]{1,0:T(8,128)...) custom-call(f32[16]{0:T(128)S(1)} %fusion.5.flip_ref, ...), custom_call_target="tpu_custom_call" | custom-call | tf_op jit(solution)/shard_map/local_turn/pallas_call | solution.py:278
  16.6 1.7 collective-permute-start.8
  18.3 2.2 collective-permute-start.10
  22.2 4.2 %collective-permute-start.9 = (bf16[576,128]{1,0:T(8,128)(2,1)S(1)}, bf16[576,128]{1,0:T(8,128)(2,1)S(1)}, u32[]{:S(2)}, u32[]{:S(2)}) collective-permute-start(bf16[576,128]{1,0:T(8,128)(2,1)S(1)} %collective-permute-done.8), channel_id=1, source_target_pairs={{0,96},{16,112},{32,64},{48,80},{64,32},{80,48},{96,0},{112,16},{1... | collective-permute-start | bytes 442376 | tf_op jit(solution)/shard_map/ppermute | solution.py:60
  27.9 6.4 %collective-permute-done.9.refs_3_ = bf16[576,128]{1,0:T(8,128)(2,1)S(1)} collective-permute-done((bf16[576,128]{1,0:T(8,128)(2,1)S(1)}, bf16[576,128]{1,0:T(8,128)(2,1)S(1)}, u32[]{:S(2)}, u32[]{:S(2)}) %collective-permute-start.9) | collective-permute-done | bytes 147488 | tf_op jit(solution)/shard_map/ppermute | solution.py:60
  35.5 2.3 collective-permute-start.4
  37.8 1.3 collective-permute-start
  39.1 1.1 collective-permute-start.1
  40.2 3.9 %collective-permute-done.2 = bf16[864,128]{1,0:T(8,128)(2,1)} collective-permute-done((bf16[864,128]{1,0:T(8,128)(2,1)}, bf16[864,128]{1,0:T(8,128)(2,1)}, u32[]{:S(2)}, u32[]{:S(2)}) %collective-permute-start.2) | collective-permute-done | bytes 221216 | tf_op jit(solution)/shard_map/ppermute | solution.py:60
  44.0 2.2 collective-permute-start.3
  47.2 11.7 %collective-permute-done.3.refs_3_ = bf16[864,128]{1,0:T(8,128)(2,1)S(1)} collective-permute-done((bf16[864,128]{1,0:T(8,128)(2,1)}, bf16[864,128]{1,0:T(8,128)(2,1)S(1)}, u32[]{:S(2)}, u32[]{:S(2)}) %collective-permute-start.3) | collective-permute-done | bytes 221216 | tf_op jit(solution)/shard_map/ppermute | solution.py:60
  58.9 1.7 y_turn.4.mine_ref
  60.8 2.3 collective-permute-start.23
  63.0 2.0 collective-permute-start.19
  65.1 1.1 collective-permute-start.20
  67.5 1.1 collective-permute-done.23
  68.6 1.6 collective-permute-done.21
  70.1 1.1 collective-permute-start.22
  72.1 1.3 core_turn.4
  76.4 2.5 collective-permute-done.24.refs_4_
  78.8 1.3 spread.3
  80.2 20.0 %all_to_all.30.in_ref = bf16[4,4,528,128]{3,2,1,0:T(8,128)(2,1)S(1)} all-to-all(bf16[4,4,528,128]{3,2,1,0:T(8,128)(2,1)S(1)} %spread.3), channel_id=1, replica_groups={{0,1,4,5},{3,2,7,6},{12,13,8,9},{15,14,11,10},{16,19,28,31},{17,18,29,3..., dimensions={0} | all-to-all | bytes 4325376 | tf_op jit(solution)/shard_map/all_to_all | solution.py:88
  100.3 1.3 copy-done.3
  101.7 6.2 %all-to-all-start.2 = ((bf16[4,4,528,128]{3,2,1,0:T(8,128)(2,1)}), bf16[4,4,528,128]{3,2,1,0:T(8,128)(2,1)S(1)}, u32[]{:S(2)}, u32[]{:S(2)}) async-start(bf16[4,4,528,128]{3,2,1,0:T(8,128)(2,1)} %copy-done.3), calls=%async_computation.2 | async-start | bytes 4325376 | tf_op jit(solution)/shard_map/all_to_all | solution.py:88
  108.1 1.2 collective-permute-start.17
  109.3 1.4 collective-permute-start.13
  110.7 5.3 %collective-permute-done.15 = bf16[864,128]{1,0:T(8,128)(2,1)S(1)} collective-permute-done((bf16[864,128]{1,0:T(8,128)(2,1)}, bf16[864,128]{1,0:T(8,128)(2,1)S(1)}, u32[]{:S(2)}, u32[]{:S(2)}) %collective-permute-start.15) | collective-permute-done | bytes 221216 | tf_op jit(solution)/shard_map/ppermute | solution.py:60
  116.0 1.1 collective-permute-start.16
  118.3 1.3 collective-permute-start.29
  120.3 5.0 %collective-permute-done.16.refs_3_ = bf16[864,128]{1,0:T(8,128)(2,1)S(1)} collective-permute-done((bf16[864,128]{1,0:T(8,128)(2,1)S(1)}, bf16[864,128]{1,0:T(8,128)(2,1)S(1)}, u32[]{:S(2)}, u32[]{:S(2)}) %collective-permute-start.16) | collective-permute-done | bytes 221216 | tf_op jit(solution)/shard_map/ppermute | solution.py:60
  126.3 4.0 %collective-permute-done.18.refs_4_ = bf16[864,128]{1,0:T(8,128)(2,1)S(1)} collective-permute-done((bf16[864,128]{1,0:T(8,128)(2,1)S(1)}, bf16[864,128]{1,0:T(8,128)(2,1)S(1)}, u32[]{:S(2)}, u32[]{:S(2)}) %collective-permute-start.18) | collective-permute-done | bytes 221216 | tf_op jit(solution)/shard_map/ppermute | solution.py:60
  130.3 1.1 collective-permute-start.14
  131.4 2.1 collective-permute-start.31
  133.5 1.6 collective-permute-done.29
  135.1 1.1 collective-permute-start.30
  136.2 17.7 %collective-permute-done.31 = bf16[864,128]{1,0:T(8,128)(2,1)S(1)} collective-permute-done((bf16[864,128]{1,0:T(8,128)(2,1)}, bf16[864,128]{1,0:T(8,128)(2,1)S(1)}, u32[]{:S(2)}, u32[]{:S(2)}) %collective-permute-start.31) | collective-permute-done | bytes 221216 | tf_op jit(solution)/shard_map/ppermute | solution.py:60
  153.9 1.2 y_turn.5.mine_ref
  155.1 1.2 copy-done.4
  156.3 3.5 %collective-permute-done.32.refs_4_ = bf16[864,128]{1,0:T(8,128)(2,1)S(1)} collective-permute-done((bf16[864,128]{1,0:T(8,128)(2,1)S(1)}, bf16[864,128]{1,0:T(8,128)(2,1)S(1)}, u32[]{:S(2)}, u32[]{:S(2)}) %collective-permute-start.32) | collective-permute-done | bytes 221216 | tf_op jit(solution)/shard_map/ppermute | solution.py:60
  159.8 2.5 spread.4
  162.4 1.3 copy-done.1
  163.7 3.7 %all-to-all-start.1 = ((bf16[4,4,784,128]{3,2,1,0:T(8,128)(2,1)}), bf16[4,4,784,128]{3,2,1,0:T(8,128)(2,1)S(1)}, u32[]{:S(2)}, u32[]{:S(2)}) async-start(bf16[4,4,784,128]{3,2,1,0:T(8,128)(2,1)} %spread.4), calls=%async_computation.1 | async-start | bytes 6422528 | tf_op jit(solution)/shard_map/all_to_all | solution.py:88
  168.3 3.1 %collective-permute-done.26.other_ref = bf16[4,1728,128]{2,1,0:T(8,128)(2,1)S(1)} collective-permute-done((bf16[4,1728,128]{2,1,0:T(8,128)(2,1)}, bf16[4,1728,128]{2,1,0:T(8,128)(2,1)S(1)}, u32[]{:S(2)}, u32[]{:S(2)}) %collective-permute-start.26) | collective-permute-done | bytes 1769504 | tf_op jit(solution)/shard_map/ppermute | solution.py:60
  171.4 1.5 copy-done.5
  172.9 1.4 core_turn.5
  177.2 5.6 %pack.3 = (f32[16,128]{1,0:T(8,128)S(1)}, bf16[1,16,128,2048]{3,2,1,0:T(8,128)(2,1)}) custom-call(s32[16]{0:T(128)S(1)} %select_reduce_fusion.1.from_ref, s32[16]{0:T(128)S(1)} %convert_element_type.10.live_ref, s32[4]{0:T(128)S(1)} %xor_multiply_fusion.place_ref, bf16[4,4,528,128]{3,2,1,0:T(8,128)(2,1)S(1)} %copy-done.2), custom_call_target="tpu_custom_call" | custom-call | tf_op jit(solution)/shard_map/pack/pallas_call | solution.py:349
  182.8 5.6 %all-to-all-done.1.in_ref = bf16[4,4,784,128]{3,2,1,0:T(8,128)(2,1)S(1)} async-done(((bf16[4,4,784,128]{3,2,1,0:T(8,128)(2,1)}), bf16[4,4,784,128]{3,2,1,0:T(8,128)(2,1)S(1)}, u32[]{:S(2)}, u32[]{:S(2)}) %all-to-all-start.1) | async-done | bytes 3211296 | tf_op jit(solution)/shard_map/all_to_all | solution.py:88
  188.6 1.7 copy-done
  190.3 3.7 %all-to-all-start.4 = ((bf16[4,4,784,128]{3,2,1,0:T(8,128)(2,1)}), bf16[4,4,784,128]{3,2,1,0:T(8,128)(2,1)S(1)}, u32[]{:S(2)}, u32[]{:S(2)}) async-start(bf16[4,4,784,128]{3,2,1,0:T(8,128)(2,1)} %copy-done), calls=%async_computation.4 | async-start | bytes 6422528 | tf_op jit(solution)/shard_map/all_to_all | solution.py:88
  194.1 2.0 collective-permute-start.33
  196.1 1.0 collective-permute-start.34
  197.1 2.2 collective-permute-start.37
  199.3 3.2 %collective-permute-done.35 = bf16[880,128]{1,0:T(8,128)(2,1)S(1)} collective-permute-done((bf16[880,128]{1,0:T(8,128)(2,1)S(1)}, bf16[880,128]{1,0:T(8,128)(2,1)S(1)}, u32[]{:S(2)}, u32[]{:S(2)}) %collective-permute-start.35) | collective-permute-done | bytes 225312 | tf_op jit(solution)/shard_map/ppermute | solution.py:60
  203.5 9.8 %collective-permute-done.37 = bf16[864,128]{1,0:T(8,128)(2,1)S(1)} collective-permute-done((bf16[864,128]{1,0:T(8,128)(2,1)}, bf16[864,128]{1,0:T(8,128)(2,1)S(1)}, u32[]{:S(2)}, u32[]{:S(2)}) %collective-permute-start.37) | collective-permute-done | bytes 221216 | tf_op jit(solution)/shard_map/ppermute | solution.py:60
  213.3 5.9 %collective-permute-done.38.refs_4_ = bf16[864,128]{1,0:T(8,128)(2,1)S(1)} collective-permute-done((bf16[864,128]{1,0:T(8,128)(2,1)S(1)}, bf16[864,128]{1,0:T(8,128)(2,1)S(1)}, u32[]{:S(2)}, u32[]{:S(2)}) %collective-permute-start.38) | collective-permute-done | bytes 221216 | tf_op jit(solution)/shard_map/ppermute | solution.py:60
  219.3 1.0 copy-done.10
  220.3 2.6 spread.5
  222.9 4.7 %all-to-all-start.3 = ((bf16[4,4,784,128]{3,2,1,0:T(8,128)(2,1)}), bf16[4,4,784,128]{3,2,1,0:T(8,128)(2,1)}, u32[]{:S(2)}, u32[]{:S(2)}) async-start(bf16[4,4,784,128]{3,2,1,0:T(8,128)(2,1)} %spread.5), calls=%async_computation.3 | async-start | bytes 6422528 | tf_op jit(solution)/shard_map/all_to_all | solution.py:88
  227.6 5.8 %pack.4 = (f32[16,128]{1,0:T(8,128)S(1)}, bf16[1,16,128,2048]{3,2,1,0:T(8,128)(2,1)}) custom-call(s32[16]{0:T(128)S(1)} %select_reduce_fusion.1.from_ref, s32[16]{0:T(128)S(1)} %convert_element_type.10.live_ref, s32[4]{0:T(128)S(1)} %xor_multiply_fusion.place_ref, ...), custom_call_target="tpu_custom_call", output_to_operand_aliasing={{1}: (5, {})} | custom-call | tf_op jit(solution)/shard_map/pack/pallas_call | solution.py:349
  233.4 15.2 %all-to-all-done.3.in_ref = bf16[4,4,784,128]{3,2,1,0:T(8,128)(2,1)} async-done(((bf16[4,4,784,128]{3,2,1,0:T(8,128)(2,1)}), bf16[4,4,784,128]{3,2,1,0:T(8,128)(2,1)}, u32[]{:S(2)}, u32[]{:S(2)}) %all-to-all-start.3) | async-done | bytes 3211296 | tf_op jit(solution)/shard_map/all_to_all | solution.py:88
  248.6 2.1 regroup.5
  250.8 27.9 %all_to_all.31.in_ref = bf16[4,4,784,128]{3,2,1,0:T(8,128)(2,1)S(1)} all-to-all(bf16[4,4,784,128]{3,2,1,0:T(8,128)(2,1)S(1)} %regroup.5), channel_id=1, replica_groups={{0,3,12,15},{1,2,13,14},{4,7,8,11},{5,6,9,10},{16,17,20,21},{19,18,23,2..., dimensions={0} | all-to-all | bytes 6422528 | tf_op jit(solution)/shard_map/all_to_all | solution.py:88
  278.6 6.4 %pack.5 = (f32[16,128]{1,0:T(8,128)}, bf16[1,16,128,2048]{3,2,1,0:T(8,128)(2,1)}) custom-call(s32[16]{0:T(128)S(1)} %select_reduce_fusion.1.from_ref, s32[16]{0:T(128)S(1)} %convert_element_type.10.live_ref, s32[4]{0:T(128)S(1)} %xor_multiply_fusion.place_ref, bf16[4,4,784,128]{3,2,1,0:T(8,128)(2,1)S(1)} %all_to_all.31.in_ref, ...), custom_call_target="tpu_custom_call", output_to_operand_aliasing={{1}: (5, {})} | custom-call | tf_op jit(solution)/shard_map/pack/pallas_call | solution.py:349
  (139 shorter events, 27.1 us)
Async XLA Ops:
  0.6 26.0 %copy-start.41 = (f32[4,4]{1,0:T(4,128)S(1)}, f32[4,4]{1,0:T(4,128)}, u32[]{:S(2)}) copy-start(f32[4,4]{1,0:T(4,128)} %constant.65.clone) | copy-start | bytes 196
  1.4 2.3 copy-start.6
  16.6 5.6 %collective-permute-start.8 = (bf16[576,128]{1,0:T(8,128)(2,1)S(1)}, bf16[576,128]{1,0:T(8,128)(2,1)S(1)}, u32[]{:S(2)}, u32[]{:S(2)}) collective-permute-start(bf16[576,128]{1,0:T(8,128)(2,1)S(1)} %get-tuple-element.93), channel_id=1, source_target_pairs={{0,32},{16,48},{32,0},{48,16},{64,96},{80,112},{96,64},{112,80},{1... | collective-permute-start | bytes 442376 | tf_op jit(solution)/shard_map/ppermute | solution.py:60
  18.3 8.2 %collective-permute-start.10 = (bf16[576,128]{1,0:T(8,128)(2,1)S(1)}, bf16[576,128]{1,0:T(8,128)(2,1)S(1)}, u32[]{:S(2)}, u32[]{:S(2)}) collective-permute-start(bf16[576,128]{1,0:T(8,128)(2,1)S(1)} %get-tuple-element.94), channel_id=1, source_target_pairs={{0,96},{16,112},{32,64},{48,80},{64,32},{80,48},{96,0},{112,16},{1... | collective-permute-start | bytes 442376 | tf_op jit(solution)/shard_map/ppermute | solution.py:60
  20.5 13.8 %collective-permute-start.6 = (bf16[1152,128]{1,0:T(8,128)(2,1)S(1)}, bf16[1152,128]{1,0:T(8,128)(2,1)S(1)}, u32[]{:S(2)}, u32[]{:S(2)}) collective-permute-start(bf16[1152,128]{1,0:T(8,128)(2,1)S(1)} %get-tuple-element.91), channel_id=1, source_target_pairs={{0,32},{16,48},{32,0},{48,16},{64,96},{80,112},{96,64},{112,80},{1... | collective-permute-start | bytes 884744 | tf_op jit(solution)/shard_map/ppermute | solution.py:60
  21.2 13.1 %collective-permute-start.7 = (bf16[1152,128]{1,0:T(8,128)(2,1)S(1)}, bf16[1152,128]{1,0:T(8,128)(2,1)S(1)}, u32[]{:S(2)}, u32[]{:S(2)}) collective-permute-start(bf16[1152,128]{1,0:T(8,128)(2,1)S(1)} %get-tuple-element.92), channel_id=1, source_target_pairs={{0,96},{16,112},{32,64},{48,80},{64,32},{80,48},{96,0},{112,16},{1... | collective-permute-start | bytes 884744 | tf_op jit(solution)/shard_map/ppermute | solution.py:60
  22.2 12.1 %collective-permute-start.9 = (bf16[576,128]{1,0:T(8,128)(2,1)S(1)}, bf16[576,128]{1,0:T(8,128)(2,1)S(1)}, u32[]{:S(2)}, u32[]{:S(2)}) collective-permute-start(bf16[576,128]{1,0:T(8,128)(2,1)S(1)} %collective-permute-done.8), channel_id=1, source_target_pairs={{0,96},{16,112},{32,64},{48,80},{64,32},{80,48},{96,0},{112,16},{1... | collective-permute-start | bytes 442376 | tf_op jit(solution)/shard_map/ppermute | solution.py:60
  26.5 7.8 %collective-permute-start.11 = (bf16[576,128]{1,0:T(8,128)(2,1)S(1)}, bf16[576,128]{1,0:T(8,128)(2,1)S(1)}, u32[]{:S(2)}, u32[]{:S(2)}) collective-permute-start(bf16[576,128]{1,0:T(8,128)(2,1)S(1)} %collective-permute-done.10), channel_id=1, source_target_pairs={{0,32},{16,48},{32,0},{48,16},{64,96},{80,112},{96,64},{112,80},{1... | collective-permute-start | bytes 442376 | tf_op jit(solution)/shard_map/ppermute | solution.py:60
  35.3 30.8 %copy-start.39 = (s32[16]{0:T(128)S(1)}, s32[16]{0:T(128)}, u32[]{:S(2)}) copy-start(s32[16]{0:T(128)} %constant.68.clone) | copy-start | bytes 196
  35.3 30.8 %copy-start.40 = (s32[16]{0:T(128)S(1)}, s32[16]{0:T(128)}, u32[]{:S(2)}) copy-start(s32[16]{0:T(128)} %constant.67.clone) | copy-start | bytes 196
  35.3 10.9 %collective-permute-start.12 = (bf16[4,1152,128]{2,1,0:T(8,128)(2,1)S(1)}, bf16[4,1152,128]{2,1,0:T(8,128)(2,1)S(1)}, u32[]{:S(2)}, u32[]{:S(2)}) collective-permute-start(bf16[4,1152,128]{2,1,0:T(8,128)(2,1)S(1)} %y_turn.3.mine_ref), channel_id=1, source_target_pairs={{0,16},{16,0},{32,48},{48,32},{64,80},{80,64},{96,112},{112,96},{1... | collective-permute-start | bytes 3538952 | tf_op jit(solution)/shard_map/ppermute | solution.py:60
  35.4 8.6 %collective-permute-start.2 = (bf16[864,128]{1,0:T(8,128)(2,1)}, bf16[864,128]{1,0:T(8,128)(2,1)}, u32[]{:S(2)}, u32[]{:S(2)}) collective-permute-start(bf16[864,128]{1,0:T(8,128)(2,1)} %copy-done.32), channel_id=1, source_target_pairs={{0,32},{16,48},{32,0},{48,16},{64,96},{80,112},{96,64},{112,80},{1... | collective-permute-start | bytes 663560 | tf_op jit(solution)/shard_map/ppermute | solution.py:60
  35.5 10.7 %collective-permute-start.4 = (bf16[864,128]{1,0:T(8,128)(2,1)}, bf16[864,128]{1,0:T(8,128)(2,1)}, u32[]{:S(2)}, u32[]{:S(2)}) collective-permute-start(bf16[864,128]{1,0:T(8,128)(2,1)} %copy-done.30), channel_id=1, source_target_pairs={{0,96},{16,112},{32,64},{48,80},{64,32},{80,48},{96,0},{112,16},{1... | collective-permute-start | bytes 663560 | tf_op jit(solution)/shard_map/ppermute | solution.py:60
  37.8 21.1 %collective-permute-start = (bf16[1728,128]{1,0:T(8,128)(2,1)}, bf16[1728,128]{1,0:T(8,128)(2,1)S(1)}, u32[]{:S(2)}, u32[]{:S(2)}) collective-permute-start(bf16[1728,128]{1,0:T(8,128)(2,1)} %copy-done.24), channel_id=1, source_target_pairs={{0,32},{16,48},{32,0},{48,16},{64,96},{80,112},{96,64},{112,80},{1... | collective-permute-start | bytes 1327112 | tf_op jit(solution)/shard_map/ppermute | solution.py:60
  39.1 19.8 %collective-permute-start.1 = (bf16[1728,128]{1,0:T(8,128)(2,1)}, bf16[1728,128]{1,0:T(8,128)(2,1)}, u32[]{:S(2)}, u32[]{:S(2)}) collective-permute-start(bf16[1728,128]{1,0:T(8,128)(2,1)} %copy-done.23), channel_id=1, source_target_pairs={{0,96},{16,112},{32,64},{48,80},{64,32},{80,48},{96,0},{112,16},{1... | collective-permute-start | bytes 1327112 | tf_op jit(solution)/shard_map/ppermute | solution.py:60
  44.0 14.8 %collective-permute-start.3 = (bf16[864,128]{1,0:T(8,128)(2,1)}, bf16[864,128]{1,0:T(8,128)(2,1)S(1)}, u32[]{:S(2)}, u32[]{:S(2)}) collective-permute-start(bf16[864,128]{1,0:T(8,128)(2,1)} %collective-permute-done.2), channel_id=1, source_target_pairs={{0,96},{16,112},{32,64},{48,80},{64,32},{80,48},{96,0},{112,16},{1... | collective-permute-start | bytes 663560 | tf_op jit(solution)/shard_map/ppermute | solution.py:60
  46.2 12.7 %collective-permute-start.5 = (bf16[864,128]{1,0:T(8,128)(2,1)}, bf16[864,128]{1,0:T(8,128)(2,1)}, u32[]{:S(2)}, u32[]{:S(2)}) collective-permute-start(bf16[864,128]{1,0:T(8,128)(2,1)} %collective-permute-done.4), channel_id=1, source_target_pairs={{0,32},{16,48},{32,0},{48,16},{64,96},{80,112},{96,64},{112,80},{1... | collective-permute-start | bytes 663560 | tf_op jit(solution)/shard_map/ppermute | solution.py:60
  47.2 13.4 %copy-start.13 = (bf16[1168,128]{1,0:T(8,128)(2,1)}, bf16[1168,128]{1,0:T(8,128)(2,1)S(1)}, u32[]{:S(2)}) copy-start(bf16[1168,128]{1,0:T(8,128)(2,1)S(1)} %get-tuple-element.115.refs_0_) | copy-start | bytes 897028
  47.2 13.4 %copy-start.25 = (bf16[1168,128]{1,0:T(8,128)(2,1)}, bf16[1168,128]{1,0:T(8,128)(2,1)S(1)}, u32[]{:S(2)}) copy-start(bf16[1168,128]{1,0:T(8,128)(2,1)S(1)} %get-tuple-element.109) | copy-start | bytes 897028
  47.2 13.5 %copy-start.26 = (bf16[1168,128]{1,0:T(8,128)(2,1)}, bf16[1168,128]{1,0:T(8,128)(2,1)S(1)}, u32[]{:S(2)}) copy-start(bf16[1168,128]{1,0:T(8,128)(2,1)S(1)} %get-tuple-element.108) | copy-start | bytes 897028
  47.2 13.5 %copy-start.34 = (bf16[592,128]{1,0:T(8,128)(2,1)}, bf16[592,128]{1,0:T(8,128)(2,1)S(1)}, u32[]{:S(2)}) copy-start(bf16[592,128]{1,0:T(8,128)(2,1)S(1)} %get-tuple-element.110) | copy-start | bytes 454660
  47.2 13.5 %copy-start.35 = (bf16[576,128]{1,0:T(8,128)(2,1)}, bf16[576,128]{1,0:T(8,128)(2,1)S(1)}, u32[]{:S(2)}) copy-start(bf16[576,128]{1,0:T(8,128)(2,1)S(1)} %get-tuple-element.111) | copy-start | bytes 442372
  60.7 11.4 %collective-permute-start.25 = (bf16[4,1728,128]{2,1,0:T(8,128)(2,1)S(1)}, bf16[4,1728,128]{2,1,0:T(8,128)(2,1)S(1)}, u32[]{:S(2)}, u32[]{:S(2)}) collective-permute-start(bf16[4,1728,128]{2,1,0:T(8,128)(2,1)S(1)} %y_turn.4.mine_ref), channel_id=1, source_target_pairs={{0,16},{16,0},{32,48},{48,32},{64,80},{80,64},{96,112},{112,96},{1... | collective-permute-start | bytes 5308424 | tf_op jit(solution)/shard_map/ppermute | solution.py:60
  60.8 7.8 %collective-permute-start.23 = (bf16[576,128]{1,0:T(8,128)(2,1)}, bf16[576,128]{1,0:T(8,128)(2,1)}, u32[]{:S(2)}, u32[]{:S(2)}) collective-permute-start(bf16[576,128]{1,0:T(8,128)(2,1)} %copy-done.35), channel_id=1, source_target_pairs={{0,96},{16,112},{32,64},{48,80},{64,32},{80,48},{96,0},{112,16},{1... | collective-permute-start | bytes 442376 | tf_op jit(solution)/shard_map/ppermute | solution.py:60
  63.0 7.1 %collective-permute-start.21 = (bf16[592,128]{1,0:T(8,128)(2,1)}, bf16[592,128]{1,0:T(8,128)(2,1)}, u32[]{:S(2)}, u32[]{:S(2)}) collective-permute-start(bf16[592,128]{1,0:T(8,128)(2,1)} %copy-done.34), channel_id=1, source_target_pairs={{0,32},{16,48},{32,0},{48,16},{64,96},{80,112},{96,64},{112,80},{1... | collective-permute-start | bytes 454664 | tf_op jit(solution)/shard_map/ppermute | solution.py:60
  63.0 15.8 %collective-permute-start.19 = (bf16[1168,128]{1,0:T(8,128)(2,1)}, bf16[1168,128]{1,0:T(8,128)(2,1)}, u32[]{:S(2)}, u32[]{:S(2)}) collective-permute-start(bf16[1168,128]{1,0:T(8,128)(2,1)} %copy-done.26), channel_id=1, source_target_pairs={{0,32},{16,48},{32,0},{48,16},{64,96},{80,112},{96,64},{112,80},{1... | collective-permute-start | bytes 897032 | tf_op jit(solution)/shard_map/ppermute | solution.py:60
  65.1 13.7 %collective-permute-start.20 = (bf16[1168,128]{1,0:T(8,128)(2,1)}, bf16[1168,128]{1,0:T(8,128)(2,1)}, u32[]{:S(2)}, u32[]{:S(2)}) collective-permute-start(bf16[1168,128]{1,0:T(8,128)(2,1)} %copy-done.25), channel_id=1, source_target_pairs={{0,96},{16,112},{32,64},{48,80},{64,32},{80,48},{96,0},{112,16},{1... | collective-permute-start | bytes 897032 | tf_op jit(solution)/shard_map/ppermute | solution.py:60
  67.5 3.7 %copy-start.36 = (s32[16,9]{1,0:T(8,128)}, s32[16,9]{1,0:T(8,128)S(1)}, u32[]{:S(2)}) copy-start(s32[16,9]{1,0:T(8,128)S(1)} %reshape.18) | copy-start | bytes 1732
  67.5 11.3 %copy-start.14 = (bf16[1168,128]{1,0:T(8,128)(2,1)S(1)}, bf16[1168,128]{1,0:T(8,128)(2,1)}, u32[]{:S(2)}) copy-start(bf16[1168,128]{1,0:T(8,128)(2,1)} %copy-done.13) | copy-start | bytes 897028
  68.6 10.2 %collective-permute-start.24 = (bf16[576,128]{1,0:T(8,128)(2,1)}, bf16[576,128]{1,0:T(8,128)(2,1)S(1)}, u32[]{:S(2)}, u32[]{:S(2)}) collective-permute-start(bf16[576,128]{1,0:T(8,128)(2,1)} %collective-permute-done.23), channel_id=1, source_target_pairs={{0,32},{16,48},{32,0},{48,16},{64,96},{80,112},{96,64},{112,80},{1... | collective-permute-start | bytes 442376 | tf_op jit(solution)/shard_map/ppermute | solution.py:60
  70.1 8.7 %collective-permute-start.22 = (bf16[592,128]{1,0:T(8,128)(2,1)}, bf16[592,128]{1,0:T(8,128)(2,1)S(1)}, u32[]{:S(2)}, u32[]{:S(2)}) collective-permute-start(bf16[592,128]{1,0:T(8,128)(2,1)} %collective-permute-done.21), channel_id=1, source_target_pairs={{0,96},{16,112},{32,64},{48,80},{64,32},{80,48},{96,0},{112,16},{1... | collective-permute-start | bytes 454664 | tf_op jit(solution)/shard_map/ppermute | solution.py:60
  76.4 2.5 copy-start.18
  100.3 1.3 copy-start.3
  101.6 23.7 %copy-start.17 = (bf16[1744,128]{1,0:T(8,128)(2,1)S(1)}, bf16[1744,128]{1,0:T(8,128)(2,1)}, u32[]{:S(2)}) copy-start(bf16[1744,128]{1,0:T(8,128)(2,1)} %copy-done.16) | copy-start | bytes 1339396
  101.6 52.2 %copy-start.12 = (bf16[1728,128]{1,0:T(8,128)(2,1)S(1)}, bf16[1728,128]{1,0:T(8,128)(2,1)}, u32[]{:S(2)}) copy-start(bf16[1728,128]{1,0:T(8,128)(2,1)} %copy-done.11) | copy-start | bytes 1327108
  101.7 58.2 %copy-start.8 = (bf16[1744,128]{1,0:T(8,128)(2,1)S(1)}, bf16[1744,128]{1,0:T(8,128)(2,1)}, u32[]{:S(2)}) copy-start(bf16[1744,128]{1,0:T(8,128)(2,1)} %copy-done.7) | copy-start | bytes 1339396
  101.7 60.7 %all-to-all-start.2 = ((bf16[4,4,528,128]{3,2,1,0:T(8,128)(2,1)}), bf16[4,4,528,128]{3,2,1,0:T(8,128)(2,1)S(1)}, u32[]{:S(2)}, u32[]{:S(2)}) async-start(bf16[4,4,528,128]{3,2,1,0:T(8,128)(2,1)} %copy-done.3), calls=%async_computation.2 | async-start | bytes 4325376 | tf_op jit(solution)/shard_map/all_to_all | solution.py:88
  107.8 8.2 %collective-permute-start.15 = (bf16[864,128]{1,0:T(8,128)(2,1)}, bf16[864,128]{1,0:T(8,128)(2,1)S(1)}, u32[]{:S(2)}, u32[]{:S(2)}) collective-permute-start(bf16[864,128]{1,0:T(8,128)(2,1)} %copy-done.29), channel_id=1, source_target_pairs={{0,32},{16,48},{32,0},{48,16},{64,96},{80,112},{96,64},{112,80},{1... | collective-permute-start | bytes 663560 | tf_op jit(solution)/shard_map/ppermute | solution.py:60
  108.1 9.4 %collective-permute-start.17 = (bf16[864,128]{1,0:T(8,128)(2,1)}, bf16[864,128]{1,0:T(8,128)(2,1)S(1)}, u32[]{:S(2)}, u32[]{:S(2)}) collective-permute-start(bf16[864,128]{1,0:T(8,128)(2,1)} %copy-done.28), channel_id=1, source_target_pairs={{0,96},{16,112},{32,64},{48,80},{64,32},{80,48},{96,0},{112,16},{1... | collective-permute-start | bytes 663560 | tf_op jit(solution)/shard_map/ppermute | solution.py:60
  109.3 22.1 %collective-permute-start.13 = (bf16[1728,128]{1,0:T(8,128)(2,1)}, bf16[1728,128]{1,0:T(8,128)(2,1)S(1)}, u32[]{:S(2)}, u32[]{:S(2)}) collective-permute-start(bf16[1728,128]{1,0:T(8,128)(2,1)} %copy-done.22), channel_id=1, source_target_pairs={{0,32},{16,48},{32,0},{48,16},{64,96},{80,112},{96,64},{112,80},{1... | collective-permute-start | bytes 1327112 | tf_op jit(solution)/shard_map/ppermute | solution.py:60
  116.0 9.3 %collective-permute-start.16 = (bf16[864,128]{1,0:T(8,128)(2,1)S(1)}, bf16[864,128]{1,0:T(8,128)(2,1)S(1)}, u32[]{:S(2)}, u32[]{:S(2)}) collective-permute-start(bf16[864,128]{1,0:T(8,128)(2,1)S(1)} %collective-permute-done.15), channel_id=1, source_target_pairs={{0,96},{16,112},{32,64},{48,80},{64,32},{80,48},{96,0},{112,16},{1... | collective-permute-start | bytes 663560 | tf_op jit(solution)/shard_map/ppermute | solution.py:60
  117.5 12.8 %collective-permute-start.18 = (bf16[864,128]{1,0:T(8,128)(2,1)S(1)}, bf16[864,128]{1,0:T(8,128)(2,1)S(1)}, u32[]{:S(2)}, u32[]{:S(2)}) collective-permute-start(bf16[864,128]{1,0:T(8,128)(2,1)S(1)} %collective-permute-done.17), channel_id=1, source_target_pairs={{0,32},{16,48},{32,0},{48,16},{64,96},{80,112},{96,64},{112,80},{1... | collective-permute-start | bytes 663560 | tf_op jit(solution)/shard_map/ppermute | solution.py:60
  118.3 16.8 %collective-permute-start.29 = (bf16[880,128]{1,0:T(8,128)(2,1)}, bf16[880,128]{1,0:T(8,128)(2,1)S(1)}, u32[]{:S(2)}, u32[]{:S(2)}) collective-permute-start(bf16[880,128]{1,0:T(8,128)(2,1)} %copy-done.27), channel_id=1, source_target_pairs={{0,32},{16,48},{32,0},{48,16},{64,96},{80,112},{96,64},{112,80},{1... | collective-permute-start | bytes 675848 | tf_op jit(solution)/shard_map/ppermute | solution.py:60
  119.5 40.3 %collective-permute-start.27 = (bf16[1744,128]{1,0:T(8,128)(2,1)}, bf16[1744,128]{1,0:T(8,128)(2,1)S(1)}, u32[]{:S(2)}, u32[]{:S(2)}) collective-permute-start(bf16[1744,128]{1,0:T(8,128)(2,1)} %copy-done.18), channel_id=1, source_target_pairs={{0,32},{16,48},{32,0},{48,16},{64,96},{80,112},{96,64},{112,80},{1... | collective-permute-start | bytes 1339400 | tf_op jit(solution)/shard_map/ppermute | solution.py:60
  125.3 34.5 %collective-permute-start.28 = (bf16[1744,128]{1,0:T(8,128)(2,1)S(1)}, bf16[1744,128]{1,0:T(8,128)(2,1)S(1)}, u32[]{:S(2)}, u32[]{:S(2)}) collective-permute-start(bf16[1744,128]{1,0:T(8,128)(2,1)S(1)} %copy-done.17), channel_id=1, source_target_pairs={{0,96},{16,112},{32,64},{48,80},{64,32},{80,48},{96,0},{112,16},{1... | collective-permute-start | bytes 1339400 | tf_op jit(solution)/shard_map/ppermute | solution.py:60
  130.3 23.6 %collective-permute-start.14 = (bf16[1728,128]{1,0:T(8,128)(2,1)}, bf16[1728,128]{1,0:T(8,128)(2,1)S(1)}, u32[]{:S(2)}, u32[]{:S(2)}) collective-permute-start(bf16[1728,128]{1,0:T(8,128)(2,1)} %copy-done.21), channel_id=1, source_target_pairs={{0,96},{16,112},{32,64},{48,80},{64,32},{80,48},{96,0},{112,16},{1... | collective-permute-start | bytes 1327112 | tf_op jit(solution)/shard_map/ppermute | solution.py:60
  131.4 22.5 %collective-permute-start.31 = (bf16[864,128]{1,0:T(8,128)(2,1)}, bf16[864,128]{1,0:T(8,128)(2,1)S(1)}, u32[]{:S(2)}, u32[]{:S(2)}) collective-permute-start(bf16[864,128]{1,0:T(8,128)(2,1)} %copy-done.31), channel_id=1, source_target_pairs={{0,96},{16,112},{32,64},{48,80},{64,32},{80,48},{96,0},{112,16},{1... | collective-permute-start | bytes 663560 | tf_op jit(solution)/shard_map/ppermute | solution.py:60
  135.1 24.7 %collective-permute-start.30 = (bf16[880,128]{1,0:T(8,128)(2,1)S(1)}, bf16[880,128]{1,0:T(8,128)(2,1)S(1)}, u32[]{:S(2)}, u32[]{:S(2)}) collective-permute-start(bf16[880,128]{1,0:T(8,128)(2,1)S(1)} %collective-permute-done.29), channel_id=1, source_target_pairs={{0,96},{16,112},{32,64},{48,80},{64,32},{80,48},{96,0},{112,16},{1... | collective-permute-start | bytes 675848 | tf_op jit(solution)/shard_map/ppermute | solution.py:60
  153.9 5.9 %collective-permute-start.32 = (bf16[864,128]{1,0:T(8,128)(2,1)S(1)}, bf16[864,128]{1,0:T(8,128)(2,1)S(1)}, u32[]{:S(2)}, u32[]{:S(2)}) collective-permute-start(bf16[864,128]{1,0:T(8,128)(2,1)S(1)} %collective-permute-done.31), channel_id=1, source_target_pairs={{0,32},{16,48},{32,0},{48,16},{64,96},{80,112},{96,64},{112,80},{1... | collective-permute-start | bytes 663560 | tf_op jit(solution)/shard_map/ppermute | solution.py:60
  162.3 5.2 %copy-start.37 = (s32[16,9]{1,0:T(8,128)S(1)}, s32[16,9]{1,0:T(8,128)}, u32[]{:S(2)}) copy-start(s32[16,9]{1,0:T(8,128)} %copy-done.36) | copy-start | bytes 1732
  162.3 5.3 %copy-start.38 = (s32[16]{0:T(128)S(1)}, s32[16]{0:T(128)}, u32[]{:S(2)}) copy-start(s32[16]{0:T(128)} %get-tuple-element.159) | copy-start | bytes 196
  163.7 24.7 %all-to-all-start.1 = ((bf16[4,4,784,128]{3,2,1,0:T(8,128)(2,1)}), bf16[4,4,784,128]{3,2,1,0:T(8,128)(2,1)S(1)}, u32[]{:S(2)}, u32[]{:S(2)}) async-start(bf16[4,4,784,128]{3,2,1,0:T(8,128)(2,1)} %spread.4), calls=%async_computation.1 | async-start | bytes 6422528 | tf_op jit(solution)/shard_map/all_to_all | solution.py:88
  167.4 9.8 %copy-start.2 = (bf16[4,4,528,128]{3,2,1,0:T(8,128)(2,1)S(1)}, bf16[4,4,528,128]{3,2,1,0:T(8,128)(2,1)}, u32[]{:S(2)}) copy-start(bf16[4,4,528,128]{3,2,1,0:T(8,128)(2,1)} %copy-done.1) | copy-start | bytes 6488068
  167.4 4.0 %collective-permute-start.26 = (bf16[4,1728,128]{2,1,0:T(8,128)(2,1)}, bf16[4,1728,128]{2,1,0:T(8,128)(2,1)S(1)}, u32[]{:S(2)}, u32[]{:S(2)}) collective-permute-start(bf16[4,1728,128]{2,1,0:T(8,128)(2,1)} %copy-done.4), channel_id=1, source_target_pairs={{0,16},{16,0},{32,48},{48,32},{64,80},{80,64},{96,112},{112,96},{1... | collective-permute-start | bytes 5308424 | tf_op jit(solution)/shard_map/ppermute | solution.py:60
  171.4 1.5 copy-start.5
  188.6 1.7 copy-start
  190.3 32.6 %all-to-all-start.4 = ((bf16[4,4,784,128]{3,2,1,0:T(8,128)(2,1)}), bf16[4,4,784,128]{3,2,1,0:T(8,128)(2,1)S(1)}, u32[]{:S(2)}, u32[]{:S(2)}) async-start(bf16[4,4,784,128]{3,2,1,0:T(8,128)(2,1)} %copy-done), calls=%async_computation.4 | async-start | bytes 6422528 | tf_op jit(solution)/shard_map/all_to_all | solution.py:88
  194.0 8.5 %collective-permute-start.35 = (bf16[880,128]{1,0:T(8,128)(2,1)S(1)}, bf16[880,128]{1,0:T(8,128)(2,1)S(1)}, u32[]{:S(2)}, u32[]{:S(2)}) collective-permute-start(bf16[880,128]{1,0:T(8,128)(2,1)S(1)} %get-tuple-element.140), channel_id=1, source_target_pairs={{0,32},{16,48},{32,0},{48,16},{64,96},{80,112},{96,64},{112,80},{1... | collective-permute-start | bytes 675848 | tf_op jit(solution)/shard_map/ppermute | solution.py:60
  194.1 25.2 %collective-permute-start.33 = (bf16[1744,128]{1,0:T(8,128)(2,1)}, bf16[1744,128]{1,0:T(8,128)(2,1)S(1)}, u32[]{:S(2)}, u32[]{:S(2)}) collective-permute-start(bf16[1744,128]{1,0:T(8,128)(2,1)} %copy-done.20), channel_id=1, source_target_pairs={{0,32},{16,48},{32,0},{48,16},{64,96},{80,112},{96,64},{112,80},{1... | collective-permute-start | bytes 1339400 | tf_op jit(solution)/shard_map/ppermute | solution.py:60
  196.1 23.2 %collective-permute-start.34 = (bf16[1744,128]{1,0:T(8,128)(2,1)}, bf16[1744,128]{1,0:T(8,128)(2,1)S(1)}, u32[]{:S(2)}, u32[]{:S(2)}) collective-permute-start(bf16[1744,128]{1,0:T(8,128)(2,1)} %copy-done.19), channel_id=1, source_target_pairs={{0,96},{16,112},{32,64},{48,80},{64,32},{80,48},{96,0},{112,16},{1... | collective-permute-start | bytes 1339400 | tf_op jit(solution)/shard_map/ppermute | solution.py:60
  197.1 16.3 %collective-permute-start.37 = (bf16[864,128]{1,0:T(8,128)(2,1)}, bf16[864,128]{1,0:T(8,128)(2,1)S(1)}, u32[]{:S(2)}, u32[]{:S(2)}) collective-permute-start(bf16[864,128]{1,0:T(8,128)(2,1)} %copy-done.33), channel_id=1, source_target_pairs={{0,96},{16,112},{32,64},{48,80},{64,32},{80,48},{96,0},{112,16},{1... | collective-permute-start | bytes 663560 | tf_op jit(solution)/shard_map/ppermute | solution.py:60
  202.5 16.8 %collective-permute-start.36 = (bf16[880,128]{1,0:T(8,128)(2,1)S(1)}, bf16[880,128]{1,0:T(8,128)(2,1)S(1)}, u32[]{:S(2)}, u32[]{:S(2)}) collective-permute-start(bf16[880,128]{1,0:T(8,128)(2,1)S(1)} %collective-permute-done.35), channel_id=1, source_target_pairs={{0,96},{16,112},{32,64},{48,80},{64,32},{80,48},{96,0},{112,16},{1... | collective-permute-start | bytes 675848 | tf_op jit(solution)/shard_map/ppermute | solution.py:60
  213.3 5.9 %collective-permute-start.38 = (bf16[864,128]{1,0:T(8,128)(2,1)S(1)}, bf16[864,128]{1,0:T(8,128)(2,1)S(1)}, u32[]{:S(2)}, u32[]{:S(2)}) collective-permute-start(bf16[864,128]{1,0:T(8,128)(2,1)S(1)} %collective-permute-done.37), channel_id=1, source_target_pairs={{0,32},{16,48},{32,0},{48,16},{64,96},{80,112},{96,64},{112,80},{1... | collective-permute-start | bytes 663560 | tf_op jit(solution)/shard_map/ppermute | solution.py:60
  222.9 25.8 %all-to-all-start.3 = ((bf16[4,4,784,128]{3,2,1,0:T(8,128)(2,1)}), bf16[4,4,784,128]{3,2,1,0:T(8,128)(2,1)}, u32[]{:S(2)}, u32[]{:S(2)}) async-start(bf16[4,4,784,128]{3,2,1,0:T(8,128)(2,1)} %spread.5), calls=%async_computation.3 | async-start | bytes 6422528 | tf_op jit(solution)/shard_map/all_to_all | solution.py:88
  (21 other events, 16.9 us)

commit v3 on v2

--- a/solution.py
+++ b/solution.py
@@ -10,29 +10,27 @@
 
 HEAD_DIM = 128
 HAD = 128
-CHUNKS = ((0, 32), (32, 48), (80, 48))
+CHUNKS = ((0, 48), (48, 48), (96, 32))
+DIRECT = 2
 ORDER = (
     ("start", 0),
     ("start", 1),
     ("y_turn", 0),
     ("core_turn", 0),
     ("y_turn", 1),
+    ("spread", 0),
     ("start", 2),
     ("core_turn", 1),
-    ("spread", 0),
-    ("regroup", 0),
     ("y_turn", 2),
+    ("core_turn", 2),
     ("spread", 1),
-    ("core_turn", 2),
+    ("spread", 2),
     ("pack", 0),
-    ("regroup", 1),
-    ("spread", 2),
     ("pack", 1),
-    ("regroup", 2),
     ("pack", 2),
 )
 TAIL = 16
-VMEM_BYTES = 24 * 1024 * 1024
+VMEM_BYTES = 12 * 1024 * 1024
 BOTH = ("fsdp", "tp")
 
 
@@ -67,25 +65,65 @@
     return own, one, three, hop(two_a, 6), hop(two_b, 2)
 
 
-def owner_table(core):
-    one, two = ((1, 3), (3, 1))[core]
-    table = np.zeros((4, 4), np.int32)
-    for i in range(4):
-        for j in range(4):
-            x = (i & 1) * one ^ (j & 1) * two
-            z = (i >> 1) * one ^ (j >> 1) * two
-            table[i, j] = 4 * z + x
+PAIRINGS = ((1, 3), (3, 1))
+BITS_A = ((1, 0), (4, 0), (1, 1), (4, 1))
+BITS_B = ((4, 0), (1, 0), (4, 1), (1, 1))
+
+
+def owner_offsets(core, bits):
+    table = np.zeros(1 << len(bits), np.int32)
+    for index in range(len(table)):
+        for bit, (factor, which) in enumerate(bits):
+            if index >> bit & 1:
+                table[index] ^= factor * PAIRINGS[core][which]
     return table
 
 
-def pair_exchange(array, second):
+def owner_hop(array, factor, which):
     groups, owners = lax.axis_size("fsdp"), lax.axis_size("tp")
-    members = []
+    pairs = []
     for f in range(groups):
-        table = owner_table(f & 1)
-        table = table if second else table.T
-        members += [[f * owners + int(t) for t in row] for row in table]
-    return lax.all_to_all(array, BOTH, split_axis=0, concat_axis=0, tiled=True, axis_index_groups=members)
+        flip = factor * PAIRINGS[f & 1][which]
+        pairs += [(f * owners + t, f * owners + (t ^ flip)) for t in range(owners)]
+    return lax.ppermute(array, BOTH, pairs)
+
+
+def regroup_kernel(plan, *refs):
+    out_ref = refs[-1]
+    for row, (array, index) in enumerate(plan):
+        out_ref[row] = refs[array][index]
+
+
+def hypercube(keep, send, bits):
+    held = [keep, owner_hop(send, *bits[0])]
+    for step in range(1, len(bits)):
+        plan = []
+        for array in range(len(held)):
+            origins = 1 << max(array - 1, 0)
+            size = keep.shape[0] // origins
+            for origin in range(origins):
+                width = keep.shape[0] >> step
+                plan += [(array, origin * size + width + i) for i in range(width)]
+        vmem_spec = pl.BlockSpec(memory_space=pltpu.VMEM)
+        payload = pl.pallas_call(
+            functools.partial(regroup_kernel, tuple(plan)),
+            in_specs=[vmem_spec] * len(held),
+            out_specs=vmem_spec,
+            out_shape=jax.ShapeDtypeStruct(keep.shape, keep.dtype),
+            compiler_params=pltpu.CompilerParams(vmem_limit_bytes=VMEM_BYTES),
+            name="regroup",
+        )(*held)
+        held.append(owner_hop(payload, *bits[step]))
+    return held
+
+
+def first_slots(bits):
+    slots = [(0, 0)]
+    for array in range(1, bits + 1):
+        origins = 1 << (array - 1)
+        size = (1 << (bits - 1)) // origins
+        slots += [(array, origin * size) for origin in range(origins)]
+    return slots
 
 
 def local_turn_kernel(rows_a, flip_ref, weight_ref, signs_ref, *refs):
@@ -166,62 +204,69 @@
 
 
 def spread_kernel(heads, chans, head_ref, *refs):
-    in_refs, out_ref = refs[:-1], refs[-1]
+    in_refs, out_refs = refs[:5], refs[5:]
     peaks = None
     for in_ref in in_refs[:4]:
         part = join_parts(in_ref[in_ref.shape[0] - TAIL :, :].astype(jnp.float32), chans)
         peaks = part if peaks is None else jnp.maximum(peaks, part)
     row_id = lax.broadcasted_iota(jnp.int32, (TAIL, HAD), 0)
-    span = 4 * chans
-    half = 2 * chans
-    own, one, three, two_a, two_b = in_refs
+    span, half = 4 * chans, 2 * chans
+    sizes = ((0, span), (1, span), (3, half), (4, half), (2, span))
     for slot in range(16):
-        head = head_ref[slot]
-        whole = pl.ds(pl.multiple_of(head * span, 16), span)
-        part = pl.ds(pl.multiple_of(head * half, 16), half)
-        i, j = slot // 4, slot % 4
-        out_ref[i, j, 0:span, :] = own[whole, :]
-        out_ref[i, j, span : 2 * span, :] = one[whole, :]
-        out_ref[i, j, 2 * span : 2 * span + half, :] = two_a[part, :]
-        out_ref[i, j, 2 * span + half : 3 * span, :] = two_b[part, :]
-        out_ref[i, j, 3 * span : 4 * span, :] = three[whole, :]
-        peak = jnp.sum(jnp.where(row_id == head, peaks, 0.0), axis=0, keepdims=True)
-        out_ref[i, j, 4 * span :, :] = split_parts(jnp.broadcast_to(peak, (TAIL, HAD)), chans)
-
-
-def regroup_kernel(in_ref, out_ref):
-    for i in range(4):
-        for j in range(4):
-            out_ref[j, i] = in_ref[i, j]
-
-
-def pack_kernel(owners, chunk, has_past, from_ref, live_ref, place_ref, in_ref, *refs):
+        if len(out_refs) == 1:
+            parts = ((out_refs[0], slot, head_ref[slot], sizes, True),)
+        else:
+            parts = (
+                (out_refs[slot // 8], slot % 8, head_ref[slot], sizes[:2], False),
+                (out_refs[2 + slot // 8], slot % 8, head_ref[16 + slot], sizes[2:], True),
+            )
+        for out_ref, index, head, arrays, with_tail in parts:
+            start = 0
+            for array, size in arrays:
+                rows = pl.ds(pl.multiple_of(head * size, 16), size)
+                out_ref[index, start : start + size, :] = in_refs[array][rows, :]
+                start += size
+            if with_tail:
+                peak = jnp.sum(jnp.where(row_id == head, peaks, 0.0), axis=0, keepdims=True)
+                out_ref[index, start:, :] = split_parts(jnp.broadcast_to(peak, (TAIL, HAD)), chans)
+
+
+def pack_kernel(owners, chunk, has_past, slot_ref, live_ref, place_ref, *refs):
     first, chans = chunk
-    past_ref = refs[0] if has_past else None
     peak_ref, out_ref, buffer, sems = refs[-4:]
+    past_ref = refs[-6] if has_past else None
+    in_refs = refs[: -6 if has_past else -4]
     lane = lax.broadcasted_iota(jnp.int32, (TAIL, HAD), 1)
     depth = buffer.shape[0]
     copies = [None] * depth
-    for slot in range(owners):
-        part = slot % depth
+    slots = first_slots(4)
+    for origin in range(owners):
+        if len(in_refs) == 1:
+            halves = ((in_refs[0], origin, 0), (in_refs[0], origin, 8 * chans))
+        else:
+            a_array, a_index = slots[origin]
+            b_array, b_index = slots[((origin & 5) << 1) | ((origin & 10) >> 1)]
+            halves = ((in_refs[a_array], a_index, 0), (in_refs[5 + b_array], b_index, 0))
+        part = origin % depth
         if copies[part] is not None:
             copies[part].wait()
-        live = live_ref[slot] != 0
-        origin = from_ref[slot]
-        i, j = origin // 4, origin % 4
-        tail = in_ref[i, j, 16 * chans :, :].astype(jnp.float32)
+        live = live_ref[origin] != 0
+        slot = slot_ref[origin]
+        last_ref, last_index, last_start = halves[1]
+        tail = last_ref[last_index, last_start + 8 * chans :, :].astype(jnp.float32)
         row = jnp.where((lane < chans) & live, join_parts(tail, chans), 0.0)[:1, :]
         scale = jnp.where(live, 1.0 / (row + 1e-06), 0.0)
         scale = jnp.broadcast_to(scale, (HEAD_DIM, HAD)).T[:chans, :]
         row = pltpu.roll(jnp.broadcast_to(row, (8, HAD)), first, 1)[:1, :] if first else row
         if has_past:
-            row = row + past_ref[slot : slot + 1, :]
-        peak_ref[slot : slot + 1, :] = row
+            row = row + past_ref[pl.ds(slot, 1), :]
+        peak_ref[pl.ds(slot, 1), :] = row
         for o in range(4):
+            in_ref, index, offset = halves[o // 2]
             for e in range(4):
-                start = (o * 4 + e) * chans
+                start = offset + (o % 2 * 4 + e) * chans
                 lanes = pl.ds(pl.multiple_of(place_ref[o] + e * HAD, HAD), HAD)
-                block = in_ref[i, j, start : start + chans, :]
+                block = in_ref[index, start : start + chans, :]
                 buffer[part, :, lanes] = (block.astype(jnp.float32) * scale).astype(jnp.bfloat16)
         copies[part] = pltpu.make_async_copy(
             buffer.at[part], out_ref.at[0, slot, first : first + chans, :], sems.at[part]
@@ -261,19 +306,31 @@
     blocks = placement.reshape(owners, heads)
     head_ids = jnp.arange(heads, dtype=jnp.int32)
     owner_ids = jnp.arange(owners, dtype=jnp.int32)
-    by_core = [owner_table(c) for c in range(2)]
-    send_to = jnp.where(core == 0, jnp.asarray(by_core[0].reshape(-1)), jnp.asarray(by_core[1].reshape(-1)))
-    source = jnp.where(core == 0, jnp.asarray(by_core[0].T.reshape(-1)), jnp.asarray(by_core[1].T.reshape(-1)))
     my_owners = lax.dynamic_slice_in_dim(blocks, me, 1, axis=0)
-    head_for = jnp.sum(jnp.where(my_owners == send_to[:, None], head_ids[None, :], 0), axis=1)
     has = jnp.any(blocks == me, axis=1)
-    present = jnp.any(has[None, :] & (source[:, None] == owner_ids[None, :]), axis=1)
-    rank = jnp.sum(((source[None, :] < source[:, None]) & present[None, :]).astype(jnp.int32), axis=1)
-    taken = present[None, :] & (rank[None, :] == owner_ids[:, None])
-    come_from = jnp.sum(jnp.where(taken, owner_ids[None, :], 0), axis=1)
-    live = jnp.any(taken, axis=1).astype(jnp.int32)
+
+    def pick(bits):
+        return jnp.where(core == 0, *(jnp.asarray(owner_offsets(c, bits)) for c in range(2))) ^ me
+
+    def heads_for(to):
+        return jnp.sum(jnp.where(my_owners == to[:, None], head_ids[None, :], 0), axis=1)
+
+    def slots_of(source):
+        live = jnp.any(has[None, :] & (source[:, None] == owner_ids[None, :]), axis=1)
+        before = source[None, :] < source[:, None]
+        rank = jnp.sum((before & live[None, :]).astype(jnp.int32), axis=1)
+        spare = jnp.sum((before & ~live[None, :]).astype(jnp.int32), axis=1) + jnp.sum(live.astype(jnp.int32))
+        return jnp.where(live, rank, spare), live.astype(jnp.int32)
+
+    direct_heads = heads_for(owner_ids)
+    direct_slots = slots_of(owner_ids)
+    cube_heads = jnp.concatenate([heads_for(pick(bits[::-1])) for bits in (BITS_A, BITS_B)])
+    cube_slots = slots_of(pick(BITS_A))
 
     signs = jnp.asarray(hadamard_table(HAD), jnp.bfloat16)
+    tables = (flip_a, flip_in, flip_out, sign, place, direct_heads, direct_slots, cube_heads, cube_slots)
+    tables, qkv_weight = lax.optimization_barrier((tables, qkv_weight))
+    flip_a, flip_in, flip_out, sign, place, direct_heads, direct_slots, cube_heads, cube_slots = tables
     first_blocks = [shape for _, chans in CHUNKS for shape in blocks_of(chans, 0)]
     turned = pl.pallas_call(
         functools.partial(local_turn_kernel, rows_a),
@@ -326,39 +383,39 @@
             token = outs[0]
             state[index] = ring_exchange(outs)
         elif stage == "spread":
-            token = pl.pallas_call(
+            direct = index < DIRECT
+            if direct:
+                shapes = [(owners, 16 * chans + TAIL)]
+            else:
+                shapes = [(owners // 2, 8 * chans)] * 2 + [(owners // 2, 8 * chans + TAIL)] * 2
+            outs = pl.pallas_call(
                 functools.partial(spread_kernel, heads, chans),
                 in_specs=[smem_spec] + [vmem_spec] * 5,
-                out_specs=vmem_spec,
-                out_shape=jax.ShapeDtypeStruct((4, 4, 16 * chans + TAIL, HAD), jnp.bfloat16),
+                out_specs=[vmem_spec] * len(shapes),
+                out_shape=[jax.ShapeDtypeStruct(shape + (HAD,), jnp.bfloat16) for shape in shapes],
                 compiler_params=params,
                 name="spread",
-            )(head_for, *arrays)
-            state[index] = [pair_exchange(token, False)]
-        elif stage == "regroup":
-            token = pl.pallas_call(
-                regroup_kernel,
-                in_specs=[vmem_spec],
-                out_specs=vmem_spec,
-                out_shape=jax.ShapeDtypeStruct(arrays[0].shape, jnp.bfloat16),
-                compiler_params=params,
-                name="regroup",
-            )(*arrays)
-            state[index] = [pair_exchange(token, True)]
+            )(direct_heads if direct else cube_heads, *arrays)
+            token = outs[0]
+            if direct:
+                state[index] = [lax.all_to_all(outs[0], "tp", split_axis=0, concat_axis=0, tiled=True)]
+            else:
+                state[index] = hypercube(*outs[:2], BITS_A) + hypercube(*outs[2:], BITS_B)
         else:
+            slot, live = direct_slots if index < DIRECT else cube_slots
             past = pl.pallas_call(
                 functools.partial(pack_kernel, owners, chunk, bool(past)),
-                in_specs=[smem_spec] * 3 + [vmem_spec] + ([vmem_spec, any_spec] if past else []),
+                in_specs=[smem_spec] * 3 + [vmem_spec] * len(arrays) + ([vmem_spec, any_spec] if past else []),
                 out_specs=[vmem_spec, any_spec],
                 out_shape=[
                     jax.ShapeDtypeStruct((owners, HEAD_DIM), jnp.float32),
                     jax.ShapeDtypeStruct((1, owners, HEAD_DIM, rows_local), jnp.bfloat16),
                 ],
                 scratch_shapes=[pltpu.VMEM((3, chans, rows_local), jnp.bfloat16), pltpu.SemaphoreType.DMA((3,))],
-                input_output_aliases={5: 1} if past else {},
+                input_output_aliases={4 + len(arrays): 1} if past else {},
                 compiler_params=params,
                 name="pack",
-            )(come_from, live, place, *arrays, *past)
+            )(slot, live, place, *arrays, *past)
             token = past[0]
     peaks, packed = past
     return packed, peaks[None]

time: 286 us -> 253 us (0.88)
  blocking collectives: 47.9 us -> 0 us
  starting transfers between devices: 59.8 us -> 77.2 us
  local copies, waits for them, and re-layouts: 25.8 us -> 12.8 us
  waiting for transfers between devices: 108 us -> 115 us
    all_to_all x2 -> x0, blocking collectives: 47.9 us -> none  [pair_exchange(): lax.all_to_all(array, BOTH, split_axis=0, concat_axis=0, tiled=True, axis...]
    ppermute x0 -> x8, waiting for transfers between devices: none -> 30.6 us  [owner_hop(): return lax.ppermute(array, BOTH, pairs)]
    all_to_all x4 -> x2, waiting for transfers between devices: 20.8 us -> 0.01 us  [per_device(): lax.all_to_all(outs[0], 'tp', split_axis=0, concat_axis=0, tiled=True)]
    ppermute x0 -> x8, starting transfers between devices: none -> 15.4 us  [owner_hop(): return lax.ppermute(array, BOTH, pairs)]
    unnamed x84 -> x56, local copies, waits for them, and re-layouts: 23.8 us -> 9.38 us
    ppermute x39, starting transfers between devices: 41.5 us -> 46.8 us  [hop(): return lax.ppermute(array, 'fsdp', [(i, i ^ flip) for i in range(size)])]
    all_to_all x4 -> x2, starting transfers between devices: 18.3 us -> 15.1 us  [per_device(): lax.all_to_all(outs[0], 'tp', split_axis=0, concat_axis=0, tiled=True)]
  transfers between devices with their start and end apart: 43 -> 49, of which waited for: 20 -> 22; matrix products, arithmetic and copies ran while one was open for 1% -> 0% of each run, Pallas kernels for 7% -> 10%
where the time goes in v3:
time: 253 us; the launch traced here: 252 us
  waiting for transfers between devices  115 us (45%)
  starting transfers between devices  77.2 us (31%)
  Pallas kernels  40.4 us (16%)
  local copies, waits for them, and re-layouts  12.8 us (5%)
  other arithmetic  5.54 us (2%)
    ppermute x39, waiting for transfers between devices, hop(): return lax.ppermute(array, 'fsdp', [(i, i ^ flip) for i in range(size)])  84.4 us
    ppermute x39, starting transfers between devices, hop(): return lax.ppermute(array, 'fsdp', [(i, i ^ flip) for i in range(size)])  46.8 us
    ppermute x8, waiting for transfers between devices, owner_hop(): return lax.ppermute(array, BOTH, pairs)  30.6 us
    pallas_call x3, Pallas kernels, per_device(): pl.pallas_call(functools.partial(pack_kernel, owners, chunk, bool(past)),...  19.9 us
    ppermute x8, starting transfers between devices, owner_hop(): return lax.ppermute(array, BOTH, pairs)  15.4 us
    all_to_all x2, starting transfers between devices, per_device(): lax.all_to_all(outs[0], 'tp', split_axis=0, concat_axis=0, tiled=True)  15.1 us
    unnamed x56, local copies, waits for them, and re-layouts  9.38 us
    pallas_call x3, Pallas kernels, per_device(): pl.pallas_call(functools.partial(spread_kernel, heads, chans), in_specs=[...  5.88 us
  transfers between devices with their start and end apart: 49, of which 22 were waited for; matrix products, arithmetic and copies ran while one was open for 0% of the time, Pallas kernels for 10%

profile of v3, /device:TPU:0, one launch (start us, length us, event | category | flops | bytes accessed | tf_op | source)
XLA Modules:
  0.0 252.2 jit_solution(8756821619926018323)
XLA Ops:
  4.1 1.3 dynamic_slice.14
  5.4 1.3 broadcast_multiply_fusion.flip_out_ref
  9.7 2.3 copy-done.14
  12.8 5.5 %local_turn.1 = (bf16[1728,128]{1,0:T(8,128)(2,1)S(1)}, bf16[1728,128]{1,0:T(8,128)(2,1)S(1)}, bf16[1728,128]{1,0:T(8,128)(2,1)S(1)}, bf16[864,128]{1,0:T(8,128)...) custom-call(f32[16]{0:T(128)S(1)} %fusion.6.flip_ref, ...), custom_call_target="tpu_custom_call" | custom-call | tf_op jit(solution)/shard_map/local_turn/pallas_call | solution.py:335
  19.1 1.7 collective-permute-start.2
  20.7 2.2 collective-permute-start.4
  24.2 3.2 %collective-permute-done.2 = bf16[864,128]{1,0:T(8,128)(2,1)S(1)} collective-permute-done((bf16[864,128]{1,0:T(8,128)(2,1)S(1)}, bf16[864,128]{1,0:T(8,128)(2,1)S(1)}, u32[]{:S(2)}, u32[]{:S(2)}) %collective-permute-start.2) | collective-permute-done | bytes 221216 | tf_op jit(solution)/shard_map/ppermute | solution.py:58
  27.4 3.1 %collective-permute-start.3 = (bf16[864,128]{1,0:T(8,128)(2,1)S(1)}, bf16[864,128]{1,0:T(8,128)(2,1)S(1)}, u32[]{:S(2)}, u32[]{:S(2)}) collective-permute-start(bf16[864,128]{1,0:T(8,128)(2,1)S(1)} %collective-permute-done.2), channel_id=1, source_target_pairs={{0,96},{16,112},{32,64},{48,80},{64,32},{80,48},{96,0},{112,16},{1... | collective-permute-start | bytes 663560 | tf_op jit(solution)/shard_map/ppermute | solution.py:58
  30.6 12.4 %collective-permute-done.3.refs_3_ = bf16[864,128]{1,0:T(8,128)(2,1)S(1)} collective-permute-done((bf16[864,128]{1,0:T(8,128)(2,1)S(1)}, bf16[864,128]{1,0:T(8,128)(2,1)S(1)}, u32[]{:S(2)}, u32[]{:S(2)}) %collective-permute-start.3) | collective-permute-done | bytes 221216 | tf_op jit(solution)/shard_map/ppermute | solution.py:58
  43.1 1.2 y_turn.3.mine_ref
  44.4 2.3 collective-permute-start.17
  46.7 1.3 collective-permute-start.13
  48.0 4.6 %collective-permute-done.15 = bf16[864,128]{1,0:T(8,128)(2,1)S(1)} collective-permute-done((bf16[864,128]{1,0:T(8,128)(2,1)S(1)}, bf16[864,128]{1,0:T(8,128)(2,1)S(1)}, u32[]{:S(2)}, u32[]{:S(2)}) %collective-permute-start.15) | collective-permute-done | bytes 221216 | tf_op jit(solution)/shard_map/ppermute | solution.py:58
  52.7 2.2 collective-permute-start.16
  54.9 1.3 core_turn.3
  56.2 2.1 collective-permute-start.9
  58.4 2.0 collective-permute-done.16.refs_3_
  60.4 2.2 collective-permute-start.8
  62.6 4.3 %collective-permute-done.18.refs_4_ = bf16[864,128]{1,0:T(8,128)(2,1)S(1)} collective-permute-done((bf16[864,128]{1,0:T(8,128)(2,1)S(1)}, bf16[864,128]{1,0:T(8,128)(2,1)S(1)}, u32[]{:S(2)}, u32[]{:S(2)}) %collective-permute-start.18) | collective-permute-done | bytes 221216 | tf_op jit(solution)/shard_map/ppermute | solution.py:58
  66.9 2.2 collective-permute-start.14
  70.1 1.6 collective-permute-done.9
  71.7 2.2 collective-permute-start.10
  73.9 14.4 %collective-permute-done.11 = bf16[864,128]{1,0:T(8,128)(2,1)S(1)} collective-permute-done((bf16[864,128]{1,0:T(8,128)(2,1)S(1)}, bf16[864,128]{1,0:T(8,128)(2,1)S(1)}, u32[]{:S(2)}, u32[]{:S(2)}) %collective-permute-start.11) | collective-permute-done | bytes 221216 | tf_op jit(solution)/shard_map/ppermute | solution.py:58
  88.3 1.2 y_turn.4.mine_ref
  89.5 1.3 copy-done.8
  90.8 3.5 %collective-permute-done.12.refs_4_ = bf16[864,128]{1,0:T(8,128)(2,1)S(1)} collective-permute-done((bf16[864,128]{1,0:T(8,128)(2,1)S(1)}, bf16[864,128]{1,0:T(8,128)(2,1)S(1)}, u32[]{:S(2)}, u32[]{:S(2)}) %collective-permute-start.12) | collective-permute-done | bytes 221216 | tf_op jit(solution)/shard_map/ppermute | solution.py:58
  94.2 2.5 %spread.3 = bf16[16,784,128]{2,1,0:T(8,128)(2,1)} custom-call(s32[16]{0:T(128)S(1)} %get-tuple-element.116.head_ref, bf16[1744,128]{1,0:T(8,128)(2,1)S(1)} %get-tuple-element.139.refs_0_, bf16[1744,128]{1,0:T(8,128)(2,1)S(1)} %collective-permute-done.7.refs_1_, bf16[1744,128]{1,0:T(8,128)(2,1)S(1)} %collective-permute-done.8.refs_2_, ...), custom_call_target="tpu_custom_call" | custom-call | tf_op jit(solution)/shard_map/spread/pallas_call | solution.py:391
  96.8 7.9 %all-to-all-start.1 = ((bf16[16,784,128]{2,1,0:T(8,128)(2,1)}), bf16[16,784,128]{2,1,0:T(8,128)(2,1)S(1)}, u32[]{:S(2)}, u32[]{:S(2)}) async-start(bf16[16,784,128]{2,1,0:T(8,128)(2,1)} %spread.3), calls=%async_computation.1 | async-start | bytes 6422528 | tf_op jit(solution)/shard_map/all_to_all | solution.py:401
  104.8 2.0 collective-permute-start.19
  106.9 2.2 collective-permute-start.20
  109.0 1.1 collective-permute-start.23
  110.1 1.6 collective-permute-done.21
  111.7 2.2 collective-permute-start.22
  113.9 7.5 %collective-permute-done.23 = bf16[576,128]{1,0:T(8,128)(2,1)S(1)} collective-permute-done((bf16[576,128]{1,0:T(8,128)(2,1)}, bf16[576,128]{1,0:T(8,128)(2,1)S(1)}, u32[]{:S(2)}, u32[]{:S(2)}) %collective-permute-start.23) | collective-permute-done | bytes 147488 | tf_op jit(solution)/shard_map/ppermute | solution.py:58
  121.3 1.5 copy-done.9
  122.8 1.4 core_turn.4
  124.2 2.3 collective-permute-done.24.refs_4_
  127.6 2.0 collective-permute-start.33
  129.7 2.2 collective-permute-start.34
  132.9 3.1 %collective-permute-done.35 = bf16[880,128]{1,0:T(8,128)(2,1)S(1)} collective-permute-done((bf16[880,128]{1,0:T(8,128)(2,1)S(1)}, bf16[880,128]{1,0:T(8,128)(2,1)S(1)}, u32[]{:S(2)}, u32[]{:S(2)}) %collective-permute-start.35) | collective-permute-done | bytes 225312 | tf_op jit(solution)/shard_map/ppermute | solution.py:58
  136.0 2.2 collective-permute-start.36
  138.1 10.6 %collective-permute-done.37 = bf16[864,128]{1,0:T(8,128)(2,1)S(1)} collective-permute-done((bf16[864,128]{1,0:T(8,128)(2,1)S(1)}, bf16[864,128]{1,0:T(8,128)(2,1)S(1)}, u32[]{:S(2)}, u32[]{:S(2)}) %collective-permute-start.37) | collective-permute-done | bytes 221216 | tf_op jit(solution)/shard_map/ppermute | solution.py:58
  152.5 2.2 collective-permute-done.38.refs_4_
  154.7 2.6 %spread.4 = bf16[16,784,128]{2,1,0:T(8,128)(2,1)} custom-call(s32[16]{0:T(128)S(1)} %get-tuple-element.116.head_ref, bf16[1744,128]{1,0:T(8,128)(2,1)S(1)} %get-tuple-element.168.refs_0_, bf16[1744,128]{1,0:T(8,128)(2,1)S(1)} %collective-permute-done.33.refs_1_, bf16[1744,128]{1,0:T(8,128)(2,1)S(1)} %collective-permute-done.34.refs_2_, ...), custom_call_target="tpu_custom_call" | custom-call | tf_op jit(solution)/shard_map/spread/pallas_call | solution.py:391
  157.3 7.2 %all-to-all-start = ((bf16[16,784,128]{2,1,0:T(8,128)(2,1)}), bf16[16,784,128]{2,1,0:T(8,128)(2,1)}, u32[]{:S(2)}, u32[]{:S(2)}) async-start(bf16[16,784,128]{2,1,0:T(8,128)(2,1)} %spread.4), calls=%async_computation | async-start | bytes 6422528 | tf_op jit(solution)/shard_map/all_to_all | solution.py:401
  164.5 2.0 collective-permute-start.27
  166.5 2.2 collective-permute-start.28
  168.7 1.1 collective-permute-start.31
  170.5 2.2 collective-permute-start.30
  172.7 5.2 %collective-permute-done.31 = bf16[576,128]{1,0:T(8,128)(2,1)S(1)} collective-permute-done((bf16[576,128]{1,0:T(8,128)(2,1)}, bf16[576,128]{1,0:T(8,128)(2,1)S(1)}, u32[]{:S(2)}, u32[]{:S(2)}) %collective-permute-start.31) | collective-permute-done | bytes 147488 | tf_op jit(solution)/shard_map/ppermute | solution.py:58
  178.0 5.1 %collective-permute-done.32.refs_4_ = bf16[576,128]{1,0:T(8,128)(2,1)S(1)} collective-permute-done((bf16[576,128]{1,0:T(8,128)(2,1)S(1)}, bf16[576,128]{1,0:T(8,128)(2,1)S(1)}, u32[]{:S(2)}, u32[]{:S(2)}) %collective-permute-start.32) | collective-permute-done | bytes 147488 | tf_op jit(solution)/shard_map/ppermute | solution.py:58
  183.9 1.6 collective-permute-start.43
  185.5 1.5 collective-permute-start.39
  187.0 17.3 %collective-permute-done.43.refs_1_.refs_6_ = bf16[8,272,128]{2,1,0:T(8,128)(2,1)S(1)} collective-permute-done((bf16[8,272,128]{2,1,0:T(8,128)(2,1)S(1)}, bf16[8,272,128]{2,1,0:T(8,128)(2,1)S(1)}, u32[]{:S(2)}, u32[]{:S(2)}) %collective-permute-start.43) | collective-permute-done | bytes 557088 | tf_op jit(solution)/shard_map/ppermute | solution.py:88
  204.3 1.7 collective-permute-start.44
  206.0 1.1 collective-permute-done.39.refs_1_
  207.9 6.1 %collective-permute-done.44.refs_2_.refs_7_ = bf16[8,272,128]{2,1,0:T(8,128)(2,1)S(1)} collective-permute-done((bf16[8,272,128]{2,1,0:T(8,128)(2,1)S(1)}, bf16[8,272,128]{2,1,0:T(8,128)(2,1)S(1)}, u32[]{:S(2)}, u32[]{:S(2)}) %collective-permute-start.44) | collective-permute-done | bytes 557088 | tf_op jit(solution)/shard_map/ppermute | solution.py:88
  214.0 1.7 collective-permute-start.45
  216.4 3.0 %collective-permute-start.41 = (bf16[8,256,128]{2,1,0:T(8,128)(2,1)S(1)}, bf16[8,256,128]{2,1,0:T(8,128)(2,1)S(1)}, u32[]{:S(2)}, u32[]{:S(2)}) collective-permute-start(bf16[8,256,128]{2,1,0:T(8,128)(2,1)S(1)} %regroup.7), channel_id=1, source_target_pairs={{0,3},{1,2},{2,1},{3,0},{4,7},{5,6},{6,5},{7,4},{8,11},{9,10},{10,... | collective-permute-start | bytes 1572872 | tf_op jit(solution)/shard_map/ppermute | solution.py:88
  219.4 5.4 %collective-permute-done.45.refs_3_.refs_8_ = bf16[8,272,128]{2,1,0:T(8,128)(2,1)S(1)} collective-permute-done((bf16[8,272,128]{2,1,0:T(8,128)(2,1)S(1)}, bf16[8,272,128]{2,1,0:T(8,128)(2,1)S(1)}, u32[]{:S(2)}, u32[]{:S(2)}) %collective-permute-start.45) | collective-permute-done | bytes 557088 | tf_op jit(solution)/shard_map/ppermute | solution.py:88
  225.7 4.5 %collective-permute-start.46 = (bf16[8,272,128]{2,1,0:T(8,128)(2,1)}, bf16[8,272,128]{2,1,0:T(8,128)(2,1)}, u32[]{:S(2)}, u32[]{:S(2)}) collective-permute-start(bf16[8,272,128]{2,1,0:T(8,128)(2,1)} %regroup.11), channel_id=1, source_target_pairs={{0,3},{1,2},{2,1},{3,0},{4,7},{5,6},{6,5},{7,4},{8,11},{9,10},{10,... | collective-permute-start | bytes 1671176 | tf_op jit(solution)/shard_map/ppermute | solution.py:88
  231.9 5.8 %pack.3 = (f32[16,128]{1,0:T(8,128)S(1)}, bf16[1,16,128,2048]{3,2,1,0:T(8,128)(2,1)}) custom-call(s32[16]{0:T(128)S(1)} %add_select_fusion.1.slot_ref, s32[16]{0:T(128)S(1)} %get-tuple-element.183.live_ref, s32[4]{0:T(128)S(1)} %xor_multiply_fusion.place_ref, bf16[16,784,128]{2,1,0:T(8,128)(2,1)S(1)} %all-to-all-done.1.refs_0_), custom_call_target="tpu_custom_call" | custom-call | tf_op jit(solution)/shard_map/pack/pallas_call | solution.py:406
  237.8 7.3 %pack.4 = (f32[16,128]{1,0:T(8,128)S(1)}, bf16[1,16,128,2048]{3,2,1,0:T(8,128)(2,1)}) custom-call(s32[16]{0:T(128)S(1)} %add_select_fusion.1.slot_ref, s32[16]{0:T(128)S(1)} %get-tuple-element.183.live_ref, s32[4]{0:T(128)S(1)} %xor_multiply_fusion.place_ref, bf16[16,784,128]{2,1,0:T(8,128)(2,1)} %all-to-all-done.refs_0_, ...), custom_call_target="tpu_custom_call", output_to_operand_aliasing={{1}: (5, {})} | custom-call | tf_op jit(solution)/shard_map/pack/pallas_call | solution.py:406
  245.2 6.8 %pack.5 = (f32[16,128]{1,0:T(8,128)}, bf16[1,16,128,2048]{3,2,1,0:T(8,128)(2,1)}) custom-call(s32[16]{0:T(128)S(1)} %add_select_fusion.slot_ref, s32[16]{0:T(128)S(1)} %get-tuple-element.103.live_ref, s32[4]{0:T(128)S(1)} %xor_multiply_fusion.place_ref, bf16[8,256,128]{2,1,0:T(8,128)(2,1)S(1)} %copy-done.5, ...), custom_call_target="tpu_custom_call", output_to_operand_aliasing={{1}: (14, {})} | custom-call | tf_op jit(solution)/shard_map/pack/pallas_call | solution.py:406
  (129 shorter events, 22.7 us)
Async XLA Ops:
  19.1 37.1 %copy-start.22 = (bf16[1152,128]{1,0:T(8,128)(2,1)}, bf16[1152,128]{1,0:T(8,128)(2,1)S(1)}, u32[]{:S(2)}) copy-start(bf16[1152,128]{1,0:T(8,128)(2,1)S(1)} %get-tuple-element.146) | copy-start | bytes 884740
  19.1 37.1 %copy-start.25 = (bf16[576,128]{1,0:T(8,128)(2,1)}, bf16[576,128]{1,0:T(8,128)(2,1)S(1)}, u32[]{:S(2)}) copy-start(bf16[576,128]{1,0:T(8,128)(2,1)S(1)} %get-tuple-element.148) | copy-start | bytes 442372
  19.1 37.2 %copy-start.26 = (bf16[576,128]{1,0:T(8,128)(2,1)}, bf16[576,128]{1,0:T(8,128)(2,1)S(1)}, u32[]{:S(2)}) copy-start(bf16[576,128]{1,0:T(8,128)(2,1)S(1)} %get-tuple-element.147) | copy-start | bytes 442372
  19.1 8.3 %collective-permute-start.2 = (bf16[864,128]{1,0:T(8,128)(2,1)S(1)}, bf16[864,128]{1,0:T(8,128)(2,1)S(1)}, u32[]{:S(2)}, u32[]{:S(2)}) collective-permute-start(bf16[864,128]{1,0:T(8,128)(2,1)S(1)} %get-tuple-element.120), channel_id=1, source_target_pairs={{0,32},{16,48},{32,0},{48,16},{64,96},{80,112},{96,64},{112,80},{1... | collective-permute-start | bytes 663560 | tf_op jit(solution)/shard_map/ppermute | solution.py:58
  20.7 9.8 %collective-permute-start.4 = (bf16[864,128]{1,0:T(8,128)(2,1)S(1)}, bf16[864,128]{1,0:T(8,128)(2,1)S(1)}, u32[]{:S(2)}, u32[]{:S(2)}) collective-permute-start(bf16[864,128]{1,0:T(8,128)(2,1)S(1)} %get-tuple-element.121), channel_id=1, source_target_pairs={{0,96},{16,112},{32,64},{48,80},{64,32},{80,48},{96,0},{112,16},{1... | collective-permute-start | bytes 663560 | tf_op jit(solution)/shard_map/ppermute | solution.py:58
  22.9 20.1 %collective-permute-start = (bf16[1728,128]{1,0:T(8,128)(2,1)S(1)}, bf16[1728,128]{1,0:T(8,128)(2,1)S(1)}, u32[]{:S(2)}, u32[]{:S(2)}) collective-permute-start(bf16[1728,128]{1,0:T(8,128)(2,1)S(1)} %get-tuple-element.118), channel_id=1, source_target_pairs={{0,32},{16,48},{32,0},{48,16},{64,96},{80,112},{96,64},{112,80},{1... | collective-permute-start | bytes 1327112 | tf_op jit(solution)/shard_map/ppermute | solution.py:58
  23.6 19.5 %collective-permute-start.1 = (bf16[1728,128]{1,0:T(8,128)(2,1)S(1)}, bf16[1728,128]{1,0:T(8,128)(2,1)S(1)}, u32[]{:S(2)}, u32[]{:S(2)}) collective-permute-start(bf16[1728,128]{1,0:T(8,128)(2,1)S(1)} %get-tuple-element.119), channel_id=1, source_target_pairs={{0,96},{16,112},{32,64},{48,80},{64,32},{80,48},{96,0},{112,16},{1... | collective-permute-start | bytes 1327112 | tf_op jit(solution)/shard_map/ppermute | solution.py:58
  27.4 15.6 %collective-permute-start.3 = (bf16[864,128]{1,0:T(8,128)(2,1)S(1)}, bf16[864,128]{1,0:T(8,128)(2,1)S(1)}, u32[]{:S(2)}, u32[]{:S(2)}) collective-permute-start(bf16[864,128]{1,0:T(8,128)(2,1)S(1)} %collective-permute-done.2), channel_id=1, source_target_pairs={{0,96},{16,112},{32,64},{48,80},{64,32},{80,48},{96,0},{112,16},{1... | collective-permute-start | bytes 663560 | tf_op jit(solution)/shard_map/ppermute | solution.py:58
  30.5 12.6 %collective-permute-start.5 = (bf16[864,128]{1,0:T(8,128)(2,1)S(1)}, bf16[864,128]{1,0:T(8,128)(2,1)S(1)}, u32[]{:S(2)}, u32[]{:S(2)}) collective-permute-start(bf16[864,128]{1,0:T(8,128)(2,1)S(1)} %collective-permute-done.4), channel_id=1, source_target_pairs={{0,32},{16,48},{32,0},{48,16},{64,96},{80,112},{96,64},{112,80},{1... | collective-permute-start | bytes 663560 | tf_op jit(solution)/shard_map/ppermute | solution.py:58
  44.3 10.6 %collective-permute-start.6 = (bf16[4,1728,128]{2,1,0:T(8,128)(2,1)S(1)}, bf16[4,1728,128]{2,1,0:T(8,128)(2,1)S(1)}, u32[]{:S(2)}, u32[]{:S(2)}) collective-permute-start(bf16[4,1728,128]{2,1,0:T(8,128)(2,1)S(1)} %y_turn.3.mine_ref), channel_id=1, source_target_pairs={{0,16},{16,0},{32,48},{48,32},{64,80},{80,64},{96,112},{112,96},{1... | collective-permute-start | bytes 5308424 | tf_op jit(solution)/shard_map/ppermute | solution.py:58
  44.4 8.3 %collective-permute-start.15 = (bf16[864,128]{1,0:T(8,128)(2,1)S(1)}, bf16[864,128]{1,0:T(8,128)(2,1)S(1)}, u32[]{:S(2)}, u32[]{:S(2)}) collective-permute-start(bf16[864,128]{1,0:T(8,128)(2,1)S(1)} %get-tuple-element.132), channel_id=1, source_target_pairs={{0,32},{16,48},{32,0},{48,16},{64,96},{80,112},{96,64},{112,80},{1... | collective-permute-start | bytes 663560 | tf_op jit(solution)/shard_map/ppermute | solution.py:58
  44.4 10.4 %collective-permute-start.17 = (bf16[864,128]{1,0:T(8,128)(2,1)S(1)}, bf16[864,128]{1,0:T(8,128)(2,1)S(1)}, u32[]{:S(2)}, u32[]{:S(2)}) collective-permute-start(bf16[864,128]{1,0:T(8,128)(2,1)S(1)} %get-tuple-element.133), channel_id=1, source_target_pairs={{0,96},{16,112},{32,64},{48,80},{64,32},{80,48},{96,0},{112,16},{1... | collective-permute-start | bytes 663560 | tf_op jit(solution)/shard_map/ppermute | solution.py:58
  46.7 22.4 %collective-permute-start.13 = (bf16[1728,128]{1,0:T(8,128)(2,1)S(1)}, bf16[1728,128]{1,0:T(8,128)(2,1)S(1)}, u32[]{:S(2)}, u32[]{:S(2)}) collective-permute-start(bf16[1728,128]{1,0:T(8,128)(2,1)S(1)} %get-tuple-element.130), channel_id=1, source_target_pairs={{0,32},{16,48},{32,0},{48,16},{64,96},{80,112},{96,64},{112,80},{1... | collective-permute-start | bytes 1327112 | tf_op jit(solution)/shard_map/ppermute | solution.py:58
  52.7 7.7 %collective-permute-start.16 = (bf16[864,128]{1,0:T(8,128)(2,1)S(1)}, bf16[864,128]{1,0:T(8,128)(2,1)S(1)}, u32[]{:S(2)}, u32[]{:S(2)}) collective-permute-start(bf16[864,128]{1,0:T(8,128)(2,1)S(1)} %collective-permute-done.15), channel_id=1, source_target_pairs={{0,96},{16,112},{32,64},{48,80},{64,32},{80,48},{96,0},{112,16},{1... | collective-permute-start | bytes 663560 | tf_op jit(solution)/shard_map/ppermute | solution.py:58
  54.9 12.0 %collective-permute-start.18 = (bf16[864,128]{1,0:T(8,128)(2,1)S(1)}, bf16[864,128]{1,0:T(8,128)(2,1)S(1)}, u32[]{:S(2)}, u32[]{:S(2)}) collective-permute-start(bf16[864,128]{1,0:T(8,128)(2,1)S(1)} %collective-permute-done.17), channel_id=1, source_target_pairs={{0,32},{16,48},{32,0},{48,16},{64,96},{80,112},{96,64},{112,80},{1... | collective-permute-start | bytes 663560 | tf_op jit(solution)/shard_map/ppermute | solution.py:58
  56.2 15.5 %collective-permute-start.9 = (bf16[880,128]{1,0:T(8,128)(2,1)S(1)}, bf16[880,128]{1,0:T(8,128)(2,1)S(1)}, u32[]{:S(2)}, u32[]{:S(2)}) collective-permute-start(bf16[880,128]{1,0:T(8,128)(2,1)S(1)} %get-tuple-element.127), channel_id=1, source_target_pairs={{0,32},{16,48},{32,0},{48,16},{64,96},{80,112},{96,64},{112,80},{1... | collective-permute-start | bytes 675848 | tf_op jit(solution)/shard_map/ppermute | solution.py:58
  58.3 35.9 %collective-permute-start.7 = (bf16[1744,128]{1,0:T(8,128)(2,1)S(1)}, bf16[1744,128]{1,0:T(8,128)(2,1)S(1)}, u32[]{:S(2)}, u32[]{:S(2)}) collective-permute-start(bf16[1744,128]{1,0:T(8,128)(2,1)S(1)} %get-tuple-element.125), channel_id=1, source_target_pairs={{0,32},{16,48},{32,0},{48,16},{64,96},{80,112},{96,64},{112,80},{1... | collective-permute-start | bytes 1339400 | tf_op jit(solution)/shard_map/ppermute | solution.py:58
  60.4 33.8 %collective-permute-start.8 = (bf16[1744,128]{1,0:T(8,128)(2,1)S(1)}, bf16[1744,128]{1,0:T(8,128)(2,1)S(1)}, u32[]{:S(2)}, u32[]{:S(2)}) collective-permute-start(bf16[1744,128]{1,0:T(8,128)(2,1)S(1)} %get-tuple-element.126), channel_id=1, source_target_pairs={{0,96},{16,112},{32,64},{48,80},{64,32},{80,48},{96,0},{112,16},{1... | collective-permute-start | bytes 1339400 | tf_op jit(solution)/shard_map/ppermute | solution.py:58
  66.9 21.4 %collective-permute-start.14 = (bf16[1728,128]{1,0:T(8,128)(2,1)S(1)}, bf16[1728,128]{1,0:T(8,128)(2,1)S(1)}, u32[]{:S(2)}, u32[]{:S(2)}) collective-permute-start(bf16[1728,128]{1,0:T(8,128)(2,1)S(1)} %get-tuple-element.131), channel_id=1, source_target_pairs={{0,96},{16,112},{32,64},{48,80},{64,32},{80,48},{96,0},{112,16},{1... | collective-permute-start | bytes 1327112 | tf_op jit(solution)/shard_map/ppermute | solution.py:58
  69.1 19.2 %collective-permute-start.11 = (bf16[864,128]{1,0:T(8,128)(2,1)S(1)}, bf16[864,128]{1,0:T(8,128)(2,1)S(1)}, u32[]{:S(2)}, u32[]{:S(2)}) collective-permute-start(bf16[864,128]{1,0:T(8,128)(2,1)S(1)} %get-tuple-element.128), channel_id=1, source_target_pairs={{0,96},{16,112},{32,64},{48,80},{64,32},{80,48},{96,0},{112,16},{1... | collective-permute-start | bytes 663560 | tf_op jit(solution)/shard_map/ppermute | solution.py:58
  71.7 22.5 %collective-permute-start.10 = (bf16[880,128]{1,0:T(8,128)(2,1)S(1)}, bf16[880,128]{1,0:T(8,128)(2,1)S(1)}, u32[]{:S(2)}, u32[]{:S(2)}) collective-permute-start(bf16[880,128]{1,0:T(8,128)(2,1)S(1)} %collective-permute-done.9), channel_id=1, source_target_pairs={{0,96},{16,112},{32,64},{48,80},{64,32},{80,48},{96,0},{112,16},{1... | collective-permute-start | bytes 675848 | tf_op jit(solution)/shard_map/ppermute | solution.py:58
  88.3 5.9 %collective-permute-start.12 = (bf16[864,128]{1,0:T(8,128)(2,1)S(1)}, bf16[864,128]{1,0:T(8,128)(2,1)S(1)}, u32[]{:S(2)}, u32[]{:S(2)}) collective-permute-start(bf16[864,128]{1,0:T(8,128)(2,1)S(1)} %collective-permute-done.11), channel_id=1, source_target_pairs={{0,32},{16,48},{32,0},{48,16},{64,96},{80,112},{96,64},{112,80},{1... | collective-permute-start | bytes 663560 | tf_op jit(solution)/shard_map/ppermute | solution.py:58
  96.8 60.5 %all-to-all-start.1 = ((bf16[16,784,128]{2,1,0:T(8,128)(2,1)}), bf16[16,784,128]{2,1,0:T(8,128)(2,1)S(1)}, u32[]{:S(2)}, u32[]{:S(2)}) async-start(bf16[16,784,128]{2,1,0:T(8,128)(2,1)} %spread.3), calls=%async_computation.1 | async-start | bytes 6422528 | tf_op jit(solution)/shard_map/all_to_all | solution.py:401
  104.7 16.7 %collective-permute-start.25 = (bf16[4,1728,128]{2,1,0:T(8,128)(2,1)}, bf16[4,1728,128]{2,1,0:T(8,128)(2,1)S(1)}, u32[]{:S(2)}, u32[]{:S(2)}) collective-permute-start(bf16[4,1728,128]{2,1,0:T(8,128)(2,1)} %copy-done.8), channel_id=1, source_target_pairs={{0,16},{16,0},{32,48},{48,32},{64,80},{80,64},{96,112},{112,96},{1... | collective-permute-start | bytes 5308424 | tf_op jit(solution)/shard_map/ppermute | solution.py:58
  104.7 6.9 %collective-permute-start.21 = (bf16[576,128]{1,0:T(8,128)(2,1)}, bf16[576,128]{1,0:T(8,128)(2,1)S(1)}, u32[]{:S(2)}, u32[]{:S(2)}) collective-permute-start(bf16[576,128]{1,0:T(8,128)(2,1)} %copy-done.26), channel_id=1, source_target_pairs={{0,32},{16,48},{32,0},{48,16},{64,96},{80,112},{96,64},{112,80},{1... | collective-permute-start | bytes 442376 | tf_op jit(solution)/shard_map/ppermute | solution.py:58
  104.8 19.3 %collective-permute-start.19 = (bf16[1152,128]{1,0:T(8,128)(2,1)}, bf16[1152,128]{1,0:T(8,128)(2,1)S(1)}, u32[]{:S(2)}, u32[]{:S(2)}) collective-permute-start(bf16[1152,128]{1,0:T(8,128)(2,1)} %copy-done.23), channel_id=1, source_target_pairs={{0,32},{16,48},{32,0},{48,16},{64,96},{80,112},{96,64},{112,80},{1... | collective-permute-start | bytes 884744 | tf_op jit(solution)/shard_map/ppermute | solution.py:58
  106.9 17.3 %collective-permute-start.20 = (bf16[1152,128]{1,0:T(8,128)(2,1)}, bf16[1152,128]{1,0:T(8,128)(2,1)S(1)}, u32[]{:S(2)}, u32[]{:S(2)}) collective-permute-start(bf16[1152,128]{1,0:T(8,128)(2,1)} %copy-done.22), channel_id=1, source_target_pairs={{0,96},{16,112},{32,64},{48,80},{64,32},{80,48},{96,0},{112,16},{1... | collective-permute-start | bytes 884744 | tf_op jit(solution)/shard_map/ppermute | solution.py:58
  109.0 12.3 %collective-permute-start.23 = (bf16[576,128]{1,0:T(8,128)(2,1)}, bf16[576,128]{1,0:T(8,128)(2,1)S(1)}, u32[]{:S(2)}, u32[]{:S(2)}) collective-permute-start(bf16[576,128]{1,0:T(8,128)(2,1)} %copy-done.25), channel_id=1, source_target_pairs={{0,96},{16,112},{32,64},{48,80},{64,32},{80,48},{96,0},{112,16},{1... | collective-permute-start | bytes 442376 | tf_op jit(solution)/shard_map/ppermute | solution.py:58
  111.7 12.5 %collective-permute-start.22 = (bf16[576,128]{1,0:T(8,128)(2,1)S(1)}, bf16[576,128]{1,0:T(8,128)(2,1)S(1)}, u32[]{:S(2)}, u32[]{:S(2)}) collective-permute-start(bf16[576,128]{1,0:T(8,128)(2,1)S(1)} %collective-permute-done.21), channel_id=1, source_target_pairs={{0,96},{16,112},{32,64},{48,80},{64,32},{80,48},{96,0},{112,16},{1... | collective-permute-start | bytes 442376 | tf_op jit(solution)/shard_map/ppermute | solution.py:58
  121.3 5.1 %collective-permute-start.24 = (bf16[576,128]{1,0:T(8,128)(2,1)S(1)}, bf16[576,128]{1,0:T(8,128)(2,1)S(1)}, u32[]{:S(2)}, u32[]{:S(2)}) collective-permute-start(bf16[576,128]{1,0:T(8,128)(2,1)S(1)} %collective-permute-done.23), channel_id=1, source_target_pairs={{0,32},{16,48},{32,0},{48,16},{64,96},{80,112},{96,64},{112,80},{1... | collective-permute-start | bytes 442376 | tf_op jit(solution)/shard_map/ppermute | solution.py:58
  127.5 21.3 %collective-permute-start.26 = (bf16[4,1152,128]{2,1,0:T(8,128)(2,1)S(1)}, bf16[4,1152,128]{2,1,0:T(8,128)(2,1)S(1)}, u32[]{:S(2)}, u32[]{:S(2)}) collective-permute-start(bf16[4,1152,128]{2,1,0:T(8,128)(2,1)S(1)} %y_turn.5.mine_ref), channel_id=1, source_target_pairs={{0,16},{16,0},{32,48},{48,32},{64,80},{80,64},{96,112},{112,96},{1... | collective-permute-start | bytes 3538952 | tf_op jit(solution)/shard_map/ppermute | solution.py:58
  127.5 8.4 %collective-permute-start.35 = (bf16[880,128]{1,0:T(8,128)(2,1)S(1)}, bf16[880,128]{1,0:T(8,128)(2,1)S(1)}, u32[]{:S(2)}, u32[]{:S(2)}) collective-permute-start(bf16[880,128]{1,0:T(8,128)(2,1)S(1)} %get-tuple-element.166), channel_id=1, source_target_pairs={{0,32},{16,48},{32,0},{48,16},{64,96},{80,112},{96,64},{112,80},{1... | collective-permute-start | bytes 675848 | tf_op jit(solution)/shard_map/ppermute | solution.py:58
  127.6 27.0 %collective-permute-start.33 = (bf16[1744,128]{1,0:T(8,128)(2,1)S(1)}, bf16[1744,128]{1,0:T(8,128)(2,1)S(1)}, u32[]{:S(2)}, u32[]{:S(2)}) collective-permute-start(bf16[1744,128]{1,0:T(8,128)(2,1)S(1)} %get-tuple-element.164), channel_id=1, source_target_pairs={{0,32},{16,48},{32,0},{48,16},{64,96},{80,112},{96,64},{112,80},{1... | collective-permute-start | bytes 1339400 | tf_op jit(solution)/shard_map/ppermute | solution.py:58
  129.7 25.0 %collective-permute-start.34 = (bf16[1744,128]{1,0:T(8,128)(2,1)S(1)}, bf16[1744,128]{1,0:T(8,128)(2,1)S(1)}, u32[]{:S(2)}, u32[]{:S(2)}) collective-permute-start(bf16[1744,128]{1,0:T(8,128)(2,1)S(1)} %get-tuple-element.165), channel_id=1, source_target_pairs={{0,96},{16,112},{32,64},{48,80},{64,32},{80,48},{96,0},{112,16},{1... | collective-permute-start | bytes 1339400 | tf_op jit(solution)/shard_map/ppermute | solution.py:58
  131.8 16.9 %collective-permute-start.37 = (bf16[864,128]{1,0:T(8,128)(2,1)S(1)}, bf16[864,128]{1,0:T(8,128)(2,1)S(1)}, u32[]{:S(2)}, u32[]{:S(2)}) collective-permute-start(bf16[864,128]{1,0:T(8,128)(2,1)S(1)} %get-tuple-element.167), channel_id=1, source_target_pairs={{0,96},{16,112},{32,64},{48,80},{64,32},{80,48},{96,0},{112,16},{1... | collective-permute-start | bytes 663560 | tf_op jit(solution)/shard_map/ppermute | solution.py:58
  136.0 18.7 %collective-permute-start.36 = (bf16[880,128]{1,0:T(8,128)(2,1)S(1)}, bf16[880,128]{1,0:T(8,128)(2,1)S(1)}, u32[]{:S(2)}, u32[]{:S(2)}) collective-permute-start(bf16[880,128]{1,0:T(8,128)(2,1)S(1)} %collective-permute-done.35), channel_id=1, source_target_pairs={{0,96},{16,112},{32,64},{48,80},{64,32},{80,48},{96,0},{112,16},{1... | collective-permute-start | bytes 675848 | tf_op jit(solution)/shard_map/ppermute | solution.py:58
  148.7 5.9 %collective-permute-start.38 = (bf16[864,128]{1,0:T(8,128)(2,1)S(1)}, bf16[864,128]{1,0:T(8,128)(2,1)S(1)}, u32[]{:S(2)}, u32[]{:S(2)}) collective-permute-start(bf16[864,128]{1,0:T(8,128)(2,1)S(1)} %collective-permute-done.37), channel_id=1, source_target_pairs={{0,32},{16,48},{32,0},{48,16},{64,96},{80,112},{96,64},{112,80},{1... | collective-permute-start | bytes 663560 | tf_op jit(solution)/shard_map/ppermute | solution.py:58
  157.3 80.5 %all-to-all-start = ((bf16[16,784,128]{2,1,0:T(8,128)(2,1)}), bf16[16,784,128]{2,1,0:T(8,128)(2,1)}, u32[]{:S(2)}, u32[]{:S(2)}) async-start(bf16[16,784,128]{2,1,0:T(8,128)(2,1)} %spread.4), calls=%async_computation | async-start | bytes 6422528 | tf_op jit(solution)/shard_map/all_to_all | solution.py:401
  164.4 6.1 %collective-permute-start.29 = (bf16[592,128]{1,0:T(8,128)(2,1)}, bf16[592,128]{1,0:T(8,128)(2,1)S(1)}, u32[]{:S(2)}, u32[]{:S(2)}) collective-permute-start(bf16[592,128]{1,0:T(8,128)(2,1)} %copy-done.24), channel_id=1, source_target_pairs={{0,32},{16,48},{32,0},{48,16},{64,96},{80,112},{96,64},{112,80},{1... | collective-permute-start | bytes 454664 | tf_op jit(solution)/shard_map/ppermute | solution.py:58
  164.5 18.6 %collective-permute-start.27 = (bf16[1168,128]{1,0:T(8,128)(2,1)}, bf16[1168,128]{1,0:T(8,128)(2,1)S(1)}, u32[]{:S(2)}, u32[]{:S(2)}) collective-permute-start(bf16[1168,128]{1,0:T(8,128)(2,1)} %copy-done.21), channel_id=1, source_target_pairs={{0,32},{16,48},{32,0},{48,16},{64,96},{80,112},{96,64},{112,80},{1... | collective-permute-start | bytes 897032 | tf_op jit(solution)/shard_map/ppermute | solution.py:58
  166.5 16.6 %collective-permute-start.28 = (bf16[1168,128]{1,0:T(8,128)(2,1)}, bf16[1168,128]{1,0:T(8,128)(2,1)S(1)}, u32[]{:S(2)}, u32[]{:S(2)}) collective-permute-start(bf16[1168,128]{1,0:T(8,128)(2,1)} %copy-done.20), channel_id=1, source_target_pairs={{0,96},{16,112},{32,64},{48,80},{64,32},{80,48},{96,0},{112,16},{1... | collective-permute-start | bytes 897032 | tf_op jit(solution)/shard_map/ppermute | solution.py:58
  168.7 9.2 %collective-permute-start.31 = (bf16[576,128]{1,0:T(8,128)(2,1)}, bf16[576,128]{1,0:T(8,128)(2,1)S(1)}, u32[]{:S(2)}, u32[]{:S(2)}) collective-permute-start(bf16[576,128]{1,0:T(8,128)(2,1)} %copy-done.27), channel_id=1, source_target_pairs={{0,96},{16,112},{32,64},{48,80},{64,32},{80,48},{96,0},{112,16},{1... | collective-permute-start | bytes 442376 | tf_op jit(solution)/shard_map/ppermute | solution.py:58
  170.5 12.6 %collective-permute-start.30 = (bf16[592,128]{1,0:T(8,128)(2,1)S(1)}, bf16[592,128]{1,0:T(8,128)(2,1)S(1)}, u32[]{:S(2)}, u32[]{:S(2)}) collective-permute-start(bf16[592,128]{1,0:T(8,128)(2,1)S(1)} %collective-permute-done.29), channel_id=1, source_target_pairs={{0,96},{16,112},{32,64},{48,80},{64,32},{80,48},{96,0},{112,16},{1... | collective-permute-start | bytes 454664 | tf_op jit(solution)/shard_map/ppermute | solution.py:58
  177.9 5.1 %collective-permute-start.32 = (bf16[576,128]{1,0:T(8,128)(2,1)S(1)}, bf16[576,128]{1,0:T(8,128)(2,1)S(1)}, u32[]{:S(2)}, u32[]{:S(2)}) collective-permute-start(bf16[576,128]{1,0:T(8,128)(2,1)S(1)} %collective-permute-done.31), channel_id=1, source_target_pairs={{0,32},{16,48},{32,0},{48,16},{64,96},{80,112},{96,64},{112,80},{1... | collective-permute-start | bytes 442376 | tf_op jit(solution)/shard_map/ppermute | solution.py:58
  183.9 40.9 %copy-start = (bf16[8,272,128]{2,1,0:T(8,128)(2,1)}, bf16[8,272,128]{2,1,0:T(8,128)(2,1)S(1)}, u32[]{:S(2)}) copy-start(bf16[8,272,128]{2,1,0:T(8,128)(2,1)S(1)} %get-tuple-element.194.refs_0_.refs_5_) | copy-start | bytes 1671172
  183.9 46.3 %copy-start.4 = (bf16[8,256,128]{2,1,0:T(8,128)(2,1)}, bf16[8,256,128]{2,1,0:T(8,128)(2,1)S(1)}, u32[]{:S(2)}) copy-start(bf16[8,256,128]{2,1,0:T(8,128)(2,1)S(1)} %get-tuple-element.189.refs_0_) | copy-start | bytes 1572868
  183.9 20.4 %collective-permute-start.43 = (bf16[8,272,128]{2,1,0:T(8,128)(2,1)S(1)}, bf16[8,272,128]{2,1,0:T(8,128)(2,1)S(1)}, u32[]{:S(2)}, u32[]{:S(2)}) collective-permute-start(bf16[8,272,128]{2,1,0:T(8,128)(2,1)S(1)} %get-tuple-element.181), channel_id=1, source_target_pairs={{0,4},{1,5},{2,6},{3,7},{4,0},{5,1},{6,2},{7,3},{8,12},{9,13},{10,... | collective-permute-start | bytes 1671176 | tf_op jit(solution)/shard_map/ppermute | solution.py:88
  185.5 21.5 %collective-permute-start.39 = (bf16[8,256,128]{2,1,0:T(8,128)(2,1)S(1)}, bf16[8,256,128]{2,1,0:T(8,128)(2,1)S(1)}, u32[]{:S(2)}, u32[]{:S(2)}) collective-permute-start(bf16[8,256,128]{2,1,0:T(8,128)(2,1)S(1)} %get-tuple-element.179), channel_id=1, source_target_pairs={{0,1},{1,0},{2,3},{3,2},{4,5},{5,4},{6,7},{7,6},{8,9},{9,8},{10,11... | collective-permute-start | bytes 1572872 | tf_op jit(solution)/shard_map/ppermute | solution.py:88
  204.3 20.5 %copy-start.2 = (bf16[8,272,128]{2,1,0:T(8,128)(2,1)}, bf16[8,272,128]{2,1,0:T(8,128)(2,1)S(1)}, u32[]{:S(2)}) copy-start(bf16[8,272,128]{2,1,0:T(8,128)(2,1)S(1)} %collective-permute-done.43.refs_1_.refs_6_) | copy-start | bytes 1671172
  204.3 9.6 %collective-permute-start.44 = (bf16[8,272,128]{2,1,0:T(8,128)(2,1)S(1)}, bf16[8,272,128]{2,1,0:T(8,128)(2,1)S(1)}, u32[]{:S(2)}, u32[]{:S(2)}) collective-permute-start(bf16[8,272,128]{2,1,0:T(8,128)(2,1)S(1)} %regroup.9), channel_id=1, source_target_pairs={{0,1},{1,0},{2,3},{3,2},{4,5},{5,4},{6,7},{7,6},{8,9},{9,8},{10,11... | collective-permute-start | bytes 1671176 | tf_op jit(solution)/shard_map/ppermute | solution.py:88
  207.1 23.1 %copy-start.6 = (bf16[8,256,128]{2,1,0:T(8,128)(2,1)}, bf16[8,256,128]{2,1,0:T(8,128)(2,1)S(1)}, u32[]{:S(2)}) copy-start(bf16[8,256,128]{2,1,0:T(8,128)(2,1)S(1)} %collective-permute-done.39.refs_1_) | copy-start | bytes 1572868
  207.1 9.3 %collective-permute-start.40 = (bf16[8,256,128]{2,1,0:T(8,128)(2,1)S(1)}, bf16[8,256,128]{2,1,0:T(8,128)(2,1)S(1)}, u32[]{:S(2)}, u32[]{:S(2)}) collective-permute-start(bf16[8,256,128]{2,1,0:T(8,128)(2,1)S(1)} %regroup.6), channel_id=1, source_target_pairs={{0,4},{1,5},{2,6},{3,7},{4,0},{5,1},{6,2},{7,3},{8,12},{9,13},{10,... | collective-permute-start | bytes 1572872 | tf_op jit(solution)/shard_map/ppermute | solution.py:88
  213.9 11.8 %copy-start.10 = (bf16[8,272,128]{2,1,0:T(8,128)(2,1)}, bf16[8,272,128]{2,1,0:T(8,128)(2,1)S(1)}, u32[]{:S(2)}) copy-start(bf16[8,272,128]{2,1,0:T(8,128)(2,1)S(1)} %collective-permute-done.44.refs_2_.refs_7_) | copy-start | bytes 1671172
  214.0 10.8 %collective-permute-start.45 = (bf16[8,272,128]{2,1,0:T(8,128)(2,1)S(1)}, bf16[8,272,128]{2,1,0:T(8,128)(2,1)S(1)}, u32[]{:S(2)}, u32[]{:S(2)}) collective-permute-start(bf16[8,272,128]{2,1,0:T(8,128)(2,1)S(1)} %regroup.10), channel_id=1, source_target_pairs={{0,12},{1,13},{2,14},{3,15},{4,8},{5,9},{6,10},{7,11},{8,4},{9,5},... | collective-permute-start | bytes 1671176 | tf_op jit(solution)/shard_map/ppermute | solution.py:88
  216.4 14.8 %copy-start.12 = (bf16[8,256,128]{2,1,0:T(8,128)(2,1)}, bf16[8,256,128]{2,1,0:T(8,128)(2,1)S(1)}, u32[]{:S(2)}) copy-start(bf16[8,256,128]{2,1,0:T(8,128)(2,1)S(1)} %collective-permute-done.40.refs_2_) | copy-start | bytes 1572868
  216.4 13.8 %collective-permute-start.41 = (bf16[8,256,128]{2,1,0:T(8,128)(2,1)S(1)}, bf16[8,256,128]{2,1,0:T(8,128)(2,1)S(1)}, u32[]{:S(2)}, u32[]{:S(2)}) collective-permute-start(bf16[8,256,128]{2,1,0:T(8,128)(2,1)S(1)} %regroup.7), channel_id=1, source_target_pairs={{0,3},{1,2},{2,1},{3,0},{4,7},{5,6},{6,5},{7,4},{8,11},{9,10},{10,... | collective-permute-start | bytes 1572872 | tf_op jit(solution)/shard_map/ppermute | solution.py:88
  225.7 19.4 %collective-permute-start.46 = (bf16[8,272,128]{2,1,0:T(8,128)(2,1)}, bf16[8,272,128]{2,1,0:T(8,128)(2,1)}, u32[]{:S(2)}, u32[]{:S(2)}) collective-permute-start(bf16[8,272,128]{2,1,0:T(8,128)(2,1)} %regroup.11), channel_id=1, source_target_pairs={{0,3},{1,2},{2,1},{3,0},{4,7},{5,6},{6,5},{7,4},{8,11},{9,10},{10,... | collective-permute-start | bytes 1671176 | tf_op jit(solution)/shard_map/ppermute | solution.py:88
  231.1 14.0 %collective-permute-start.42 = (bf16[8,256,128]{2,1,0:T(8,128)(2,1)}, bf16[8,256,128]{2,1,0:T(8,128)(2,1)}, u32[]{:S(2)}, u32[]{:S(2)}) collective-permute-start(bf16[8,256,128]{2,1,0:T(8,128)(2,1)} %regroup.8), channel_id=1, source_target_pairs={{0,12},{1,13},{2,14},{3,15},{4,8},{5,9},{6,10},{7,11},{8,4},{9,5},... | collective-permute-start | bytes 1572872 | tf_op jit(solution)/shard_map/ppermute | solution.py:88
  237.7 7.4 %copy-start.1 = (bf16[8,272,128]{2,1,0:T(8,128)(2,1)S(1)}, bf16[8,272,128]{2,1,0:T(8,128)(2,1)}, u32[]{:S(2)}) copy-start(bf16[8,272,128]{2,1,0:T(8,128)(2,1)} %copy-done) | copy-start | bytes 1671172
  237.7 7.4 %copy-start.3 = (bf16[8,272,128]{2,1,0:T(8,128)(2,1)S(1)}, bf16[8,272,128]{2,1,0:T(8,128)(2,1)}, u32[]{:S(2)}) copy-start(bf16[8,272,128]{2,1,0:T(8,128)(2,1)} %copy-done.2) | copy-start | bytes 1671172
  237.7 7.4 %copy-start.5 = (bf16[8,256,128]{2,1,0:T(8,128)(2,1)S(1)}, bf16[8,256,128]{2,1,0:T(8,128)(2,1)}, u32[]{:S(2)}) copy-start(bf16[8,256,128]{2,1,0:T(8,128)(2,1)} %copy-done.4) | copy-start | bytes 1572868
  237.7 7.4 %copy-start.7 = (bf16[8,256,128]{2,1,0:T(8,128)(2,1)S(1)}, bf16[8,256,128]{2,1,0:T(8,128)(2,1)}, u32[]{:S(2)}) copy-start(bf16[8,256,128]{2,1,0:T(8,128)(2,1)} %copy-done.6) | copy-start | bytes 1572868
  237.7 7.4 %copy-start.11 = (bf16[8,272,128]{2,1,0:T(8,128)(2,1)S(1)}, bf16[8,272,128]{2,1,0:T(8,128)(2,1)}, u32[]{:S(2)}) copy-start(bf16[8,272,128]{2,1,0:T(8,128)(2,1)} %copy-done.10) | copy-start | bytes 1671172
  237.8 7.4 %copy-start.13 = (bf16[8,256,128]{2,1,0:T(8,128)(2,1)S(1)}, bf16[8,256,128]{2,1,0:T(8,128)(2,1)}, u32[]{:S(2)}) copy-start(bf16[8,256,128]{2,1,0:T(8,128)(2,1)} %copy-done.12) | copy-start | bytes 1572868
  (13 other events, 33.0 us)

commit v4 on v3

v4 whole, which is shorter than its diff:
```python
import functools

import numpy as np
import jax
import jax.numpy as jnp
from jax import lax
from jax.experimental import pallas as pl
from jax.experimental.pallas import tpu as pltpu
from jax.sharding import PartitionSpec as P

HEAD_DIM = 128
HAD = 128
CHUNKS = ((0, 48), (48, 48), (96, 32))
DIRECT = 2
ORDER = (
    ("start", 0),
    ("cross", 0),
    ("start", 1),
    ("spread", 0),
    ("cross", 1),
    ("start", 2),
    ("spread", 1),
    ("cross", 2),
    ("pack", 0),
    ("spread", 2),
    ("pack", 1),
    ("pack", 2),
)
TAIL = 16
VMEM_BYTES = 12 * 1024 * 1024
BOTH = ("fsdp", "tp")


def hadamard_table(order):
    matrix = np.ones((1, 1), np.float32)
    while matrix.shape[0] < order:
        matrix = np.block([[matrix, matrix], [matrix, -matrix]])
    return matrix


def butterfly(values):
    values = list(values)
    half = 1
    while half < len(values):
        for low in range(len(values)):
            if not low & half:
                first, second = values[low], values[low + half]
                values[low], values[low + half] = first + second, first - second
        half *= 2
    return values


PATHS = {4: (2, 6), 5: (6, 3), 2: (2,), 6: (6,), 3: (3,), 7: (7,), 1: (1,)}


def ring_exchange(blocks):
    size = lax.axis_size("fsdp")
    out = list(blocks)
    for offset, hops in PATHS.items():
        for flip in hops:
            out[offset] = lax.ppermute(out[offset], "fsdp", [(i, i ^ flip) for i in range(size)])
    return out


PAIRINGS = ((1, 3), (3, 1))
BITS_A = ((1, 0), (4, 0), (1, 1), (4, 1))
BITS_B = ((4, 0), (1, 0), (4, 1), (1, 1))


def owner_offsets(core, bits):
    table = np.zeros(1 << len(bits), np.int32)
    for index in range(len(table)):
        for bit, (factor, which) in enumerate(bits):
            if index >> bit & 1:
                table[index] ^= factor * PAIRINGS[core][which]
    return table


def owner_hop(array, factor, which):
    groups, owners = lax.axis_size("fsdp"), lax.axis_size("tp")
    pairs = []
    for f in range(groups):
        flip = factor * PAIRINGS[f & 1][which]
        pairs += [(f * owners + t, f * owners + (t ^ flip)) for t in range(owners)]
    return lax.ppermute(array, BOTH, pairs)


def regroup_kernel(plan, *refs):
    out_ref = refs[-1]
    for row, (array, index) in enumerate(plan):
        out_ref[row] = refs[array][index]


def hypercube(keep, send, bits):
    held = [keep, owner_hop(send, *bits[0])]
    for step in range(1, len(bits)):
        plan = []
        for array in range(len(held)):
            origins = 1 << max(array - 1, 0)
            size = keep.shape[0] // origins
            for origin in range(origins):
                width = keep.shape[0] >> step
                plan += [(array, origin * size + width + i) for i in range(width)]
        vmem_spec = pl.BlockSpec(memory_space=pltpu.VMEM)
        payload = pl.pallas_call(
            functools.partial(regroup_kernel, tuple(plan)),
            in_specs=[vmem_spec] * len(held),
            out_specs=vmem_spec,
            out_shape=jax.ShapeDtypeStruct(keep.shape, keep.dtype),
            compiler_params=pltpu.CompilerParams(vmem_limit_bytes=VMEM_BYTES),
            name="regroup",
        )(*held)
        held.append(owner_hop(payload, *bits[step]))
    return held


def first_slots(bits):
    slots = [(0, 0)]
    for array in range(1, bits + 1):
        origins = 1 << (array - 1)
        size = (1 << (bits - 1)) // origins
        slots += [(array, origin * size) for origin in range(origins)]
    return slots


def sign_of(value, bits):
    both = value & bits
    both = both ^ (both >> 2)
    both = both ^ (both >> 1)
    return (1 - 2 * (both & 1)).astype(jnp.float32)


def local_turn_kernel(rows_a, weight_ref, signs_ref, *refs):
    out_refs, turned = refs[:-1], refs[-1]
    group = lax.axis_index("fsdp")
    flips = [sign_of(group, a >> 1) * (1.0 / HAD) for a in range(rows_a)]
    columns = jnp.concatenate([weight_ref[a * HAD : (a + 1) * HAD, :].T for a in range(rows_a)], axis=0)
    turned[...] = jnp.dot(columns, signs_ref[...], preferred_element_type=jnp.float32)
    for index, (first, chans) in enumerate(CHUNKS):
        for low in range(0, chans, 16):
            outs = []
            for a in range(rows_a):
                start = a * HEAD_DIM + first + low
                outs.append(turned[start : start + 16, :] * flips[a])
            outs = butterfly(outs)
            for a in range(rows_a):
                row = a % 2 * chans + low
                out_refs[8 * index + a // 2][row : row + 16, :] = outs[a].astype(jnp.bfloat16)


def join_parts(value, chans):
    return value + pltpu.roll(value, HAD - chans, 1)


def split_parts(value, chans):
    high = value.astype(jnp.bfloat16).astype(jnp.float32)
    lane = lax.broadcasted_iota(jnp.int32, value.shape, 1)
    both = jnp.where(lane < chans, high, pltpu.roll(value - high, chans, 1))
    return jnp.where(lane < 2 * chans, both, 0.0).astype(jnp.bfloat16)


def cross_turn_kernel(heads, chans, *refs):
    in_refs, out_refs = refs[:8], refs[8:]
    group = lax.axis_index("fsdp")
    flips_in = [sign_of(group, s) for s in range(8)]
    flips_out = [flip * sign_of(group, group) for flip in flips_in]
    row_id = lax.broadcasted_iota(jnp.int32, (TAIL, HAD), 0)
    tail = jnp.zeros((TAIL, HAD), jnp.float32)
    for head in range(heads):
        columns = []
        for low in range(0, chans, 16):
            largest = None
            for e in range(2):
                row = (head * 2 + e) * chans + low
                outs = butterfly([in_refs[s][row : row + 16, :].astype(jnp.float32) * flips_in[s] for s in range(8)])
                for s in range(8):
                    out_refs[s][row : row + 16, :] = (outs[s] * flips_out[s]).astype(jnp.bfloat16)
                    magnitude = jnp.abs(outs[s])
                    largest = magnitude if largest is None else jnp.maximum(largest, magnitude)
            columns.append(largest)
        columns.append(jnp.zeros((HAD - chans, HAD), jnp.float32))
        peak = jnp.max(jnp.concatenate(columns, axis=0).T, axis=0, keepdims=True)
        tail = jnp.where(row_id == head, peak, tail)
    tail = split_parts(tail, chans)
    for out_ref in out_refs:
        out_ref[heads * 2 * chans :, :] = tail


def cube_offset(core, bits, index):
    offsets = [int(owner_offsets(c, bits)[index]) for c in range(2)]
    return jnp.where(core == 0, offsets[0], offsets[1])


def spread_kernel(heads, chans, placement_ref, *refs):
    in_refs, out_refs = refs[:8], refs[8:]
    me, core = lax.axis_index("tp"), lax.axis_index("fsdp") & 1
    mine = [placement_ref[me * heads + head] for head in range(heads)]

    def head_for(owner):
        head = 0
        for index in range(1, heads):
            head = jnp.where(mine[index] == owner, index, head)
        return head

    peaks = None
    for in_ref in in_refs:
        part = join_parts(in_ref[heads * 2 * chans :, :].astype(jnp.float32), chans)
        peaks = part if peaks is None else jnp.maximum(peaks, part)
    row_id = lax.broadcasted_iota(jnp.int32, (TAIL, HAD), 0)
    span = 2 * chans
    for slot in range(16):
        if len(out_refs) == 1:
            parts = ((out_refs[0], slot, head_for(slot), in_refs, True),)
        else:
            to_a, to_b = (me ^ cube_offset(core, bits[::-1], slot) for bits in (BITS_A, BITS_B))
            parts = (
                (out_refs[slot // 8], slot % 8, head_for(to_a), in_refs[:4], False),
                (out_refs[2 + slot // 8], slot % 8, head_for(to_b), in_refs[4:], True),
            )
        for out_ref, index, head, arrays, with_tail in parts:
            rows = pl.ds(pl.multiple_of(head * span, 16), span)
            for s, array in enumerate(arrays):
                out_ref[index, s * span : (s + 1) * span, :] = array[rows, :]
            if with_tail:
                peak = jnp.sum(jnp.where(row_id == head, peaks, 0.0), axis=0, keepdims=True)
                out_ref[index, len(arrays) * span :, :] = split_parts(jnp.broadcast_to(peak, (TAIL, HAD)), chans)


def pack_kernel(owners, heads, chunk, has_past, placement_ref, *refs):
    first, chans = chunk
    peak_ref, out_ref, buffer, sems, live_ref, slot_ref = refs[-6:]
    past_ref = refs[-8] if has_past else None
    in_refs = refs[: -8 if has_past else -6]
    me, group = lax.axis_index("tp"), lax.axis_index("fsdp")
    count = 0
    for source in range(owners):
        live = 0
        for head in range(heads):
            live = jnp.where(placement_ref[source * heads + head] == me, 1, live)
        live_ref[source] = live
        slot_ref[source] = count
        count = count + live
    lane = lax.broadcasted_iota(jnp.int32, (TAIL, HAD), 1)
    depth = buffer.shape[0]
    copies = [None] * depth
    slots = first_slots(4)
    for origin in range(owners):
        if len(in_refs) == 1:
            source = origin
            halves = ((in_refs[0], origin, 0), (in_refs[0], origin, 8 * chans))
        else:
            source = me ^ cube_offset(group & 1, BITS_A, origin)
            a_array, a_index = slots[origin]
            b_array, b_index = slots[((origin & 5) << 1) | ((origin & 10) >> 1)]
            halves = ((in_refs[a_array], a_index, 0), (in_refs[5 + b_array], b_index, 0))
        part = origin % depth
        if copies[part] is not None:
            copies[part].wait()
        live = live_ref[source] != 0
        slot = jnp.where(live, slot_ref[source], count + source - slot_ref[source])
        last_ref, last_index, last_start = halves[1]
        tail = last_ref[last_index, last_start + 8 * chans :, :].astype(jnp.float32)
        row = jnp.where((lane < chans) & live, join_parts(tail, chans), 0.0)[:1, :]
        scale = jnp.where(live, 1.0 / (row + 1e-06), 0.0)
        scale = jnp.broadcast_to(scale, (HEAD_DIM, HAD)).T[:chans, :]
        row = pltpu.roll(jnp.broadcast_to(row, (8, HAD)), first, 1)[:1, :] if first else row
        if has_past:
            row = row + past_ref[pl.ds(slot, 1), :]
        peak_ref[pl.ds(slot, 1), :] = row
        for s in range(8):
            in_ref, index, offset = halves[s // 4]
            for e in range(2):
                start = offset + (s % 4 * 2 + e) * chans
                lanes = pl.ds(pl.multiple_of(((group ^ s) * 2 + e) * HAD, HAD), HAD)
                block = in_ref[index, start : start + chans, :]
                buffer[part, :, lanes] = (block.astype(jnp.float32) * scale).astype(jnp.bfloat16)
        copies[part] = pltpu.make_async_copy(
            buffer.at[part], out_ref.at[0, slot, first : first + chans, :], sems.at[part]
        )
        copies[part].start()
    for copy in copies:
        copy.wait()


def per_device(qkv_weight, placement):
    rows_local, cols_local = qkv_weight.shape
    heads = cols_local // HEAD_DIM
    owners = lax.axis_size("tp")
    rows_a = rows_local // HAD
    params = pltpu.CompilerParams(vmem_limit_bytes=VMEM_BYTES)
    any_spec = pl.BlockSpec(memory_space=pl.ANY)
    smem_spec = pl.BlockSpec(memory_space=pltpu.SMEM)
    vmem_spec = pl.BlockSpec(memory_space=pltpu.VMEM)

    def blocks_of(chans, tail):
        return [jax.ShapeDtypeStruct((heads * 2 * chans + tail, HAD), jnp.bfloat16)] * 8

    signs = jnp.asarray(hadamard_table(HAD), jnp.bfloat16)
    first_blocks = [shape for _, chans in CHUNKS for shape in blocks_of(chans, 0)]
    turned = pl.pallas_call(
        functools.partial(local_turn_kernel, rows_a),
        grid=(heads,),
        in_specs=[
            pl.BlockSpec((rows_local, HEAD_DIM), lambda h: (0, h)),
            pl.BlockSpec((HAD, HAD), lambda h: (0, 0)),
        ],
        out_specs=[pl.BlockSpec((shape.shape[0] // heads, HAD), lambda h: (h, 0)) for shape in first_blocks],
        out_shape=first_blocks,
        scratch_shapes=[pltpu.VMEM((rows_local, HAD), jnp.float32)],
        compiler_params=params,
        name="local_turn",
    )(qkv_weight, signs)

    state = [turned[8 * index : 8 * index + 8] for index in range(len(CHUNKS))]
    token = None
    past = []

    def tie(arrays):
        if token is None:
            return list(arrays)
        return list(lax.optimization_barrier((list(arrays), token))[0])

    for stage, index in ORDER:
        first, chans = chunk = CHUNKS[index]
        arrays = tie(state[index])
        if stage == "start":
            state[index] = ring_exchange(arrays)
        elif stage == "cross":
            outs = pl.pallas_call(
                functools.partial(cross_turn_kernel, heads, chans),
                in_specs=[vmem_spec] * 8,
                out_specs=[vmem_spec] * 8,
                out_shape=blocks_of(chans, TAIL),
                compiler_params=params,
                name="cross_turn",
            )(*arrays)
            token = outs[0]
            state[index] = ring_exchange(outs)
        elif stage == "spread":
            direct = index < DIRECT
            if direct:
                shapes = [(owners, 16 * chans + TAIL)]
            else:
                shapes = [(owners // 2, 8 * chans)] * 2 + [(owners // 2, 8 * chans + TAIL)] * 2
            outs = pl.pallas_call(
                functools.partial(spread_kernel, heads, chans),
                in_specs=[smem_spec] + [vmem_spec] * 8,
                out_specs=[vmem_spec] * len(shapes),
                out_shape=[jax.ShapeDtypeStruct(shape + (HAD,), jnp.bfloat16) for shape in shapes],
                compiler_params=params,
                name="spread",
            )(placement, *arrays)
            token = outs[0]
            if direct:
                state[index] = [lax.all_to_all(outs[0], "tp", split_axis=0, concat_axis=0, tiled=True)]
            else:
                state[index] = hypercube(*outs[:2], BITS_A) + hypercube(*outs[2:], BITS_B)
        else:
            past = pl.pallas_call(
                functools.partial(pack_kernel, owners, heads, chunk, bool(past)),
                in_specs=[smem_spec] + [vmem_spec] * len(arrays) + ([vmem_spec, any_spec] if past else []),
                out_specs=[vmem_spec, any_spec],
                out_shape=[
                    jax.ShapeDtypeStruct((owners, HEAD_DIM), jnp.float32),
                    jax.ShapeDtypeStruct((1, owners, HEAD_DIM, rows_local), jnp.bfloat16),
                ],
                scratch_shapes=[
                    pltpu.VMEM((3, chans, rows_local), jnp.bfloat16),
                    pltpu.SemaphoreType.DMA((3,)),
                    pltpu.SMEM((owners,), jnp.int32),
                    pltpu.SMEM((owners,), jnp.int32),
                ],
                input_output_aliases={2 + len(arrays): 1} if past else {},
                compiler_params=params,
                name="pack",
            )(placement, *arrays, *past)
            token = past[0]
    peaks, packed = past
    return packed, peaks[None]


def solution(mesh):
    in_specs = (P("fsdp", "tp"), P())
    out_specs = (P("tp", None, None, "fsdp"), P("tp", None, None))
    return jax.shard_map(
        per_device, mesh=mesh, in_specs=in_specs, out_specs=out_specs, check_vma=False
    )
```

time: 253 us -> 229 us (0.905)
  waiting for transfers between devices: 115 us -> 93.9 us
  starting transfers between devices: 77.2 us -> 90.6 us
  Pallas kernels: 40.4 us -> 32.4 us
  other arithmetic: 5.54 us -> 0 us
    ppermute x39 -> x54, starting transfers between devices: 46.8 us -> 61.2 us  [ring_exchange(): lax.ppermute(out[offset], 'fsdp', [(i, i ^ flip) for i in range(size)])]
    ppermute x39 -> x54, waiting for transfers between devices: 84.4 us -> 70.8 us  [ring_exchange(): lax.ppermute(out[offset], 'fsdp', [(i, i ^ flip) for i in range(size)])]
    ppermute x8, waiting for transfers between devices: 30.6 us -> 23.1 us  [owner_hop(): return lax.ppermute(array, BOTH, pairs)]
    pallas_call x9 -> x6, Pallas kernels: 27 us -> 22.8 us  [the longest x3 20.1 us: per_device(): pl.pallas_call(functools.partial(pack_kernel, owners, heads, chunk, bool(...]
    pallas_call x3, Pallas kernels: 5.88 us -> 2.56 us  [per_device(): pl.pallas_call(functools.partial(spread_kernel, heads, chans), in_specs=[...]
    unnamed x56 -> x74, local copies, waits for them, and re-layouts: 9.38 us -> 10.7 us
  transfers between devices with their start and end apart: 49 -> 64, of which waited for: 22 -> 32; matrix products, arithmetic and copies ran while one was open for 0% -> 0% of each run, Pallas kernels for 10% -> 8%
where the time goes in v4:
time: 229 us
  waiting for transfers between devices  93.9 us (41%)
  starting transfers between devices  90.6 us (40%)
  Pallas kernels  32.4 us (14%)
  local copies, waits for them, and re-layouts  10.7 us (5%)
    ppermute x54, waiting for transfers between devices, ring_exchange(): lax.ppermute(out[offset], 'fsdp', [(i, i ^ flip) for i in range(size)])  70.8 us
    ppermute x54, starting transfers between devices, ring_exchange(): lax.ppermute(out[offset], 'fsdp', [(i, i ^ flip) for i in range(size)])  61.2 us
    ppermute x8, waiting for transfers between devices, owner_hop(): return lax.ppermute(array, BOTH, pairs)  23.1 us
    pallas_call x3, Pallas kernels, per_device(): pl.pallas_call(functools.partial(pack_kernel, owners, heads, chunk, bool(...  20.1 us
    all_to_all x2, starting transfers between devices, per_device(): lax.all_to_all(outs[0], 'tp', split_axis=0, concat_axis=0, tiled=True)  15.1 us
    ppermute x8, starting transfers between devices, owner_hop(): return lax.ppermute(array, BOTH, pairs)  14.3 us
    unnamed x74, local copies, waits for them, and re-layouts  10.7 us
    pallas_call x1, Pallas kernels, per_device(): pl.pallas_call(functools.partial(local_turn_kernel, rows_a), grid=(heads,...  5.04 us
  transfers between devices with their start and end apart: 64, of which 32 were waited for; matrix products, arithmetic and copies ran while one was open for 0% of the time, Pallas kernels for 8%

profile of v4, /device:TPU:0, one launch (start us, length us, event | category | flops | bytes accessed | tf_op | source)
XLA Modules:
  0.0 228.9 jit_solution(17007075506824335606)
XLA Ops:
  0.6 2.3 %copy-done.14 = bf16[2048,1152]{1,0:T(8,128)(2,1)S(1)} copy-done((bf16[2048,1152]{1,0:T(8,128)(2,1)S(1)}, bf16[2048,1152]{1,0:T(8,128)(2,1)}, u32[]{:S(2)}) %copy-start.14) | copy-done | bytes 4718616
  3.7 5.0 %local_turn.1 = (bf16[864,128]{1,0:T(8,128)(2,1)S(1)}, bf16[864,128]{1,0:T(8,128)(2,1)S(1)}, bf16[864,128]{1,0:T(8,128)(2,1)S(1)}, bf16[864,128]{1,0:T(8,128)(2,...) custom-call(bf16[2048,1152]{1,0:T(8,128)(2,1)S(1)} %copy-done.14, ...), custom_call_target="tpu_custom_call" | custom-call | tf_op jit(solution)/shard_map/local_turn/pallas_call | solution.py:300
  13.1 1.7 collective-permute-start.1
  15.2 3.1 %collective-permute-start.5 = (bf16[864,128]{1,0:T(8,128)(2,1)S(1)}, bf16[864,128]{1,0:T(8,128)(2,1)S(1)}, u32[]{:S(2)}, u32[]{:S(2)}) collective-permute-start(bf16[864,128]{1,0:T(8,128)(2,1)S(1)} %get-tuple-element.149), channel_id=1, source_target_pairs={{0,96},{16,112},{32,64},{48,80},{64,32},{80,48},{96,0},{112,16},{1... | collective-permute-start | bytes 663560 | tf_op jit(solution)/shard_map/ppermute | solution.py:61
  18.7 2.7 %collective-permute-done.1.refs_2_ = bf16[864,128]{1,0:T(8,128)(2,1)S(1)} collective-permute-done((bf16[864,128]{1,0:T(8,128)(2,1)S(1)}, bf16[864,128]{1,0:T(8,128)(2,1)S(1)}, u32[]{:S(2)}, u32[]{:S(2)}) %collective-permute-start.1) | collective-permute-done | bytes 221216 | tf_op jit(solution)/shard_map/ppermute | solution.py:61
  21.4 1.9 collective-permute-start.8
  23.3 2.9 %collective-permute-done.3 = bf16[864,128]{1,0:T(8,128)(2,1)S(1)} collective-permute-done((bf16[864,128]{1,0:T(8,128)(2,1)S(1)}, bf16[864,128]{1,0:T(8,128)(2,1)S(1)}, u32[]{:S(2)}, u32[]{:S(2)}) %collective-permute-start.3) | collective-permute-done | bytes 221216 | tf_op jit(solution)/shard_map/ppermute | solution.py:61
  26.2 3.1 %collective-permute-start.4 = (bf16[864,128]{1,0:T(8,128)(2,1)S(1)}, bf16[864,128]{1,0:T(8,128)(2,1)S(1)}, u32[]{:S(2)}, u32[]{:S(2)}) collective-permute-start(bf16[864,128]{1,0:T(8,128)(2,1)S(1)} %collective-permute-done.3), channel_id=1, source_target_pairs={{0,96},{16,112},{32,64},{48,80},{64,32},{80,48},{96,0},{112,16},{1... | collective-permute-start | bytes 663560 | tf_op jit(solution)/shard_map/ppermute | solution.py:61
  30.0 3.7 %collective-permute-done.8.refs_7_ = bf16[864,128]{1,0:T(8,128)(2,1)S(1)} collective-permute-done((bf16[864,128]{1,0:T(8,128)(2,1)S(1)}, bf16[864,128]{1,0:T(8,128)(2,1)S(1)}, u32[]{:S(2)}, u32[]{:S(2)}) %collective-permute-start.8) | collective-permute-done | bytes 221216 | tf_op jit(solution)/shard_map/ppermute | solution.py:61
  33.6 4.4 %collective-permute-done.4.refs_4_ = bf16[864,128]{1,0:T(8,128)(2,1)S(1)} collective-permute-done((bf16[864,128]{1,0:T(8,128)(2,1)S(1)}, bf16[864,128]{1,0:T(8,128)(2,1)S(1)}, u32[]{:S(2)}, u32[]{:S(2)}) %collective-permute-start.4) | collective-permute-done | bytes 221216 | tf_op jit(solution)/shard_map/ppermute | solution.py:61
  39.4 1.7 collective-permute-start.21
  41.2 3.0 %collective-permute-start.23 = (bf16[880,128]{1,0:T(8,128)(2,1)S(1)}, bf16[880,128]{1,0:T(8,128)(2,1)S(1)}, u32[]{:S(2)}, u32[]{:S(2)}) collective-permute-start(bf16[880,128]{1,0:T(8,128)(2,1)S(1)} %get-tuple-element.165), channel_id=1, source_target_pairs={{0,96},{16,112},{32,64},{48,80},{64,32},{80,48},{96,0},{112,16},{1... | collective-permute-start | bytes 675848 | tf_op jit(solution)/shard_map/ppermute | solution.py:61
  44.4 3.1 %collective-permute-done.19.refs_2_ = bf16[880,128]{1,0:T(8,128)(2,1)S(1)} collective-permute-done((bf16[880,128]{1,0:T(8,128)(2,1)S(1)}, bf16[880,128]{1,0:T(8,128)(2,1)S(1)}, u32[]{:S(2)}, u32[]{:S(2)}) %collective-permute-start.19) | collective-permute-done | bytes 225312 | tf_op jit(solution)/shard_map/ppermute | solution.py:61
  47.5 1.7 collective-permute-start.26
  49.2 3.1 %collective-permute-done.21 = bf16[880,128]{1,0:T(8,128)(2,1)S(1)} collective-permute-done((bf16[880,128]{1,0:T(8,128)(2,1)S(1)}, bf16[880,128]{1,0:T(8,128)(2,1)S(1)}, u32[]{:S(2)}, u32[]{:S(2)}) %collective-permute-start.21) | collective-permute-done | bytes 225312 | tf_op jit(solution)/shard_map/ppermute | solution.py:61
  52.3 3.0 %collective-permute-start.22 = (bf16[880,128]{1,0:T(8,128)(2,1)S(1)}, bf16[880,128]{1,0:T(8,128)(2,1)S(1)}, u32[]{:S(2)}, u32[]{:S(2)}) collective-permute-start(bf16[880,128]{1,0:T(8,128)(2,1)S(1)} %collective-permute-done.21), channel_id=1, source_target_pairs={{0,96},{16,112},{32,64},{48,80},{64,32},{80,48},{96,0},{112,16},{1... | collective-permute-start | bytes 675848 | tf_op jit(solution)/shard_map/ppermute | solution.py:61
  56.2 3.5 %collective-permute-done.26.refs_7_ = bf16[880,128]{1,0:T(8,128)(2,1)S(1)} collective-permute-done((bf16[880,128]{1,0:T(8,128)(2,1)S(1)}, bf16[880,128]{1,0:T(8,128)(2,1)S(1)}, u32[]{:S(2)}, u32[]{:S(2)}) %collective-permute-start.26) | collective-permute-done | bytes 225312 | tf_op jit(solution)/shard_map/ppermute | solution.py:61
  59.7 4.5 %collective-permute-done.22.refs_4_ = bf16[880,128]{1,0:T(8,128)(2,1)S(1)} collective-permute-done((bf16[880,128]{1,0:T(8,128)(2,1)S(1)}, bf16[880,128]{1,0:T(8,128)(2,1)S(1)}, u32[]{:S(2)}, u32[]{:S(2)}) %collective-permute-start.22) | collective-permute-done | bytes 225312 | tf_op jit(solution)/shard_map/ppermute | solution.py:61
  65.1 1.7 copy-done.1
  66.8 7.9 %all-to-all-start = ((bf16[16,784,128]{2,1,0:T(8,128)(2,1)}), bf16[16,784,128]{2,1,0:T(8,128)(2,1)S(1)}, u32[]{:S(2)}, u32[]{:S(2)}) async-start(bf16[16,784,128]{2,1,0:T(8,128)(2,1)} %copy-done.1), calls=%async_computation | async-start | bytes 6422528 | tf_op jit(solution)/shard_map/all_to_all | solution.py:355
  74.9 2.0 collective-permute-start.12
  76.9 3.0 %collective-permute-start.14 = (bf16[864,128]{1,0:T(8,128)(2,1)}, bf16[864,128]{1,0:T(8,128)(2,1)S(1)}, u32[]{:S(2)}, u32[]{:S(2)}) collective-permute-start(bf16[864,128]{1,0:T(8,128)(2,1)} %copy-done.26), channel_id=1, source_target_pairs={{0,96},{16,112},{32,64},{48,80},{64,32},{80,48},{96,0},{112,16},{1... | collective-permute-start | bytes 663560 | tf_op jit(solution)/shard_map/ppermute | solution.py:61
  80.1 3.2 %collective-permute-done.10.refs_2_ = bf16[864,128]{1,0:T(8,128)(2,1)S(1)} collective-permute-done((bf16[864,128]{1,0:T(8,128)(2,1)}, bf16[864,128]{1,0:T(8,128)(2,1)S(1)}, u32[]{:S(2)}, u32[]{:S(2)}) %collective-permute-start.10) | collective-permute-done | bytes 221216 | tf_op jit(solution)/shard_map/ppermute | solution.py:61
  83.3 1.7 collective-permute-start.17
  85.0 3.0 %collective-permute-done.12 = bf16[864,128]{1,0:T(8,128)(2,1)S(1)} collective-permute-done((bf16[864,128]{1,0:T(8,128)(2,1)}, bf16[864,128]{1,0:T(8,128)(2,1)S(1)}, u32[]{:S(2)}, u32[]{:S(2)}) %collective-permute-start.12) | collective-permute-done | bytes 221216 | tf_op jit(solution)/shard_map/ppermute | solution.py:61
  88.0 3.0 %collective-permute-start.13 = (bf16[864,128]{1,0:T(8,128)(2,1)S(1)}, bf16[864,128]{1,0:T(8,128)(2,1)S(1)}, u32[]{:S(2)}, u32[]{:S(2)}) collective-permute-start(bf16[864,128]{1,0:T(8,128)(2,1)S(1)} %collective-permute-done.12), channel_id=1, source_target_pairs={{0,96},{16,112},{32,64},{48,80},{64,32},{80,48},{96,0},{112,16},{1... | collective-permute-start | bytes 663560 | tf_op jit(solution)/shard_map/ppermute | solution.py:61
  91.8 3.6 %collective-permute-done.17.refs_7_ = bf16[864,128]{1,0:T(8,128)(2,1)S(1)} collective-permute-done((bf16[864,128]{1,0:T(8,128)(2,1)}, bf16[864,128]{1,0:T(8,128)(2,1)S(1)}, u32[]{:S(2)}, u32[]{:S(2)}) %collective-permute-start.17) | collective-permute-done | bytes 221216 | tf_op jit(solution)/shard_map/ppermute | solution.py:61
  95.5 4.3 %collective-permute-done.13.refs_4_ = bf16[864,128]{1,0:T(8,128)(2,1)S(1)} collective-permute-done((bf16[864,128]{1,0:T(8,128)(2,1)S(1)}, bf16[864,128]{1,0:T(8,128)(2,1)S(1)}, u32[]{:S(2)}, u32[]{:S(2)}) %collective-permute-start.13) | collective-permute-done | bytes 221216 | tf_op jit(solution)/shard_map/ppermute | solution.py:61
  100.8 2.0 collective-permute-start.39
  102.9 3.0 %collective-permute-start.41 = (bf16[880,128]{1,0:T(8,128)(2,1)S(1)}, bf16[880,128]{1,0:T(8,128)(2,1)S(1)}, u32[]{:S(2)}, u32[]{:S(2)}) collective-permute-start(bf16[880,128]{1,0:T(8,128)(2,1)S(1)} %get-tuple-element.197), channel_id=1, source_target_pairs={{0,96},{16,112},{32,64},{48,80},{64,32},{80,48},{96,0},{112,16},{1... | collective-permute-start | bytes 675848 | tf_op jit(solution)/shard_map/ppermute | solution.py:61
  106.1 3.1 %collective-permute-done.37.refs_2_ = bf16[880,128]{1,0:T(8,128)(2,1)S(1)} collective-permute-done((bf16[880,128]{1,0:T(8,128)(2,1)S(1)}, bf16[880,128]{1,0:T(8,128)(2,1)S(1)}, u32[]{:S(2)}, u32[]{:S(2)}) %collective-permute-start.37) | collective-permute-done | bytes 225312 | tf_op jit(solution)/shard_map/ppermute | solution.py:61
  109.2 1.7 collective-permute-start.44
  110.9 3.1 %collective-permute-done.39 = bf16[880,128]{1,0:T(8,128)(2,1)S(1)} collective-permute-done((bf16[880,128]{1,0:T(8,128)(2,1)S(1)}, bf16[880,128]{1,0:T(8,128)(2,1)S(1)}, u32[]{:S(2)}, u32[]{:S(2)}) %collective-permute-start.39) | collective-permute-done | bytes 225312 | tf_op jit(solution)/shard_map/ppermute | solution.py:61
  114.0 3.0 %collective-permute-start.40 = (bf16[880,128]{1,0:T(8,128)(2,1)S(1)}, bf16[880,128]{1,0:T(8,128)(2,1)S(1)}, u32[]{:S(2)}, u32[]{:S(2)}) collective-permute-start(bf16[880,128]{1,0:T(8,128)(2,1)S(1)} %collective-permute-done.39), channel_id=1, source_target_pairs={{0,96},{16,112},{32,64},{48,80},{64,32},{80,48},{96,0},{112,16},{1... | collective-permute-start | bytes 675848 | tf_op jit(solution)/shard_map/ppermute | solution.py:61
  117.9 3.5 %collective-permute-done.44.refs_7_ = bf16[880,128]{1,0:T(8,128)(2,1)S(1)} collective-permute-done((bf16[880,128]{1,0:T(8,128)(2,1)S(1)}, bf16[880,128]{1,0:T(8,128)(2,1)S(1)}, u32[]{:S(2)}, u32[]{:S(2)}) %collective-permute-start.44) | collective-permute-done | bytes 225312 | tf_op jit(solution)/shard_map/ppermute | solution.py:61
  121.4 4.5 %collective-permute-done.40.refs_4_ = bf16[880,128]{1,0:T(8,128)(2,1)S(1)} collective-permute-done((bf16[880,128]{1,0:T(8,128)(2,1)S(1)}, bf16[880,128]{1,0:T(8,128)(2,1)S(1)}, u32[]{:S(2)}, u32[]{:S(2)}) %collective-permute-start.40) | collective-permute-done | bytes 225312 | tf_op jit(solution)/shard_map/ppermute | solution.py:61
  126.7 1.7 copy-done
  128.4 7.2 %all-to-all-start.1 = ((bf16[16,784,128]{2,1,0:T(8,128)(2,1)}), bf16[16,784,128]{2,1,0:T(8,128)(2,1)}, u32[]{:S(2)}, u32[]{:S(2)}) async-start(bf16[16,784,128]{2,1,0:T(8,128)(2,1)} %copy-done), calls=%async_computation.1 | async-start | bytes 6422528 | tf_op jit(solution)/shard_map/all_to_all | solution.py:355
  135.8 2.0 collective-permute-start.30
  137.8 3.0 %collective-permute-start.32 = (bf16[576,128]{1,0:T(8,128)(2,1)}, bf16[576,128]{1,0:T(8,128)(2,1)S(1)}, u32[]{:S(2)}, u32[]{:S(2)}) collective-permute-start(bf16[576,128]{1,0:T(8,128)(2,1)} %copy-done.33), channel_id=1, source_target_pairs={{0,96},{16,112},{32,64},{48,80},{64,32},{80,48},{96,0},{112,16},{1... | collective-permute-start | bytes 442376 | tf_op jit(solution)/shard_map/ppermute | solution.py:61
  141.0 1.6 collective-permute-done.28.refs_2_
  142.6 1.8 collective-permute-start.35
  144.5 1.3 collective-permute-done.30
  145.8 3.0 %collective-permute-start.31 = (bf16[576,128]{1,0:T(8,128)(2,1)S(1)}, bf16[576,128]{1,0:T(8,128)(2,1)S(1)}, u32[]{:S(2)}, u32[]{:S(2)}) collective-permute-start(bf16[576,128]{1,0:T(8,128)(2,1)S(1)} %collective-permute-done.30), channel_id=1, source_target_pairs={{0,96},{16,112},{32,64},{48,80},{64,32},{80,48},{96,0},{112,16},{1... | collective-permute-start | bytes 442376 | tf_op jit(solution)/shard_map/ppermute | solution.py:61
  148.9 2.5 %collective-permute-done.35.refs_7_ = bf16[576,128]{1,0:T(8,128)(2,1)S(1)} collective-permute-done((bf16[576,128]{1,0:T(8,128)(2,1)}, bf16[576,128]{1,0:T(8,128)(2,1)S(1)}, u32[]{:S(2)}, u32[]{:S(2)}) %collective-permute-start.35) | collective-permute-done | bytes 147488 | tf_op jit(solution)/shard_map/ppermute | solution.py:61
  151.4 2.9 %collective-permute-done.31.refs_4_ = bf16[576,128]{1,0:T(8,128)(2,1)S(1)} collective-permute-done((bf16[576,128]{1,0:T(8,128)(2,1)S(1)}, bf16[576,128]{1,0:T(8,128)(2,1)S(1)}, u32[]{:S(2)}, u32[]{:S(2)}) %collective-permute-start.31) | collective-permute-done | bytes 147488 | tf_op jit(solution)/shard_map/ppermute | solution.py:61
  157.2 3.0 %collective-permute-start.50 = (bf16[592,128]{1,0:T(8,128)(2,1)S(1)}, bf16[592,128]{1,0:T(8,128)(2,1)S(1)}, u32[]{:S(2)}, u32[]{:S(2)}) collective-permute-start(bf16[592,128]{1,0:T(8,128)(2,1)S(1)} %get-tuple-element.221), channel_id=1, source_target_pairs={{0,96},{16,112},{32,64},{48,80},{64,32},{80,48},{96,0},{112,16},{1... | collective-permute-start | bytes 454664 | tf_op jit(solution)/shard_map/ppermute | solution.py:61
  160.4 1.5 collective-permute-done.46.refs_2_
  161.9 1.8 collective-permute-start.53
  163.7 1.4 collective-permute-done.48
  165.2 3.0 %collective-permute-start.49 = (bf16[592,128]{1,0:T(8,128)(2,1)S(1)}, bf16[592,128]{1,0:T(8,128)(2,1)S(1)}, u32[]{:S(2)}, u32[]{:S(2)}) collective-permute-start(bf16[592,128]{1,0:T(8,128)(2,1)S(1)} %collective-permute-done.48), channel_id=1, source_target_pairs={{0,96},{16,112},{32,64},{48,80},{64,32},{80,48},{96,0},{112,16},{1... | collective-permute-start | bytes 454664 | tf_op jit(solution)/shard_map/ppermute | solution.py:61
  168.1 5.8 %pack.3 = (f32[16,128]{1,0:T(8,128)S(1)}, bf16[1,16,128,2048]{3,2,1,0:T(8,128)(2,1)}) custom-call(s32[144]{0:T(256)S(1)} %copy-done.21, bf16[16,784,128]{2,1,0:T(8,128)(2,1)S(1)} %all-to-all-done.refs_0_), custom_call_target="tpu_custom_call" | custom-call | tf_op jit(solution)/shard_map/pack/pallas_call | solution.py:359
  174.9 1.9 collective-permute-start.58
  176.8 1.5 collective-permute-start.54
  178.2 7.2 %collective-permute-done.58.refs_1_.refs_6_ = bf16[8,272,128]{2,1,0:T(8,128)(2,1)S(1)} collective-permute-done((bf16[8,272,128]{2,1,0:T(8,128)(2,1)S(1)}, bf16[8,272,128]{2,1,0:T(8,128)(2,1)S(1)}, u32[]{:S(2)}, u32[]{:S(2)}) %collective-permute-start.58) | collective-permute-done | bytes 557088 | tf_op jit(solution)/shard_map/ppermute | solution.py:85
  186.5 1.8 collective-permute-start.55
  188.2 6.9 %collective-permute-done.59.refs_2_.refs_7_ = bf16[8,272,128]{2,1,0:T(8,128)(2,1)S(1)} collective-permute-done((bf16[8,272,128]{2,1,0:T(8,128)(2,1)S(1)}, bf16[8,272,128]{2,1,0:T(8,128)(2,1)S(1)}, u32[]{:S(2)}, u32[]{:S(2)}) %collective-permute-start.59) | collective-permute-done | bytes 557088 | tf_op jit(solution)/shard_map/ppermute | solution.py:85
  195.1 4.1 %collective-permute-start.60 = (bf16[8,272,128]{2,1,0:T(8,128)(2,1)S(1)}, bf16[8,272,128]{2,1,0:T(8,128)(2,1)S(1)}, u32[]{:S(2)}, u32[]{:S(2)}) collective-permute-start(bf16[8,272,128]{2,1,0:T(8,128)(2,1)S(1)} %regroup.10), channel_id=1, source_target_pairs={{0,12},{1,13},{2,14},{3,15},{4,8},{5,9},{6,10},{7,11},{8,4},{9,5},... | collective-permute-start | bytes 1671176 | tf_op jit(solution)/shard_map/ppermute | solution.py:85
  200.1 6.7 %collective-permute-done.60.refs_3_.refs_8_ = bf16[8,272,128]{2,1,0:T(8,128)(2,1)S(1)} collective-permute-done((bf16[8,272,128]{2,1,0:T(8,128)(2,1)S(1)}, bf16[8,272,128]{2,1,0:T(8,128)(2,1)S(1)}, u32[]{:S(2)}, u32[]{:S(2)}) %collective-permute-start.60) | collective-permute-done | bytes 557088 | tf_op jit(solution)/shard_map/ppermute | solution.py:85
  207.7 1.2 collective-permute-start.61
  210.7 2.1 collective-permute-start.57
  212.9 7.3 %pack.4 = (f32[16,128]{1,0:T(8,128)S(1)}, bf16[1,16,128,2048]{3,2,1,0:T(8,128)(2,1)}) custom-call(s32[144]{0:T(256)S(1)} %copy-done.21, bf16[16,784,128]{2,1,0:T(8,128)(2,1)} %all-to-all-done.1.refs_0_, f32[16,128]{1,0:T(8,128)S(1)} %get-tuple-element.225.refs_1_, bf16[1,16,128,2048]{3,2,1,0:T(8,128)(2,1)} %get-tuple-element.239.refs_2_), custom_call_target="tpu_custom_call", output_to_operand_aliasing={{1}: (3, {})} | custom-call | tf_op jit(solution)/shard_map/pack/pallas_call | solution.py:359
  220.2 1.4 collective-permute-done.57.refs_4_
  221.8 6.9 %pack.5 = (f32[16,128]{1,0:T(8,128)}, bf16[1,16,128,2048]{3,2,1,0:T(8,128)(2,1)}) custom-call(s32[144]{0:T(256)S(1)} %copy-done.21, bf16[8,256,128]{2,1,0:T(8,128)(2,1)S(1)} %copy-done.7, bf16[8,256,128]{2,1,0:T(8,128)(2,1)S(1)} %copy-done.9, bf16[8,256,128]{2,1,0:T(8,128)(2,1)S(1)} %copy-done.13, ...), custom_call_target="tpu_custom_call", output_to_operand_aliasing={{1}: (12, {})} | custom-call | tf_op jit(solution)/shard_map/pack/pallas_call | solution.py:359
  (154 shorter events, 23.7 us)
Async XLA Ops:
  13.0 5.3 %collective-permute-start = (bf16[864,128]{1,0:T(8,128)(2,1)S(1)}, bf16[864,128]{1,0:T(8,128)(2,1)S(1)}, u32[]{:S(2)}, u32[]{:S(2)}) collective-permute-start(bf16[864,128]{1,0:T(8,128)(2,1)S(1)} %get-tuple-element.145), channel_id=1, source_target_pairs={{0,16},{16,0},{32,48},{48,32},{64,80},{80,64},{96,112},{112,96},{1... | collective-permute-start | bytes 663560 | tf_op jit(solution)/shard_map/ppermute | solution.py:61
  13.1 8.3 %collective-permute-start.1 = (bf16[864,128]{1,0:T(8,128)(2,1)S(1)}, bf16[864,128]{1,0:T(8,128)(2,1)S(1)}, u32[]{:S(2)}, u32[]{:S(2)}) collective-permute-start(bf16[864,128]{1,0:T(8,128)(2,1)S(1)} %get-tuple-element.146), channel_id=1, source_target_pairs={{0,32},{16,48},{32,0},{48,16},{64,96},{80,112},{96,64},{112,80},{1... | collective-permute-start | bytes 663560 | tf_op jit(solution)/shard_map/ppermute | solution.py:61
  14.9 11.3 %collective-permute-start.3 = (bf16[864,128]{1,0:T(8,128)(2,1)S(1)}, bf16[864,128]{1,0:T(8,128)(2,1)S(1)}, u32[]{:S(2)}, u32[]{:S(2)}) collective-permute-start(bf16[864,128]{1,0:T(8,128)(2,1)S(1)} %get-tuple-element.148), channel_id=1, source_target_pairs={{0,32},{16,48},{32,0},{48,16},{64,96},{80,112},{96,64},{112,80},{1... | collective-permute-start | bytes 663560 | tf_op jit(solution)/shard_map/ppermute | solution.py:61
  15.2 14.1 %collective-permute-start.5 = (bf16[864,128]{1,0:T(8,128)(2,1)S(1)}, bf16[864,128]{1,0:T(8,128)(2,1)S(1)}, u32[]{:S(2)}, u32[]{:S(2)}) collective-permute-start(bf16[864,128]{1,0:T(8,128)(2,1)S(1)} %get-tuple-element.149), channel_id=1, source_target_pairs={{0,96},{16,112},{32,64},{48,80},{64,32},{80,48},{96,0},{112,16},{1... | collective-permute-start | bytes 663560 | tf_op jit(solution)/shard_map/ppermute | solution.py:61
  18.3 11.6 %collective-permute-start.2 = (bf16[864,128]{1,0:T(8,128)(2,1)S(1)}, bf16[864,128]{1,0:T(8,128)(2,1)S(1)}, u32[]{:S(2)}, u32[]{:S(2)}) collective-permute-start(bf16[864,128]{1,0:T(8,128)(2,1)S(1)} %get-tuple-element.147), channel_id=1, source_target_pairs={{0,48},{16,32},{32,16},{48,0},{64,112},{80,96},{96,80},{112,64},{1... | collective-permute-start | bytes 663560 | tf_op jit(solution)/shard_map/ppermute | solution.py:61
  18.3 11.6 %collective-permute-start.7 = (bf16[864,128]{1,0:T(8,128)(2,1)S(1)}, bf16[864,128]{1,0:T(8,128)(2,1)S(1)}, u32[]{:S(2)}, u32[]{:S(2)}) collective-permute-start(bf16[864,128]{1,0:T(8,128)(2,1)S(1)} %get-tuple-element.150), channel_id=1, source_target_pairs={{0,96},{16,112},{32,64},{48,80},{64,32},{80,48},{96,0},{112,16},{1... | collective-permute-start | bytes 663560 | tf_op jit(solution)/shard_map/ppermute | solution.py:61
  21.4 12.2 %collective-permute-start.8 = (bf16[864,128]{1,0:T(8,128)(2,1)S(1)}, bf16[864,128]{1,0:T(8,128)(2,1)S(1)}, u32[]{:S(2)}, u32[]{:S(2)}) collective-permute-start(bf16[864,128]{1,0:T(8,128)(2,1)S(1)} %get-tuple-element.151), channel_id=1, source_target_pairs={{0,112},{16,96},{32,80},{48,64},{64,48},{80,32},{96,16},{112,0},{1... | collective-permute-start | bytes 663560 | tf_op jit(solution)/shard_map/ppermute | solution.py:61
  26.2 11.8 %collective-permute-start.4 = (bf16[864,128]{1,0:T(8,128)(2,1)S(1)}, bf16[864,128]{1,0:T(8,128)(2,1)S(1)}, u32[]{:S(2)}, u32[]{:S(2)}) collective-permute-start(bf16[864,128]{1,0:T(8,128)(2,1)S(1)} %collective-permute-done.3), channel_id=1, source_target_pairs={{0,96},{16,112},{32,64},{48,80},{64,32},{80,48},{96,0},{112,16},{1... | collective-permute-start | bytes 663560 | tf_op jit(solution)/shard_map/ppermute | solution.py:61
  29.3 8.7 %collective-permute-start.6 = (bf16[864,128]{1,0:T(8,128)(2,1)S(1)}, bf16[864,128]{1,0:T(8,128)(2,1)S(1)}, u32[]{:S(2)}, u32[]{:S(2)}) collective-permute-start(bf16[864,128]{1,0:T(8,128)(2,1)S(1)} %collective-permute-done.5), channel_id=1, source_target_pairs={{0,48},{16,32},{32,16},{48,0},{64,112},{80,96},{96,80},{112,64},{1... | collective-permute-start | bytes 663560 | tf_op jit(solution)/shard_map/ppermute | solution.py:61
  39.0 5.1 %collective-permute-start.18 = (bf16[880,128]{1,0:T(8,128)(2,1)S(1)}, bf16[880,128]{1,0:T(8,128)(2,1)S(1)}, u32[]{:S(2)}, u32[]{:S(2)}) collective-permute-start(bf16[880,128]{1,0:T(8,128)(2,1)S(1)} %get-tuple-element.161), channel_id=1, source_target_pairs={{0,16},{16,0},{32,48},{48,32},{64,80},{80,64},{96,112},{112,96},{1... | collective-permute-start | bytes 675848 | tf_op jit(solution)/shard_map/ppermute | solution.py:61
  39.0 8.4 %collective-permute-start.19 = (bf16[880,128]{1,0:T(8,128)(2,1)S(1)}, bf16[880,128]{1,0:T(8,128)(2,1)S(1)}, u32[]{:S(2)}, u32[]{:S(2)}) collective-permute-start(bf16[880,128]{1,0:T(8,128)(2,1)S(1)} %get-tuple-element.162), channel_id=1, source_target_pairs={{0,32},{16,48},{32,0},{48,16},{64,96},{80,112},{96,64},{112,80},{1... | collective-permute-start | bytes 675848 | tf_op jit(solution)/shard_map/ppermute | solution.py:61
  39.4 12.9 %collective-permute-start.21 = (bf16[880,128]{1,0:T(8,128)(2,1)S(1)}, bf16[880,128]{1,0:T(8,128)(2,1)S(1)}, u32[]{:S(2)}, u32[]{:S(2)}) collective-permute-start(bf16[880,128]{1,0:T(8,128)(2,1)S(1)} %get-tuple-element.164), channel_id=1, source_target_pairs={{0,32},{16,48},{32,0},{48,16},{64,96},{80,112},{96,64},{112,80},{1... | collective-permute-start | bytes 675848 | tf_op jit(solution)/shard_map/ppermute | solution.py:61
  41.2 14.1 %collective-permute-start.23 = (bf16[880,128]{1,0:T(8,128)(2,1)S(1)}, bf16[880,128]{1,0:T(8,128)(2,1)S(1)}, u32[]{:S(2)}, u32[]{:S(2)}) collective-permute-start(bf16[880,128]{1,0:T(8,128)(2,1)S(1)} %get-tuple-element.165), channel_id=1, source_target_pairs={{0,96},{16,112},{32,64},{48,80},{64,32},{80,48},{96,0},{112,16},{1... | collective-permute-start | bytes 675848 | tf_op jit(solution)/shard_map/ppermute | solution.py:61
  44.1 12.1 %collective-permute-start.20 = (bf16[880,128]{1,0:T(8,128)(2,1)S(1)}, bf16[880,128]{1,0:T(8,128)(2,1)S(1)}, u32[]{:S(2)}, u32[]{:S(2)}) collective-permute-start(bf16[880,128]{1,0:T(8,128)(2,1)S(1)} %get-tuple-element.163), channel_id=1, source_target_pairs={{0,48},{16,32},{32,16},{48,0},{64,112},{80,96},{96,80},{112,64},{1... | collective-permute-start | bytes 675848 | tf_op jit(solution)/shard_map/ppermute | solution.py:61
  44.1 12.0 %collective-permute-start.25 = (bf16[880,128]{1,0:T(8,128)(2,1)S(1)}, bf16[880,128]{1,0:T(8,128)(2,1)S(1)}, u32[]{:S(2)}, u32[]{:S(2)}) collective-permute-start(bf16[880,128]{1,0:T(8,128)(2,1)S(1)} %get-tuple-element.166), channel_id=1, source_target_pairs={{0,96},{16,112},{32,64},{48,80},{64,32},{80,48},{96,0},{112,16},{1... | collective-permute-start | bytes 675848 | tf_op jit(solution)/shard_map/ppermute | solution.py:61
  47.5 12.2 %collective-permute-start.26 = (bf16[880,128]{1,0:T(8,128)(2,1)S(1)}, bf16[880,128]{1,0:T(8,128)(2,1)S(1)}, u32[]{:S(2)}, u32[]{:S(2)}) collective-permute-start(bf16[880,128]{1,0:T(8,128)(2,1)S(1)} %get-tuple-element.167), channel_id=1, source_target_pairs={{0,112},{16,96},{32,80},{48,64},{64,48},{80,32},{96,16},{112,0},{1... | collective-permute-start | bytes 675848 | tf_op jit(solution)/shard_map/ppermute | solution.py:61
  52.3 11.9 %collective-permute-start.22 = (bf16[880,128]{1,0:T(8,128)(2,1)S(1)}, bf16[880,128]{1,0:T(8,128)(2,1)S(1)}, u32[]{:S(2)}, u32[]{:S(2)}) collective-permute-start(bf16[880,128]{1,0:T(8,128)(2,1)S(1)} %collective-permute-done.21), channel_id=1, source_target_pairs={{0,96},{16,112},{32,64},{48,80},{64,32},{80,48},{96,0},{112,16},{1... | collective-permute-start | bytes 675848 | tf_op jit(solution)/shard_map/ppermute | solution.py:61
  55.2 8.9 %collective-permute-start.24 = (bf16[880,128]{1,0:T(8,128)(2,1)S(1)}, bf16[880,128]{1,0:T(8,128)(2,1)S(1)}, u32[]{:S(2)}, u32[]{:S(2)}) collective-permute-start(bf16[880,128]{1,0:T(8,128)(2,1)S(1)} %collective-permute-done.23), channel_id=1, source_target_pairs={{0,48},{16,32},{32,16},{48,0},{64,112},{80,96},{96,80},{112,64},{1... | collective-permute-start | bytes 675848 | tf_op jit(solution)/shard_map/ppermute | solution.py:61
  66.8 61.6 %all-to-all-start = ((bf16[16,784,128]{2,1,0:T(8,128)(2,1)}), bf16[16,784,128]{2,1,0:T(8,128)(2,1)S(1)}, u32[]{:S(2)}, u32[]{:S(2)}) async-start(bf16[16,784,128]{2,1,0:T(8,128)(2,1)} %copy-done.1), calls=%async_computation | async-start | bytes 6422528 | tf_op jit(solution)/shard_map/all_to_all | solution.py:355
  74.7 5.2 %collective-permute-start.9 = (bf16[864,128]{1,0:T(8,128)(2,1)}, bf16[864,128]{1,0:T(8,128)(2,1)S(1)}, u32[]{:S(2)}, u32[]{:S(2)}) collective-permute-start(bf16[864,128]{1,0:T(8,128)(2,1)} %copy-done.29), channel_id=1, source_target_pairs={{0,16},{16,0},{32,48},{48,32},{64,80},{80,64},{96,112},{112,96},{1... | collective-permute-start | bytes 663560 | tf_op jit(solution)/shard_map/ppermute | solution.py:61
  74.8 8.5 %collective-permute-start.10 = (bf16[864,128]{1,0:T(8,128)(2,1)}, bf16[864,128]{1,0:T(8,128)(2,1)S(1)}, u32[]{:S(2)}, u32[]{:S(2)}) collective-permute-start(bf16[864,128]{1,0:T(8,128)(2,1)} %copy-done.28), channel_id=1, source_target_pairs={{0,32},{16,48},{32,0},{48,16},{64,96},{80,112},{96,64},{112,80},{1... | collective-permute-start | bytes 663560 | tf_op jit(solution)/shard_map/ppermute | solution.py:61
  74.9 13.2 %collective-permute-start.12 = (bf16[864,128]{1,0:T(8,128)(2,1)}, bf16[864,128]{1,0:T(8,128)(2,1)S(1)}, u32[]{:S(2)}, u32[]{:S(2)}) collective-permute-start(bf16[864,128]{1,0:T(8,128)(2,1)} %copy-done.27), channel_id=1, source_target_pairs={{0,32},{16,48},{32,0},{48,16},{64,96},{80,112},{96,64},{112,80},{1... | collective-permute-start | bytes 663560 | tf_op jit(solution)/shard_map/ppermute | solution.py:61
  76.9 14.1 %collective-permute-start.14 = (bf16[864,128]{1,0:T(8,128)(2,1)}, bf16[864,128]{1,0:T(8,128)(2,1)S(1)}, u32[]{:S(2)}, u32[]{:S(2)}) collective-permute-start(bf16[864,128]{1,0:T(8,128)(2,1)} %copy-done.26), channel_id=1, source_target_pairs={{0,96},{16,112},{32,64},{48,80},{64,32},{80,48},{96,0},{112,16},{1... | collective-permute-start | bytes 663560 | tf_op jit(solution)/shard_map/ppermute | solution.py:61
  79.8 12.0 %collective-permute-start.11 = (bf16[864,128]{1,0:T(8,128)(2,1)}, bf16[864,128]{1,0:T(8,128)(2,1)S(1)}, u32[]{:S(2)}, u32[]{:S(2)}) collective-permute-start(bf16[864,128]{1,0:T(8,128)(2,1)} %copy-done.25), channel_id=1, source_target_pairs={{0,48},{16,32},{32,16},{48,0},{64,112},{80,96},{96,80},{112,64},{1... | collective-permute-start | bytes 663560 | tf_op jit(solution)/shard_map/ppermute | solution.py:61
  79.8 12.0 %collective-permute-start.16 = (bf16[864,128]{1,0:T(8,128)(2,1)}, bf16[864,128]{1,0:T(8,128)(2,1)S(1)}, u32[]{:S(2)}, u32[]{:S(2)}) collective-permute-start(bf16[864,128]{1,0:T(8,128)(2,1)} %copy-done.24), channel_id=1, source_target_pairs={{0,96},{16,112},{32,64},{48,80},{64,32},{80,48},{96,0},{112,16},{1... | collective-permute-start | bytes 663560 | tf_op jit(solution)/shard_map/ppermute | solution.py:61
  83.3 12.2 %collective-permute-start.17 = (bf16[864,128]{1,0:T(8,128)(2,1)}, bf16[864,128]{1,0:T(8,128)(2,1)S(1)}, u32[]{:S(2)}, u32[]{:S(2)}) collective-permute-start(bf16[864,128]{1,0:T(8,128)(2,1)} %copy-done.23), channel_id=1, source_target_pairs={{0,112},{16,96},{32,80},{48,64},{64,48},{80,32},{96,16},{112,0},{1... | collective-permute-start | bytes 663560 | tf_op jit(solution)/shard_map/ppermute | solution.py:61
  88.0 11.7 %collective-permute-start.13 = (bf16[864,128]{1,0:T(8,128)(2,1)S(1)}, bf16[864,128]{1,0:T(8,128)(2,1)S(1)}, u32[]{:S(2)}, u32[]{:S(2)}) collective-permute-start(bf16[864,128]{1,0:T(8,128)(2,1)S(1)} %collective-permute-done.12), channel_id=1, source_target_pairs={{0,96},{16,112},{32,64},{48,80},{64,32},{80,48},{96,0},{112,16},{1... | collective-permute-start | bytes 663560 | tf_op jit(solution)/shard_map/ppermute | solution.py:61
  91.0 8.7 %collective-permute-start.15 = (bf16[864,128]{1,0:T(8,128)(2,1)S(1)}, bf16[864,128]{1,0:T(8,128)(2,1)S(1)}, u32[]{:S(2)}, u32[]{:S(2)}) collective-permute-start(bf16[864,128]{1,0:T(8,128)(2,1)S(1)} %collective-permute-done.14), channel_id=1, source_target_pairs={{0,48},{16,32},{32,16},{48,0},{64,112},{80,96},{96,80},{112,64},{1... | collective-permute-start | bytes 663560 | tf_op jit(solution)/shard_map/ppermute | solution.py:61
  100.7 5.1 %collective-permute-start.36 = (bf16[880,128]{1,0:T(8,128)(2,1)S(1)}, bf16[880,128]{1,0:T(8,128)(2,1)S(1)}, u32[]{:S(2)}, u32[]{:S(2)}) collective-permute-start(bf16[880,128]{1,0:T(8,128)(2,1)S(1)} %get-tuple-element.193), channel_id=1, source_target_pairs={{0,16},{16,0},{32,48},{48,32},{64,80},{80,64},{96,112},{112,96},{1... | collective-permute-start | bytes 675848 | tf_op jit(solution)/shard_map/ppermute | solution.py:61
  100.8 8.4 %collective-permute-start.37 = (bf16[880,128]{1,0:T(8,128)(2,1)S(1)}, bf16[880,128]{1,0:T(8,128)(2,1)S(1)}, u32[]{:S(2)}, u32[]{:S(2)}) collective-permute-start(bf16[880,128]{1,0:T(8,128)(2,1)S(1)} %get-tuple-element.194), channel_id=1, source_target_pairs={{0,32},{16,48},{32,0},{48,16},{64,96},{80,112},{96,64},{112,80},{1... | collective-permute-start | bytes 675848 | tf_op jit(solution)/shard_map/ppermute | solution.py:61
  100.8 13.1 %collective-permute-start.39 = (bf16[880,128]{1,0:T(8,128)(2,1)S(1)}, bf16[880,128]{1,0:T(8,128)(2,1)S(1)}, u32[]{:S(2)}, u32[]{:S(2)}) collective-permute-start(bf16[880,128]{1,0:T(8,128)(2,1)S(1)} %get-tuple-element.196), channel_id=1, source_target_pairs={{0,32},{16,48},{32,0},{48,16},{64,96},{80,112},{96,64},{112,80},{1... | collective-permute-start | bytes 675848 | tf_op jit(solution)/shard_map/ppermute | solution.py:61
  102.9 14.1 %collective-permute-start.41 = (bf16[880,128]{1,0:T(8,128)(2,1)S(1)}, bf16[880,128]{1,0:T(8,128)(2,1)S(1)}, u32[]{:S(2)}, u32[]{:S(2)}) collective-permute-start(bf16[880,128]{1,0:T(8,128)(2,1)S(1)} %get-tuple-element.197), channel_id=1, source_target_pairs={{0,96},{16,112},{32,64},{48,80},{64,32},{80,48},{96,0},{112,16},{1... | collective-permute-start | bytes 675848 | tf_op jit(solution)/shard_map/ppermute | solution.py:61
  105.8 12.1 %collective-permute-start.38 = (bf16[880,128]{1,0:T(8,128)(2,1)S(1)}, bf16[880,128]{1,0:T(8,128)(2,1)S(1)}, u32[]{:S(2)}, u32[]{:S(2)}) collective-permute-start(bf16[880,128]{1,0:T(8,128)(2,1)S(1)} %get-tuple-element.195), channel_id=1, source_target_pairs={{0,48},{16,32},{32,16},{48,0},{64,112},{80,96},{96,80},{112,64},{1... | collective-permute-start | bytes 675848 | tf_op jit(solution)/shard_map/ppermute | solution.py:61
  105.8 12.0 %collective-permute-start.43 = (bf16[880,128]{1,0:T(8,128)(2,1)S(1)}, bf16[880,128]{1,0:T(8,128)(2,1)S(1)}, u32[]{:S(2)}, u32[]{:S(2)}) collective-permute-start(bf16[880,128]{1,0:T(8,128)(2,1)S(1)} %get-tuple-element.198), channel_id=1, source_target_pairs={{0,96},{16,112},{32,64},{48,80},{64,32},{80,48},{96,0},{112,16},{1... | collective-permute-start | bytes 675848 | tf_op jit(solution)/shard_map/ppermute | solution.py:61
  109.2 12.2 %collective-permute-start.44 = (bf16[880,128]{1,0:T(8,128)(2,1)S(1)}, bf16[880,128]{1,0:T(8,128)(2,1)S(1)}, u32[]{:S(2)}, u32[]{:S(2)}) collective-permute-start(bf16[880,128]{1,0:T(8,128)(2,1)S(1)} %get-tuple-element.199), channel_id=1, source_target_pairs={{0,112},{16,96},{32,80},{48,64},{64,48},{80,32},{96,16},{112,0},{1... | collective-permute-start | bytes 675848 | tf_op jit(solution)/shard_map/ppermute | solution.py:61
  114.0 11.9 %collective-permute-start.40 = (bf16[880,128]{1,0:T(8,128)(2,1)S(1)}, bf16[880,128]{1,0:T(8,128)(2,1)S(1)}, u32[]{:S(2)}, u32[]{:S(2)}) collective-permute-start(bf16[880,128]{1,0:T(8,128)(2,1)S(1)} %collective-permute-done.39), channel_id=1, source_target_pairs={{0,96},{16,112},{32,64},{48,80},{64,32},{80,48},{96,0},{112,16},{1... | collective-permute-start | bytes 675848 | tf_op jit(solution)/shard_map/ppermute | solution.py:61
  116.9 8.9 %collective-permute-start.42 = (bf16[880,128]{1,0:T(8,128)(2,1)S(1)}, bf16[880,128]{1,0:T(8,128)(2,1)S(1)}, u32[]{:S(2)}, u32[]{:S(2)}) collective-permute-start(bf16[880,128]{1,0:T(8,128)(2,1)S(1)} %collective-permute-done.41), channel_id=1, source_target_pairs={{0,48},{16,32},{32,16},{48,0},{64,112},{80,96},{96,80},{112,64},{1... | collective-permute-start | bytes 675848 | tf_op jit(solution)/shard_map/ppermute | solution.py:61
  128.4 84.4 %all-to-all-start.1 = ((bf16[16,784,128]{2,1,0:T(8,128)(2,1)}), bf16[16,784,128]{2,1,0:T(8,128)(2,1)}, u32[]{:S(2)}, u32[]{:S(2)}) async-start(bf16[16,784,128]{2,1,0:T(8,128)(2,1)} %copy-done), calls=%async_computation.1 | async-start | bytes 6422528 | tf_op jit(solution)/shard_map/all_to_all | solution.py:355
  135.6 5.2 %collective-permute-start.27 = (bf16[576,128]{1,0:T(8,128)(2,1)}, bf16[576,128]{1,0:T(8,128)(2,1)S(1)}, u32[]{:S(2)}, u32[]{:S(2)}) collective-permute-start(bf16[576,128]{1,0:T(8,128)(2,1)} %copy-done.36), channel_id=1, source_target_pairs={{0,16},{16,0},{32,48},{48,32},{64,80},{80,64},{96,112},{112,96},{1... | collective-permute-start | bytes 442376 | tf_op jit(solution)/shard_map/ppermute | solution.py:61
  135.7 6.9 %collective-permute-start.28 = (bf16[576,128]{1,0:T(8,128)(2,1)}, bf16[576,128]{1,0:T(8,128)(2,1)S(1)}, u32[]{:S(2)}, u32[]{:S(2)}) collective-permute-start(bf16[576,128]{1,0:T(8,128)(2,1)} %copy-done.35), channel_id=1, source_target_pairs={{0,32},{16,48},{32,0},{48,16},{64,96},{80,112},{96,64},{112,80},{1... | collective-permute-start | bytes 442376 | tf_op jit(solution)/shard_map/ppermute | solution.py:61
  135.8 10.0 %collective-permute-start.30 = (bf16[576,128]{1,0:T(8,128)(2,1)}, bf16[576,128]{1,0:T(8,128)(2,1)S(1)}, u32[]{:S(2)}, u32[]{:S(2)}) collective-permute-start(bf16[576,128]{1,0:T(8,128)(2,1)} %copy-done.34), channel_id=1, source_target_pairs={{0,32},{16,48},{32,0},{48,16},{64,96},{80,112},{96,64},{112,80},{1... | collective-permute-start | bytes 442376 | tf_op jit(solution)/shard_map/ppermute | solution.py:61
  137.8 11.0 %collective-permute-start.32 = (bf16[576,128]{1,0:T(8,128)(2,1)}, bf16[576,128]{1,0:T(8,128)(2,1)S(1)}, u32[]{:S(2)}, u32[]{:S(2)}) collective-permute-start(bf16[576,128]{1,0:T(8,128)(2,1)} %copy-done.33), channel_id=1, source_target_pairs={{0,96},{16,112},{32,64},{48,80},{64,32},{80,48},{96,0},{112,16},{1... | collective-permute-start | bytes 442376 | tf_op jit(solution)/shard_map/ppermute | solution.py:61
  140.7 8.0 %collective-permute-start.29 = (bf16[576,128]{1,0:T(8,128)(2,1)}, bf16[576,128]{1,0:T(8,128)(2,1)S(1)}, u32[]{:S(2)}, u32[]{:S(2)}) collective-permute-start(bf16[576,128]{1,0:T(8,128)(2,1)} %copy-done.32), channel_id=1, source_target_pairs={{0,48},{16,32},{32,16},{48,0},{64,112},{80,96},{96,80},{112,64},{1... | collective-permute-start | bytes 442376 | tf_op jit(solution)/shard_map/ppermute | solution.py:61
  140.7 8.2 %collective-permute-start.34 = (bf16[576,128]{1,0:T(8,128)(2,1)}, bf16[576,128]{1,0:T(8,128)(2,1)S(1)}, u32[]{:S(2)}, u32[]{:S(2)}) collective-permute-start(bf16[576,128]{1,0:T(8,128)(2,1)} %copy-done.31), channel_id=1, source_target_pairs={{0,96},{16,112},{32,64},{48,80},{64,32},{80,48},{96,0},{112,16},{1... | collective-permute-start | bytes 442376 | tf_op jit(solution)/shard_map/ppermute | solution.py:61
  142.6 8.8 %collective-permute-start.35 = (bf16[576,128]{1,0:T(8,128)(2,1)}, bf16[576,128]{1,0:T(8,128)(2,1)S(1)}, u32[]{:S(2)}, u32[]{:S(2)}) collective-permute-start(bf16[576,128]{1,0:T(8,128)(2,1)} %copy-done.30), channel_id=1, source_target_pairs={{0,112},{16,96},{32,80},{48,64},{64,48},{80,32},{96,16},{112,0},{1... | collective-permute-start | bytes 442376 | tf_op jit(solution)/shard_map/ppermute | solution.py:61
  145.8 8.5 %collective-permute-start.31 = (bf16[576,128]{1,0:T(8,128)(2,1)S(1)}, bf16[576,128]{1,0:T(8,128)(2,1)S(1)}, u32[]{:S(2)}, u32[]{:S(2)}) collective-permute-start(bf16[576,128]{1,0:T(8,128)(2,1)S(1)} %collective-permute-done.30), channel_id=1, source_target_pairs={{0,96},{16,112},{32,64},{48,80},{64,32},{80,48},{96,0},{112,16},{1... | collective-permute-start | bytes 442376 | tf_op jit(solution)/shard_map/ppermute | solution.py:61
  148.7 5.6 %collective-permute-start.33 = (bf16[576,128]{1,0:T(8,128)(2,1)S(1)}, bf16[576,128]{1,0:T(8,128)(2,1)S(1)}, u32[]{:S(2)}, u32[]{:S(2)}) collective-permute-start(bf16[576,128]{1,0:T(8,128)(2,1)S(1)} %collective-permute-done.32), channel_id=1, source_target_pairs={{0,48},{16,32},{32,16},{48,0},{64,112},{80,96},{96,80},{112,64},{1... | collective-permute-start | bytes 442376 | tf_op jit(solution)/shard_map/ppermute | solution.py:61
  155.0 5.1 %collective-permute-start.45 = (bf16[592,128]{1,0:T(8,128)(2,1)S(1)}, bf16[592,128]{1,0:T(8,128)(2,1)S(1)}, u32[]{:S(2)}, u32[]{:S(2)}) collective-permute-start(bf16[592,128]{1,0:T(8,128)(2,1)S(1)} %get-tuple-element.217), channel_id=1, source_target_pairs={{0,16},{16,0},{32,48},{48,32},{64,80},{80,64},{96,112},{112,96},{1... | collective-permute-start | bytes 454664 | tf_op jit(solution)/shard_map/ppermute | solution.py:61
  155.1 6.8 %collective-permute-start.46 = (bf16[592,128]{1,0:T(8,128)(2,1)S(1)}, bf16[592,128]{1,0:T(8,128)(2,1)S(1)}, u32[]{:S(2)}, u32[]{:S(2)}) collective-permute-start(bf16[592,128]{1,0:T(8,128)(2,1)S(1)} %get-tuple-element.218), channel_id=1, source_target_pairs={{0,32},{16,48},{32,0},{48,16},{64,96},{80,112},{96,64},{112,80},{1... | collective-permute-start | bytes 454664 | tf_op jit(solution)/shard_map/ppermute | solution.py:61
  156.1 9.1 %collective-permute-start.48 = (bf16[592,128]{1,0:T(8,128)(2,1)S(1)}, bf16[592,128]{1,0:T(8,128)(2,1)S(1)}, u32[]{:S(2)}, u32[]{:S(2)}) collective-permute-start(bf16[592,128]{1,0:T(8,128)(2,1)S(1)} %get-tuple-element.220), channel_id=1, source_target_pairs={{0,32},{16,48},{32,0},{48,16},{64,96},{80,112},{96,64},{112,80},{1... | collective-permute-start | bytes 454664 | tf_op jit(solution)/shard_map/ppermute | solution.py:61
  157.2 10.9 %collective-permute-start.50 = (bf16[592,128]{1,0:T(8,128)(2,1)S(1)}, bf16[592,128]{1,0:T(8,128)(2,1)S(1)}, u32[]{:S(2)}, u32[]{:S(2)}) collective-permute-start(bf16[592,128]{1,0:T(8,128)(2,1)S(1)} %get-tuple-element.221), channel_id=1, source_target_pairs={{0,96},{16,112},{32,64},{48,80},{64,32},{80,48},{96,0},{112,16},{1... | collective-permute-start | bytes 454664 | tf_op jit(solution)/shard_map/ppermute | solution.py:61
  160.1 13.8 %collective-permute-start.47 = (bf16[592,128]{1,0:T(8,128)(2,1)S(1)}, bf16[592,128]{1,0:T(8,128)(2,1)S(1)}, u32[]{:S(2)}, u32[]{:S(2)}) collective-permute-start(bf16[592,128]{1,0:T(8,128)(2,1)S(1)} %get-tuple-element.219), channel_id=1, source_target_pairs={{0,48},{16,32},{32,16},{48,0},{64,112},{80,96},{96,80},{112,64},{1... | collective-permute-start | bytes 454664 | tf_op jit(solution)/shard_map/ppermute | solution.py:61
  160.2 13.8 %collective-permute-start.52 = (bf16[592,128]{1,0:T(8,128)(2,1)S(1)}, bf16[592,128]{1,0:T(8,128)(2,1)S(1)}, u32[]{:S(2)}, u32[]{:S(2)}) collective-permute-start(bf16[592,128]{1,0:T(8,128)(2,1)S(1)} %get-tuple-element.222), channel_id=1, source_target_pairs={{0,96},{16,112},{32,64},{48,80},{64,32},{80,48},{96,0},{112,16},{1... | collective-permute-start | bytes 454664 | tf_op jit(solution)/shard_map/ppermute | solution.py:61
  161.9 12.1 %collective-permute-start.53 = (bf16[592,128]{1,0:T(8,128)(2,1)S(1)}, bf16[592,128]{1,0:T(8,128)(2,1)S(1)}, u32[]{:S(2)}, u32[]{:S(2)}) collective-permute-start(bf16[592,128]{1,0:T(8,128)(2,1)S(1)} %get-tuple-element.223), channel_id=1, source_target_pairs={{0,112},{16,96},{32,80},{48,64},{64,48},{80,32},{96,16},{112,0},{1... | collective-permute-start | bytes 454664 | tf_op jit(solution)/shard_map/ppermute | solution.py:61
  165.2 8.9 %collective-permute-start.49 = (bf16[592,128]{1,0:T(8,128)(2,1)S(1)}, bf16[592,128]{1,0:T(8,128)(2,1)S(1)}, u32[]{:S(2)}, u32[]{:S(2)}) collective-permute-start(bf16[592,128]{1,0:T(8,128)(2,1)S(1)} %collective-permute-done.48), channel_id=1, source_target_pairs={{0,96},{16,112},{32,64},{48,80},{64,32},{80,48},{96,0},{112,16},{1... | collective-permute-start | bytes 454664 | tf_op jit(solution)/shard_map/ppermute | solution.py:61
  168.1 5.9 %collective-permute-start.51 = (bf16[592,128]{1,0:T(8,128)(2,1)S(1)}, bf16[592,128]{1,0:T(8,128)(2,1)S(1)}, u32[]{:S(2)}, u32[]{:S(2)}) collective-permute-start(bf16[592,128]{1,0:T(8,128)(2,1)S(1)} %collective-permute-done.50), channel_id=1, source_target_pairs={{0,48},{16,32},{32,16},{48,0},{64,112},{80,96},{96,80},{112,64},{1... | collective-permute-start | bytes 454664 | tf_op jit(solution)/shard_map/ppermute | solution.py:61
  174.9 10.6 %collective-permute-start.58 = (bf16[8,272,128]{2,1,0:T(8,128)(2,1)S(1)}, bf16[8,272,128]{2,1,0:T(8,128)(2,1)S(1)}, u32[]{:S(2)}, u32[]{:S(2)}) collective-permute-start(bf16[8,272,128]{2,1,0:T(8,128)(2,1)S(1)} %get-tuple-element.237), channel_id=1, source_target_pairs={{0,4},{1,5},{2,6},{3,7},{4,0},{5,1},{6,2},{7,3},{8,12},{9,13},{10,... | collective-permute-start | bytes 1671176 | tf_op jit(solution)/shard_map/ppermute | solution.py:85
  176.8 9.7 %collective-permute-start.54 = (bf16[8,256,128]{2,1,0:T(8,128)(2,1)S(1)}, bf16[8,256,128]{2,1,0:T(8,128)(2,1)S(1)}, u32[]{:S(2)}, u32[]{:S(2)}) collective-permute-start(bf16[8,256,128]{2,1,0:T(8,128)(2,1)S(1)} %get-tuple-element.235), channel_id=1, source_target_pairs={{0,1},{1,0},{2,3},{3,2},{4,5},{5,4},{6,7},{7,6},{8,9},{9,8},{10,11... | collective-permute-start | bytes 1572872 | tf_op jit(solution)/shard_map/ppermute | solution.py:85
  185.5 9.6 %collective-permute-start.59 = (bf16[8,272,128]{2,1,0:T(8,128)(2,1)S(1)}, bf16[8,272,128]{2,1,0:T(8,128)(2,1)S(1)}, u32[]{:S(2)}, u32[]{:S(2)}) collective-permute-start(bf16[8,272,128]{2,1,0:T(8,128)(2,1)S(1)} %regroup.9), channel_id=1, source_target_pairs={{0,1},{1,0},{2,3},{3,2},{4,5},{5,4},{6,7},{7,6},{8,9},{9,8},{10,11... | collective-permute-start | bytes 1671176 | tf_op jit(solution)/shard_map/ppermute | solution.py:85
  186.5 12.8 %collective-permute-start.55 = (bf16[8,256,128]{2,1,0:T(8,128)(2,1)S(1)}, bf16[8,256,128]{2,1,0:T(8,128)(2,1)S(1)}, u32[]{:S(2)}, u32[]{:S(2)}) collective-permute-start(bf16[8,256,128]{2,1,0:T(8,128)(2,1)S(1)} %regroup.6), channel_id=1, source_target_pairs={{0,4},{1,5},{2,6},{3,7},{4,0},{5,1},{6,2},{7,3},{8,12},{9,13},{10,... | collective-permute-start | bytes 1572872 | tf_op jit(solution)/shard_map/ppermute | solution.py:85
  195.1 11.6 %collective-permute-start.60 = (bf16[8,272,128]{2,1,0:T(8,128)(2,1)S(1)}, bf16[8,272,128]{2,1,0:T(8,128)(2,1)S(1)}, u32[]{:S(2)}, u32[]{:S(2)}) collective-permute-start(bf16[8,272,128]{2,1,0:T(8,128)(2,1)S(1)} %regroup.10), channel_id=1, source_target_pairs={{0,12},{1,13},{2,14},{3,15},{4,8},{5,9},{6,10},{7,11},{8,4},{9,5},... | collective-permute-start | bytes 1671176 | tf_op jit(solution)/shard_map/ppermute | solution.py:85
  199.3 10.5 %collective-permute-start.56 = (bf16[8,256,128]{2,1,0:T(8,128)(2,1)S(1)}, bf16[8,256,128]{2,1,0:T(8,128)(2,1)S(1)}, u32[]{:S(2)}, u32[]{:S(2)}) collective-permute-start(bf16[8,256,128]{2,1,0:T(8,128)(2,1)S(1)} %regroup.7), channel_id=1, source_target_pairs={{0,3},{1,2},{2,1},{3,0},{4,7},{5,6},{6,5},{7,4},{8,11},{9,10},{10,... | collective-permute-start | bytes 1572872 | tf_op jit(solution)/shard_map/ppermute | solution.py:85
  207.7 14.0 %collective-permute-start.61 = (bf16[8,272,128]{2,1,0:T(8,128)(2,1)}, bf16[8,272,128]{2,1,0:T(8,128)(2,1)}, u32[]{:S(2)}, u32[]{:S(2)}) collective-permute-start(bf16[8,272,128]{2,1,0:T(8,128)(2,1)} %regroup.11), channel_id=1, source_target_pairs={{0,3},{1,2},{2,1},{3,0},{4,7},{5,6},{6,5},{7,4},{8,11},{9,10},{10,... | collective-permute-start | bytes 1671176 | tf_op jit(solution)/shard_map/ppermute | solution.py:85
  210.7 11.0 %collective-permute-start.57 = (bf16[8,256,128]{2,1,0:T(8,128)(2,1)}, bf16[8,256,128]{2,1,0:T(8,128)(2,1)}, u32[]{:S(2)}, u32[]{:S(2)}) collective-permute-start(bf16[8,256,128]{2,1,0:T(8,128)(2,1)} %regroup.8), channel_id=1, source_target_pairs={{0,12},{1,13},{2,14},{3,15},{4,8},{5,9},{6,10},{7,11},{8,4},{9,5},... | collective-permute-start | bytes 1572872 | tf_op jit(solution)/shard_map/ppermute | solution.py:85
  (37 other events, 781.4 us)

commit v5 on v4

v5 whole, which is shorter than its diff:
```python
import functools

import numpy as np
import jax
import jax.numpy as jnp
from jax import lax
from jax.experimental import pallas as pl
from jax.experimental.pallas import tpu as pltpu
from jax.sharding import PartitionSpec as P

HEAD_DIM = 128
HAD = 128
CHUNKS = ((0, 32), (32, 48), (80, 48))
ORDER = (
    ("start", 0),
    ("start", 1),
    ("y_regroup", 0),
    ("y_regroup", 1),
    ("cross", 0),
    ("start", 2),
    ("y_regroup", 0),
    ("cross", 1),
    ("spread", 0),
    ("y_regroup", 2),
    ("y_regroup", 1),
    ("regroup", 0),
    ("cross", 2),
    ("spread", 1),
    ("pack", 0),
    ("y_regroup", 2),
    ("regroup", 1),
    ("spread", 2),
    ("pack", 1),
    ("regroup", 2),
    ("pack", 2),
)
TAIL = 16
VMEM_BYTES = 12 * 1024 * 1024
BOTH = ("fsdp", "tp")


def hadamard_table(order):
    matrix = np.ones((1, 1), np.float32)
    while matrix.shape[0] < order:
        matrix = np.block([[matrix, matrix], [matrix, -matrix]])
    return matrix


def butterfly(values):
    values = list(values)
    half = 1
    while half < len(values):
        for low in range(len(values)):
            if not low & half:
                first, second = values[low], values[low + half]
                values[low], values[low + half] = first + second, first - second
        half *= 2
    return values


PAIRINGS = ((1, 3), (3, 1))


def hop(array, rule):
    groups, owners = lax.axis_size("fsdp"), lax.axis_size("tp")
    pairs = []
    for f in range(groups):
        for t in range(owners):
            to_f, to_t = rule(f, t)
            pairs.append((f * owners + t, to_f * owners + to_t))
    return lax.ppermute(array, BOTH, pairs)


def y_first(blocks):
    own, core, pair, both = blocks
    pair = hop(pair, lambda f, t: (f ^ 2 * PAIRINGS[f & 1][0], t))
    both = hop(both, lambda f, t: (f ^ 1 ^ 2 * PAIRINGS[1 - (f & 1)][0], t))
    core = hop(core, lambda f, t: (f ^ 1, t))
    return [own, core, pair, both]


def y_second(payload):
    return hop(payload, lambda f, t: (f ^ 2 * PAIRINGS[f & 1][1], t))


def owner_hops(blocks, which):
    out = [None] * 3
    for place in (2, 0, 1):
        factor = (1, 4, 5)[place]
        out[place] = hop(blocks[place], lambda f, t: (f, t ^ factor * PAIRINGS[f & 1][which]))
    return out


def to_slots(values, swap):
    return (
        (values[0], jnp.where(swap, values[2], values[6])),
        (values[1], jnp.where(swap, values[7], values[3])),
        (jnp.where(swap, values[6], values[2]), values[4]),
        (jnp.where(swap, values[3], values[7]), values[5]),
    )


def from_origins(values, swap):
    return (
        values[0],
        values[1],
        jnp.where(swap, values[4], values[2]),
        jnp.where(swap, values[5], values[3]),
        values[6],
        values[7],
        jnp.where(swap, values[2], values[4]),
        jnp.where(swap, values[3], values[5]),
    )


def y_regroup_kernel(*refs):
    for index, in_ref in enumerate(refs[:4]):
        refs[4][index] = in_ref[1]


def regroup_kernel(*refs):
    in_refs, out_refs = refs[:4], refs[4:]
    for slot, out_ref in enumerate(out_refs):
        for index, in_ref in enumerate(in_refs):
            out_ref[index] = in_ref[slot + 1]


def sign_of(value, bits):
    both = value & bits
    both = both ^ (both >> 2)
    both = both ^ (both >> 1)
    return (1 - 2 * (both & 1)).astype(jnp.float32)


def local_turn_kernel(rows_a, weight_ref, signs_ref, *refs):
    out_refs, turned = refs[:-1], refs[-1]
    group = lax.axis_index("fsdp")
    swap = group & 1 != 0
    flips = [sign_of(group, a >> 1) * (1.0 / HAD) for a in range(rows_a)]
    columns = jnp.concatenate([weight_ref[a * HAD : (a + 1) * HAD, :].T for a in range(rows_a)], axis=0)
    turned[...] = jnp.dot(columns, signs_ref[...], preferred_element_type=jnp.float32)
    for index, (first, chans) in enumerate(CHUNKS):
        for low in range(0, chans, 16):
            outs = []
            for a in range(rows_a):
                start = a * HEAD_DIM + first + low
                outs.append(turned[start : start + 16, :] * flips[a])
            outs = butterfly(outs)
            for e in range(2):
                row = e * chans + low
                for array, values in enumerate(to_slots(outs[e::2], swap)):
                    for slot, value in enumerate(values):
                        out_refs[4 * index + array][slot, row : row + 16, :] = value.astype(jnp.bfloat16)


def join_parts(value, chans):
    return value + pltpu.roll(value, HAD - chans, 1)


def split_parts(value, chans):
    high = value.astype(jnp.bfloat16).astype(jnp.float32)
    lane = lax.broadcasted_iota(jnp.int32, value.shape, 1)
    both = jnp.where(lane < chans, high, pltpu.roll(value - high, chans, 1))
    return jnp.where(lane < 2 * chans, both, 0.0).astype(jnp.bfloat16)


def cross_turn_kernel(heads, chans, *refs):
    in_refs, out_refs = refs[:5], refs[5:]
    group = lax.axis_index("fsdp")
    swap = group & 1 != 0
    flips_in = [sign_of(group, s) for s in range(8)]
    flips_out = [flip * sign_of(group, group) for flip in flips_in]
    row_id = lax.broadcasted_iota(jnp.int32, (TAIL, HAD), 0)
    tail = jnp.zeros((TAIL, HAD), jnp.float32)
    for head in range(heads):
        columns = []
        for low in range(0, chans, 16):
            largest = None
            for e in range(2):
                rows = slice((head * 2 + e) * chans + low, (head * 2 + e) * chans + low + 16)
                got = [in_ref[0, rows, :] for in_ref in in_refs[:4]] + [in_refs[4][i, rows, :] for i in range(4)]
                got = from_origins([value.astype(jnp.float32) for value in got], swap)
                outs = butterfly([got[s] * flips_in[s] for s in range(8)])
                for s in range(8):
                    magnitude = jnp.abs(outs[s])
                    largest = magnitude if largest is None else jnp.maximum(largest, magnitude)
                outs = [outs[s] * flips_out[s] for s in range(8)]
                for array, values in enumerate(to_slots(outs, swap)):
                    for slot, value in enumerate(values):
                        out_refs[array][slot, rows, :] = value.astype(jnp.bfloat16)
            columns.append(largest)
        columns.append(jnp.zeros((HAD - chans, HAD), jnp.float32))
        peak = jnp.max(jnp.concatenate(columns, axis=0).T, axis=0, keepdims=True)
        tail = jnp.where(row_id == head, peak, tail)
    tail = split_parts(tail, chans)
    for out_ref in out_refs:
        for slot in range(2):
            out_ref[slot, heads * 2 * chans :, :] = tail


def pairing_offset(core, which, index):
    factor = (index & 1) + 4 * (index >> 1)
    return factor * jnp.where(core == 0, PAIRINGS[0][which], PAIRINGS[1][which])


def spread_kernel(heads, chans, placement_ref, *refs):
    in_refs, out_refs = refs[:5], refs[5:]
    me, core = lax.axis_index("tp"), lax.axis_index("fsdp") & 1
    mine = [placement_ref[me * heads + head] for head in range(heads)]
    blocks = [(in_ref, 0) for in_ref in in_refs[:4]] + [(in_refs[4], index) for index in range(4)]
    peaks = None
    for in_ref, index in blocks:
        part = join_parts(in_ref[index, heads * 2 * chans :, :].astype(jnp.float32), chans)
        peaks = part if peaks is None else jnp.maximum(peaks, part)
    row_id = lax.broadcasted_iota(jnp.int32, (TAIL, HAD), 0)
    span = 2 * chans
    for i, out_ref in enumerate(out_refs):
        for j in range(4):
            owner = me ^ pairing_offset(core, 0, i) ^ pairing_offset(core, 1, j)
            head = 0
            for index in range(1, heads):
                head = jnp.where(mine[index] == owner, index, head)
            rows = pl.ds(pl.multiple_of(head * span, 16), span)
            for s, (in_ref, index) in enumerate(blocks):
                out_ref[j, s * span : (s + 1) * span, :] = in_ref[index, rows, :]
            peak = jnp.sum(jnp.where(row_id == head, peaks, 0.0), axis=0, keepdims=True)
            out_ref[j, 8 * span :, :] = split_parts(jnp.broadcast_to(peak, (TAIL, HAD)), chans)


def pack_kernel(owners, heads, chunk, has_past, placement_ref, *refs):
    first, chans = chunk
    peak_ref, out_ref, buffer, sems, live_ref, slot_ref = refs[-6:]
    past_ref = refs[-8] if has_past else None
    in_refs = refs[: -8 if has_past else -6]
    me, group = lax.axis_index("tp"), lax.axis_index("fsdp")
    count = 0
    for source in range(owners):
        live = 0
        for head in range(heads):
            live = jnp.where(placement_ref[source * heads + head] == me, 1, live)
        live_ref[source] = live
        slot_ref[source] = count
        count = count + live
    lane = lax.broadcasted_iota(jnp.int32, (TAIL, HAD), 1)
    depth = buffer.shape[0]
    copies = [None] * depth
    core = group & 1
    pair = jnp.where(core == 0, 2, 6)
    offsets = (0, 1, pair, pair ^ 1, pair ^ 4, pair ^ 5, 4, 5)
    for origin in range(owners):
        i, j = origin % 4, origin // 4
        in_ref, index = (in_refs[3 + j], i) if j else (in_refs[i], 0)
        source = me ^ pairing_offset(core, 0, i) ^ pairing_offset(core, 1, j)
        part = origin % depth
        if copies[part] is not None:
            copies[part].wait()
        live = live_ref[source] != 0
        slot = jnp.where(live, slot_ref[source], count + source - slot_ref[source])
        tail = in_ref[index, 16 * chans :, :].astype(jnp.float32)
        row = jnp.where((lane < chans) & live, join_parts(tail, chans), 0.0)[:1, :]
        scale = jnp.where(live, 1.0 / (row + 1e-06), 0.0)
        scale = jnp.broadcast_to(scale, (HEAD_DIM, HAD)).T[:chans, :]
        row = pltpu.roll(jnp.broadcast_to(row, (8, HAD)), first, 1)[:1, :] if first else row
        if has_past:
            row = row + past_ref[pl.ds(slot, 1), :]
        peak_ref[pl.ds(slot, 1), :] = row
        for s in range(8):
            for e in range(2):
                start = (s * 2 + e) * chans
                lanes = pl.ds(pl.multiple_of(((group ^ offsets[s]) * 2 + e) * HAD, HAD), HAD)
                block = in_ref[index, start : start + chans, :]
                buffer[part, :, lanes] = (block.astype(jnp.float32) * scale).astype(jnp.bfloat16)
        copies[part] = pltpu.make_async_copy(
            buffer.at[part], out_ref.at[0, slot, first : first + chans, :], sems.at[part]
        )
        copies[part].start()
    for copy in copies:
        copy.wait()


def per_device(qkv_weight, placement):
    rows_local, cols_local = qkv_weight.shape
    heads = cols_local // HEAD_DIM
    owners = lax.axis_size("tp")
    rows_a = rows_local // HAD
    params = pltpu.CompilerParams(vmem_limit_bytes=VMEM_BYTES)
    any_spec = pl.BlockSpec(memory_space=pl.ANY)
    smem_spec = pl.BlockSpec(memory_space=pltpu.SMEM)
    vmem_spec = pl.BlockSpec(memory_space=pltpu.VMEM)

    def call(kernel, name, shapes, *arrays, table=False):
        return pl.pallas_call(
            kernel,
            in_specs=[smem_spec] * table + [vmem_spec] * (len(arrays) - table),
            out_specs=[vmem_spec] * len(shapes),
            out_shape=[jax.ShapeDtypeStruct(shape + (HAD,), jnp.bfloat16) for shape in shapes],
            compiler_params=params,
            name=name,
        )(*arrays)

    signs = jnp.asarray(hadamard_table(HAD), jnp.bfloat16)
    widths = [2 * chans for _, chans in CHUNKS for _ in range(4)]
    turned = pl.pallas_call(
        functools.partial(local_turn_kernel, rows_a),
        grid=(heads,),
        in_specs=[
            pl.BlockSpec((rows_local, HEAD_DIM), lambda h: (0, h)),
            pl.BlockSpec((HAD, HAD), lambda h: (0, 0)),
        ],
        out_specs=[pl.BlockSpec((2, width, HAD), lambda h: (0, h, 0)) for width in widths],
        out_shape=[jax.ShapeDtypeStruct((2, heads * width, HAD), jnp.bfloat16) for width in widths],
        scratch_shapes=[pltpu.VMEM((rows_local, HAD), jnp.float32)],
        compiler_params=params,
        name="local_turn",
    )(qkv_weight, signs)

    state = [turned[4 * index : 4 * index + 4] for index in range(len(CHUNKS))]
    token = None
    past = []

    def tie(arrays):
        if token is None:
            return list(arrays)
        return list(lax.optimization_barrier((list(arrays), token))[0])

    for stage, index in ORDER:
        first, chans = chunk = CHUNKS[index]
        arrays = tie(state[index])
        if stage == "start":
            state[index] = y_first(arrays)
        elif stage == "y_regroup":
            (token,) = call(y_regroup_kernel, stage, [(4,) + arrays[0].shape[1:2]], *arrays)
            state[index] = arrays + [y_second(token)]
        elif stage == "cross":
            shapes = [(2, heads * 2 * chans + TAIL)] * 4
            outs = call(functools.partial(cross_turn_kernel, heads, chans), stage, shapes, *arrays)
            token = outs[0]
            state[index] = y_first(outs)
        elif stage == "spread":
            shapes = [(4, 16 * chans + TAIL)] * 4
            kernel = functools.partial(spread_kernel, heads, chans)
            outs = call(kernel, stage, shapes, placement, *arrays, table=True)
            token = outs[0]
            state[index] = [outs[0]] + owner_hops(outs[1:], 0)
        elif stage == "regroup":
            outs = call(regroup_kernel, stage, [arrays[0].shape[:2]] * 3, *arrays)
            token = outs[0]
            state[index] = arrays + owner_hops(outs, 1)
        else:
            past = pl.pallas_call(
                functools.partial(pack_kernel, owners, heads, chunk, bool(past)),
                in_specs=[smem_spec] + [vmem_spec] * len(arrays) + ([vmem_spec, any_spec] if past else []),
                out_specs=[vmem_spec, any_spec],
                out_shape=[
                    jax.ShapeDtypeStruct((owners, HEAD_DIM), jnp.float32),
                    jax.ShapeDtypeStruct((1, owners, HEAD_DIM, rows_local), jnp.bfloat16),
                ],
                scratch_shapes=[
                    pltpu.VMEM((3, chans, rows_local), jnp.bfloat16),
                    pltpu.SemaphoreType.DMA((3,)),
                    pltpu.SMEM((owners,), jnp.int32),
                    pltpu.SMEM((owners,), jnp.int32),
                ],
                input_output_aliases={2 + len(arrays): 1} if past else {},
                compiler_params=params,
                name="pack",
            )(placement, *arrays, *past)
            token = past[0]
    peaks, packed = past
    return packed, peaks[None]


def solution(mesh):
    in_specs = (P("fsdp", "tp"), P())
    out_specs = (P("tp", None, None, "fsdp"), P("tp", None, None))
    return jax.shard_map(
        per_device, mesh=mesh, in_specs=in_specs, out_specs=out_specs, check_vma=False
    )
```

time: 229 us -> 212 us (0.926)
  starting transfers between devices: 90.6 us -> 55.2 us
  waiting for transfers between devices: 93.9 us -> 122 us
  local copies, waits for them, and re-layouts: 10.7 us -> 3.09 us
  Pallas kernels: 32.4 us -> 30 us
    ppermute x62 -> x42, waiting for transfers between devices: 93.9 us -> 122 us  [hop(): return lax.ppermute(array, BOTH, pairs)]
    ppermute x62 -> x42, starting transfers between devices: 75.5 us -> 55.2 us  [hop(): return lax.ppermute(array, BOTH, pairs)]
    all_to_all x2 -> x0, starting transfers between devices: 15.1 us -> none  [per_device(): lax.all_to_all(outs[0], 'tp', split_axis=0, concat_axis=0, tiled=True)]
    unnamed x74 -> x6, local copies, waits for them, and re-layouts: 10.7 us -> 3.09 us
    pallas_call x12 -> x15, Pallas kernels: 7.22 us -> 6.35 us  [call(): pl.pallas_call(kernel, in_specs=[smem_spec] * table + [vmem_spec] * (len(...]
  transfers between devices with their start and end apart: 64 -> 42, of which waited for: 32 -> 21; matrix products, arithmetic and copies ran while one was open for 0% -> 0% of each run, Pallas kernels for 8% -> 8%
where the time goes in v5:
time: 212 us
  waiting for transfers between devices  122 us (58%)
  starting transfers between devices  55.2 us (26%)
  Pallas kernels  30 us (14%)
  local copies, waits for them, and re-layouts  3.09 us (1%)
    ppermute x42, waiting for transfers between devices, hop(): return lax.ppermute(array, BOTH, pairs)  122 us
    ppermute x42, starting transfers between devices, hop(): return lax.ppermute(array, BOTH, pairs)  55.2 us
    pallas_call x3, Pallas kernels, per_device(): pl.pallas_call(functools.partial(pack_kernel, owners, heads, chunk, bool(...  18 us
    pallas_call x15, Pallas kernels, call(): pl.pallas_call(kernel, in_specs=[smem_spec] * table + [vmem_spec] * (len(...  6.35 us
    pallas_call x1, Pallas kernels, per_device(): pl.pallas_call(functools.partial(local_turn_kernel, rows_a), grid=(heads,...  5.64 us
  transfers between devices with their start and end apart: 42, of which 21 were waited for; matrix products, arithmetic and copies ran while one was open for 0% of the time, Pallas kernels for 8%

profile of v5, /device:TPU:0, one launch (start us, length us, event | category | flops | bytes accessed | tf_op | source)
XLA Modules:
  0.0 211.7 jit_solution(10075239631615377093)
XLA Ops:
  0.6 2.3 %copy-done = bf16[2048,1152]{1,0:T(8,128)(2,1)S(1)} copy-done((bf16[2048,1152]{1,0:T(8,128)(2,1)S(1)}, bf16[2048,1152]{1,0:T(8,128)(2,1)}, u32[]{:S(2)}) %copy-start) | copy-done | bytes 4718616
  3.0 0.8 copy-done.2
  3.7 5.6 %local_turn.1 = (bf16[2,576,128]{2,1,0:T(8,128)(2,1)S(1)}, bf16[2,576,128]{2,1,0:T(8,128)(2,1)S(1)}, bf16[2,576,128]{2,1,0:T(8,128)(2,1)S(1)}, bf16[2,576,128]{2...) custom-call(bf16[2048,1152]{1,0:T(8,128)(2,1)S(1)} %copy-done, ...), custom_call_target="tpu_custom_call" | custom-call | tf_op jit(solution)/shard_map/local_turn/pallas_call | solution.py:303
  9.5 1.7 collective-permute-start.1
  11.2 1.5 collective-permute-start.2
  12.8 0.6 collective-permute-start.5
  13.4 2.4 %collective-permute-start.6 = (bf16[2,864,128]{2,1,0:T(8,128)(2,1)S(1)}, bf16[2,864,128]{2,1,0:T(8,128)(2,1)S(1)}, u32[]{:S(2)}, u32[]{:S(2)}) collective-permute-start(bf16[2,864,128]{2,1,0:T(8,128)(2,1)S(1)} %get-tuple-element.151), channel_id=1, source_target_pairs={{0,112},{1,113},{2,114},{3,115},{4,116},{5,117},{6,118},{7,119},{8... | collective-permute-start | bytes 1327112 | tf_op jit(solution)/shard_map/ppermute | solution.py:71
  15.8 2.5 %collective-permute-done.1.refs_2_ = bf16[2,576,128]{2,1,0:T(8,128)(2,1)S(1)} collective-permute-done((bf16[2,576,128]{2,1,0:T(8,128)(2,1)S(1)}, bf16[2,576,128]{2,1,0:T(8,128)(2,1)S(1)}, u32[]{:S(2)}, u32[]{:S(2)}) %collective-permute-start.1) | collective-permute-done | bytes 294944 | tf_op jit(solution)/shard_map/ppermute | solution.py:71
  18.3 2.2 %collective-permute-done.2.refs_3_ = bf16[2,576,128]{2,1,0:T(8,128)(2,1)S(1)} collective-permute-done((bf16[2,576,128]{2,1,0:T(8,128)(2,1)S(1)}, bf16[2,576,128]{2,1,0:T(8,128)(2,1)S(1)}, u32[]{:S(2)}, u32[]{:S(2)}) %collective-permute-start.2) | collective-permute-done | bytes 294944 | tf_op jit(solution)/shard_map/ppermute | solution.py:71
  20.6 2.6 %collective-permute-start.3 = (bf16[4,576,128]{2,1,0:T(8,128)(2,1)S(1)}, bf16[4,576,128]{2,1,0:T(8,128)(2,1)S(1)}, u32[]{:S(2)}, u32[]{:S(2)}) collective-permute-start(bf16[4,576,128]{2,1,0:T(8,128)(2,1)S(1)} %y_regroup.6), channel_id=1, source_target_pairs={{0,96},{1,97},{2,98},{3,99},{4,100},{5,101},{6,102},{7,103},{8,104... | collective-permute-start | bytes 1769480 | tf_op jit(solution)/shard_map/ppermute | solution.py:71
  23.2 4.6 %collective-permute-done.5.refs_2_ = bf16[2,864,128]{2,1,0:T(8,128)(2,1)S(1)} collective-permute-done((bf16[2,864,128]{2,1,0:T(8,128)(2,1)S(1)}, bf16[2,864,128]{2,1,0:T(8,128)(2,1)S(1)}, u32[]{:S(2)}, u32[]{:S(2)}) %collective-permute-start.5) | collective-permute-done | bytes 442400 | tf_op jit(solution)/shard_map/ppermute | solution.py:71
  27.8 1.2 collective-permute-done.6.refs_3_
  29.0 3.1 %collective-permute-start.14 = (bf16[4,864,128]{2,1,0:T(8,128)(2,1)S(1)}, bf16[4,864,128]{2,1,0:T(8,128)(2,1)S(1)}, u32[]{:S(2)}, u32[]{:S(2)}) collective-permute-start(bf16[4,864,128]{2,1,0:T(8,128)(2,1)S(1)} %y_regroup.7), channel_id=1, source_target_pairs={{0,96},{1,97},{2,98},{3,99},{4,100},{5,101},{6,102},{7,103},{8,104... | collective-permute-start | bytes 2654216 | tf_op jit(solution)/shard_map/ppermute | solution.py:71
  32.2 3.9 %collective-permute-done.3.refs_4_ = bf16[4,576,128]{2,1,0:T(8,128)(2,1)S(1)} collective-permute-done((bf16[4,576,128]{2,1,0:T(8,128)(2,1)S(1)}, bf16[4,576,128]{2,1,0:T(8,128)(2,1)S(1)}, u32[]{:S(2)}, u32[]{:S(2)}) %collective-permute-start.3) | collective-permute-done | bytes 589856 | tf_op jit(solution)/shard_map/ppermute | solution.py:71
  36.0 0.8 cross.3
  36.9 1.0 collective-permute-start.11
  37.8 2.1 %collective-permute-start.12 = (bf16[2,592,128]{2,1,0:T(8,128)(2,1)S(1)}, bf16[2,592,128]{2,1,0:T(8,128)(2,1)S(1)}, u32[]{:S(2)}, u32[]{:S(2)}) collective-permute-start(bf16[2,592,128]{2,1,0:T(8,128)(2,1)S(1)} %get-tuple-element.168), channel_id=1, source_target_pairs={{0,112},{1,113},{2,114},{3,115},{4,116},{5,117},{6,118},{7,119},{8... | collective-permute-start | bytes 909320 | tf_op jit(solution)/shard_map/ppermute | solution.py:71
  40.1 7.0 %collective-permute-done.11.refs_2_ = bf16[2,592,128]{2,1,0:T(8,128)(2,1)S(1)} collective-permute-done((bf16[2,592,128]{2,1,0:T(8,128)(2,1)S(1)}, bf16[2,592,128]{2,1,0:T(8,128)(2,1)S(1)}, u32[]{:S(2)}, u32[]{:S(2)}) %collective-permute-start.11) | collective-permute-done | bytes 303136 | tf_op jit(solution)/shard_map/ppermute | solution.py:71
  47.1 4.2 %collective-permute-done.12.refs_3_ = bf16[2,592,128]{2,1,0:T(8,128)(2,1)S(1)} collective-permute-done((bf16[2,592,128]{2,1,0:T(8,128)(2,1)S(1)}, bf16[2,592,128]{2,1,0:T(8,128)(2,1)S(1)}, u32[]{:S(2)}, u32[]{:S(2)}) %collective-permute-start.12) | collective-permute-done | bytes 303136 | tf_op jit(solution)/shard_map/ppermute | solution.py:71
  51.3 3.1 %collective-permute-start.13 = (bf16[4,592,128]{2,1,0:T(8,128)(2,1)S(1)}, bf16[4,592,128]{2,1,0:T(8,128)(2,1)S(1)}, u32[]{:S(2)}, u32[]{:S(2)}) collective-permute-start(bf16[4,592,128]{2,1,0:T(8,128)(2,1)S(1)} %y_regroup.8), channel_id=1, source_target_pairs={{0,96},{1,97},{2,98},{3,99},{4,100},{5,101},{6,102},{7,103},{8,104... | collective-permute-start | bytes 1818632 | tf_op jit(solution)/shard_map/ppermute | solution.py:71
  54.4 1.1 cross.4
  55.6 0.2 collective-permute-start.20
  55.8 1.9 collective-permute-start.8
  57.7 1.0 collective-permute-start.9
  58.7 8.8 %collective-permute-done.13.refs_4_ = bf16[4,592,128]{2,1,0:T(8,128)(2,1)S(1)} collective-permute-done((bf16[4,592,128]{2,1,0:T(8,128)(2,1)S(1)}, bf16[4,592,128]{2,1,0:T(8,128)(2,1)S(1)}, u32[]{:S(2)}, u32[]{:S(2)}) %collective-permute-start.13) | collective-permute-done | bytes 606240 | tf_op jit(solution)/shard_map/ppermute | solution.py:71
  67.5 0.5 collective-permute-start.21
  68.0 0.8 spread.3
  68.8 9.6 %collective-permute-done.8.refs_2_ = bf16[2,864,128]{2,1,0:T(8,128)(2,1)S(1)} collective-permute-done((bf16[2,864,128]{2,1,0:T(8,128)(2,1)S(1)}, bf16[2,864,128]{2,1,0:T(8,128)(2,1)S(1)}, u32[]{:S(2)}, u32[]{:S(2)}) %collective-permute-start.8) | collective-permute-done | bytes 442400 | tf_op jit(solution)/shard_map/ppermute | solution.py:71
  78.5 0.5 collective-permute-start.15
  79.0 1.5 collective-permute-start.16
  80.5 1.9 collective-permute-start.17
  82.6 2.9 %collective-permute-start.28 = (bf16[4,880,128]{2,1,0:T(8,128)(2,1)S(1)}, bf16[4,880,128]{2,1,0:T(8,128)(2,1)S(1)}, u32[]{:S(2)}, u32[]{:S(2)}) collective-permute-start(bf16[4,880,128]{2,1,0:T(8,128)(2,1)S(1)} %y_regroup.10), channel_id=1, source_target_pairs={{0,96},{1,97},{2,98},{3,99},{4,100},{5,101},{6,102},{7,103},{8,104... | collective-permute-start | bytes 2703368 | tf_op jit(solution)/shard_map/ppermute | solution.py:71
  85.5 2.9 %collective-permute-done.16.refs_1_ = bf16[4,528,128]{2,1,0:T(8,128)(2,1)S(1)} collective-permute-done((bf16[4,528,128]{2,1,0:T(8,128)(2,1)S(1)}, bf16[4,528,128]{2,1,0:T(8,128)(2,1)S(1)}, u32[]{:S(2)}, u32[]{:S(2)}) %collective-permute-start.16) | collective-permute-done | bytes 540704 | tf_op jit(solution)/shard_map/ppermute | solution.py:71
  88.4 7.3 %collective-permute-done.17.refs_2_ = bf16[4,528,128]{2,1,0:T(8,128)(2,1)S(1)} collective-permute-done((bf16[4,528,128]{2,1,0:T(8,128)(2,1)S(1)}, bf16[4,528,128]{2,1,0:T(8,128)(2,1)S(1)}, u32[]{:S(2)}, u32[]{:S(2)}) %collective-permute-start.17) | collective-permute-done | bytes 540704 | tf_op jit(solution)/shard_map/ppermute | solution.py:71
  95.8 4.1 %collective-permute-start.26 = (bf16[4,528,128]{2,1,0:T(8,128)(2,1)S(1)}, bf16[4,528,128]{2,1,0:T(8,128)(2,1)S(1)}, u32[]{:S(2)}, u32[]{:S(2)}) collective-permute-start(bf16[4,528,128]{2,1,0:T(8,128)(2,1)S(1)} %get-tuple-element.213), channel_id=1, source_target_pairs={{0,12},{1,13},{2,14},{3,15},{4,8},{5,9},{6,10},{7,11},{8,4},{9,5},... | collective-permute-start | bytes 1622024 | tf_op jit(solution)/shard_map/ppermute | solution.py:71
  99.9 1.6 collective-permute-start.27
  101.5 1.1 collective-permute-start.25
  102.7 1.1 cross.5
  104.0 0.9 spread.4
  105.0 7.7 %collective-permute-done.26.refs_5_ = bf16[4,528,128]{2,1,0:T(8,128)(2,1)S(1)} collective-permute-done((bf16[4,528,128]{2,1,0:T(8,128)(2,1)S(1)}, bf16[4,528,128]{2,1,0:T(8,128)(2,1)S(1)}, u32[]{:S(2)}, u32[]{:S(2)}) %collective-permute-start.26) | collective-permute-done | bytes 540704 | tf_op jit(solution)/shard_map/ppermute | solution.py:71
  112.9 0.4 collective-permute-done.27.refs_6_
  113.3 1.7 collective-permute-start.32
  115.0 7.3 %collective-permute-done.25.refs_4_ = bf16[4,528,128]{2,1,0:T(8,128)(2,1)S(1)} collective-permute-done((bf16[4,528,128]{2,1,0:T(8,128)(2,1)S(1)}, bf16[4,528,128]{2,1,0:T(8,128)(2,1)S(1)}, u32[]{:S(2)}, u32[]{:S(2)}) %collective-permute-start.25) | collective-permute-done | bytes 540704 | tf_op jit(solution)/shard_map/ppermute | solution.py:71
  122.3 1.1 collective-permute-start.23
  123.4 5.6 %pack.3 = (f32[16,128]{1,0:T(8,128)S(1)}, bf16[1,16,128,2048]{3,2,1,0:T(8,128)(2,1)}) custom-call(s32[144]{0:T(256)S(1)} %copy-done.1, bf16[4,528,128]{2,1,0:T(8,128)(2,1)S(1)} %get-tuple-element.221.refs_0_, bf16[4,528,128]{2,1,0:T(8,128)(2,1)S(1)} %collective-permute-done.16.refs_1_, bf16[4,528,128]{2,1,0:T(8,128)(2,1)S(1)} %collective-permute-done.17.refs_2_, ...), custom_call_target="tpu_custom_call" | custom-call | tf_op jit(solution)/shard_map/pack/pallas_call | solution.py:350
  129.1 6.0 %collective-permute-done.23.refs_2_ = bf16[2,880,128]{2,1,0:T(8,128)(2,1)S(1)} collective-permute-done((bf16[2,880,128]{2,1,0:T(8,128)(2,1)S(1)}, bf16[2,880,128]{2,1,0:T(8,128)(2,1)S(1)}, u32[]{:S(2)}, u32[]{:S(2)}) %collective-permute-start.23) | collective-permute-done | bytes 450592 | tf_op jit(solution)/shard_map/ppermute | solution.py:71
  135.1 0.5 collective-permute-done.24.refs_3_
  135.6 2.4 %collective-permute-start.29 = (bf16[4,880,128]{2,1,0:T(8,128)(2,1)S(1)}, bf16[4,880,128]{2,1,0:T(8,128)(2,1)S(1)}, u32[]{:S(2)}, u32[]{:S(2)}) collective-permute-start(bf16[4,880,128]{2,1,0:T(8,128)(2,1)S(1)} %y_regroup.11), channel_id=1, source_target_pairs={{0,96},{1,97},{2,98},{3,99},{4,100},{5,101},{6,102},{7,103},{8,104... | collective-permute-start | bytes 2703368 | tf_op jit(solution)/shard_map/ppermute | solution.py:71
  138.2 3.2 %collective-permute-start.37 = (bf16[4,784,128]{2,1,0:T(8,128)(2,1)S(1)}, bf16[4,784,128]{2,1,0:T(8,128)(2,1)S(1)}, u32[]{:S(2)}, u32[]{:S(2)}) collective-permute-start(bf16[4,784,128]{2,1,0:T(8,128)(2,1)S(1)} %get-tuple-element.250), channel_id=1, source_target_pairs={{0,12},{1,13},{2,14},{3,15},{4,8},{5,9},{6,10},{7,11},{8,4},{9,5},... | collective-permute-start | bytes 2408456 | tf_op jit(solution)/shard_map/ppermute | solution.py:71
  141.4 1.6 collective-permute-start.38
  143.0 1.1 collective-permute-start.36
  144.1 6.0 %collective-permute-done.29.refs_4_ = bf16[4,880,128]{2,1,0:T(8,128)(2,1)S(1)} collective-permute-done((bf16[4,880,128]{2,1,0:T(8,128)(2,1)S(1)}, bf16[4,880,128]{2,1,0:T(8,128)(2,1)S(1)}, u32[]{:S(2)}, u32[]{:S(2)}) %collective-permute-start.29) | collective-permute-done | bytes 901152 | tf_op jit(solution)/shard_map/ppermute | solution.py:71
  150.1 0.9 spread.5
  151.0 1.2 collective-permute-start.33
  152.2 12.6 %collective-permute-done.37.refs_5_ = bf16[4,784,128]{2,1,0:T(8,128)(2,1)S(1)} collective-permute-done((bf16[4,784,128]{2,1,0:T(8,128)(2,1)S(1)}, bf16[4,784,128]{2,1,0:T(8,128)(2,1)S(1)}, u32[]{:S(2)}, u32[]{:S(2)}) %collective-permute-start.37) | collective-permute-done | bytes 802848 | tf_op jit(solution)/shard_map/ppermute | solution.py:71
  164.8 0.5 collective-permute-start.35
  165.3 8.9 %collective-permute-done.36.refs_4_ = bf16[4,784,128]{2,1,0:T(8,128)(2,1)S(1)} collective-permute-done((bf16[4,784,128]{2,1,0:T(8,128)(2,1)S(1)}, bf16[4,784,128]{2,1,0:T(8,128)(2,1)S(1)}, u32[]{:S(2)}, u32[]{:S(2)}) %collective-permute-start.36) | collective-permute-done | bytes 802848 | tf_op jit(solution)/shard_map/ppermute | solution.py:71
  174.2 5.9 %pack.4 = (f32[16,128]{1,0:T(8,128)S(1)}, bf16[1,16,128,2048]{3,2,1,0:T(8,128)(2,1)}) custom-call(s32[144]{0:T(256)S(1)} %copy-done.1, bf16[4,784,128]{2,1,0:T(8,128)(2,1)S(1)} %get-tuple-element.252.refs_0_, bf16[4,784,128]{2,1,0:T(8,128)(2,1)S(1)} %collective-permute-done.30.refs_1_, ...), custom_call_target="tpu_custom_call", output_to_operand_aliasing={{1}: (9, {})} | custom-call | tf_op jit(solution)/shard_map/pack/pallas_call | solution.py:350
  180.3 3.2 %collective-permute-start.40 = (bf16[4,784,128]{2,1,0:T(8,128)(2,1)S(1)}, bf16[4,784,128]{2,1,0:T(8,128)(2,1)S(1)}, u32[]{:S(2)}, u32[]{:S(2)}) collective-permute-start(bf16[4,784,128]{2,1,0:T(8,128)(2,1)S(1)} %get-tuple-element.266), channel_id=1, source_target_pairs={{0,12},{1,13},{2,14},{3,15},{4,8},{5,9},{6,10},{7,11},{8,4},{9,5},... | collective-permute-start | bytes 2408456 | tf_op jit(solution)/shard_map/ppermute | solution.py:71
  183.5 1.6 collective-permute-start.41
  185.2 1.1 collective-permute-start.39
  186.3 16.1 %collective-permute-done.40.refs_5_ = bf16[4,784,128]{2,1,0:T(8,128)(2,1)S(1)} collective-permute-done((bf16[4,784,128]{2,1,0:T(8,128)(2,1)S(1)}, bf16[4,784,128]{2,1,0:T(8,128)(2,1)S(1)}, u32[]{:S(2)}, u32[]{:S(2)}) %collective-permute-start.40) | collective-permute-done | bytes 802848 | tf_op jit(solution)/shard_map/ppermute | solution.py:71
  202.4 2.7 %collective-permute-done.39.refs_4_ = bf16[4,784,128]{2,1,0:T(8,128)(2,1)S(1)} collective-permute-done((bf16[4,784,128]{2,1,0:T(8,128)(2,1)S(1)}, bf16[4,784,128]{2,1,0:T(8,128)(2,1)S(1)}, u32[]{:S(2)}, u32[]{:S(2)}) %collective-permute-start.39) | collective-permute-done | bytes 802848 | tf_op jit(solution)/shard_map/ppermute | solution.py:71
  205.1 6.5 %pack.5 = (f32[16,128]{1,0:T(8,128)}, bf16[1,16,128,2048]{3,2,1,0:T(8,128)(2,1)}) custom-call(s32[144]{0:T(256)S(1)} %copy-done.1, bf16[4,784,128]{2,1,0:T(8,128)(2,1)S(1)} %get-tuple-element.268.refs_0_, bf16[4,784,128]{2,1,0:T(8,128)(2,1)S(1)} %collective-permute-done.33.refs_1_, ...), custom_call_target="tpu_custom_call", output_to_operand_aliasing={{1}: (9, {})} | custom-call | tf_op jit(solution)/shard_map/pack/pallas_call | solution.py:350
  (45 shorter events, 1.7 us)
Async XLA Ops:
  0.6 2.3 %copy-start = (bf16[2048,1152]{1,0:T(8,128)(2,1)S(1)}, bf16[2048,1152]{1,0:T(8,128)(2,1)}, u32[]{:S(2)}) copy-start(bf16[2048,1152]{1,0:T(8,128)(2,1)} %weight_ref.1) | copy-start | bytes 14155780
  3.0 0.8 copy-start.2
  3.7 64.3 %copy-start.1 = (s32[144]{0:T(256)S(1)}, s32[144]{0:T(256)}, u32[]{:S(2)}) copy-start(s32[144]{0:T(256)} %placement_ref.11) | copy-start | bytes 1732
  9.4 4.0 %collective-permute-start = (bf16[2,576,128]{2,1,0:T(8,128)(2,1)S(1)}, bf16[2,576,128]{2,1,0:T(8,128)(2,1)S(1)}, u32[]{:S(2)}, u32[]{:S(2)}) collective-permute-start(bf16[2,576,128]{2,1,0:T(8,128)(2,1)S(1)} %get-tuple-element.145), channel_id=1, source_target_pairs={{0,16},{1,17},{2,18},{3,19},{4,20},{5,21},{6,22},{7,23},{8,24},{9,... | collective-permute-start | bytes 884744 | tf_op jit(solution)/shard_map/ppermute | solution.py:71
  9.5 8.9 %collective-permute-start.1 = (bf16[2,576,128]{2,1,0:T(8,128)(2,1)S(1)}, bf16[2,576,128]{2,1,0:T(8,128)(2,1)S(1)}, u32[]{:S(2)}, u32[]{:S(2)}) collective-permute-start(bf16[2,576,128]{2,1,0:T(8,128)(2,1)S(1)} %get-tuple-element.146), channel_id=1, source_target_pairs={{0,32},{1,33},{2,34},{3,35},{4,36},{5,37},{6,38},{7,39},{8,40},{9,... | collective-permute-start | bytes 884744 | tf_op jit(solution)/shard_map/ppermute | solution.py:71
  11.2 9.3 %collective-permute-start.2 = (bf16[2,576,128]{2,1,0:T(8,128)(2,1)S(1)}, bf16[2,576,128]{2,1,0:T(8,128)(2,1)S(1)}, u32[]{:S(2)}, u32[]{:S(2)}) collective-permute-start(bf16[2,576,128]{2,1,0:T(8,128)(2,1)S(1)} %get-tuple-element.147), channel_id=1, source_target_pairs={{0,112},{1,113},{2,114},{3,115},{4,116},{5,117},{6,118},{7,119},{8... | collective-permute-start | bytes 884744 | tf_op jit(solution)/shard_map/ppermute | solution.py:71
  12.7 10.5 %collective-permute-start.4 = (bf16[2,864,128]{2,1,0:T(8,128)(2,1)S(1)}, bf16[2,864,128]{2,1,0:T(8,128)(2,1)S(1)}, u32[]{:S(2)}, u32[]{:S(2)}) collective-permute-start(bf16[2,864,128]{2,1,0:T(8,128)(2,1)S(1)} %get-tuple-element.149), channel_id=1, source_target_pairs={{0,16},{1,17},{2,18},{3,19},{4,20},{5,21},{6,22},{7,23},{8,24},{9,... | collective-permute-start | bytes 1327112 | tf_op jit(solution)/shard_map/ppermute | solution.py:71
  12.8 15.0 %collective-permute-start.5 = (bf16[2,864,128]{2,1,0:T(8,128)(2,1)S(1)}, bf16[2,864,128]{2,1,0:T(8,128)(2,1)S(1)}, u32[]{:S(2)}, u32[]{:S(2)}) collective-permute-start(bf16[2,864,128]{2,1,0:T(8,128)(2,1)S(1)} %get-tuple-element.150), channel_id=1, source_target_pairs={{0,32},{1,33},{2,34},{3,35},{4,36},{5,37},{6,38},{7,39},{8,40},{9,... | collective-permute-start | bytes 1327112 | tf_op jit(solution)/shard_map/ppermute | solution.py:71
  13.4 15.6 %collective-permute-start.6 = (bf16[2,864,128]{2,1,0:T(8,128)(2,1)S(1)}, bf16[2,864,128]{2,1,0:T(8,128)(2,1)S(1)}, u32[]{:S(2)}, u32[]{:S(2)}) collective-permute-start(bf16[2,864,128]{2,1,0:T(8,128)(2,1)S(1)} %get-tuple-element.151), channel_id=1, source_target_pairs={{0,112},{1,113},{2,114},{3,115},{4,116},{5,117},{6,118},{7,119},{8... | collective-permute-start | bytes 1327112 | tf_op jit(solution)/shard_map/ppermute | solution.py:71
  20.6 15.5 %collective-permute-start.3 = (bf16[4,576,128]{2,1,0:T(8,128)(2,1)S(1)}, bf16[4,576,128]{2,1,0:T(8,128)(2,1)S(1)}, u32[]{:S(2)}, u32[]{:S(2)}) collective-permute-start(bf16[4,576,128]{2,1,0:T(8,128)(2,1)S(1)} %y_regroup.6), channel_id=1, source_target_pairs={{0,96},{1,97},{2,98},{3,99},{4,100},{5,101},{6,102},{7,103},{8,104... | collective-permute-start | bytes 1769480 | tf_op jit(solution)/shard_map/ppermute | solution.py:71
  29.0 25.4 %collective-permute-start.14 = (bf16[4,864,128]{2,1,0:T(8,128)(2,1)S(1)}, bf16[4,864,128]{2,1,0:T(8,128)(2,1)S(1)}, u32[]{:S(2)}, u32[]{:S(2)}) collective-permute-start(bf16[4,864,128]{2,1,0:T(8,128)(2,1)S(1)} %y_regroup.7), channel_id=1, source_target_pairs={{0,96},{1,97},{2,98},{3,99},{4,100},{5,101},{6,102},{7,103},{8,104... | collective-permute-start | bytes 2654216 | tf_op jit(solution)/shard_map/ppermute | solution.py:71
  36.9 3.2 %collective-permute-start.10 = (bf16[2,592,128]{2,1,0:T(8,128)(2,1)S(1)}, bf16[2,592,128]{2,1,0:T(8,128)(2,1)S(1)}, u32[]{:S(2)}, u32[]{:S(2)}) collective-permute-start(bf16[2,592,128]{2,1,0:T(8,128)(2,1)S(1)} %get-tuple-element.166), channel_id=1, source_target_pairs={{0,16},{1,17},{2,18},{3,19},{4,20},{5,21},{6,22},{7,23},{8,24},{9,... | collective-permute-start | bytes 909320 | tf_op jit(solution)/shard_map/ppermute | solution.py:71
  36.9 10.2 %collective-permute-start.11 = (bf16[2,592,128]{2,1,0:T(8,128)(2,1)S(1)}, bf16[2,592,128]{2,1,0:T(8,128)(2,1)S(1)}, u32[]{:S(2)}, u32[]{:S(2)}) collective-permute-start(bf16[2,592,128]{2,1,0:T(8,128)(2,1)S(1)} %get-tuple-element.167), channel_id=1, source_target_pairs={{0,32},{1,33},{2,34},{3,35},{4,36},{5,37},{6,38},{7,39},{8,40},{9,... | collective-permute-start | bytes 909320 | tf_op jit(solution)/shard_map/ppermute | solution.py:71
  37.8 13.4 %collective-permute-start.12 = (bf16[2,592,128]{2,1,0:T(8,128)(2,1)S(1)}, bf16[2,592,128]{2,1,0:T(8,128)(2,1)S(1)}, u32[]{:S(2)}, u32[]{:S(2)}) collective-permute-start(bf16[2,592,128]{2,1,0:T(8,128)(2,1)S(1)} %get-tuple-element.168), channel_id=1, source_target_pairs={{0,112},{1,113},{2,114},{3,115},{4,116},{5,117},{6,118},{7,119},{8... | collective-permute-start | bytes 909320 | tf_op jit(solution)/shard_map/ppermute | solution.py:71
  40.0 17.7 %collective-permute-start.7 = (bf16[2,864,128]{2,1,0:T(8,128)(2,1)S(1)}, bf16[2,864,128]{2,1,0:T(8,128)(2,1)S(1)}, u32[]{:S(2)}, u32[]{:S(2)}) collective-permute-start(bf16[2,864,128]{2,1,0:T(8,128)(2,1)S(1)} %get-tuple-element.163), channel_id=1, source_target_pairs={{0,16},{1,17},{2,18},{3,19},{4,20},{5,21},{6,22},{7,23},{8,24},{9,... | collective-permute-start | bytes 1327112 | tf_op jit(solution)/shard_map/ppermute | solution.py:71
  51.3 16.2 %collective-permute-start.13 = (bf16[4,592,128]{2,1,0:T(8,128)(2,1)S(1)}, bf16[4,592,128]{2,1,0:T(8,128)(2,1)S(1)}, u32[]{:S(2)}, u32[]{:S(2)}) collective-permute-start(bf16[4,592,128]{2,1,0:T(8,128)(2,1)S(1)} %y_regroup.8), channel_id=1, source_target_pairs={{0,96},{1,97},{2,98},{3,99},{4,100},{5,101},{6,102},{7,103},{8,104... | collective-permute-start | bytes 1818632 | tf_op jit(solution)/shard_map/ppermute | solution.py:71
  55.6 24.9 %collective-permute-start.19 = (bf16[2,880,128]{2,1,0:T(8,128)(2,1)S(1)}, bf16[2,880,128]{2,1,0:T(8,128)(2,1)S(1)}, u32[]{:S(2)}, u32[]{:S(2)}) collective-permute-start(bf16[2,880,128]{2,1,0:T(8,128)(2,1)S(1)} %get-tuple-element.192), channel_id=1, source_target_pairs={{0,16},{1,17},{2,18},{3,19},{4,20},{5,21},{6,22},{7,23},{8,24},{9,... | collective-permute-start | bytes 1351688 | tf_op jit(solution)/shard_map/ppermute | solution.py:71
  55.6 26.8 %collective-permute-start.20 = (bf16[2,880,128]{2,1,0:T(8,128)(2,1)S(1)}, bf16[2,880,128]{2,1,0:T(8,128)(2,1)S(1)}, u32[]{:S(2)}, u32[]{:S(2)}) collective-permute-start(bf16[2,880,128]{2,1,0:T(8,128)(2,1)S(1)} %get-tuple-element.193), channel_id=1, source_target_pairs={{0,32},{1,33},{2,34},{3,35},{4,36},{5,37},{6,38},{7,39},{8,40},{9,... | collective-permute-start | bytes 1351688 | tf_op jit(solution)/shard_map/ppermute | solution.py:71
  55.8 22.6 %collective-permute-start.8 = (bf16[2,864,128]{2,1,0:T(8,128)(2,1)S(1)}, bf16[2,864,128]{2,1,0:T(8,128)(2,1)S(1)}, u32[]{:S(2)}, u32[]{:S(2)}) collective-permute-start(bf16[2,864,128]{2,1,0:T(8,128)(2,1)S(1)} %get-tuple-element.164), channel_id=1, source_target_pairs={{0,32},{1,33},{2,34},{3,35},{4,36},{5,37},{6,38},{7,39},{8,40},{9,... | collective-permute-start | bytes 1327112 | tf_op jit(solution)/shard_map/ppermute | solution.py:71
  57.7 20.7 %collective-permute-start.9 = (bf16[2,864,128]{2,1,0:T(8,128)(2,1)S(1)}, bf16[2,864,128]{2,1,0:T(8,128)(2,1)S(1)}, u32[]{:S(2)}, u32[]{:S(2)}) collective-permute-start(bf16[2,864,128]{2,1,0:T(8,128)(2,1)S(1)} %get-tuple-element.165), channel_id=1, source_target_pairs={{0,112},{1,113},{2,114},{3,115},{4,116},{5,117},{6,118},{7,119},{8... | collective-permute-start | bytes 1327112 | tf_op jit(solution)/shard_map/ppermute | solution.py:71
  67.5 15.0 %collective-permute-start.21 = (bf16[2,880,128]{2,1,0:T(8,128)(2,1)S(1)}, bf16[2,880,128]{2,1,0:T(8,128)(2,1)S(1)}, u32[]{:S(2)}, u32[]{:S(2)}) collective-permute-start(bf16[2,880,128]{2,1,0:T(8,128)(2,1)S(1)} %get-tuple-element.194), channel_id=1, source_target_pairs={{0,112},{1,113},{2,114},{3,115},{4,116},{5,117},{6,118},{7,119},{8... | collective-permute-start | bytes 1351688 | tf_op jit(solution)/shard_map/ppermute | solution.py:71
  78.5 24.1 %collective-permute-start.15 = (bf16[4,864,128]{2,1,0:T(8,128)(2,1)S(1)}, bf16[4,864,128]{2,1,0:T(8,128)(2,1)S(1)}, u32[]{:S(2)}, u32[]{:S(2)}) collective-permute-start(bf16[4,864,128]{2,1,0:T(8,128)(2,1)S(1)} %y_regroup.9), channel_id=1, source_target_pairs={{0,96},{1,97},{2,98},{3,99},{4,100},{5,101},{6,102},{7,103},{8,104... | collective-permute-start | bytes 2654216 | tf_op jit(solution)/shard_map/ppermute | solution.py:71
  79.0 9.4 %collective-permute-start.16 = (bf16[4,528,128]{2,1,0:T(8,128)(2,1)S(1)}, bf16[4,528,128]{2,1,0:T(8,128)(2,1)S(1)}, u32[]{:S(2)}, u32[]{:S(2)}) collective-permute-start(bf16[4,528,128]{2,1,0:T(8,128)(2,1)S(1)} %get-tuple-element.189), channel_id=1, source_target_pairs={{0,1},{1,0},{2,3},{3,2},{4,5},{5,4},{6,7},{7,6},{8,9},{9,8},{10,11... | collective-permute-start | bytes 1622024 | tf_op jit(solution)/shard_map/ppermute | solution.py:71
  80.5 15.2 %collective-permute-start.17 = (bf16[4,528,128]{2,1,0:T(8,128)(2,1)S(1)}, bf16[4,528,128]{2,1,0:T(8,128)(2,1)S(1)}, u32[]{:S(2)}, u32[]{:S(2)}) collective-permute-start(bf16[4,528,128]{2,1,0:T(8,128)(2,1)S(1)} %get-tuple-element.190), channel_id=1, source_target_pairs={{0,4},{1,5},{2,6},{3,7},{4,0},{5,1},{6,2},{7,3},{8,12},{9,13},{10,... | collective-permute-start | bytes 1622024 | tf_op jit(solution)/shard_map/ppermute | solution.py:71
  82.4 13.2 %collective-permute-start.18 = (bf16[4,528,128]{2,1,0:T(8,128)(2,1)S(1)}, bf16[4,528,128]{2,1,0:T(8,128)(2,1)S(1)}, u32[]{:S(2)}, u32[]{:S(2)}) collective-permute-start(bf16[4,528,128]{2,1,0:T(8,128)(2,1)S(1)} %get-tuple-element.191), channel_id=1, source_target_pairs={{0,5},{1,4},{2,7},{3,6},{4,1},{5,0},{6,3},{7,2},{8,13},{9,12},{10,... | collective-permute-start | bytes 1622024 | tf_op jit(solution)/shard_map/ppermute | solution.py:71
  82.6 21.4 %collective-permute-start.28 = (bf16[4,880,128]{2,1,0:T(8,128)(2,1)S(1)}, bf16[4,880,128]{2,1,0:T(8,128)(2,1)S(1)}, u32[]{:S(2)}, u32[]{:S(2)}) collective-permute-start(bf16[4,880,128]{2,1,0:T(8,128)(2,1)S(1)} %y_regroup.10), channel_id=1, source_target_pairs={{0,96},{1,97},{2,98},{3,99},{4,100},{5,101},{6,102},{7,103},{8,104... | collective-permute-start | bytes 2703368 | tf_op jit(solution)/shard_map/ppermute | solution.py:71
  95.8 16.9 %collective-permute-start.26 = (bf16[4,528,128]{2,1,0:T(8,128)(2,1)S(1)}, bf16[4,528,128]{2,1,0:T(8,128)(2,1)S(1)}, u32[]{:S(2)}, u32[]{:S(2)}) collective-permute-start(bf16[4,528,128]{2,1,0:T(8,128)(2,1)S(1)} %get-tuple-element.213), channel_id=1, source_target_pairs={{0,12},{1,13},{2,14},{3,15},{4,8},{5,9},{6,10},{7,11},{8,4},{9,5},... | collective-permute-start | bytes 1622024 | tf_op jit(solution)/shard_map/ppermute | solution.py:71
  99.9 13.4 %collective-permute-start.27 = (bf16[4,528,128]{2,1,0:T(8,128)(2,1)S(1)}, bf16[4,528,128]{2,1,0:T(8,128)(2,1)S(1)}, u32[]{:S(2)}, u32[]{:S(2)}) collective-permute-start(bf16[4,528,128]{2,1,0:T(8,128)(2,1)S(1)} %get-tuple-element.214), channel_id=1, source_target_pairs={{0,15},{1,14},{2,13},{3,12},{4,11},{5,10},{6,9},{7,8},{8,7},{9,6},... | collective-permute-start | bytes 1622024 | tf_op jit(solution)/shard_map/ppermute | solution.py:71
  101.5 20.8 %collective-permute-start.25 = (bf16[4,528,128]{2,1,0:T(8,128)(2,1)S(1)}, bf16[4,528,128]{2,1,0:T(8,128)(2,1)S(1)}, u32[]{:S(2)}, u32[]{:S(2)}) collective-permute-start(bf16[4,528,128]{2,1,0:T(8,128)(2,1)S(1)} %get-tuple-element.203), channel_id=1, source_target_pairs={{0,3},{1,2},{2,1},{3,0},{4,7},{5,6},{6,5},{7,4},{8,11},{9,10},{10,... | collective-permute-start | bytes 1622024 | tf_op jit(solution)/shard_map/ppermute | solution.py:71
  103.8 19.7 %collective-permute-start.22 = (bf16[2,880,128]{2,1,0:T(8,128)(2,1)S(1)}, bf16[2,880,128]{2,1,0:T(8,128)(2,1)S(1)}, u32[]{:S(2)}, u32[]{:S(2)}) collective-permute-start(bf16[2,880,128]{2,1,0:T(8,128)(2,1)S(1)} %get-tuple-element.210), channel_id=1, source_target_pairs={{0,16},{1,17},{2,18},{3,19},{4,20},{5,21},{6,22},{7,23},{8,24},{9,... | collective-permute-start | bytes 1351688 | tf_op jit(solution)/shard_map/ppermute | solution.py:71
  104.9 33.1 %collective-permute-start.30 = (bf16[4,784,128]{2,1,0:T(8,128)(2,1)S(1)}, bf16[4,784,128]{2,1,0:T(8,128)(2,1)S(1)}, u32[]{:S(2)}, u32[]{:S(2)}) collective-permute-start(bf16[4,784,128]{2,1,0:T(8,128)(2,1)S(1)} %get-tuple-element.233), channel_id=1, source_target_pairs={{0,1},{1,0},{2,3},{3,2},{4,5},{5,4},{6,7},{7,6},{8,9},{9,8},{10,11... | collective-permute-start | bytes 2408456 | tf_op jit(solution)/shard_map/ppermute | solution.py:71
  112.7 25.3 %collective-permute-start.31 = (bf16[4,784,128]{2,1,0:T(8,128)(2,1)S(1)}, bf16[4,784,128]{2,1,0:T(8,128)(2,1)S(1)}, u32[]{:S(2)}, u32[]{:S(2)}) collective-permute-start(bf16[4,784,128]{2,1,0:T(8,128)(2,1)S(1)} %get-tuple-element.234), channel_id=1, source_target_pairs={{0,4},{1,5},{2,6},{3,7},{4,0},{5,1},{6,2},{7,3},{8,12},{9,13},{10,... | collective-permute-start | bytes 2408456 | tf_op jit(solution)/shard_map/ppermute | solution.py:71
  113.3 24.7 %collective-permute-start.32 = (bf16[4,784,128]{2,1,0:T(8,128)(2,1)S(1)}, bf16[4,784,128]{2,1,0:T(8,128)(2,1)S(1)}, u32[]{:S(2)}, u32[]{:S(2)}) collective-permute-start(bf16[4,784,128]{2,1,0:T(8,128)(2,1)S(1)} %get-tuple-element.235), channel_id=1, source_target_pairs={{0,5},{1,4},{2,7},{3,6},{4,1},{5,0},{6,3},{7,2},{8,13},{9,12},{10,... | collective-permute-start | bytes 2408456 | tf_op jit(solution)/shard_map/ppermute | solution.py:71
  122.3 12.7 %collective-permute-start.23 = (bf16[2,880,128]{2,1,0:T(8,128)(2,1)S(1)}, bf16[2,880,128]{2,1,0:T(8,128)(2,1)S(1)}, u32[]{:S(2)}, u32[]{:S(2)}) collective-permute-start(bf16[2,880,128]{2,1,0:T(8,128)(2,1)S(1)} %get-tuple-element.211), channel_id=1, source_target_pairs={{0,32},{1,33},{2,34},{3,35},{4,36},{5,37},{6,38},{7,39},{8,40},{9,... | collective-permute-start | bytes 1351688 | tf_op jit(solution)/shard_map/ppermute | solution.py:71
  123.4 12.1 %collective-permute-start.24 = (bf16[2,880,128]{2,1,0:T(8,128)(2,1)S(1)}, bf16[2,880,128]{2,1,0:T(8,128)(2,1)S(1)}, u32[]{:S(2)}, u32[]{:S(2)}) collective-permute-start(bf16[2,880,128]{2,1,0:T(8,128)(2,1)S(1)} %get-tuple-element.212), channel_id=1, source_target_pairs={{0,112},{1,113},{2,114},{3,115},{4,116},{5,117},{6,118},{7,119},{8... | collective-permute-start | bytes 1351688 | tf_op jit(solution)/shard_map/ppermute | solution.py:71
  135.6 14.5 %collective-permute-start.29 = (bf16[4,880,128]{2,1,0:T(8,128)(2,1)S(1)}, bf16[4,880,128]{2,1,0:T(8,128)(2,1)S(1)}, u32[]{:S(2)}, u32[]{:S(2)}) collective-permute-start(bf16[4,880,128]{2,1,0:T(8,128)(2,1)S(1)} %y_regroup.11), channel_id=1, source_target_pairs={{0,96},{1,97},{2,98},{3,99},{4,100},{5,101},{6,102},{7,103},{8,104... | collective-permute-start | bytes 2703368 | tf_op jit(solution)/shard_map/ppermute | solution.py:71
  138.2 26.7 %collective-permute-start.37 = (bf16[4,784,128]{2,1,0:T(8,128)(2,1)S(1)}, bf16[4,784,128]{2,1,0:T(8,128)(2,1)S(1)}, u32[]{:S(2)}, u32[]{:S(2)}) collective-permute-start(bf16[4,784,128]{2,1,0:T(8,128)(2,1)S(1)} %get-tuple-element.250), channel_id=1, source_target_pairs={{0,12},{1,13},{2,14},{3,15},{4,8},{5,9},{6,10},{7,11},{8,4},{9,5},... | collective-permute-start | bytes 2408456 | tf_op jit(solution)/shard_map/ppermute | solution.py:71
  141.4 23.9 %collective-permute-start.38 = (bf16[4,784,128]{2,1,0:T(8,128)(2,1)S(1)}, bf16[4,784,128]{2,1,0:T(8,128)(2,1)S(1)}, u32[]{:S(2)}, u32[]{:S(2)}) collective-permute-start(bf16[4,784,128]{2,1,0:T(8,128)(2,1)S(1)} %get-tuple-element.251), channel_id=1, source_target_pairs={{0,15},{1,14},{2,13},{3,12},{4,11},{5,10},{6,9},{7,8},{8,7},{9,6},... | collective-permute-start | bytes 2408456 | tf_op jit(solution)/shard_map/ppermute | solution.py:71
  143.0 31.2 %collective-permute-start.36 = (bf16[4,784,128]{2,1,0:T(8,128)(2,1)S(1)}, bf16[4,784,128]{2,1,0:T(8,128)(2,1)S(1)}, u32[]{:S(2)}, u32[]{:S(2)}) collective-permute-start(bf16[4,784,128]{2,1,0:T(8,128)(2,1)S(1)} %get-tuple-element.240), channel_id=1, source_target_pairs={{0,3},{1,2},{2,1},{3,0},{4,7},{5,6},{6,5},{7,4},{8,11},{9,10},{10,... | collective-permute-start | bytes 2408456 | tf_op jit(solution)/shard_map/ppermute | solution.py:71
  151.0 29.1 %collective-permute-start.33 = (bf16[4,784,128]{2,1,0:T(8,128)(2,1)S(1)}, bf16[4,784,128]{2,1,0:T(8,128)(2,1)S(1)}, u32[]{:S(2)}, u32[]{:S(2)}) collective-permute-start(bf16[4,784,128]{2,1,0:T(8,128)(2,1)S(1)} %get-tuple-element.247), channel_id=1, source_target_pairs={{0,1},{1,0},{2,3},{3,2},{4,5},{5,4},{6,7},{7,6},{8,9},{9,8},{10,11... | collective-permute-start | bytes 2408456 | tf_op jit(solution)/shard_map/ppermute | solution.py:71
  152.2 27.9 %collective-permute-start.34 = (bf16[4,784,128]{2,1,0:T(8,128)(2,1)S(1)}, bf16[4,784,128]{2,1,0:T(8,128)(2,1)S(1)}, u32[]{:S(2)}, u32[]{:S(2)}) collective-permute-start(bf16[4,784,128]{2,1,0:T(8,128)(2,1)S(1)} %get-tuple-element.248), channel_id=1, source_target_pairs={{0,4},{1,5},{2,6},{3,7},{4,0},{5,1},{6,2},{7,3},{8,12},{9,13},{10,... | collective-permute-start | bytes 2408456 | tf_op jit(solution)/shard_map/ppermute | solution.py:71
  164.8 15.3 %collective-permute-start.35 = (bf16[4,784,128]{2,1,0:T(8,128)(2,1)S(1)}, bf16[4,784,128]{2,1,0:T(8,128)(2,1)S(1)}, u32[]{:S(2)}, u32[]{:S(2)}) collective-permute-start(bf16[4,784,128]{2,1,0:T(8,128)(2,1)S(1)} %get-tuple-element.249), channel_id=1, source_target_pairs={{0,5},{1,4},{2,7},{3,6},{4,1},{5,0},{6,3},{7,2},{8,13},{9,12},{10,... | collective-permute-start | bytes 2408456 | tf_op jit(solution)/shard_map/ppermute | solution.py:71
  180.3 22.1 %collective-permute-start.40 = (bf16[4,784,128]{2,1,0:T(8,128)(2,1)S(1)}, bf16[4,784,128]{2,1,0:T(8,128)(2,1)S(1)}, u32[]{:S(2)}, u32[]{:S(2)}) collective-permute-start(bf16[4,784,128]{2,1,0:T(8,128)(2,1)S(1)} %get-tuple-element.266), channel_id=1, source_target_pairs={{0,12},{1,13},{2,14},{3,15},{4,8},{5,9},{6,10},{7,11},{8,4},{9,5},... | collective-permute-start | bytes 2408456 | tf_op jit(solution)/shard_map/ppermute | solution.py:71
  183.5 18.8 %collective-permute-start.41 = (bf16[4,784,128]{2,1,0:T(8,128)(2,1)S(1)}, bf16[4,784,128]{2,1,0:T(8,128)(2,1)S(1)}, u32[]{:S(2)}, u32[]{:S(2)}) collective-permute-start(bf16[4,784,128]{2,1,0:T(8,128)(2,1)S(1)} %get-tuple-element.267), channel_id=1, source_target_pairs={{0,15},{1,14},{2,13},{3,12},{4,11},{5,10},{6,9},{7,8},{8,7},{9,6},... | collective-permute-start | bytes 2408456 | tf_op jit(solution)/shard_map/ppermute | solution.py:71
  185.2 19.9 %collective-permute-start.39 = (bf16[4,784,128]{2,1,0:T(8,128)(2,1)S(1)}, bf16[4,784,128]{2,1,0:T(8,128)(2,1)S(1)}, u32[]{:S(2)}, u32[]{:S(2)}) collective-permute-start(bf16[4,784,128]{2,1,0:T(8,128)(2,1)S(1)} %get-tuple-element.265), channel_id=1, source_target_pairs={{0,3},{1,2},{2,1},{3,0},{4,7},{5,6},{6,5},{7,4},{8,11},{9,10},{10,... | collective-permute-start | bytes 2408456 | tf_op jit(solution)/shard_map/ppermute | solution.py:71

commit v6 on v5

--- a/solution.py
+++ b/solution.py
@@ -10,29 +10,36 @@
 
 HEAD_DIM = 128
 HAD = 128
-CHUNKS = ((0, 32), (32, 48), (80, 48))
+CHUNKS = ((0, 32), (32, 32), (64, 32), (96, 32))
 ORDER = (
     ("start", 0),
     ("start", 1),
+    ("start", 2),
     ("y_regroup", 0),
+    ("start", 3),
+    ("cross", 0),
     ("y_regroup", 1),
-    ("cross", 0),
-    ("start", 2),
     ("y_regroup", 0),
     ("cross", 1),
     ("spread", 0),
+    ("y_regroup", 1),
     ("y_regroup", 2),
-    ("y_regroup", 1),
     ("regroup", 0),
+    ("spread", 1),
+    ("y_regroup", 3),
     ("cross", 2),
-    ("spread", 1),
+    ("cross", 3),
+    ("y_regroup", 2),
     ("pack", 0),
-    ("y_regroup", 2),
     ("regroup", 1),
+    ("y_regroup", 3),
     ("spread", 2),
+    ("spread", 3),
     ("pack", 1),
     ("regroup", 2),
+    ("regroup", 3),
     ("pack", 2),
+    ("pack", 3),
 )
 TAIL = 16
 VMEM_BYTES = 12 * 1024 * 1024
@@ -247,23 +254,28 @@
     core = group & 1
     pair = jnp.where(core == 0, 2, 6)
     offsets = (0, 1, pair, pair ^ 1, pair ^ 4, pair ^ 5, 4, 5)
+    blocks, rows = [], []
     for origin in range(owners):
         i, j = origin % 4, origin // 4
         in_ref, index = (in_refs[3 + j], i) if j else (in_refs[i], 0)
         source = me ^ pairing_offset(core, 0, i) ^ pairing_offset(core, 1, j)
+        live = live_ref[source] != 0
+        slot = jnp.where(live, slot_ref[source], count + source - slot_ref[source])
+        tail = in_ref[index, 16 * chans :, :].astype(jnp.float32)
+        row = jnp.where((lane < chans) & live, join_parts(tail, chans), 0.0)
+        rows.append(jnp.where(live, 1.0 / (row[:1, :] + 1e-06), 0.0))
+        row = (pltpu.roll(row, first, 1) if first else row)[:1, :]
+        if has_past:
+            row = row + past_ref[pl.ds(slot, 1), :]
+        peak_ref[pl.ds(slot, 1), :] = row
+        blocks.append((in_ref, index, slot))
+    rows.append(jnp.zeros((HAD - owners, HAD), jnp.float32))
+    scales = jnp.concatenate(rows, axis=0).T
+    for origin, (in_ref, index, slot) in enumerate(blocks):
         part = origin % depth
         if copies[part] is not None:
             copies[part].wait()
-        live = live_ref[source] != 0
-        slot = jnp.where(live, slot_ref[source], count + source - slot_ref[source])
-        tail = in_ref[index, 16 * chans :, :].astype(jnp.float32)
-        row = jnp.where((lane < chans) & live, join_parts(tail, chans), 0.0)[:1, :]
-        scale = jnp.where(live, 1.0 / (row + 1e-06), 0.0)
-        scale = jnp.broadcast_to(scale, (HEAD_DIM, HAD)).T[:chans, :]
-        row = pltpu.roll(jnp.broadcast_to(row, (8, HAD)), first, 1)[:1, :] if first else row
-        if has_past:
-            row = row + past_ref[pl.ds(slot, 1), :]
-        peak_ref[pl.ds(slot, 1), :] = row
+        scale = scales[:chans, origin : origin + 1]
         for s in range(8):
             for e in range(2):
                 start = (s * 2 + e) * chans

time: 212 us -> 229 us (1.080)
  the two profiles are of different devices: /device:TPU:0 before, /device:TPU:30 now
where the time goes in v6:
time: 229 us
  waiting for transfers between devices  120 us (52%)
  starting transfers between devices  69.4 us (30%)
  Pallas kernels  35.1 us (15%)
  local copies, waits for them, and re-layouts  3.09 us (1%)
    ppermute x56, waiting for transfers between devices, hop(): return lax.ppermute(array, BOTH, pairs)  120 us
    ppermute x56, starting transfers between devices, hop(): return lax.ppermute(array, BOTH, pairs)  69.4 us
    pallas_call x4, Pallas kernels, per_device(): pl.pallas_call(functools.partial(pack_kernel, owners, heads, chunk, bool(...  22.1 us
    pallas_call x20, Pallas kernels, call(): pl.pallas_call(kernel, in_specs=[smem_spec] * table + [vmem_spec] * (len(...  7.27 us
    pallas_call x1, Pallas kernels, per_device(): pl.pallas_call(functools.partial(local_turn_kernel, rows_a), grid=(heads,...  5.8 us
  transfers between devices with their start and end apart: 56, of which 22 were waited for; matrix products, arithmetic and copies ran while one was open for 0% of the time, Pallas kernels for 10%

profile of v6, /device:TPU:30, one launch (start us, length us, event | category | flops | bytes accessed | tf_op | source)
XLA Modules:
  0.0 229.2 jit_solution(10916256507230593765)
XLA Ops:
  0.6 2.3 %copy-done = bf16[2048,1152]{1,0:T(8,128)(2,1)S(1)} copy-done((bf16[2048,1152]{1,0:T(8,128)(2,1)S(1)}, bf16[2048,1152]{1,0:T(8,128)(2,1)}, u32[]{:S(2)}) %copy-start) | copy-done | bytes 4718616
  3.0 0.8 copy-done.2
  3.7 5.8 %local_turn.1 = (bf16[2,576,128]{2,1,0:T(8,128)(2,1)S(1)}, bf16[2,576,128]{2,1,0:T(8,128)(2,1)S(1)}, bf16[2,576,128]{2,1,0:T(8,128)(2,1)S(1)}, bf16[2,576,128]{2...) custom-call(bf16[2048,1152]{1,0:T(8,128)(2,1)S(1)} %copy-done, ...), custom_call_target="tpu_custom_call" | custom-call | tf_op jit(solution)/shard_map/local_turn/pallas_call | solution.py:315
  9.6 0.8 collective-permute-start.1
  10.5 2.2 collective-permute-start.2
  12.7 6.7 %collective-permute-done.1.refs_2_ = bf16[2,576,128]{2,1,0:T(8,128)(2,1)S(1)} collective-permute-done((bf16[2,576,128]{2,1,0:T(8,128)(2,1)S(1)}, bf16[2,576,128]{2,1,0:T(8,128)(2,1)S(1)}, u32[]{:S(2)}, u32[]{:S(2)}) %collective-permute-start.1) | collective-permute-done | bytes 294944 | tf_op jit(solution)/shard_map/ppermute | solution.py:78
  20.3 1.7 collective-permute-start.7
  21.9 1.2 collective-permute-start.8
  23.1 10.7 %collective-permute-done.9.refs_4_ = bf16[4,576,128]{2,1,0:T(8,128)(2,1)S(1)} collective-permute-done((bf16[4,576,128]{2,1,0:T(8,128)(2,1)S(1)}, bf16[4,576,128]{2,1,0:T(8,128)(2,1)S(1)}, u32[]{:S(2)}, u32[]{:S(2)}) %collective-permute-start.9) | collective-permute-done | bytes 589856 | tf_op jit(solution)/shard_map/ppermute | solution.py:78
  33.8 0.8 cross.4
  34.7 3.0 %collective-permute-start.13 = (bf16[2,592,128]{2,1,0:T(8,128)(2,1)S(1)}, bf16[2,592,128]{2,1,0:T(8,128)(2,1)S(1)}, u32[]{:S(2)}, u32[]{:S(2)}) collective-permute-start(bf16[2,592,128]{2,1,0:T(8,128)(2,1)S(1)} %get-tuple-element.214), channel_id=1, source_target_pairs={{0,112},{1,113},{2,114},{3,115},{4,116},{5,117},{6,118},{7,119},{8... | collective-permute-start | bytes 909320 | tf_op jit(solution)/shard_map/ppermute | solution.py:78
  37.8 0.5 collective-permute-start.10
  38.2 6.5 %collective-permute-done.12.refs_2_ = bf16[2,592,128]{2,1,0:T(8,128)(2,1)S(1)} collective-permute-done((bf16[2,592,128]{2,1,0:T(8,128)(2,1)S(1)}, bf16[2,592,128]{2,1,0:T(8,128)(2,1)S(1)}, u32[]{:S(2)}, u32[]{:S(2)}) %collective-permute-start.12) | collective-permute-done | bytes 303136 | tf_op jit(solution)/shard_map/ppermute | solution.py:78
  44.7 0.5 collective-permute-start.17
  45.5 6.3 %collective-permute-done.10.refs_4_ = bf16[4,576,128]{2,1,0:T(8,128)(2,1)S(1)} collective-permute-done((bf16[4,576,128]{2,1,0:T(8,128)(2,1)S(1)}, bf16[4,576,128]{2,1,0:T(8,128)(2,1)S(1)}, u32[]{:S(2)}, u32[]{:S(2)}) %collective-permute-start.10) | collective-permute-done | bytes 589856 | tf_op jit(solution)/shard_map/ppermute | solution.py:78
  51.8 0.8 cross.5
  52.7 3.0 %collective-permute-start.16 = (bf16[2,592,128]{2,1,0:T(8,128)(2,1)S(1)}, bf16[2,592,128]{2,1,0:T(8,128)(2,1)S(1)}, u32[]{:S(2)}, u32[]{:S(2)}) collective-permute-start(bf16[2,592,128]{2,1,0:T(8,128)(2,1)S(1)} %get-tuple-element.227), channel_id=1, source_target_pairs={{0,112},{1,113},{2,114},{3,115},{4,116},{5,117},{6,118},{7,119},{8... | collective-permute-start | bytes 909320 | tf_op jit(solution)/shard_map/ppermute | solution.py:78
  55.7 3.9 %collective-permute-done.17.refs_4_ = bf16[4,592,128]{2,1,0:T(8,128)(2,1)S(1)} collective-permute-done((bf16[4,592,128]{2,1,0:T(8,128)(2,1)S(1)}, bf16[4,592,128]{2,1,0:T(8,128)(2,1)S(1)}, u32[]{:S(2)}, u32[]{:S(2)}) %collective-permute-start.17) | collective-permute-done | bytes 606240 | tf_op jit(solution)/shard_map/ppermute | solution.py:78
  59.5 0.8 spread.4
  60.4 0.9 collective-permute-start.19
  61.3 1.6 collective-permute-done.15.refs_2_
  62.8 1.9 collective-permute-start.20
  64.7 1.8 collective-permute-start.21
  66.6 2.5 %collective-permute-done.23.refs_2_ = bf16[2,576,128]{2,1,0:T(8,128)(2,1)S(1)} collective-permute-done((bf16[2,576,128]{2,1,0:T(8,128)(2,1)S(1)}, bf16[2,576,128]{2,1,0:T(8,128)(2,1)S(1)}, u32[]{:S(2)}, u32[]{:S(2)}) %collective-permute-start.23) | collective-permute-done | bytes 294944 | tf_op jit(solution)/shard_map/ppermute | solution.py:78
  70.0 2.5 %collective-permute-start.26 = (bf16[4,576,128]{2,1,0:T(8,128)(2,1)S(1)}, bf16[4,576,128]{2,1,0:T(8,128)(2,1)S(1)}, u32[]{:S(2)}, u32[]{:S(2)}) collective-permute-start(bf16[4,576,128]{2,1,0:T(8,128)(2,1)S(1)} %y_regroup.12), channel_id=1, source_target_pairs={{0,96},{1,97},{2,98},{3,99},{4,100},{5,101},{6,102},{7,103},{8,104... | collective-permute-start | bytes 1769480 | tf_op jit(solution)/shard_map/ppermute | solution.py:78
  72.5 5.5 %collective-permute-done.20.refs_2_ = bf16[4,528,128]{2,1,0:T(8,128)(2,1)S(1)} collective-permute-done((bf16[4,528,128]{2,1,0:T(8,128)(2,1)S(1)}, bf16[4,528,128]{2,1,0:T(8,128)(2,1)S(1)}, u32[]{:S(2)}, u32[]{:S(2)}) %collective-permute-start.20) | collective-permute-done | bytes 540704 | tf_op jit(solution)/shard_map/ppermute | solution.py:78
  78.0 4.5 %collective-permute-start.5 = (bf16[2,576,128]{2,1,0:T(8,128)(2,1)S(1)}, bf16[2,576,128]{2,1,0:T(8,128)(2,1)S(1)}, u32[]{:S(2)}, u32[]{:S(2)}) collective-permute-start(bf16[2,576,128]{2,1,0:T(8,128)(2,1)S(1)} %get-tuple-element.197), channel_id=1, source_target_pairs={{0,112},{1,113},{2,114},{3,115},{4,116},{5,117},{6,118},{7,119},{8... | collective-permute-start | bytes 884744 | tf_op jit(solution)/shard_map/ppermute | solution.py:78
  82.6 0.8 spread.5
  83.4 4.5 %collective-permute-done.4.refs_2_ = bf16[2,576,128]{2,1,0:T(8,128)(2,1)S(1)} collective-permute-done((bf16[2,576,128]{2,1,0:T(8,128)(2,1)S(1)}, bf16[2,576,128]{2,1,0:T(8,128)(2,1)S(1)}, u32[]{:S(2)}, u32[]{:S(2)}) %collective-permute-start.4) | collective-permute-done | bytes 294944 | tf_op jit(solution)/shard_map/ppermute | solution.py:78
  87.9 3.5 %collective-permute-done.5.refs_3_ = bf16[2,576,128]{2,1,0:T(8,128)(2,1)S(1)} collective-permute-done((bf16[2,576,128]{2,1,0:T(8,128)(2,1)S(1)}, bf16[2,576,128]{2,1,0:T(8,128)(2,1)S(1)}, u32[]{:S(2)}, u32[]{:S(2)}) %collective-permute-start.5) | collective-permute-done | bytes 294944 | tf_op jit(solution)/shard_map/ppermute | solution.py:78
  91.4 0.8 cross.6
  92.2 1.7 collective-permute-start.36
  93.9 2.7 %collective-permute-start.38 = (bf16[2,592,128]{2,1,0:T(8,128)(2,1)S(1)}, bf16[2,592,128]{2,1,0:T(8,128)(2,1)S(1)}, u32[]{:S(2)}, u32[]{:S(2)}) collective-permute-start(bf16[2,592,128]{2,1,0:T(8,128)(2,1)S(1)} %get-tuple-element.286), channel_id=1, source_target_pairs={{0,112},{1,113},{2,114},{3,115},{4,116},{5,117},{6,118},{7,119},{8... | collective-permute-start | bytes 909320 | tf_op jit(solution)/shard_map/ppermute | solution.py:78
  97.0 4.0 %collective-permute-start.34 = (bf16[4,528,128]{2,1,0:T(8,128)(2,1)S(1)}, bf16[4,528,128]{2,1,0:T(8,128)(2,1)S(1)}, u32[]{:S(2)}, u32[]{:S(2)}) collective-permute-start(bf16[4,528,128]{2,1,0:T(8,128)(2,1)S(1)} %get-tuple-element.282), channel_id=1, source_target_pairs={{0,12},{1,13},{2,14},{3,15},{4,8},{5,9},{6,10},{7,11},{8,4},{9,5},... | collective-permute-start | bytes 1622024 | tf_op jit(solution)/shard_map/ppermute | solution.py:78
  101.0 0.9 collective-permute-start.35
  101.9 2.0 collective-permute-done.37.refs_2_
  103.9 1.4 collective-permute-start.33
  105.4 8.4 %collective-permute-done.34.refs_5_ = bf16[4,528,128]{2,1,0:T(8,128)(2,1)S(1)} collective-permute-done((bf16[4,528,128]{2,1,0:T(8,128)(2,1)S(1)}, bf16[4,528,128]{2,1,0:T(8,128)(2,1)S(1)}, u32[]{:S(2)}, u32[]{:S(2)}) %collective-permute-start.34) | collective-permute-done | bytes 540704 | tf_op jit(solution)/shard_map/ppermute | solution.py:78
  114.0 2.3 %collective-permute-start.32 = (bf16[4,528,128]{2,1,0:T(8,128)(2,1)S(1)}, bf16[4,528,128]{2,1,0:T(8,128)(2,1)S(1)}, u32[]{:S(2)}, u32[]{:S(2)}) collective-permute-start(bf16[4,528,128]{2,1,0:T(8,128)(2,1)S(1)} %get-tuple-element.281), channel_id=1, source_target_pairs={{0,5},{1,4},{2,7},{3,6},{4,1},{5,0},{6,3},{7,2},{8,13},{9,12},{10,... | collective-permute-start | bytes 1622024 | tf_op jit(solution)/shard_map/ppermute | solution.py:78
  116.3 0.8 cross.7
  117.2 8.2 %collective-permute-done.33.refs_4_ = bf16[4,528,128]{2,1,0:T(8,128)(2,1)S(1)} collective-permute-done((bf16[4,528,128]{2,1,0:T(8,128)(2,1)S(1)}, bf16[4,528,128]{2,1,0:T(8,128)(2,1)S(1)}, u32[]{:S(2)}, u32[]{:S(2)}) %collective-permute-start.33) | collective-permute-done | bytes 540704 | tf_op jit(solution)/shard_map/ppermute | solution.py:78
  125.5 5.4 %pack.4 = (f32[16,128]{1,0:T(8,128)S(1)}, bf16[1,16,128,2048]{3,2,1,0:T(8,128)(2,1)}) custom-call(s32[144]{0:T(256)S(1)} %copy-done.1, bf16[4,528,128]{2,1,0:T(8,128)(2,1)S(1)} %get-tuple-element.291.refs_0_, bf16[4,528,128]{2,1,0:T(8,128)(2,1)S(1)} %collective-permute-done.19.refs_1_, bf16[4,528,128]{2,1,0:T(8,128)(2,1)S(1)} %collective-permute-done.20.refs_2_, ...), custom_call_target="tpu_custom_call" | custom-call | tf_op jit(solution)/shard_map/pack/pallas_call | solution.py:362
  130.8 5.7 %collective-permute-start.40 = (bf16[4,592,128]{2,1,0:T(8,128)(2,1)S(1)}, bf16[4,592,128]{2,1,0:T(8,128)(2,1)S(1)}, u32[]{:S(2)}, u32[]{:S(2)}) collective-permute-start(bf16[4,592,128]{2,1,0:T(8,128)(2,1)S(1)} %y_regroup.14), channel_id=1, source_target_pairs={{0,96},{1,97},{2,98},{3,99},{4,100},{5,101},{6,102},{7,103},{8,104... | collective-permute-start | bytes 1818632 | tf_op jit(solution)/shard_map/ppermute | solution.py:78
  136.7 3.9 %collective-permute-start.39 = (bf16[4,592,128]{2,1,0:T(8,128)(2,1)S(1)}, bf16[4,592,128]{2,1,0:T(8,128)(2,1)S(1)}, u32[]{:S(2)}, u32[]{:S(2)}) collective-permute-start(bf16[4,592,128]{2,1,0:T(8,128)(2,1)S(1)} %y_regroup.15), channel_id=1, source_target_pairs={{0,96},{1,97},{2,98},{3,99},{4,100},{5,101},{6,102},{7,103},{8,104... | collective-permute-start | bytes 1818632 | tf_op jit(solution)/shard_map/ppermute | solution.py:78
  140.6 2.1 collective-permute-start.48
  142.8 3.7 %collective-permute-start.47 = (bf16[4,528,128]{2,1,0:T(8,128)(2,1)S(1)}, bf16[4,528,128]{2,1,0:T(8,128)(2,1)S(1)}, u32[]{:S(2)}, u32[]{:S(2)}) collective-permute-start(bf16[4,528,128]{2,1,0:T(8,128)(2,1)S(1)} %get-tuple-element.303), channel_id=1, source_target_pairs={{0,3},{1,2},{2,1},{3,0},{4,7},{5,6},{6,5},{7,4},{8,11},{9,10},{10,... | collective-permute-start | bytes 1622024 | tf_op jit(solution)/shard_map/ppermute | solution.py:78
  146.5 0.8 spread.6
  147.4 5.4 %collective-permute-done.48.refs_5_ = bf16[4,528,128]{2,1,0:T(8,128)(2,1)S(1)} collective-permute-done((bf16[4,528,128]{2,1,0:T(8,128)(2,1)S(1)}, bf16[4,528,128]{2,1,0:T(8,128)(2,1)S(1)}, u32[]{:S(2)}, u32[]{:S(2)}) %collective-permute-start.48) | collective-permute-done | bytes 540704 | tf_op jit(solution)/shard_map/ppermute | solution.py:78
  152.8 2.1 collective-permute-start.46
  155.0 0.8 spread.7
  155.8 5.4 %collective-permute-done.49.refs_6_ = bf16[4,528,128]{2,1,0:T(8,128)(2,1)S(1)} collective-permute-done((bf16[4,528,128]{2,1,0:T(8,128)(2,1)S(1)}, bf16[4,528,128]{2,1,0:T(8,128)(2,1)S(1)}, u32[]{:S(2)}, u32[]{:S(2)}) %collective-permute-start.49) | collective-permute-done | bytes 540704 | tf_op jit(solution)/shard_map/ppermute | solution.py:78
  161.2 10.1 %collective-permute-done.47.refs_4_ = bf16[4,528,128]{2,1,0:T(8,128)(2,1)S(1)} collective-permute-done((bf16[4,528,128]{2,1,0:T(8,128)(2,1)S(1)}, bf16[4,528,128]{2,1,0:T(8,128)(2,1)S(1)}, u32[]{:S(2)}, u32[]{:S(2)}) %collective-permute-start.47) | collective-permute-done | bytes 540704 | tf_op jit(solution)/shard_map/ppermute | solution.py:78
  171.3 5.4 %pack.5 = (f32[16,128]{1,0:T(8,128)S(1)}, bf16[1,16,128,2048]{3,2,1,0:T(8,128)(2,1)}) custom-call(s32[144]{0:T(256)S(1)} %copy-done.1, bf16[4,528,128]{2,1,0:T(8,128)(2,1)S(1)} %get-tuple-element.328.refs_0_, bf16[4,528,128]{2,1,0:T(8,128)(2,1)S(1)} %collective-permute-done.30.refs_1_, ...), custom_call_target="tpu_custom_call", output_to_operand_aliasing={{1}: (9, {})} | custom-call | tf_op jit(solution)/shard_map/pack/pallas_call | solution.py:362
  176.7 3.6 %collective-permute-start.43 = (bf16[4,528,128]{2,1,0:T(8,128)(2,1)S(1)}, bf16[4,528,128]{2,1,0:T(8,128)(2,1)S(1)}, u32[]{:S(2)}, u32[]{:S(2)}) collective-permute-start(bf16[4,528,128]{2,1,0:T(8,128)(2,1)S(1)} %get-tuple-element.322), channel_id=1, source_target_pairs={{0,5},{1,4},{2,7},{3,6},{4,1},{5,0},{6,3},{7,2},{8,13},{9,12},{10,... | collective-permute-start | bytes 1622024 | tf_op jit(solution)/shard_map/ppermute | solution.py:78
  180.4 2.1 collective-permute-start.54
  182.7 3.6 %collective-permute-done.41.refs_1_ = bf16[4,528,128]{2,1,0:T(8,128)(2,1)S(1)} collective-permute-done((bf16[4,528,128]{2,1,0:T(8,128)(2,1)S(1)}, bf16[4,528,128]{2,1,0:T(8,128)(2,1)S(1)}, u32[]{:S(2)}, u32[]{:S(2)}) %collective-permute-start.41) | collective-permute-done | bytes 540704 | tf_op jit(solution)/shard_map/ppermute | solution.py:78
  186.4 17.5 %collective-permute-done.42.refs_2_ = bf16[4,528,128]{2,1,0:T(8,128)(2,1)S(1)} collective-permute-done((bf16[4,528,128]{2,1,0:T(8,128)(2,1)S(1)}, bf16[4,528,128]{2,1,0:T(8,128)(2,1)S(1)}, u32[]{:S(2)}, u32[]{:S(2)}) %collective-permute-start.42) | collective-permute-done | bytes 540704 | tf_op jit(solution)/shard_map/ppermute | solution.py:78
  203.9 1.4 collective-permute-start.51
  205.3 0.8 collective-permute-start.52
  206.2 3.8 %collective-permute-start.50 = (bf16[4,528,128]{2,1,0:T(8,128)(2,1)S(1)}, bf16[4,528,128]{2,1,0:T(8,128)(2,1)S(1)}, u32[]{:S(2)}, u32[]{:S(2)}) collective-permute-start(bf16[4,528,128]{2,1,0:T(8,128)(2,1)S(1)} %get-tuple-element.346), channel_id=1, source_target_pairs={{0,3},{1,2},{2,1},{3,0},{4,7},{5,6},{6,5},{7,4},{8,11},{9,10},{10,... | collective-permute-start | bytes 1622024 | tf_op jit(solution)/shard_map/ppermute | solution.py:78
  209.9 5.4 %pack.6 = (f32[16,128]{1,0:T(8,128)S(1)}, bf16[1,16,128,2048]{3,2,1,0:T(8,128)(2,1)}) custom-call(s32[144]{0:T(256)S(1)} %copy-done.1, bf16[4,528,128]{2,1,0:T(8,128)(2,1)S(1)} %get-tuple-element.351.refs_0_, bf16[4,528,128]{2,1,0:T(8,128)(2,1)S(1)} %collective-permute-done.44.refs_1_, ...), custom_call_target="tpu_custom_call", output_to_operand_aliasing={{1}: (9, {})} | custom-call | tf_op jit(solution)/shard_map/pack/pallas_call | solution.py:362
  215.3 5.1 %collective-permute-done.51.refs_5_ = bf16[4,528,128]{2,1,0:T(8,128)(2,1)S(1)} collective-permute-done((bf16[4,528,128]{2,1,0:T(8,128)(2,1)S(1)}, bf16[4,528,128]{2,1,0:T(8,128)(2,1)S(1)}, u32[]{:S(2)}, u32[]{:S(2)}) %collective-permute-start.51) | collective-permute-done | bytes 540704 | tf_op jit(solution)/shard_map/ppermute | solution.py:78
  220.4 2.7 %collective-permute-done.50.refs_4_ = bf16[4,528,128]{2,1,0:T(8,128)(2,1)S(1)} collective-permute-done((bf16[4,528,128]{2,1,0:T(8,128)(2,1)S(1)}, bf16[4,528,128]{2,1,0:T(8,128)(2,1)S(1)}, u32[]{:S(2)}, u32[]{:S(2)}) %collective-permute-start.50) | collective-permute-done | bytes 540704 | tf_op jit(solution)/shard_map/ppermute | solution.py:78
  223.1 6.0 %pack.7 = (f32[16,128]{1,0:T(8,128)}, bf16[1,16,128,2048]{3,2,1,0:T(8,128)(2,1)}) custom-call(s32[144]{0:T(256)S(1)} %copy-done.1, bf16[4,528,128]{2,1,0:T(8,128)(2,1)S(1)} %get-tuple-element.360.refs_0_, bf16[4,528,128]{2,1,0:T(8,128)(2,1)S(1)} %collective-permute-done.41.refs_1_, ...), custom_call_target="tpu_custom_call", output_to_operand_aliasing={{1}: (9, {})} | custom-call | tf_op jit(solution)/shard_map/pack/pallas_call | solution.py:362
  (79 shorter events, 4.3 us)
Async XLA Ops:
  0.6 2.3 %copy-start = (bf16[2048,1152]{1,0:T(8,128)(2,1)S(1)}, bf16[2048,1152]{1,0:T(8,128)(2,1)}, u32[]{:S(2)}) copy-start(bf16[2048,1152]{1,0:T(8,128)(2,1)} %weight_ref.1) | copy-start | bytes 14155780
  3.0 0.8 copy-start.2
  3.7 55.8 %copy-start.1 = (s32[144]{0:T(256)S(1)}, s32[144]{0:T(256)}, u32[]{:S(2)}) copy-start(s32[144]{0:T(256)} %placement_ref.15) | copy-start | bytes 1732
  9.5 3.2 %collective-permute-start = (bf16[2,576,128]{2,1,0:T(8,128)(2,1)S(1)}, bf16[2,576,128]{2,1,0:T(8,128)(2,1)S(1)}, u32[]{:S(2)}, u32[]{:S(2)}) collective-permute-start(bf16[2,576,128]{2,1,0:T(8,128)(2,1)S(1)} %get-tuple-element.191), channel_id=1, source_target_pairs={{0,16},{1,17},{2,18},{3,19},{4,20},{5,21},{6,22},{7,23},{8,24},{9,... | collective-permute-start | bytes 884744 | tf_op jit(solution)/shard_map/ppermute | solution.py:78
  9.6 9.8 %collective-permute-start.1 = (bf16[2,576,128]{2,1,0:T(8,128)(2,1)S(1)}, bf16[2,576,128]{2,1,0:T(8,128)(2,1)S(1)}, u32[]{:S(2)}, u32[]{:S(2)}) collective-permute-start(bf16[2,576,128]{2,1,0:T(8,128)(2,1)S(1)} %get-tuple-element.192), channel_id=1, source_target_pairs={{0,32},{1,33},{2,34},{3,35},{4,36},{5,37},{6,38},{7,39},{8,40},{9,... | collective-permute-start | bytes 884744 | tf_op jit(solution)/shard_map/ppermute | solution.py:78
  10.5 9.1 %collective-permute-start.2 = (bf16[2,576,128]{2,1,0:T(8,128)(2,1)S(1)}, bf16[2,576,128]{2,1,0:T(8,128)(2,1)S(1)}, u32[]{:S(2)}, u32[]{:S(2)}) collective-permute-start(bf16[2,576,128]{2,1,0:T(8,128)(2,1)S(1)} %get-tuple-element.193), channel_id=1, source_target_pairs={{0,112},{1,113},{2,114},{3,115},{4,116},{5,117},{6,118},{7,119},{8... | collective-permute-start | bytes 884744 | tf_op jit(solution)/shard_map/ppermute | solution.py:78
  19.6 14.2 %collective-permute-start.9 = (bf16[4,576,128]{2,1,0:T(8,128)(2,1)S(1)}, bf16[4,576,128]{2,1,0:T(8,128)(2,1)S(1)}, u32[]{:S(2)}, u32[]{:S(2)}) collective-permute-start(bf16[4,576,128]{2,1,0:T(8,128)(2,1)S(1)} %y_regroup.8), channel_id=1, source_target_pairs={{0,96},{1,97},{2,98},{3,99},{4,100},{5,101},{6,102},{7,103},{8,104... | collective-permute-start | bytes 1769480 | tf_op jit(solution)/shard_map/ppermute | solution.py:78
  19.9 14.8 %collective-permute-start.6 = (bf16[2,576,128]{2,1,0:T(8,128)(2,1)S(1)}, bf16[2,576,128]{2,1,0:T(8,128)(2,1)S(1)}, u32[]{:S(2)}, u32[]{:S(2)}) collective-permute-start(bf16[2,576,128]{2,1,0:T(8,128)(2,1)S(1)} %get-tuple-element.199), channel_id=1, source_target_pairs={{0,16},{1,17},{2,18},{3,19},{4,20},{5,21},{6,22},{7,23},{8,24},{9,... | collective-permute-start | bytes 884744 | tf_op jit(solution)/shard_map/ppermute | solution.py:78
  20.3 17.4 %collective-permute-start.7 = (bf16[2,576,128]{2,1,0:T(8,128)(2,1)S(1)}, bf16[2,576,128]{2,1,0:T(8,128)(2,1)S(1)}, u32[]{:S(2)}, u32[]{:S(2)}) collective-permute-start(bf16[2,576,128]{2,1,0:T(8,128)(2,1)S(1)} %get-tuple-element.200), channel_id=1, source_target_pairs={{0,32},{1,33},{2,34},{3,35},{4,36},{5,37},{6,38},{7,39},{8,40},{9,... | collective-permute-start | bytes 884744 | tf_op jit(solution)/shard_map/ppermute | solution.py:78
  21.9 15.8 %collective-permute-start.8 = (bf16[2,576,128]{2,1,0:T(8,128)(2,1)S(1)}, bf16[2,576,128]{2,1,0:T(8,128)(2,1)S(1)}, u32[]{:S(2)}, u32[]{:S(2)}) collective-permute-start(bf16[2,576,128]{2,1,0:T(8,128)(2,1)S(1)} %get-tuple-element.201), channel_id=1, source_target_pairs={{0,112},{1,113},{2,114},{3,115},{4,116},{5,117},{6,118},{7,119},{8... | collective-permute-start | bytes 884744 | tf_op jit(solution)/shard_map/ppermute | solution.py:78
  34.6 3.6 %collective-permute-start.11 = (bf16[2,592,128]{2,1,0:T(8,128)(2,1)S(1)}, bf16[2,592,128]{2,1,0:T(8,128)(2,1)S(1)}, u32[]{:S(2)}, u32[]{:S(2)}) collective-permute-start(bf16[2,592,128]{2,1,0:T(8,128)(2,1)S(1)} %get-tuple-element.212), channel_id=1, source_target_pairs={{0,16},{1,17},{2,18},{3,19},{4,20},{5,21},{6,22},{7,23},{8,24},{9,... | collective-permute-start | bytes 909320 | tf_op jit(solution)/shard_map/ppermute | solution.py:78
  34.6 10.1 %collective-permute-start.12 = (bf16[2,592,128]{2,1,0:T(8,128)(2,1)S(1)}, bf16[2,592,128]{2,1,0:T(8,128)(2,1)S(1)}, u32[]{:S(2)}, u32[]{:S(2)}) collective-permute-start(bf16[2,592,128]{2,1,0:T(8,128)(2,1)S(1)} %get-tuple-element.213), channel_id=1, source_target_pairs={{0,32},{1,33},{2,34},{3,35},{4,36},{5,37},{6,38},{7,39},{8,40},{9,... | collective-permute-start | bytes 909320 | tf_op jit(solution)/shard_map/ppermute | solution.py:78
  34.7 10.0 %collective-permute-start.13 = (bf16[2,592,128]{2,1,0:T(8,128)(2,1)S(1)}, bf16[2,592,128]{2,1,0:T(8,128)(2,1)S(1)}, u32[]{:S(2)}, u32[]{:S(2)}) collective-permute-start(bf16[2,592,128]{2,1,0:T(8,128)(2,1)S(1)} %get-tuple-element.214), channel_id=1, source_target_pairs={{0,112},{1,113},{2,114},{3,115},{4,116},{5,117},{6,118},{7,119},{8... | collective-permute-start | bytes 909320 | tf_op jit(solution)/shard_map/ppermute | solution.py:78
  37.8 14.0 %collective-permute-start.10 = (bf16[4,576,128]{2,1,0:T(8,128)(2,1)S(1)}, bf16[4,576,128]{2,1,0:T(8,128)(2,1)S(1)}, u32[]{:S(2)}, u32[]{:S(2)}) collective-permute-start(bf16[4,576,128]{2,1,0:T(8,128)(2,1)S(1)} %y_regroup.9), channel_id=1, source_target_pairs={{0,96},{1,97},{2,98},{3,99},{4,100},{5,101},{6,102},{7,103},{8,104... | collective-permute-start | bytes 1769480 | tf_op jit(solution)/shard_map/ppermute | solution.py:78
  44.7 14.8 %collective-permute-start.17 = (bf16[4,592,128]{2,1,0:T(8,128)(2,1)S(1)}, bf16[4,592,128]{2,1,0:T(8,128)(2,1)S(1)}, u32[]{:S(2)}, u32[]{:S(2)}) collective-permute-start(bf16[4,592,128]{2,1,0:T(8,128)(2,1)S(1)} %y_regroup.10), channel_id=1, source_target_pairs={{0,96},{1,97},{2,98},{3,99},{4,100},{5,101},{6,102},{7,103},{8,104... | collective-permute-start | bytes 1818632 | tf_op jit(solution)/shard_map/ppermute | solution.py:78
  45.3 10.4 %collective-permute-start.22 = (bf16[2,576,128]{2,1,0:T(8,128)(2,1)S(1)}, bf16[2,576,128]{2,1,0:T(8,128)(2,1)S(1)}, u32[]{:S(2)}, u32[]{:S(2)}) collective-permute-start(bf16[2,576,128]{2,1,0:T(8,128)(2,1)S(1)} %get-tuple-element.242), channel_id=1, source_target_pairs={{0,16},{1,17},{2,18},{3,19},{4,20},{5,21},{6,22},{7,23},{8,24},{9,... | collective-permute-start | bytes 884744 | tf_op jit(solution)/shard_map/ppermute | solution.py:78
  52.6 7.8 %collective-permute-start.14 = (bf16[2,592,128]{2,1,0:T(8,128)(2,1)S(1)}, bf16[2,592,128]{2,1,0:T(8,128)(2,1)S(1)}, u32[]{:S(2)}, u32[]{:S(2)}) collective-permute-start(bf16[2,592,128]{2,1,0:T(8,128)(2,1)S(1)} %get-tuple-element.225), channel_id=1, source_target_pairs={{0,16},{1,17},{2,18},{3,19},{4,20},{5,21},{6,22},{7,23},{8,24},{9,... | collective-permute-start | bytes 909320 | tf_op jit(solution)/shard_map/ppermute | solution.py:78
  52.6 10.2 %collective-permute-start.15 = (bf16[2,592,128]{2,1,0:T(8,128)(2,1)S(1)}, bf16[2,592,128]{2,1,0:T(8,128)(2,1)S(1)}, u32[]{:S(2)}, u32[]{:S(2)}) collective-permute-start(bf16[2,592,128]{2,1,0:T(8,128)(2,1)S(1)} %get-tuple-element.226), channel_id=1, source_target_pairs={{0,32},{1,33},{2,34},{3,35},{4,36},{5,37},{6,38},{7,39},{8,40},{9,... | collective-permute-start | bytes 909320 | tf_op jit(solution)/shard_map/ppermute | solution.py:78
  52.7 12.0 %collective-permute-start.16 = (bf16[2,592,128]{2,1,0:T(8,128)(2,1)S(1)}, bf16[2,592,128]{2,1,0:T(8,128)(2,1)S(1)}, u32[]{:S(2)}, u32[]{:S(2)}) collective-permute-start(bf16[2,592,128]{2,1,0:T(8,128)(2,1)S(1)} %get-tuple-element.227), channel_id=1, source_target_pairs={{0,112},{1,113},{2,114},{3,115},{4,116},{5,117},{6,118},{7,119},{8... | collective-permute-start | bytes 909320 | tf_op jit(solution)/shard_map/ppermute | solution.py:78
  55.7 13.5 %collective-permute-start.23 = (bf16[2,576,128]{2,1,0:T(8,128)(2,1)S(1)}, bf16[2,576,128]{2,1,0:T(8,128)(2,1)S(1)}, u32[]{:S(2)}, u32[]{:S(2)}) collective-permute-start(bf16[2,576,128]{2,1,0:T(8,128)(2,1)S(1)} %get-tuple-element.243), channel_id=1, source_target_pairs={{0,32},{1,33},{2,34},{3,35},{4,36},{5,37},{6,38},{7,39},{8,40},{9,... | collective-permute-start | bytes 884744 | tf_op jit(solution)/shard_map/ppermute | solution.py:78
  59.5 10.4 %collective-permute-start.24 = (bf16[2,576,128]{2,1,0:T(8,128)(2,1)S(1)}, bf16[2,576,128]{2,1,0:T(8,128)(2,1)S(1)}, u32[]{:S(2)}, u32[]{:S(2)}) collective-permute-start(bf16[2,576,128]{2,1,0:T(8,128)(2,1)S(1)} %get-tuple-element.244), channel_id=1, source_target_pairs={{0,112},{1,113},{2,114},{3,115},{4,116},{5,117},{6,118},{7,119},{8... | collective-permute-start | bytes 884744 | tf_op jit(solution)/shard_map/ppermute | solution.py:78
  60.4 12.1 %collective-permute-start.19 = (bf16[4,528,128]{2,1,0:T(8,128)(2,1)S(1)}, bf16[4,528,128]{2,1,0:T(8,128)(2,1)S(1)}, u32[]{:S(2)}, u32[]{:S(2)}) collective-permute-start(bf16[4,528,128]{2,1,0:T(8,128)(2,1)S(1)} %get-tuple-element.238), channel_id=1, source_target_pairs={{0,1},{1,0},{2,3},{3,2},{4,5},{5,4},{6,7},{7,6},{8,9},{9,8},{10,11... | collective-permute-start | bytes 1622024 | tf_op jit(solution)/shard_map/ppermute | solution.py:78
  62.8 15.2 %collective-permute-start.20 = (bf16[4,528,128]{2,1,0:T(8,128)(2,1)S(1)}, bf16[4,528,128]{2,1,0:T(8,128)(2,1)S(1)}, u32[]{:S(2)}, u32[]{:S(2)}) collective-permute-start(bf16[4,528,128]{2,1,0:T(8,128)(2,1)S(1)} %get-tuple-element.239), channel_id=1, source_target_pairs={{0,4},{1,5},{2,6},{3,7},{4,0},{5,1},{6,2},{7,3},{8,12},{9,13},{10,... | collective-permute-start | bytes 1622024 | tf_op jit(solution)/shard_map/ppermute | solution.py:78
  64.7 13.2 %collective-permute-start.21 = (bf16[4,528,128]{2,1,0:T(8,128)(2,1)S(1)}, bf16[4,528,128]{2,1,0:T(8,128)(2,1)S(1)}, u32[]{:S(2)}, u32[]{:S(2)}) collective-permute-start(bf16[4,528,128]{2,1,0:T(8,128)(2,1)S(1)} %get-tuple-element.240), channel_id=1, source_target_pairs={{0,5},{1,4},{2,7},{3,6},{4,1},{5,0},{6,3},{7,2},{8,13},{9,12},{10,... | collective-permute-start | bytes 1622024 | tf_op jit(solution)/shard_map/ppermute | solution.py:78
  69.1 13.4 %collective-permute-start.18 = (bf16[4,592,128]{2,1,0:T(8,128)(2,1)S(1)}, bf16[4,592,128]{2,1,0:T(8,128)(2,1)S(1)}, u32[]{:S(2)}, u32[]{:S(2)}) collective-permute-start(bf16[4,592,128]{2,1,0:T(8,128)(2,1)S(1)} %y_regroup.11), channel_id=1, source_target_pairs={{0,96},{1,97},{2,98},{3,99},{4,100},{5,101},{6,102},{7,103},{8,104... | collective-permute-start | bytes 1818632 | tf_op jit(solution)/shard_map/ppermute | solution.py:78
  70.0 21.4 %collective-permute-start.26 = (bf16[4,576,128]{2,1,0:T(8,128)(2,1)S(1)}, bf16[4,576,128]{2,1,0:T(8,128)(2,1)S(1)}, u32[]{:S(2)}, u32[]{:S(2)}) collective-permute-start(bf16[4,576,128]{2,1,0:T(8,128)(2,1)S(1)} %y_regroup.12), channel_id=1, source_target_pairs={{0,96},{1,97},{2,98},{3,99},{4,100},{5,101},{6,102},{7,103},{8,104... | collective-permute-start | bytes 1769480 | tf_op jit(solution)/shard_map/ppermute | solution.py:78
  72.5 10.9 %collective-permute-start.3 = (bf16[2,576,128]{2,1,0:T(8,128)(2,1)S(1)}, bf16[2,576,128]{2,1,0:T(8,128)(2,1)S(1)}, u32[]{:S(2)}, u32[]{:S(2)}) collective-permute-start(bf16[2,576,128]{2,1,0:T(8,128)(2,1)S(1)} %get-tuple-element.195), channel_id=1, source_target_pairs={{0,16},{1,17},{2,18},{3,19},{4,20},{5,21},{6,22},{7,23},{8,24},{9,... | collective-permute-start | bytes 884744 | tf_op jit(solution)/shard_map/ppermute | solution.py:78
  78.0 9.9 %collective-permute-start.4 = (bf16[2,576,128]{2,1,0:T(8,128)(2,1)S(1)}, bf16[2,576,128]{2,1,0:T(8,128)(2,1)S(1)}, u32[]{:S(2)}, u32[]{:S(2)}) collective-permute-start(bf16[2,576,128]{2,1,0:T(8,128)(2,1)S(1)} %get-tuple-element.196), channel_id=1, source_target_pairs={{0,32},{1,33},{2,34},{3,35},{4,36},{5,37},{6,38},{7,39},{8,40},{9,... | collective-permute-start | bytes 884744 | tf_op jit(solution)/shard_map/ppermute | solution.py:78
  78.0 13.4 %collective-permute-start.5 = (bf16[2,576,128]{2,1,0:T(8,128)(2,1)S(1)}, bf16[2,576,128]{2,1,0:T(8,128)(2,1)S(1)}, u32[]{:S(2)}, u32[]{:S(2)}) collective-permute-start(bf16[2,576,128]{2,1,0:T(8,128)(2,1)S(1)} %get-tuple-element.197), channel_id=1, source_target_pairs={{0,112},{1,113},{2,114},{3,115},{4,116},{5,117},{6,118},{7,119},{8... | collective-permute-start | bytes 884744 | tf_op jit(solution)/shard_map/ppermute | solution.py:78
  92.2 8.8 %collective-permute-start.36 = (bf16[2,592,128]{2,1,0:T(8,128)(2,1)S(1)}, bf16[2,592,128]{2,1,0:T(8,128)(2,1)S(1)}, u32[]{:S(2)}, u32[]{:S(2)}) collective-permute-start(bf16[2,592,128]{2,1,0:T(8,128)(2,1)S(1)} %get-tuple-element.284), channel_id=1, source_target_pairs={{0,16},{1,17},{2,18},{3,19},{4,20},{5,21},{6,22},{7,23},{8,24},{9,... | collective-permute-start | bytes 909320 | tf_op jit(solution)/shard_map/ppermute | solution.py:78
  93.9 10.0 %collective-permute-start.37 = (bf16[2,592,128]{2,1,0:T(8,128)(2,1)S(1)}, bf16[2,592,128]{2,1,0:T(8,128)(2,1)S(1)}, u32[]{:S(2)}, u32[]{:S(2)}) collective-permute-start(bf16[2,592,128]{2,1,0:T(8,128)(2,1)S(1)} %get-tuple-element.285), channel_id=1, source_target_pairs={{0,32},{1,33},{2,34},{3,35},{4,36},{5,37},{6,38},{7,39},{8,40},{9,... | collective-permute-start | bytes 909320 | tf_op jit(solution)/shard_map/ppermute | solution.py:78
  93.9 11.4 %collective-permute-start.38 = (bf16[2,592,128]{2,1,0:T(8,128)(2,1)S(1)}, bf16[2,592,128]{2,1,0:T(8,128)(2,1)S(1)}, u32[]{:S(2)}, u32[]{:S(2)}) collective-permute-start(bf16[2,592,128]{2,1,0:T(8,128)(2,1)S(1)} %get-tuple-element.286), channel_id=1, source_target_pairs={{0,112},{1,113},{2,114},{3,115},{4,116},{5,117},{6,118},{7,119},{8... | collective-permute-start | bytes 909320 | tf_op jit(solution)/shard_map/ppermute | solution.py:78
  96.6 17.5 %collective-permute-start.25 = (bf16[4,576,128]{2,1,0:T(8,128)(2,1)S(1)}, bf16[4,576,128]{2,1,0:T(8,128)(2,1)S(1)}, u32[]{:S(2)}, u32[]{:S(2)}) collective-permute-start(bf16[4,576,128]{2,1,0:T(8,128)(2,1)S(1)} %y_regroup.13), channel_id=1, source_target_pairs={{0,96},{1,97},{2,98},{3,99},{4,100},{5,101},{6,102},{7,103},{8,104... | collective-permute-start | bytes 1769480 | tf_op jit(solution)/shard_map/ppermute | solution.py:78
  97.0 16.7 %collective-permute-start.34 = (bf16[4,528,128]{2,1,0:T(8,128)(2,1)S(1)}, bf16[4,528,128]{2,1,0:T(8,128)(2,1)S(1)}, u32[]{:S(2)}, u32[]{:S(2)}) collective-permute-start(bf16[4,528,128]{2,1,0:T(8,128)(2,1)S(1)} %get-tuple-element.282), channel_id=1, source_target_pairs={{0,12},{1,13},{2,14},{3,15},{4,8},{5,9},{6,10},{7,11},{8,4},{9,5},... | collective-permute-start | bytes 1622024 | tf_op jit(solution)/shard_map/ppermute | solution.py:78
  101.0 16.2 %collective-permute-start.35 = (bf16[4,528,128]{2,1,0:T(8,128)(2,1)S(1)}, bf16[4,528,128]{2,1,0:T(8,128)(2,1)S(1)}, u32[]{:S(2)}, u32[]{:S(2)}) collective-permute-start(bf16[4,528,128]{2,1,0:T(8,128)(2,1)S(1)} %get-tuple-element.283), channel_id=1, source_target_pairs={{0,15},{1,14},{2,13},{3,12},{4,11},{5,10},{6,9},{7,8},{8,7},{9,6},... | collective-permute-start | bytes 1622024 | tf_op jit(solution)/shard_map/ppermute | solution.py:78
  103.9 21.5 %collective-permute-start.33 = (bf16[4,528,128]{2,1,0:T(8,128)(2,1)S(1)}, bf16[4,528,128]{2,1,0:T(8,128)(2,1)S(1)}, u32[]{:S(2)}, u32[]{:S(2)}) collective-permute-start(bf16[4,528,128]{2,1,0:T(8,128)(2,1)S(1)} %get-tuple-element.253), channel_id=1, source_target_pairs={{0,3},{1,2},{2,1},{3,0},{4,7},{5,6},{6,5},{7,4},{8,11},{9,10},{10,... | collective-permute-start | bytes 1622024 | tf_op jit(solution)/shard_map/ppermute | solution.py:78
  105.4 20.1 %collective-permute-start.30 = (bf16[4,528,128]{2,1,0:T(8,128)(2,1)S(1)}, bf16[4,528,128]{2,1,0:T(8,128)(2,1)S(1)}, u32[]{:S(2)}, u32[]{:S(2)}) collective-permute-start(bf16[4,528,128]{2,1,0:T(8,128)(2,1)S(1)} %get-tuple-element.279), channel_id=1, source_target_pairs={{0,1},{1,0},{2,3},{3,2},{4,5},{5,4},{6,7},{7,6},{8,9},{9,8},{10,11... | collective-permute-start | bytes 1622024 | tf_op jit(solution)/shard_map/ppermute | solution.py:78
  113.7 17.1 %collective-permute-start.31 = (bf16[4,528,128]{2,1,0:T(8,128)(2,1)S(1)}, bf16[4,528,128]{2,1,0:T(8,128)(2,1)S(1)}, u32[]{:S(2)}, u32[]{:S(2)}) collective-permute-start(bf16[4,528,128]{2,1,0:T(8,128)(2,1)S(1)} %get-tuple-element.280), channel_id=1, source_target_pairs={{0,4},{1,5},{2,6},{3,7},{4,0},{5,1},{6,2},{7,3},{8,12},{9,13},{10,... | collective-permute-start | bytes 1622024 | tf_op jit(solution)/shard_map/ppermute | solution.py:78
  114.0 22.5 %collective-permute-start.32 = (bf16[4,528,128]{2,1,0:T(8,128)(2,1)S(1)}, bf16[4,528,128]{2,1,0:T(8,128)(2,1)S(1)}, u32[]{:S(2)}, u32[]{:S(2)}) collective-permute-start(bf16[4,528,128]{2,1,0:T(8,128)(2,1)S(1)} %get-tuple-element.281), channel_id=1, source_target_pairs={{0,5},{1,4},{2,7},{3,6},{4,1},{5,0},{6,3},{7,2},{8,13},{9,12},{10,... | collective-permute-start | bytes 1622024 | tf_op jit(solution)/shard_map/ppermute | solution.py:78
  117.2 19.4 %collective-permute-start.27 = (bf16[2,592,128]{2,1,0:T(8,128)(2,1)S(1)}, bf16[2,592,128]{2,1,0:T(8,128)(2,1)S(1)}, u32[]{:S(2)}, u32[]{:S(2)}) collective-permute-start(bf16[2,592,128]{2,1,0:T(8,128)(2,1)S(1)} %get-tuple-element.276), channel_id=1, source_target_pairs={{0,16},{1,17},{2,18},{3,19},{4,20},{5,21},{6,22},{7,23},{8,24},{9,... | collective-permute-start | bytes 909320 | tf_op jit(solution)/shard_map/ppermute | solution.py:78
  125.4 11.2 %collective-permute-start.28 = (bf16[2,592,128]{2,1,0:T(8,128)(2,1)S(1)}, bf16[2,592,128]{2,1,0:T(8,128)(2,1)S(1)}, u32[]{:S(2)}, u32[]{:S(2)}) collective-permute-start(bf16[2,592,128]{2,1,0:T(8,128)(2,1)S(1)} %get-tuple-element.277), channel_id=1, source_target_pairs={{0,32},{1,33},{2,34},{3,35},{4,36},{5,37},{6,38},{7,39},{8,40},{9,... | collective-permute-start | bytes 909320 | tf_op jit(solution)/shard_map/ppermute | solution.py:78
  125.4 11.2 %collective-permute-start.29 = (bf16[2,592,128]{2,1,0:T(8,128)(2,1)S(1)}, bf16[2,592,128]{2,1,0:T(8,128)(2,1)S(1)}, u32[]{:S(2)}, u32[]{:S(2)}) collective-permute-start(bf16[2,592,128]{2,1,0:T(8,128)(2,1)S(1)} %get-tuple-element.278), channel_id=1, source_target_pairs={{0,112},{1,113},{2,114},{3,115},{4,116},{5,117},{6,118},{7,119},{8... | collective-permute-start | bytes 909320 | tf_op jit(solution)/shard_map/ppermute | solution.py:78
  130.8 15.7 %collective-permute-start.40 = (bf16[4,592,128]{2,1,0:T(8,128)(2,1)S(1)}, bf16[4,592,128]{2,1,0:T(8,128)(2,1)S(1)}, u32[]{:S(2)}, u32[]{:S(2)}) collective-permute-start(bf16[4,592,128]{2,1,0:T(8,128)(2,1)S(1)} %y_regroup.14), channel_id=1, source_target_pairs={{0,96},{1,97},{2,98},{3,99},{4,100},{5,101},{6,102},{7,103},{8,104... | collective-permute-start | bytes 1818632 | tf_op jit(solution)/shard_map/ppermute | solution.py:78
  136.7 16.1 %collective-permute-start.39 = (bf16[4,592,128]{2,1,0:T(8,128)(2,1)S(1)}, bf16[4,592,128]{2,1,0:T(8,128)(2,1)S(1)}, u32[]{:S(2)}, u32[]{:S(2)}) collective-permute-start(bf16[4,592,128]{2,1,0:T(8,128)(2,1)S(1)} %y_regroup.15), channel_id=1, source_target_pairs={{0,96},{1,97},{2,98},{3,99},{4,100},{5,101},{6,102},{7,103},{8,104... | collective-permute-start | bytes 1818632 | tf_op jit(solution)/shard_map/ppermute | solution.py:78
  140.6 12.2 %collective-permute-start.48 = (bf16[4,528,128]{2,1,0:T(8,128)(2,1)S(1)}, bf16[4,528,128]{2,1,0:T(8,128)(2,1)S(1)}, u32[]{:S(2)}, u32[]{:S(2)}) collective-permute-start(bf16[4,528,128]{2,1,0:T(8,128)(2,1)S(1)} %get-tuple-element.326), channel_id=1, source_target_pairs={{0,12},{1,13},{2,14},{3,15},{4,8},{5,9},{6,10},{7,11},{8,4},{9,5},... | collective-permute-start | bytes 1622024 | tf_op jit(solution)/shard_map/ppermute | solution.py:78
  142.7 18.5 %collective-permute-start.49 = (bf16[4,528,128]{2,1,0:T(8,128)(2,1)S(1)}, bf16[4,528,128]{2,1,0:T(8,128)(2,1)S(1)}, u32[]{:S(2)}, u32[]{:S(2)}) collective-permute-start(bf16[4,528,128]{2,1,0:T(8,128)(2,1)S(1)} %get-tuple-element.327), channel_id=1, source_target_pairs={{0,15},{1,14},{2,13},{3,12},{4,11},{5,10},{6,9},{7,8},{8,7},{9,6},... | collective-permute-start | bytes 1622024 | tf_op jit(solution)/shard_map/ppermute | solution.py:78
  142.8 28.5 %collective-permute-start.47 = (bf16[4,528,128]{2,1,0:T(8,128)(2,1)S(1)}, bf16[4,528,128]{2,1,0:T(8,128)(2,1)S(1)}, u32[]{:S(2)}, u32[]{:S(2)}) collective-permute-start(bf16[4,528,128]{2,1,0:T(8,128)(2,1)S(1)} %get-tuple-element.303), channel_id=1, source_target_pairs={{0,3},{1,2},{2,1},{3,0},{4,7},{5,6},{6,5},{7,4},{8,11},{9,10},{10,... | collective-permute-start | bytes 1622024 | tf_op jit(solution)/shard_map/ppermute | solution.py:78
  147.4 29.3 %collective-permute-start.44 = (bf16[4,528,128]{2,1,0:T(8,128)(2,1)S(1)}, bf16[4,528,128]{2,1,0:T(8,128)(2,1)S(1)}, u32[]{:S(2)}, u32[]{:S(2)}) collective-permute-start(bf16[4,528,128]{2,1,0:T(8,128)(2,1)S(1)} %get-tuple-element.323), channel_id=1, source_target_pairs={{0,1},{1,0},{2,3},{3,2},{4,5},{5,4},{6,7},{7,6},{8,9},{9,8},{10,11... | collective-permute-start | bytes 1622024 | tf_op jit(solution)/shard_map/ppermute | solution.py:78
  152.8 27.4 %collective-permute-start.45 = (bf16[4,528,128]{2,1,0:T(8,128)(2,1)S(1)}, bf16[4,528,128]{2,1,0:T(8,128)(2,1)S(1)}, u32[]{:S(2)}, u32[]{:S(2)}) collective-permute-start(bf16[4,528,128]{2,1,0:T(8,128)(2,1)S(1)} %get-tuple-element.324), channel_id=1, source_target_pairs={{0,4},{1,5},{2,6},{3,7},{4,0},{5,1},{6,2},{7,3},{8,12},{9,13},{10,... | collective-permute-start | bytes 1622024 | tf_op jit(solution)/shard_map/ppermute | solution.py:78
  152.8 27.4 %collective-permute-start.46 = (bf16[4,528,128]{2,1,0:T(8,128)(2,1)S(1)}, bf16[4,528,128]{2,1,0:T(8,128)(2,1)S(1)}, u32[]{:S(2)}, u32[]{:S(2)}) collective-permute-start(bf16[4,528,128]{2,1,0:T(8,128)(2,1)S(1)} %get-tuple-element.325), channel_id=1, source_target_pairs={{0,5},{1,4},{2,7},{3,6},{4,1},{5,0},{6,3},{7,2},{8,13},{9,12},{10,... | collective-permute-start | bytes 1622024 | tf_op jit(solution)/shard_map/ppermute | solution.py:78
  171.3 15.0 %collective-permute-start.41 = (bf16[4,528,128]{2,1,0:T(8,128)(2,1)S(1)}, bf16[4,528,128]{2,1,0:T(8,128)(2,1)S(1)}, u32[]{:S(2)}, u32[]{:S(2)}) collective-permute-start(bf16[4,528,128]{2,1,0:T(8,128)(2,1)S(1)} %get-tuple-element.320), channel_id=1, source_target_pairs={{0,1},{1,0},{2,3},{3,2},{4,5},{5,4},{6,7},{7,6},{8,9},{9,8},{10,11... | collective-permute-start | bytes 1622024 | tf_op jit(solution)/shard_map/ppermute | solution.py:78
  171.3 32.5 %collective-permute-start.42 = (bf16[4,528,128]{2,1,0:T(8,128)(2,1)S(1)}, bf16[4,528,128]{2,1,0:T(8,128)(2,1)S(1)}, u32[]{:S(2)}, u32[]{:S(2)}) collective-permute-start(bf16[4,528,128]{2,1,0:T(8,128)(2,1)S(1)} %get-tuple-element.321), channel_id=1, source_target_pairs={{0,4},{1,5},{2,6},{3,7},{4,0},{5,1},{6,2},{7,3},{8,12},{9,13},{10,... | collective-permute-start | bytes 1622024 | tf_op jit(solution)/shard_map/ppermute | solution.py:78
  176.7 27.1 %collective-permute-start.43 = (bf16[4,528,128]{2,1,0:T(8,128)(2,1)S(1)}, bf16[4,528,128]{2,1,0:T(8,128)(2,1)S(1)}, u32[]{:S(2)}, u32[]{:S(2)}) collective-permute-start(bf16[4,528,128]{2,1,0:T(8,128)(2,1)S(1)} %get-tuple-element.322), channel_id=1, source_target_pairs={{0,5},{1,4},{2,7},{3,6},{4,1},{5,0},{6,3},{7,2},{8,13},{9,12},{10,... | collective-permute-start | bytes 1622024 | tf_op jit(solution)/shard_map/ppermute | solution.py:78
  180.4 25.8 %collective-permute-start.54 = (bf16[4,528,128]{2,1,0:T(8,128)(2,1)S(1)}, bf16[4,528,128]{2,1,0:T(8,128)(2,1)S(1)}, u32[]{:S(2)}, u32[]{:S(2)}) collective-permute-start(bf16[4,528,128]{2,1,0:T(8,128)(2,1)S(1)} %get-tuple-element.349), channel_id=1, source_target_pairs={{0,12},{1,13},{2,14},{3,15},{4,8},{5,9},{6,10},{7,11},{8,4},{9,5},... | collective-permute-start | bytes 1622024 | tf_op jit(solution)/shard_map/ppermute | solution.py:78
  182.4 27.5 %collective-permute-start.55 = (bf16[4,528,128]{2,1,0:T(8,128)(2,1)S(1)}, bf16[4,528,128]{2,1,0:T(8,128)(2,1)S(1)}, u32[]{:S(2)}, u32[]{:S(2)}) collective-permute-start(bf16[4,528,128]{2,1,0:T(8,128)(2,1)S(1)} %get-tuple-element.350), channel_id=1, source_target_pairs={{0,15},{1,14},{2,13},{3,12},{4,11},{5,10},{6,9},{7,8},{8,7},{9,6},... | collective-permute-start | bytes 1622024 | tf_op jit(solution)/shard_map/ppermute | solution.py:78
  186.3 23.7 %collective-permute-start.53 = (bf16[4,528,128]{2,1,0:T(8,128)(2,1)S(1)}, bf16[4,528,128]{2,1,0:T(8,128)(2,1)S(1)}, u32[]{:S(2)}, u32[]{:S(2)}) collective-permute-start(bf16[4,528,128]{2,1,0:T(8,128)(2,1)S(1)} %get-tuple-element.341), channel_id=1, source_target_pairs={{0,3},{1,2},{2,1},{3,0},{4,7},{5,6},{6,5},{7,4},{8,11},{9,10},{10,... | collective-permute-start | bytes 1622024 | tf_op jit(solution)/shard_map/ppermute | solution.py:78
  203.9 16.4 %collective-permute-start.51 = (bf16[4,528,128]{2,1,0:T(8,128)(2,1)S(1)}, bf16[4,528,128]{2,1,0:T(8,128)(2,1)S(1)}, u32[]{:S(2)}, u32[]{:S(2)}) collective-permute-start(bf16[4,528,128]{2,1,0:T(8,128)(2,1)S(1)} %get-tuple-element.347), channel_id=1, source_target_pairs={{0,12},{1,13},{2,14},{3,15},{4,8},{5,9},{6,10},{7,11},{8,4},{9,5},... | collective-permute-start | bytes 1622024 | tf_op jit(solution)/shard_map/ppermute | solution.py:78
  205.3 15.1 %collective-permute-start.52 = (bf16[4,528,128]{2,1,0:T(8,128)(2,1)S(1)}, bf16[4,528,128]{2,1,0:T(8,128)(2,1)S(1)}, u32[]{:S(2)}, u32[]{:S(2)}) collective-permute-start(bf16[4,528,128]{2,1,0:T(8,128)(2,1)S(1)} %get-tuple-element.348), channel_id=1, source_target_pairs={{0,15},{1,14},{2,13},{3,12},{4,11},{5,10},{6,9},{7,8},{8,7},{9,6},... | collective-permute-start | bytes 1622024 | tf_op jit(solution)/shard_map/ppermute | solution.py:78
  206.2 16.9 %collective-permute-start.50 = (bf16[4,528,128]{2,1,0:T(8,128)(2,1)S(1)}, bf16[4,528,128]{2,1,0:T(8,128)(2,1)S(1)}, u32[]{:S(2)}, u32[]{:S(2)}) collective-permute-start(bf16[4,528,128]{2,1,0:T(8,128)(2,1)S(1)} %get-tuple-element.346), channel_id=1, source_target_pairs={{0,3},{1,2},{2,1},{3,0},{4,7},{5,6},{6,5},{7,4},{8,11},{9,10},{10,... | collective-permute-start | bytes 1622024 | tf_op jit(solution)/shard_map/ppermute | solution.py:78

commit v7 on v6

--- a/solution.py
+++ b/solution.py
@@ -10,36 +10,29 @@
 
 HEAD_DIM = 128
 HAD = 128
-CHUNKS = ((0, 32), (32, 32), (64, 32), (96, 32))
+CHUNKS = ((0, 48), (48, 48), (96, 32))
+DIRECT = 1
 ORDER = (
     ("start", 0),
+    ("y_regroup", 0),
     ("start", 1),
-    ("start", 2),
-    ("y_regroup", 0),
-    ("start", 3),
     ("cross", 0),
     ("y_regroup", 1),
     ("y_regroup", 0),
+    ("start", 2),
     ("cross", 1),
     ("spread", 0),
     ("y_regroup", 1),
     ("y_regroup", 2),
-    ("regroup", 0),
+    ("cross", 2),
     ("spread", 1),
-    ("y_regroup", 3),
-    ("cross", 2),
-    ("cross", 3),
     ("y_regroup", 2),
+    ("regroup", 1),
+    ("spread", 2),
     ("pack", 0),
-    ("regroup", 1),
-    ("y_regroup", 3),
-    ("spread", 2),
-    ("spread", 3),
+    ("regroup", 2),
     ("pack", 1),
-    ("regroup", 2),
-    ("regroup", 3),
     ("pack", 2),
-    ("pack", 3),
 )
 TAIL = 16
 VMEM_BYTES = 12 * 1024 * 1024
@@ -221,17 +214,19 @@
         peaks = part if peaks is None else jnp.maximum(peaks, part)
     row_id = lax.broadcasted_iota(jnp.int32, (TAIL, HAD), 0)
     span = 2 * chans
-    for i, out_ref in enumerate(out_refs):
+    direct = len(out_refs) == 1
+    for i in range(4):
         for j in range(4):
-            owner = me ^ pairing_offset(core, 0, i) ^ pairing_offset(core, 1, j)
+            owner = 4 * i + j if direct else me ^ pairing_offset(core, 0, i) ^ pairing_offset(core, 1, j)
+            out_ref, to = (out_refs[0], 4 * i + j) if direct else (out_refs[i], j)
             head = 0
             for index in range(1, heads):
                 head = jnp.where(mine[index] == owner, index, head)
             rows = pl.ds(pl.multiple_of(head * span, 16), span)
             for s, (in_ref, index) in enumerate(blocks):
-                out_ref[j, s * span : (s + 1) * span, :] = in_ref[index, rows, :]
+                out_ref[to, s * span : (s + 1) * span, :] = in_ref[index, rows, :]
             peak = jnp.sum(jnp.where(row_id == head, peaks, 0.0), axis=0, keepdims=True)
-            out_ref[j, 8 * span :, :] = split_parts(jnp.broadcast_to(peak, (TAIL, HAD)), chans)
+            out_ref[to, 8 * span :, :] = split_parts(jnp.broadcast_to(peak, (TAIL, HAD)), chans)
 
 
 def pack_kernel(owners, heads, chunk, has_past, placement_ref, *refs):
@@ -249,16 +244,18 @@
         slot_ref[source] = count
         count = count + live
     lane = lax.broadcasted_iota(jnp.int32, (TAIL, HAD), 1)
-    depth = buffer.shape[0]
-    copies = [None] * depth
+    copies = []
     core = group & 1
     pair = jnp.where(core == 0, 2, 6)
     offsets = (0, 1, pair, pair ^ 1, pair ^ 4, pair ^ 5, 4, 5)
     blocks, rows = [], []
     for origin in range(owners):
         i, j = origin % 4, origin // 4
-        in_ref, index = (in_refs[3 + j], i) if j else (in_refs[i], 0)
-        source = me ^ pairing_offset(core, 0, i) ^ pairing_offset(core, 1, j)
+        if len(in_refs) == 1:
+            in_ref, index, source = in_refs[0], origin, origin
+        else:
+            in_ref, index = (in_refs[3 + j], i) if j else (in_refs[i], 0)
+            source = me ^ pairing_offset(core, 0, i) ^ pairing_offset(core, 1, j)
         live = live_ref[source] != 0
         slot = jnp.where(live, slot_ref[source], count + source - slot_ref[source])
         tail = in_ref[index, 16 * chans :, :].astype(jnp.float32)
@@ -272,20 +269,16 @@
     rows.append(jnp.zeros((HAD - owners, HAD), jnp.float32))
     scales = jnp.concatenate(rows, axis=0).T
     for origin, (in_ref, index, slot) in enumerate(blocks):
-        part = origin % depth
-        if copies[part] is not None:
-            copies[part].wait()
         scale = scales[:chans, origin : origin + 1]
         for s in range(8):
             for e in range(2):
                 start = (s * 2 + e) * chans
                 lanes = pl.ds(pl.multiple_of(((group ^ offsets[s]) * 2 + e) * HAD, HAD), HAD)
                 block = in_ref[index, start : start + chans, :]
-                buffer[part, :, lanes] = (block.astype(jnp.float32) * scale).astype(jnp.bfloat16)
-        copies[part] = pltpu.make_async_copy(
-            buffer.at[part], out_ref.at[0, slot, first : first + chans, :], sems.at[part]
-        )
-        copies[part].start()
+                buffer[origin, :, lanes] = (block.astype(jnp.float32) * scale).astype(jnp.bfloat16)
+        rows = out_ref.at[0, slot, first : first + chans, :]
+        copies.append(pltpu.make_async_copy(buffer.at[origin], rows, sems.at[origin]))
+        copies[-1].start()
     for copy in copies:
         copy.wait()
 
@@ -349,11 +342,15 @@
             token = outs[0]
             state[index] = y_first(outs)
         elif stage == "spread":
-            shapes = [(4, 16 * chans + TAIL)] * 4
+            direct = index < DIRECT
+            shapes = [(owners, 16 * chans + TAIL)] if direct else [(4, 16 * chans + TAIL)] * 4
             kernel = functools.partial(spread_kernel, heads, chans)
             outs = call(kernel, stage, shapes, placement, *arrays, table=True)
             token = outs[0]
-            state[index] = [outs[0]] + owner_hops(outs[1:], 0)
+            if direct:
+                state[index] = [lax.all_to_all(token, "tp", split_axis=0, concat_axis=0, tiled=True)]
+            else:
+                state[index] = [token] + owner_hops(outs[1:], 0)
         elif stage == "regroup":
             outs = call(regroup_kernel, stage, [arrays[0].shape[:2]] * 3, *arrays)
             token = outs[0]
@@ -368,8 +365,8 @@
                     jax.ShapeDtypeStruct((1, owners, HEAD_DIM, rows_local), jnp.bfloat16),
                 ],
                 scratch_shapes=[
-                    pltpu.VMEM((3, chans, rows_local), jnp.bfloat16),
-                    pltpu.SemaphoreType.DMA((3,)),
+                    pltpu.VMEM((owners, chans, rows_local), jnp.bfloat16),
+                    pltpu.SemaphoreType.DMA((owners,)),
                     pltpu.SMEM((owners,), jnp.int32),
                     pltpu.SMEM((owners,), jnp.int32),
                 ],

time: 229 us -> 217 us (0.948)
  the two profiles are of different devices: /device:TPU:30 before, /device:TPU:0 now
where the time goes in v7:
time: 217 us; the launch traced here: 216 us
  waiting for transfers between devices  106 us (49%)
  starting transfers between devices  63.2 us (29%)
  Pallas kernels  28.1 us (13%)
  local copies, waits for them, and re-layouts  17.4 us (8%)
    ppermute x36, waiting for transfers between devices, hop(): return lax.ppermute(array, BOTH, pairs)  106 us
    ppermute x36, starting transfers between devices, hop(): return lax.ppermute(array, BOTH, pairs)  55.3 us
    unnamed x52, local copies, waits for them, and re-layouts  17.4 us
    pallas_call x14, Pallas kernels, call(): pl.pallas_call(kernel, in_specs=[smem_spec] * table + [vmem_spec] * (len(...  12.2 us
    pallas_call x3, Pallas kernels, per_device(): pl.pallas_call(functools.partial(pack_kernel, owners, heads, chunk, bool(...  10.2 us
    all_to_all x1, starting transfers between devices, per_device(): lax.all_to_all(token, 'tp', split_axis=0, concat_axis=0, tiled=True)  7.9 us
    pallas_call x1, Pallas kernels, per_device(): pl.pallas_call(functools.partial(local_turn_kernel, rows_a), grid=(heads,...  5.63 us
  transfers between devices with their start and end apart: 37, of which 16 were waited for; matrix products, arithmetic and copies ran while one was open for 0% of the time, Pallas kernels for 9%

profile of v7, /device:TPU:0, one launch (start us, length us, event | category | flops | bytes accessed | tf_op | source)
XLA Modules:
  0.0 215.9 jit_solution(11375229476171789096)
XLA Ops:
  0.6 2.3 %copy-done.1 = bf16[2048,1152]{1,0:T(8,128)(2,1)S(1)} copy-done((bf16[2048,1152]{1,0:T(8,128)(2,1)S(1)}, bf16[2048,1152]{1,0:T(8,128)(2,1)}, u32[]{:S(2)}) %copy-start.1) | copy-done | bytes 4718616
  3.7 5.6 %local_turn.1 = (bf16[2,864,128]{2,1,0:T(8,128)(2,1)S(1)}, bf16[2,864,128]{2,1,0:T(8,128)(2,1)S(1)}, bf16[2,864,128]{2,1,0:T(8,128)(2,1)S(1)}, bf16[2,864,128]{2...) custom-call(bf16[2048,1152]{1,0:T(8,128)(2,1)S(1)} %copy-done.1, ...), custom_call_target="tpu_custom_call" | custom-call | tf_op jit(solution)/shard_map/local_turn/pallas_call | solution.py:308
  9.5 1.7 collective-permute-start.1
  11.2 1.5 collective-permute-start.2
  12.7 8.8 %collective-permute-done.1.refs_2_ = bf16[2,864,128]{2,1,0:T(8,128)(2,1)S(1)} collective-permute-done((bf16[2,864,128]{2,1,0:T(8,128)(2,1)S(1)}, bf16[2,864,128]{2,1,0:T(8,128)(2,1)S(1)}, u32[]{:S(2)}, u32[]{:S(2)}) %collective-permute-start.1) | collective-permute-done | bytes 442400 | tf_op jit(solution)/shard_map/ppermute | solution.py:71
  21.5 1.1 collective-permute-done.2.refs_3_
  22.7 3.1 %collective-permute-start.3 = (bf16[4,864,128]{2,1,0:T(8,128)(2,1)S(1)}, bf16[4,864,128]{2,1,0:T(8,128)(2,1)S(1)}, u32[]{:S(2)}, u32[]{:S(2)}) collective-permute-start(bf16[4,864,128]{2,1,0:T(8,128)(2,1)S(1)} %y_regroup.6), channel_id=1, source_target_pairs={{0,96},{1,97},{2,98},{3,99},{4,100},{5,101},{6,102},{7,103},{8,104... | collective-permute-start | bytes 2654216 | tf_op jit(solution)/shard_map/ppermute | solution.py:71
  26.1 2.8 %collective-permute-start.9 = (bf16[2,864,128]{2,1,0:T(8,128)(2,1)S(1)}, bf16[2,864,128]{2,1,0:T(8,128)(2,1)S(1)}, u32[]{:S(2)}, u32[]{:S(2)}) collective-permute-start(bf16[2,864,128]{2,1,0:T(8,128)(2,1)S(1)} %get-tuple-element.151), channel_id=1, source_target_pairs={{0,112},{1,113},{2,114},{3,115},{4,116},{5,117},{6,118},{7,119},{8... | collective-permute-start | bytes 1327112 | tf_op jit(solution)/shard_map/ppermute | solution.py:71
  28.9 12.9 %collective-permute-done.3.refs_4_ = bf16[4,864,128]{2,1,0:T(8,128)(2,1)S(1)} collective-permute-done((bf16[4,864,128]{2,1,0:T(8,128)(2,1)S(1)}, bf16[4,864,128]{2,1,0:T(8,128)(2,1)S(1)}, u32[]{:S(2)}, u32[]{:S(2)}) %collective-permute-start.3) | collective-permute-done | bytes 884768 | tf_op jit(solution)/shard_map/ppermute | solution.py:71
  41.8 1.1 cross.3
  43.4 2.6 %collective-permute-start.6 = (bf16[2,880,128]{2,1,0:T(8,128)(2,1)S(1)}, bf16[2,880,128]{2,1,0:T(8,128)(2,1)S(1)}, u32[]{:S(2)}, u32[]{:S(2)}) collective-permute-start(bf16[2,880,128]{2,1,0:T(8,128)(2,1)S(1)} %get-tuple-element.143), channel_id=1, source_target_pairs={{0,112},{1,113},{2,114},{3,115},{4,116},{5,117},{6,118},{7,119},{8... | collective-permute-start | bytes 1351688 | tf_op jit(solution)/shard_map/ppermute | solution.py:71
  46.1 2.9 %collective-permute-start.13 = (bf16[4,864,128]{2,1,0:T(8,128)(2,1)S(1)}, bf16[4,864,128]{2,1,0:T(8,128)(2,1)S(1)}, u32[]{:S(2)}, u32[]{:S(2)}) collective-permute-start(bf16[4,864,128]{2,1,0:T(8,128)(2,1)S(1)} %y_regroup.7), channel_id=1, source_target_pairs={{0,96},{1,97},{2,98},{3,99},{4,100},{5,101},{6,102},{7,103},{8,104... | collective-permute-start | bytes 2654216 | tf_op jit(solution)/shard_map/ppermute | solution.py:71
  49.1 7.2 %collective-permute-done.5.refs_2_ = bf16[2,880,128]{2,1,0:T(8,128)(2,1)S(1)} collective-permute-done((bf16[2,880,128]{2,1,0:T(8,128)(2,1)S(1)}, bf16[2,880,128]{2,1,0:T(8,128)(2,1)S(1)}, u32[]{:S(2)}, u32[]{:S(2)}) %collective-permute-start.5) | collective-permute-done | bytes 450592 | tf_op jit(solution)/shard_map/ppermute | solution.py:71
  56.3 2.9 %collective-permute-start.17 = (bf16[4,880,128]{2,1,0:T(8,128)(2,1)S(1)}, bf16[4,880,128]{2,1,0:T(8,128)(2,1)S(1)}, u32[]{:S(2)}, u32[]{:S(2)}) collective-permute-start(bf16[4,880,128]{2,1,0:T(8,128)(2,1)S(1)} %y_regroup.8), channel_id=1, source_target_pairs={{0,96},{1,97},{2,98},{3,99},{4,100},{5,101},{6,102},{7,103},{8,104... | collective-permute-start | bytes 2703368 | tf_op jit(solution)/shard_map/ppermute | solution.py:71
  59.2 7.2 %collective-permute-done.13.refs_4_ = bf16[4,864,128]{2,1,0:T(8,128)(2,1)S(1)} collective-permute-done((bf16[4,864,128]{2,1,0:T(8,128)(2,1)S(1)}, bf16[4,864,128]{2,1,0:T(8,128)(2,1)S(1)}, u32[]{:S(2)}, u32[]{:S(2)}) %collective-permute-start.13) | collective-permute-done | bytes 884768 | tf_op jit(solution)/shard_map/ppermute | solution.py:71
  66.4 1.9 cross.4
  70.7 5.4 %collective-permute-done.17.refs_4_ = bf16[4,880,128]{2,1,0:T(8,128)(2,1)S(1)} collective-permute-done((bf16[4,880,128]{2,1,0:T(8,128)(2,1)S(1)}, bf16[4,880,128]{2,1,0:T(8,128)(2,1)S(1)}, u32[]{:S(2)}, u32[]{:S(2)}) %collective-permute-start.17) | collective-permute-done | bytes 901152 | tf_op jit(solution)/shard_map/ppermute | solution.py:71
  76.1 0.9 spread.3
  77.0 1.7 copy-done
  78.6 7.9 %all-to-all-start = ((bf16[16,784,128]{2,1,0:T(8,128)(2,1)}), bf16[16,784,128]{2,1,0:T(8,128)(2,1)S(1)}, u32[]{:S(2)}, u32[]{:S(2)}) async-start(bf16[16,784,128]{2,1,0:T(8,128)(2,1)} %copy-done), calls=%async_computation | async-start | bytes 6422528 | tf_op jit(solution)/shard_map/all_to_all | solution.py:351
  86.6 1.5 collective-permute-start.16
  88.8 2.5 %collective-permute-start.12 = (bf16[2,576,128]{2,1,0:T(8,128)(2,1)}, bf16[2,576,128]{2,1,0:T(8,128)(2,1)S(1)}, u32[]{:S(2)}, u32[]{:S(2)}) collective-permute-start(bf16[2,576,128]{2,1,0:T(8,128)(2,1)} %copy-done.23), channel_id=1, source_target_pairs={{0,112},{1,113},{2,114},{3,115},{4,116},{5,117},{6,118},{7,119},{8... | collective-permute-start | bytes 884744 | tf_op jit(solution)/shard_map/ppermute | solution.py:71
  91.3 8.6 %collective-permute-done.15.refs_2_ = bf16[2,880,128]{2,1,0:T(8,128)(2,1)S(1)} collective-permute-done((bf16[2,880,128]{2,1,0:T(8,128)(2,1)}, bf16[2,880,128]{2,1,0:T(8,128)(2,1)S(1)}, u32[]{:S(2)}, u32[]{:S(2)}) %collective-permute-start.15) | collective-permute-done | bytes 450592 | tf_op jit(solution)/shard_map/ppermute | solution.py:71
  100.0 1.0 copy-done.17
  101.0 1.1 y_regroup.9
  102.1 2.9 %collective-permute-start.22 = (bf16[4,880,128]{2,1,0:T(8,128)(2,1)S(1)}, bf16[4,880,128]{2,1,0:T(8,128)(2,1)S(1)}, u32[]{:S(2)}, u32[]{:S(2)}) collective-permute-start(bf16[4,880,128]{2,1,0:T(8,128)(2,1)S(1)} %y_regroup.9), channel_id=1, source_target_pairs={{0,96},{1,97},{2,98},{3,99},{4,100},{5,101},{6,102},{7,103},{8,104... | collective-permute-start | bytes 2703368 | tf_op jit(solution)/shard_map/ppermute | solution.py:71
  105.0 0.9 collective-permute-done.11.refs_2_
  105.9 3.3 %collective-permute-start.18 = (bf16[4,576,128]{2,1,0:T(8,128)(2,1)S(1)}, bf16[4,576,128]{2,1,0:T(8,128)(2,1)S(1)}, u32[]{:S(2)}, u32[]{:S(2)}) collective-permute-start(bf16[4,576,128]{2,1,0:T(8,128)(2,1)S(1)} %y_regroup.10), channel_id=1, source_target_pairs={{0,96},{1,97},{2,98},{3,99},{4,100},{5,101},{6,102},{7,103},{8,104... | collective-permute-start | bytes 1769480 | tf_op jit(solution)/shard_map/ppermute | solution.py:71
  109.3 13.6 %collective-permute-done.18.refs_4_ = bf16[4,576,128]{2,1,0:T(8,128)(2,1)S(1)} collective-permute-done((bf16[4,576,128]{2,1,0:T(8,128)(2,1)S(1)}, bf16[4,576,128]{2,1,0:T(8,128)(2,1)S(1)}, u32[]{:S(2)}, u32[]{:S(2)}) %collective-permute-start.18) | collective-permute-done | bytes 589856 | tf_op jit(solution)/shard_map/ppermute | solution.py:71
  122.9 0.8 cross.5
  124.4 2.4 %collective-permute-start.21 = (bf16[2,592,128]{2,1,0:T(8,128)(2,1)S(1)}, bf16[2,592,128]{2,1,0:T(8,128)(2,1)S(1)}, u32[]{:S(2)}, u32[]{:S(2)}) collective-permute-start(bf16[2,592,128]{2,1,0:T(8,128)(2,1)S(1)} %get-tuple-element.194), channel_id=1, source_target_pairs={{0,112},{1,113},{2,114},{3,115},{4,116},{5,117},{6,118},{7,119},{8... | collective-permute-start | bytes 909320 | tf_op jit(solution)/shard_map/ppermute | solution.py:71
  126.8 1.0 copy-done.18
  127.8 1.3 spread.4
  129.2 2.1 collective-permute-start.24
  131.3 1.5 collective-permute-start.25
  132.9 1.0 collective-permute-done.20.refs_2_
  134.0 2.7 %collective-permute-start.23 = (bf16[4,592,128]{2,1,0:T(8,128)(2,1)S(1)}, bf16[4,592,128]{2,1,0:T(8,128)(2,1)S(1)}, u32[]{:S(2)}, u32[]{:S(2)}) collective-permute-start(bf16[4,592,128]{2,1,0:T(8,128)(2,1)S(1)} %y_regroup.11), channel_id=1, source_target_pairs={{0,96},{1,97},{2,98},{3,99},{4,100},{5,101},{6,102},{7,103},{8,104... | collective-permute-start | bytes 1818632 | tf_op jit(solution)/shard_map/ppermute | solution.py:71
  136.7 4.9 %collective-permute-done.24.refs_1_ = bf16[4,784,128]{2,1,0:T(8,128)(2,1)S(1)} collective-permute-done((bf16[4,784,128]{2,1,0:T(8,128)(2,1)S(1)}, bf16[4,784,128]{2,1,0:T(8,128)(2,1)S(1)}, u32[]{:S(2)}, u32[]{:S(2)}) %collective-permute-start.24) | collective-permute-done | bytes 802848 | tf_op jit(solution)/shard_map/ppermute | solution.py:71
  141.6 10.4 %collective-permute-done.25.refs_2_ = bf16[4,784,128]{2,1,0:T(8,128)(2,1)S(1)} collective-permute-done((bf16[4,784,128]{2,1,0:T(8,128)(2,1)S(1)}, bf16[4,784,128]{2,1,0:T(8,128)(2,1)S(1)}, u32[]{:S(2)}, u32[]{:S(2)}) %collective-permute-start.25) | collective-permute-done | bytes 802848 | tf_op jit(solution)/shard_map/ppermute | solution.py:71
  152.1 1.7 regroup.2
  153.8 1.8 spread.5
  155.5 0.8 copy-done.10
  156.4 0.9 collective-permute-start.27
  157.2 2.4 %collective-permute-start.34 = (bf16[4,784,128]{2,1,0:T(8,128)(2,1)}, bf16[4,784,128]{2,1,0:T(8,128)(2,1)}, u32[]{:S(2)}, u32[]{:S(2)}) collective-permute-start(bf16[4,784,128]{2,1,0:T(8,128)(2,1)} %get-tuple-element.231), channel_id=1, source_target_pairs={{0,12},{1,13},{2,14},{3,15},{4,8},{5,9},{6,10},{7,11},{8,4},{9,5},... | collective-permute-start | bytes 2408456 | tf_op jit(solution)/shard_map/ppermute | solution.py:71
  159.9 2.7 %collective-permute-start.29 = (bf16[4,528,128]{2,1,0:T(8,128)(2,1)}, bf16[4,528,128]{2,1,0:T(8,128)(2,1)}, u32[]{:S(2)}, u32[]{:S(2)}) collective-permute-start(bf16[4,528,128]{2,1,0:T(8,128)(2,1)} %get-tuple-element.221), channel_id=1, source_target_pairs={{0,5},{1,4},{2,7},{3,6},{4,1},{5,0},{6,3},{7,2},{8,13},{9,12},{10,... | collective-permute-start | bytes 1622024 | tf_op jit(solution)/shard_map/ppermute | solution.py:71
  162.5 2.1 collective-permute-start.35
  164.6 1.2 collective-permute-done.27.refs_1_
  165.9 0.8 copy-done.13
  166.7 2.1 collective-permute-start.33
  168.8 2.8 %pack.3 = (f32[16,128]{1,0:T(8,128)S(1)}, bf16[1,16,128,2048]{3,2,1,0:T(8,128)(2,1)}) custom-call(s32[144]{0:T(256)S(1)} %copy-done.19, bf16[16,784,128]{2,1,0:T(8,128)(2,1)S(1)} %all-to-all-done.refs_0_), custom_call_target="tpu_custom_call" | custom-call | tf_op jit(solution)/shard_map/pack/pallas_call | solution.py:359
  171.6 17.9 %collective-permute-done.28.refs_2_ = bf16[4,528,128]{2,1,0:T(8,128)(2,1)} collective-permute-done((bf16[4,528,128]{2,1,0:T(8,128)(2,1)}, bf16[4,528,128]{2,1,0:T(8,128)(2,1)}, u32[]{:S(2)}, u32[]{:S(2)}) %collective-permute-start.28) | collective-permute-done | bytes 540704 | tf_op jit(solution)/shard_map/ppermute | solution.py:71
  189.5 1.0 copy-done.11
  190.5 1.0 copy-done.14
  191.6 1.3 regroup.3
  192.9 0.9 collective-permute-start.31
  193.8 4.4 %collective-permute-start.32 = (bf16[4,528,128]{2,1,0:T(8,128)(2,1)S(1)}, bf16[4,528,128]{2,1,0:T(8,128)(2,1)S(1)}, u32[]{:S(2)}, u32[]{:S(2)}) collective-permute-start(bf16[4,528,128]{2,1,0:T(8,128)(2,1)S(1)} %get-tuple-element.230), channel_id=1, source_target_pairs={{0,15},{1,14},{2,13},{3,12},{4,11},{5,10},{6,9},{7,8},{8,7},{9,6},... | collective-permute-start | bytes 1622024 | tf_op jit(solution)/shard_map/ppermute | solution.py:71
  198.9 1.1 copy-done.3
  200.0 1.1 copy-done.5
  201.2 1.1 copy-done.7
  202.3 1.1 copy-done.9
  203.5 3.9 %pack.4 = (f32[16,128]{1,0:T(8,128)S(1)}, bf16[1,16,128,2048]{3,2,1,0:T(8,128)(2,1)}) custom-call(s32[144]{0:T(256)S(1)} %copy-done.19, bf16[4,784,128]{2,1,0:T(8,128)(2,1)S(1)} %copy-done.3, bf16[4,784,128]{2,1,0:T(8,128)(2,1)S(1)} %copy-done.5, bf16[4,784,128]{2,1,0:T(8,128)(2,1)S(1)} %copy-done.7, ...), custom_call_target="tpu_custom_call", output_to_operand_aliasing={{1}: (9, {})} | custom-call | tf_op jit(solution)/shard_map/pack/pallas_call | solution.py:359
  207.3 2.0 collective-permute-done.31.refs_5_
  209.3 2.7 %collective-permute-done.30.refs_4_ = bf16[4,528,128]{2,1,0:T(8,128)(2,1)S(1)} collective-permute-done((bf16[4,528,128]{2,1,0:T(8,128)(2,1)S(1)}, bf16[4,528,128]{2,1,0:T(8,128)(2,1)S(1)}, u32[]{:S(2)}, u32[]{:S(2)}) %collective-permute-start.30) | collective-permute-done | bytes 540704 | tf_op jit(solution)/shard_map/ppermute | solution.py:71
  212.1 3.6 %pack.5 = (f32[16,128]{1,0:T(8,128)}, bf16[1,16,128,2048]{3,2,1,0:T(8,128)(2,1)}) custom-call(s32[144]{0:T(256)S(1)} %copy-done.19, bf16[4,528,128]{2,1,0:T(8,128)(2,1)S(1)} %copy-done.12, bf16[4,528,128]{2,1,0:T(8,128)(2,1)S(1)} %copy-done.15, bf16[4,528,128]{2,1,0:T(8,128)(2,1)} %collective-permute-done.28.refs_2_, ...), custom_call_target="tpu_custom_call", output_to_operand_aliasing={{1}: (9, {})} | custom-call | tf_op jit(solution)/shard_map/pack/pallas_call | solution.py:359
  (80 shorter events, 6.9 us)
Async XLA Ops:
  0.6 2.3 %copy-start.1 = (bf16[2048,1152]{1,0:T(8,128)(2,1)S(1)}, bf16[2048,1152]{1,0:T(8,128)(2,1)}, u32[]{:S(2)}) copy-start(bf16[2048,1152]{1,0:T(8,128)(2,1)} %weight_ref.1) | copy-start | bytes 14155780
  3.0 0.8 copy-start.20
  3.7 72.3 %copy-start.19 = (s32[144]{0:T(256)S(1)}, s32[144]{0:T(256)}, u32[]{:S(2)}) copy-start(s32[144]{0:T(256)} %placement_ref.11) | copy-start | bytes 1732
  9.4 16.5 %copy-start.24 = (bf16[2,576,128]{2,1,0:T(8,128)(2,1)}, bf16[2,576,128]{2,1,0:T(8,128)(2,1)S(1)}, u32[]{:S(2)}) copy-start(bf16[2,576,128]{2,1,0:T(8,128)(2,1)S(1)} %get-tuple-element.162) | copy-start | bytes 884740
  9.4 16.5 %copy-start.25 = (bf16[2,576,128]{2,1,0:T(8,128)(2,1)}, bf16[2,576,128]{2,1,0:T(8,128)(2,1)S(1)}, u32[]{:S(2)}) copy-start(bf16[2,576,128]{2,1,0:T(8,128)(2,1)S(1)} %get-tuple-element.161) | copy-start | bytes 884740
  9.4 16.5 %copy-start.23 = (bf16[2,576,128]{2,1,0:T(8,128)(2,1)}, bf16[2,576,128]{2,1,0:T(8,128)(2,1)S(1)}, u32[]{:S(2)}) copy-start(bf16[2,576,128]{2,1,0:T(8,128)(2,1)S(1)} %get-tuple-element.163) | copy-start | bytes 884740
  9.4 3.3 %collective-permute-start = (bf16[2,864,128]{2,1,0:T(8,128)(2,1)S(1)}, bf16[2,864,128]{2,1,0:T(8,128)(2,1)S(1)}, u32[]{:S(2)}, u32[]{:S(2)}) collective-permute-start(bf16[2,864,128]{2,1,0:T(8,128)(2,1)S(1)} %get-tuple-element.132), channel_id=1, source_target_pairs={{0,16},{1,17},{2,18},{3,19},{4,20},{5,21},{6,22},{7,23},{8,24},{9,... | collective-permute-start | bytes 1327112 | tf_op jit(solution)/shard_map/ppermute | solution.py:71
  9.5 12.0 %collective-permute-start.1 = (bf16[2,864,128]{2,1,0:T(8,128)(2,1)S(1)}, bf16[2,864,128]{2,1,0:T(8,128)(2,1)S(1)}, u32[]{:S(2)}, u32[]{:S(2)}) collective-permute-start(bf16[2,864,128]{2,1,0:T(8,128)(2,1)S(1)} %get-tuple-element.133), channel_id=1, source_target_pairs={{0,32},{1,33},{2,34},{3,35},{4,36},{5,37},{6,38},{7,39},{8,40},{9,... | collective-permute-start | bytes 1327112 | tf_op jit(solution)/shard_map/ppermute | solution.py:71
  11.2 11.4 %collective-permute-start.2 = (bf16[2,864,128]{2,1,0:T(8,128)(2,1)S(1)}, bf16[2,864,128]{2,1,0:T(8,128)(2,1)S(1)}, u32[]{:S(2)}, u32[]{:S(2)}) collective-permute-start(bf16[2,864,128]{2,1,0:T(8,128)(2,1)S(1)} %get-tuple-element.134), channel_id=1, source_target_pairs={{0,112},{1,113},{2,114},{3,115},{4,116},{5,117},{6,118},{7,119},{8... | collective-permute-start | bytes 1327112 | tf_op jit(solution)/shard_map/ppermute | solution.py:71
  22.7 19.1 %collective-permute-start.3 = (bf16[4,864,128]{2,1,0:T(8,128)(2,1)S(1)}, bf16[4,864,128]{2,1,0:T(8,128)(2,1)S(1)}, u32[]{:S(2)}, u32[]{:S(2)}) collective-permute-start(bf16[4,864,128]{2,1,0:T(8,128)(2,1)S(1)} %y_regroup.6), channel_id=1, source_target_pairs={{0,96},{1,97},{2,98},{3,99},{4,100},{5,101},{6,102},{7,103},{8,104... | collective-permute-start | bytes 2654216 | tf_op jit(solution)/shard_map/ppermute | solution.py:71
  25.9 17.6 %collective-permute-start.7 = (bf16[2,864,128]{2,1,0:T(8,128)(2,1)S(1)}, bf16[2,864,128]{2,1,0:T(8,128)(2,1)S(1)}, u32[]{:S(2)}, u32[]{:S(2)}) collective-permute-start(bf16[2,864,128]{2,1,0:T(8,128)(2,1)S(1)} %get-tuple-element.149), channel_id=1, source_target_pairs={{0,16},{1,17},{2,18},{3,19},{4,20},{5,21},{6,22},{7,23},{8,24},{9,... | collective-permute-start | bytes 1327112 | tf_op jit(solution)/shard_map/ppermute | solution.py:71
  25.9 20.2 %collective-permute-start.8 = (bf16[2,864,128]{2,1,0:T(8,128)(2,1)S(1)}, bf16[2,864,128]{2,1,0:T(8,128)(2,1)S(1)}, u32[]{:S(2)}, u32[]{:S(2)}) collective-permute-start(bf16[2,864,128]{2,1,0:T(8,128)(2,1)S(1)} %get-tuple-element.150), channel_id=1, source_target_pairs={{0,32},{1,33},{2,34},{3,35},{4,36},{5,37},{6,38},{7,39},{8,40},{9,... | collective-permute-start | bytes 1327112 | tf_op jit(solution)/shard_map/ppermute | solution.py:71
  26.1 20.0 %collective-permute-start.9 = (bf16[2,864,128]{2,1,0:T(8,128)(2,1)S(1)}, bf16[2,864,128]{2,1,0:T(8,128)(2,1)S(1)}, u32[]{:S(2)}, u32[]{:S(2)}) collective-permute-start(bf16[2,864,128]{2,1,0:T(8,128)(2,1)S(1)} %get-tuple-element.151), channel_id=1, source_target_pairs={{0,112},{1,113},{2,114},{3,115},{4,116},{5,117},{6,118},{7,119},{8... | collective-permute-start | bytes 1327112 | tf_op jit(solution)/shard_map/ppermute | solution.py:71
  42.9 6.1 %collective-permute-start.4 = (bf16[2,880,128]{2,1,0:T(8,128)(2,1)S(1)}, bf16[2,880,128]{2,1,0:T(8,128)(2,1)S(1)}, u32[]{:S(2)}, u32[]{:S(2)}) collective-permute-start(bf16[2,880,128]{2,1,0:T(8,128)(2,1)S(1)} %get-tuple-element.141), channel_id=1, source_target_pairs={{0,16},{1,17},{2,18},{3,19},{4,20},{5,21},{6,22},{7,23},{8,24},{9,... | collective-permute-start | bytes 1351688 | tf_op jit(solution)/shard_map/ppermute | solution.py:71
  43.0 13.3 %collective-permute-start.5 = (bf16[2,880,128]{2,1,0:T(8,128)(2,1)S(1)}, bf16[2,880,128]{2,1,0:T(8,128)(2,1)S(1)}, u32[]{:S(2)}, u32[]{:S(2)}) collective-permute-start(bf16[2,880,128]{2,1,0:T(8,128)(2,1)S(1)} %get-tuple-element.142), channel_id=1, source_target_pairs={{0,32},{1,33},{2,34},{3,35},{4,36},{5,37},{6,38},{7,39},{8,40},{9,... | collective-permute-start | bytes 1351688 | tf_op jit(solution)/shard_map/ppermute | solution.py:71
  43.4 12.8 %collective-permute-start.6 = (bf16[2,880,128]{2,1,0:T(8,128)(2,1)S(1)}, bf16[2,880,128]{2,1,0:T(8,128)(2,1)S(1)}, u32[]{:S(2)}, u32[]{:S(2)}) collective-permute-start(bf16[2,880,128]{2,1,0:T(8,128)(2,1)S(1)} %get-tuple-element.143), channel_id=1, source_target_pairs={{0,112},{1,113},{2,114},{3,115},{4,116},{5,117},{6,118},{7,119},{8... | collective-permute-start | bytes 1351688 | tf_op jit(solution)/shard_map/ppermute | solution.py:71
  46.1 20.3 %collective-permute-start.13 = (bf16[4,864,128]{2,1,0:T(8,128)(2,1)S(1)}, bf16[4,864,128]{2,1,0:T(8,128)(2,1)S(1)}, u32[]{:S(2)}, u32[]{:S(2)}) collective-permute-start(bf16[4,864,128]{2,1,0:T(8,128)(2,1)S(1)} %y_regroup.7), channel_id=1, source_target_pairs={{0,96},{1,97},{2,98},{3,99},{4,100},{5,101},{6,102},{7,103},{8,104... | collective-permute-start | bytes 2654216 | tf_op jit(solution)/shard_map/ppermute | solution.py:71
  56.3 19.7 %collective-permute-start.17 = (bf16[4,880,128]{2,1,0:T(8,128)(2,1)S(1)}, bf16[4,880,128]{2,1,0:T(8,128)(2,1)S(1)}, u32[]{:S(2)}, u32[]{:S(2)}) collective-permute-start(bf16[4,880,128]{2,1,0:T(8,128)(2,1)S(1)} %y_regroup.8), channel_id=1, source_target_pairs={{0,96},{1,97},{2,98},{3,99},{4,100},{5,101},{6,102},{7,103},{8,104... | collective-permute-start | bytes 2703368 | tf_op jit(solution)/shard_map/ppermute | solution.py:71
  68.3 0.8 copy-start.16
  69.1 0.8 copy-start.21
  69.9 0.8 copy-start.22
  70.7 18.2 %collective-permute-start.14 = (bf16[2,880,128]{2,1,0:T(8,128)(2,1)}, bf16[2,880,128]{2,1,0:T(8,128)(2,1)}, u32[]{:S(2)}, u32[]{:S(2)}) collective-permute-start(bf16[2,880,128]{2,1,0:T(8,128)(2,1)} %get-tuple-element.170), channel_id=1, source_target_pairs={{0,16},{1,17},{2,18},{3,19},{4,20},{5,21},{6,22},{7,23},{8,24},{9,... | collective-permute-start | bytes 1351688 | tf_op jit(solution)/shard_map/ppermute | solution.py:71
  76.9 1.7 copy-start
  78.6 90.2 %all-to-all-start = ((bf16[16,784,128]{2,1,0:T(8,128)(2,1)}), bf16[16,784,128]{2,1,0:T(8,128)(2,1)S(1)}, u32[]{:S(2)}, u32[]{:S(2)}) async-start(bf16[16,784,128]{2,1,0:T(8,128)(2,1)} %copy-done), calls=%async_computation | async-start | bytes 6422528 | tf_op jit(solution)/shard_map/all_to_all | solution.py:351
  86.5 13.4 %collective-permute-start.15 = (bf16[2,880,128]{2,1,0:T(8,128)(2,1)}, bf16[2,880,128]{2,1,0:T(8,128)(2,1)S(1)}, u32[]{:S(2)}, u32[]{:S(2)}) collective-permute-start(bf16[2,880,128]{2,1,0:T(8,128)(2,1)} %copy-done.22), channel_id=1, source_target_pairs={{0,32},{1,33},{2,34},{3,35},{4,36},{5,37},{6,38},{7,39},{8,40},{9,... | collective-permute-start | bytes 1351688 | tf_op jit(solution)/shard_map/ppermute | solution.py:71
  86.6 13.3 %collective-permute-start.16 = (bf16[2,880,128]{2,1,0:T(8,128)(2,1)}, bf16[2,880,128]{2,1,0:T(8,128)(2,1)S(1)}, u32[]{:S(2)}, u32[]{:S(2)}) collective-permute-start(bf16[2,880,128]{2,1,0:T(8,128)(2,1)} %copy-done.21), channel_id=1, source_target_pairs={{0,112},{1,113},{2,114},{3,115},{4,116},{5,117},{6,118},{7,119},{8... | collective-permute-start | bytes 1351688 | tf_op jit(solution)/shard_map/ppermute | solution.py:71
  88.2 16.8 %collective-permute-start.10 = (bf16[2,576,128]{2,1,0:T(8,128)(2,1)}, bf16[2,576,128]{2,1,0:T(8,128)(2,1)S(1)}, u32[]{:S(2)}, u32[]{:S(2)}) collective-permute-start(bf16[2,576,128]{2,1,0:T(8,128)(2,1)} %copy-done.25), channel_id=1, source_target_pairs={{0,16},{1,17},{2,18},{3,19},{4,20},{5,21},{6,22},{7,23},{8,24},{9,... | collective-permute-start | bytes 884744 | tf_op jit(solution)/shard_map/ppermute | solution.py:71
  88.8 17.1 %collective-permute-start.11 = (bf16[2,576,128]{2,1,0:T(8,128)(2,1)}, bf16[2,576,128]{2,1,0:T(8,128)(2,1)S(1)}, u32[]{:S(2)}, u32[]{:S(2)}) collective-permute-start(bf16[2,576,128]{2,1,0:T(8,128)(2,1)} %copy-done.24), channel_id=1, source_target_pairs={{0,32},{1,33},{2,34},{3,35},{4,36},{5,37},{6,38},{7,39},{8,40},{9,... | collective-permute-start | bytes 884744 | tf_op jit(solution)/shard_map/ppermute | solution.py:71
  88.8 17.0 %collective-permute-start.12 = (bf16[2,576,128]{2,1,0:T(8,128)(2,1)}, bf16[2,576,128]{2,1,0:T(8,128)(2,1)S(1)}, u32[]{:S(2)}, u32[]{:S(2)}) collective-permute-start(bf16[2,576,128]{2,1,0:T(8,128)(2,1)} %copy-done.23), channel_id=1, source_target_pairs={{0,112},{1,113},{2,114},{3,115},{4,116},{5,117},{6,118},{7,119},{8... | collective-permute-start | bytes 884744 | tf_op jit(solution)/shard_map/ppermute | solution.py:71
  100.0 1.0 copy-start.17
  102.1 24.7 %collective-permute-start.22 = (bf16[4,880,128]{2,1,0:T(8,128)(2,1)S(1)}, bf16[4,880,128]{2,1,0:T(8,128)(2,1)S(1)}, u32[]{:S(2)}, u32[]{:S(2)}) collective-permute-start(bf16[4,880,128]{2,1,0:T(8,128)(2,1)S(1)} %y_regroup.9), channel_id=1, source_target_pairs={{0,96},{1,97},{2,98},{3,99},{4,100},{5,101},{6,102},{7,103},{8,104... | collective-permute-start | bytes 2703368 | tf_op jit(solution)/shard_map/ppermute | solution.py:71
  105.9 17.0 %collective-permute-start.18 = (bf16[4,576,128]{2,1,0:T(8,128)(2,1)S(1)}, bf16[4,576,128]{2,1,0:T(8,128)(2,1)S(1)}, u32[]{:S(2)}, u32[]{:S(2)}) collective-permute-start(bf16[4,576,128]{2,1,0:T(8,128)(2,1)S(1)} %y_regroup.10), channel_id=1, source_target_pairs={{0,96},{1,97},{2,98},{3,99},{4,100},{5,101},{6,102},{7,103},{8,104... | collective-permute-start | bytes 1769480 | tf_op jit(solution)/shard_map/ppermute | solution.py:71
  123.7 9.0 %collective-permute-start.19 = (bf16[2,592,128]{2,1,0:T(8,128)(2,1)S(1)}, bf16[2,592,128]{2,1,0:T(8,128)(2,1)S(1)}, u32[]{:S(2)}, u32[]{:S(2)}) collective-permute-start(bf16[2,592,128]{2,1,0:T(8,128)(2,1)S(1)} %get-tuple-element.192), channel_id=1, source_target_pairs={{0,16},{1,17},{2,18},{3,19},{4,20},{5,21},{6,22},{7,23},{8,24},{9,... | collective-permute-start | bytes 909320 | tf_op jit(solution)/shard_map/ppermute | solution.py:71
  124.0 9.9 %collective-permute-start.20 = (bf16[2,592,128]{2,1,0:T(8,128)(2,1)S(1)}, bf16[2,592,128]{2,1,0:T(8,128)(2,1)S(1)}, u32[]{:S(2)}, u32[]{:S(2)}) collective-permute-start(bf16[2,592,128]{2,1,0:T(8,128)(2,1)S(1)} %get-tuple-element.193), channel_id=1, source_target_pairs={{0,32},{1,33},{2,34},{3,35},{4,36},{5,37},{6,38},{7,39},{8,40},{9,... | collective-permute-start | bytes 909320 | tf_op jit(solution)/shard_map/ppermute | solution.py:71
  124.4 9.5 %collective-permute-start.21 = (bf16[2,592,128]{2,1,0:T(8,128)(2,1)S(1)}, bf16[2,592,128]{2,1,0:T(8,128)(2,1)S(1)}, u32[]{:S(2)}, u32[]{:S(2)}) collective-permute-start(bf16[2,592,128]{2,1,0:T(8,128)(2,1)S(1)} %get-tuple-element.194), channel_id=1, source_target_pairs={{0,112},{1,113},{2,114},{3,115},{4,116},{5,117},{6,118},{7,119},{8... | collective-permute-start | bytes 909320 | tf_op jit(solution)/shard_map/ppermute | solution.py:71
  126.8 1.0 copy-start.18
  129.2 36.7 %copy-start.2 = (bf16[4,784,128]{2,1,0:T(8,128)(2,1)}, bf16[4,784,128]{2,1,0:T(8,128)(2,1)S(1)}, u32[]{:S(2)}) copy-start(bf16[4,784,128]{2,1,0:T(8,128)(2,1)S(1)} %get-tuple-element.233.refs_0_) | copy-start | bytes 2408452
  129.2 12.4 %collective-permute-start.24 = (bf16[4,784,128]{2,1,0:T(8,128)(2,1)S(1)}, bf16[4,784,128]{2,1,0:T(8,128)(2,1)S(1)}, u32[]{:S(2)}, u32[]{:S(2)}) collective-permute-start(bf16[4,784,128]{2,1,0:T(8,128)(2,1)S(1)} %get-tuple-element.205), channel_id=1, source_target_pairs={{0,1},{1,0},{2,3},{3,2},{4,5},{5,4},{6,7},{7,6},{8,9},{9,8},{10,11... | collective-permute-start | bytes 2408456 | tf_op jit(solution)/shard_map/ppermute | solution.py:71
  131.3 20.8 %collective-permute-start.25 = (bf16[4,784,128]{2,1,0:T(8,128)(2,1)S(1)}, bf16[4,784,128]{2,1,0:T(8,128)(2,1)S(1)}, u32[]{:S(2)}, u32[]{:S(2)}) collective-permute-start(bf16[4,784,128]{2,1,0:T(8,128)(2,1)S(1)} %get-tuple-element.206), channel_id=1, source_target_pairs={{0,4},{1,5},{2,6},{3,7},{4,0},{5,1},{6,2},{7,3},{8,12},{9,13},{10,... | collective-permute-start | bytes 2408456 | tf_op jit(solution)/shard_map/ppermute | solution.py:71
  132.8 19.3 %collective-permute-start.26 = (bf16[4,784,128]{2,1,0:T(8,128)(2,1)S(1)}, bf16[4,784,128]{2,1,0:T(8,128)(2,1)S(1)}, u32[]{:S(2)}, u32[]{:S(2)}) collective-permute-start(bf16[4,784,128]{2,1,0:T(8,128)(2,1)S(1)} %get-tuple-element.207), channel_id=1, source_target_pairs={{0,5},{1,4},{2,7},{3,6},{4,1},{5,0},{6,3},{7,2},{8,13},{9,12},{10,... | collective-permute-start | bytes 2408456 | tf_op jit(solution)/shard_map/ppermute | solution.py:71
  134.0 19.8 %collective-permute-start.23 = (bf16[4,592,128]{2,1,0:T(8,128)(2,1)S(1)}, bf16[4,592,128]{2,1,0:T(8,128)(2,1)S(1)}, u32[]{:S(2)}, u32[]{:S(2)}) collective-permute-start(bf16[4,592,128]{2,1,0:T(8,128)(2,1)S(1)} %y_regroup.11), channel_id=1, source_target_pairs={{0,96},{1,97},{2,98},{3,99},{4,100},{5,101},{6,102},{7,103},{8,104... | collective-permute-start | bytes 1818632 | tf_op jit(solution)/shard_map/ppermute | solution.py:71
  141.6 24.2 %copy-start.4 = (bf16[4,784,128]{2,1,0:T(8,128)(2,1)}, bf16[4,784,128]{2,1,0:T(8,128)(2,1)S(1)}, u32[]{:S(2)}) copy-start(bf16[4,784,128]{2,1,0:T(8,128)(2,1)S(1)} %collective-permute-done.24.refs_1_) | copy-start | bytes 2408452
  152.1 13.8 %copy-start.6 = (bf16[4,784,128]{2,1,0:T(8,128)(2,1)}, bf16[4,784,128]{2,1,0:T(8,128)(2,1)S(1)}, u32[]{:S(2)}) copy-start(bf16[4,784,128]{2,1,0:T(8,128)(2,1)S(1)} %collective-permute-done.25.refs_2_) | copy-start | bytes 2408452
  152.1 13.8 %copy-start.8 = (bf16[4,784,128]{2,1,0:T(8,128)(2,1)}, bf16[4,784,128]{2,1,0:T(8,128)(2,1)S(1)}, u32[]{:S(2)}) copy-start(bf16[4,784,128]{2,1,0:T(8,128)(2,1)S(1)} %collective-permute-done.26.refs_3_) | copy-start | bytes 2408452
  155.5 0.8 copy-start.10
  156.4 9.5 %collective-permute-start.27 = (bf16[4,528,128]{2,1,0:T(8,128)(2,1)S(1)}, bf16[4,528,128]{2,1,0:T(8,128)(2,1)S(1)}, u32[]{:S(2)}, u32[]{:S(2)}) collective-permute-start(bf16[4,528,128]{2,1,0:T(8,128)(2,1)S(1)} %get-tuple-element.219), channel_id=1, source_target_pairs={{0,1},{1,0},{2,3},{3,2},{4,5},{5,4},{6,7},{7,6},{8,9},{9,8},{10,11... | collective-permute-start | bytes 1622024 | tf_op jit(solution)/shard_map/ppermute | solution.py:71
  157.2 41.0 %collective-permute-start.34 = (bf16[4,784,128]{2,1,0:T(8,128)(2,1)}, bf16[4,784,128]{2,1,0:T(8,128)(2,1)}, u32[]{:S(2)}, u32[]{:S(2)}) collective-permute-start(bf16[4,784,128]{2,1,0:T(8,128)(2,1)} %get-tuple-element.231), channel_id=1, source_target_pairs={{0,12},{1,13},{2,14},{3,15},{4,8},{5,9},{6,10},{7,11},{8,4},{9,5},... | collective-permute-start | bytes 2408456 | tf_op jit(solution)/shard_map/ppermute | solution.py:71
  159.6 29.9 %collective-permute-start.28 = (bf16[4,528,128]{2,1,0:T(8,128)(2,1)}, bf16[4,528,128]{2,1,0:T(8,128)(2,1)}, u32[]{:S(2)}, u32[]{:S(2)}) collective-permute-start(bf16[4,528,128]{2,1,0:T(8,128)(2,1)} %get-tuple-element.220), channel_id=1, source_target_pairs={{0,4},{1,5},{2,6},{3,7},{4,0},{5,1},{6,2},{7,3},{8,12},{9,13},{10,... | collective-permute-start | bytes 1622024 | tf_op jit(solution)/shard_map/ppermute | solution.py:71
  159.9 29.6 %collective-permute-start.29 = (bf16[4,528,128]{2,1,0:T(8,128)(2,1)}, bf16[4,528,128]{2,1,0:T(8,128)(2,1)}, u32[]{:S(2)}, u32[]{:S(2)}) collective-permute-start(bf16[4,528,128]{2,1,0:T(8,128)(2,1)} %get-tuple-element.221), channel_id=1, source_target_pairs={{0,5},{1,4},{2,7},{3,6},{4,1},{5,0},{6,3},{7,2},{8,13},{9,12},{10,... | collective-permute-start | bytes 1622024 | tf_op jit(solution)/shard_map/ppermute | solution.py:71
  162.5 36.4 %collective-permute-start.35 = (bf16[4,784,128]{2,1,0:T(8,128)(2,1)}, bf16[4,784,128]{2,1,0:T(8,128)(2,1)}, u32[]{:S(2)}, u32[]{:S(2)}) collective-permute-start(bf16[4,784,128]{2,1,0:T(8,128)(2,1)} %get-tuple-element.232), channel_id=1, source_target_pairs={{0,15},{1,14},{2,13},{3,12},{4,11},{5,10},{6,9},{7,8},{8,7},{9,6},... | collective-permute-start | bytes 2408456 | tf_op jit(solution)/shard_map/ppermute | solution.py:71
  165.8 0.8 copy-start.13
  166.7 32.2 %collective-permute-start.33 = (bf16[4,784,128]{2,1,0:T(8,128)(2,1)}, bf16[4,784,128]{2,1,0:T(8,128)(2,1)}, u32[]{:S(2)}, u32[]{:S(2)}) collective-permute-start(bf16[4,784,128]{2,1,0:T(8,128)(2,1)} %get-tuple-element.212), channel_id=1, source_target_pairs={{0,3},{1,2},{2,1},{3,0},{4,7},{5,6},{6,5},{7,4},{8,11},{9,10},{10,... | collective-permute-start | bytes 2408456 | tf_op jit(solution)/shard_map/ppermute | solution.py:71
  168.8 43.3 %copy-start.12 = (bf16[4,528,128]{2,1,0:T(8,128)(2,1)S(1)}, bf16[4,528,128]{2,1,0:T(8,128)(2,1)}, u32[]{:S(2)}) copy-start(bf16[4,528,128]{2,1,0:T(8,128)(2,1)} %copy-done.10) | copy-start | bytes 1622020
  168.8 43.3 %copy-start.15 = (bf16[4,528,128]{2,1,0:T(8,128)(2,1)S(1)}, bf16[4,528,128]{2,1,0:T(8,128)(2,1)}, u32[]{:S(2)}) copy-start(bf16[4,528,128]{2,1,0:T(8,128)(2,1)} %copy-done.13) | copy-start | bytes 1622020
  189.5 1.0 copy-start.11
  190.5 1.0 copy-start.14
  192.9 16.4 %collective-permute-start.31 = (bf16[4,528,128]{2,1,0:T(8,128)(2,1)S(1)}, bf16[4,528,128]{2,1,0:T(8,128)(2,1)S(1)}, u32[]{:S(2)}, u32[]{:S(2)}) collective-permute-start(bf16[4,528,128]{2,1,0:T(8,128)(2,1)S(1)} %get-tuple-element.229), channel_id=1, source_target_pairs={{0,12},{1,13},{2,14},{3,15},{4,8},{5,9},{6,10},{7,11},{8,4},{9,5},... | collective-permute-start | bytes 1622024 | tf_op jit(solution)/shard_map/ppermute | solution.py:71
  193.8 15.5 %collective-permute-start.32 = (bf16[4,528,128]{2,1,0:T(8,128)(2,1)S(1)}, bf16[4,528,128]{2,1,0:T(8,128)(2,1)S(1)}, u32[]{:S(2)}, u32[]{:S(2)}) collective-permute-start(bf16[4,528,128]{2,1,0:T(8,128)(2,1)S(1)} %get-tuple-element.230), channel_id=1, source_target_pairs={{0,15},{1,14},{2,13},{3,12},{4,11},{5,10},{6,9},{7,8},{8,7},{9,6},... | collective-permute-start | bytes 1622024 | tf_op jit(solution)/shard_map/ppermute | solution.py:71
  198.2 13.9 %collective-permute-start.30 = (bf16[4,528,128]{2,1,0:T(8,128)(2,1)S(1)}, bf16[4,528,128]{2,1,0:T(8,128)(2,1)S(1)}, u32[]{:S(2)}, u32[]{:S(2)}) collective-permute-start(bf16[4,528,128]{2,1,0:T(8,128)(2,1)S(1)} %get-tuple-element.228), channel_id=1, source_target_pairs={{0,3},{1,2},{2,1},{3,0},{4,7},{5,6},{6,5},{7,4},{8,11},{9,10},{10,... | collective-permute-start | bytes 1622024 | tf_op jit(solution)/shard_map/ppermute | solution.py:71
  198.9 1.1 copy-start.3
  200.0 1.1 copy-start.5
  201.2 1.1 copy-start.7
  202.3 1.1 copy-start.9

commit v8 on v7

--- a/solution.py
+++ b/solution.py
@@ -10,26 +10,27 @@
 
 HEAD_DIM = 128
 HAD = 128
-CHUNKS = ((0, 48), (48, 48), (96, 32))
-DIRECT = 1
+CHUNKS = ((0, 32), (32, 48), (80, 48))
+DIRECT = 0
 ORDER = (
     ("start", 0),
+    ("start", 1),
     ("y_regroup", 0),
-    ("start", 1),
-    ("cross", 0),
+    ("cross", 0, 1),
+    ("y_regroup", 0),
     ("y_regroup", 1),
-    ("y_regroup", 0),
+    ("spread", 0),
+    ("cross", 1),
     ("start", 2),
-    ("cross", 1),
-    ("spread", 0),
+    ("regroup", 0, 2),
+    ("y_regroup", 2),
     ("y_regroup", 1),
+    ("cross", 2),
     ("y_regroup", 2),
-    ("cross", 2),
     ("spread", 1),
-    ("y_regroup", 2),
+    ("pack", 0),
+    ("spread", 2),
     ("regroup", 1),
-    ("spread", 2),
-    ("pack", 0),
     ("regroup", 2),
     ("pack", 1),
     ("pack", 2),
@@ -328,9 +329,11 @@
             return list(arrays)
         return list(lax.optimization_barrier((list(arrays), token))[0])
 
-    for stage, index in ORDER:
+    for stage, index, *others in ORDER:
         first, chans = chunk = CHUNKS[index]
         arrays = tie(state[index])
+        for other in others:
+            arrays, state[other] = lax.optimization_barrier((arrays, state[other]))
         if stage == "start":
             state[index] = y_first(arrays)
         elif stage == "y_regroup":

time: 217 us -> 234 us (1.078)
  the two profiles are of different devices: /device:TPU:0 before, /device:TPU:4 now
where the time goes in v8:
time: 234 us
  waiting for transfers between devices  149 us (64%)
  starting transfers between devices  60.1 us (26%)
  Pallas kernels  20.5 us (9%)
  local copies, waits for them, and re-layouts  3.09 us (1%)
    ppermute x42, waiting for transfers between devices, hop(): return lax.ppermute(array, BOTH, pairs)  149 us
    ppermute x42, starting transfers between devices, hop(): return lax.ppermute(array, BOTH, pairs)  60.1 us
    pallas_call x3, Pallas kernels, per_device(): pl.pallas_call(functools.partial(pack_kernel, owners, heads, chunk, bool(...  8.52 us
    pallas_call x15, Pallas kernels, call(): pl.pallas_call(kernel, in_specs=[smem_spec] * table + [vmem_spec] * (len(...  6.33 us
    pallas_call x1, Pallas kernels, per_device(): pl.pallas_call(functools.partial(local_turn_kernel, rows_a), grid=(heads,...  5.64 us
  transfers between devices with their start and end apart: 42, of which 21 were waited for; matrix products, arithmetic and copies ran while one was open for 0% of the time, Pallas kernels for 4%

profile of v8, /device:TPU:4, one launch (start us, length us, event | category | flops | bytes accessed | tf_op | source)
XLA Modules:
  0.0 234.1 jit_solution(10660214402829153785)
XLA Ops:
  0.6 2.3 copy-done
  3.0 0.8 copy-done.2
  3.7 5.6 %local_turn.1 = (bf16[2,576,128]{2,1,0:T(8,128)(2,1)S(1)}, bf16[2,576,128]{2,1,0:T(8,128)(2,1)S(1)}, bf16[2,576,128]{2,1,0:T(8,128)(2,1)S(1)}, bf16[2,576,128]{2...) custom-call(bf16[2048,1152]{1,0:T(8,128)(2,1)S(1)} %copy-done, ...), custom_call_target="tpu_custom_call" | custom-call | tf_op jit(solution)/shard_map/local_turn/pallas_call | solution.py:309
  9.5 1.7 collective-permute-start.1
  11.1 1.5 collective-permute-start.2
  12.6 5.8 %collective-permute-done.1.refs_2_ = bf16[2,576,128]{2,1,0:T(8,128)(2,1)S(1)} collective-permute-done((bf16[2,576,128]{2,1,0:T(8,128)(2,1)S(1)}, bf16[2,576,128]{2,1,0:T(8,128)(2,1)S(1)}, u32[]{:S(2)}, u32[]{:S(2)}) %collective-permute-start.1) | collective-permute-done | bytes 294944 | tf_op jit(solution)/shard_map/ppermute | solution.py:72
  18.4 1.0 collective-permute-done.2.refs_3_
  19.5 3.1 %collective-permute-start.3 = (bf16[4,576,128]{2,1,0:T(8,128)(2,1)S(1)}, bf16[4,576,128]{2,1,0:T(8,128)(2,1)S(1)}, u32[]{:S(2)}, u32[]{:S(2)}) collective-permute-start(bf16[4,576,128]{2,1,0:T(8,128)(2,1)S(1)} %y_regroup.6), channel_id=1, source_target_pairs={{0,96},{1,97},{2,98},{3,99},{4,100},{5,101},{6,102},{7,103},{8,104... | collective-permute-start | bytes 1769480 | tf_op jit(solution)/shard_map/ppermute | solution.py:72
  22.7 2.9 %collective-permute-start.6 = (bf16[2,864,128]{2,1,0:T(8,128)(2,1)S(1)}, bf16[2,864,128]{2,1,0:T(8,128)(2,1)S(1)}, u32[]{:S(2)}, u32[]{:S(2)}) collective-permute-start(bf16[2,864,128]{2,1,0:T(8,128)(2,1)S(1)} %get-tuple-element.169), channel_id=1, source_target_pairs={{0,112},{1,113},{2,114},{3,115},{4,116},{5,117},{6,118},{7,119},{8... | collective-permute-start | bytes 1327112 | tf_op jit(solution)/shard_map/ppermute | solution.py:72
  25.6 8.9 %collective-permute-done.3.refs_4_ = bf16[4,576,128]{2,1,0:T(8,128)(2,1)S(1)} collective-permute-done((bf16[4,576,128]{2,1,0:T(8,128)(2,1)S(1)}, bf16[4,576,128]{2,1,0:T(8,128)(2,1)S(1)}, u32[]{:S(2)}, u32[]{:S(2)}) %collective-permute-start.3) | collective-permute-done | bytes 589856 | tf_op jit(solution)/shard_map/ppermute | solution.py:72
  34.5 1.1 collective-permute-done.5.refs_2_
  35.7 3.6 %collective-permute-done.6.refs_3_ = bf16[2,864,128]{2,1,0:T(8,128)(2,1)S(1)} collective-permute-done((bf16[2,864,128]{2,1,0:T(8,128)(2,1)S(1)}, bf16[2,864,128]{2,1,0:T(8,128)(2,1)S(1)}, u32[]{:S(2)}, u32[]{:S(2)}) %collective-permute-start.6) | collective-permute-done | bytes 442400 | tf_op jit(solution)/shard_map/ppermute | solution.py:72
  39.3 0.8 cross.3
  40.1 0.7 collective-permute-start.7
  40.8 0.4 collective-permute-start.8
  41.2 2.3 collective-permute-start.9
  43.4 7.2 %collective-permute-done.8.refs_2_ = bf16[2,592,128]{2,1,0:T(8,128)(2,1)S(1)} collective-permute-done((bf16[2,592,128]{2,1,0:T(8,128)(2,1)S(1)}, bf16[2,592,128]{2,1,0:T(8,128)(2,1)S(1)}, u32[]{:S(2)}, u32[]{:S(2)}) %collective-permute-start.8) | collective-permute-done | bytes 303136 | tf_op jit(solution)/shard_map/ppermute | solution.py:72
  50.7 2.6 %collective-permute-start.10 = (bf16[4,592,128]{2,1,0:T(8,128)(2,1)S(1)}, bf16[4,592,128]{2,1,0:T(8,128)(2,1)S(1)}, u32[]{:S(2)}, u32[]{:S(2)}) collective-permute-start(bf16[4,592,128]{2,1,0:T(8,128)(2,1)S(1)} %y_regroup.7), channel_id=1, source_target_pairs={{0,96},{1,97},{2,98},{3,99},{4,100},{5,101},{6,102},{7,103},{8,104... | collective-permute-start | bytes 1818632 | tf_op jit(solution)/shard_map/ppermute | solution.py:72
  53.3 0.8 collective-permute-start.14
  54.1 7.9 %collective-permute-done.10.refs_4_ = bf16[4,592,128]{2,1,0:T(8,128)(2,1)S(1)} collective-permute-done((bf16[4,592,128]{2,1,0:T(8,128)(2,1)S(1)}, bf16[4,592,128]{2,1,0:T(8,128)(2,1)S(1)}, u32[]{:S(2)}, u32[]{:S(2)}) %collective-permute-start.10) | collective-permute-done | bytes 606240 | tf_op jit(solution)/shard_map/ppermute | solution.py:72
  62.0 0.8 spread.3
  62.9 1.3 collective-permute-start.11
  64.1 1.9 collective-permute-start.12
  66.0 0.4 collective-permute-start.13
  66.4 5.1 %collective-permute-done.14.refs_4_ = bf16[4,864,128]{2,1,0:T(8,128)(2,1)S(1)} collective-permute-done((bf16[4,864,128]{2,1,0:T(8,128)(2,1)S(1)}, bf16[4,864,128]{2,1,0:T(8,128)(2,1)S(1)}, u32[]{:S(2)}, u32[]{:S(2)}) %collective-permute-start.14) | collective-permute-done | bytes 884768 | tf_op jit(solution)/shard_map/ppermute | solution.py:72
  71.5 1.1 cross.4
  72.8 3.0 %collective-permute-start.17 = (bf16[2,864,128]{2,1,0:T(8,128)(2,1)S(1)}, bf16[2,864,128]{2,1,0:T(8,128)(2,1)S(1)}, u32[]{:S(2)}, u32[]{:S(2)}) collective-permute-start(bf16[2,864,128]{2,1,0:T(8,128)(2,1)S(1)} %get-tuple-element.217), channel_id=1, source_target_pairs={{0,112},{1,113},{2,114},{3,115},{4,116},{5,117},{6,118},{7,119},{8... | collective-permute-start | bytes 1327112 | tf_op jit(solution)/shard_map/ppermute | solution.py:72
  75.7 3.0 %collective-permute-done.12.refs_2_ = bf16[4,528,128]{2,1,0:T(8,128)(2,1)S(1)} collective-permute-done((bf16[4,528,128]{2,1,0:T(8,128)(2,1)S(1)}, bf16[4,528,128]{2,1,0:T(8,128)(2,1)S(1)}, u32[]{:S(2)}, u32[]{:S(2)}) %collective-permute-start.12) | collective-permute-done | bytes 540704 | tf_op jit(solution)/shard_map/ppermute | solution.py:72
  78.7 0.7 collective-permute-done.13.refs_3_
  79.4 5.9 %collective-permute-done.16.refs_2_ = bf16[2,864,128]{2,1,0:T(8,128)(2,1)S(1)} collective-permute-done((bf16[2,864,128]{2,1,0:T(8,128)(2,1)S(1)}, bf16[2,864,128]{2,1,0:T(8,128)(2,1)S(1)}, u32[]{:S(2)}, u32[]{:S(2)}) %collective-permute-start.16) | collective-permute-done | bytes 442400 | tf_op jit(solution)/shard_map/ppermute | solution.py:72
  85.5 2.6 %collective-permute-start.18 = (bf16[4,864,128]{2,1,0:T(8,128)(2,1)S(1)}, bf16[4,864,128]{2,1,0:T(8,128)(2,1)S(1)}, u32[]{:S(2)}, u32[]{:S(2)}) collective-permute-start(bf16[4,864,128]{2,1,0:T(8,128)(2,1)S(1)} %y_regroup.9), channel_id=1, source_target_pairs={{0,96},{1,97},{2,98},{3,99},{4,100},{5,101},{6,102},{7,103},{8,104... | collective-permute-start | bytes 2654216 | tf_op jit(solution)/shard_map/ppermute | solution.py:72
  88.3 2.9 %collective-permute-start.21 = (bf16[2,880,128]{2,1,0:T(8,128)(2,1)S(1)}, bf16[2,880,128]{2,1,0:T(8,128)(2,1)S(1)}, u32[]{:S(2)}, u32[]{:S(2)}) collective-permute-start(bf16[2,880,128]{2,1,0:T(8,128)(2,1)S(1)} %get-tuple-element.233), channel_id=1, source_target_pairs={{0,112},{1,113},{2,114},{3,115},{4,116},{5,117},{6,118},{7,119},{8... | collective-permute-start | bytes 1351688 | tf_op jit(solution)/shard_map/ppermute | solution.py:72
  91.2 10.2 %collective-permute-done.20.refs_2_ = bf16[2,880,128]{2,1,0:T(8,128)(2,1)S(1)} collective-permute-done((bf16[2,880,128]{2,1,0:T(8,128)(2,1)S(1)}, bf16[2,880,128]{2,1,0:T(8,128)(2,1)S(1)}, u32[]{:S(2)}, u32[]{:S(2)}) %collective-permute-start.20) | collective-permute-done | bytes 450592 | tf_op jit(solution)/shard_map/ppermute | solution.py:72
  101.4 6.9 %collective-permute-done.21.refs_3_ = bf16[2,880,128]{2,1,0:T(8,128)(2,1)S(1)} collective-permute-done((bf16[2,880,128]{2,1,0:T(8,128)(2,1)S(1)}, bf16[2,880,128]{2,1,0:T(8,128)(2,1)S(1)}, u32[]{:S(2)}, u32[]{:S(2)}) %collective-permute-start.21) | collective-permute-done | bytes 450592 | tf_op jit(solution)/shard_map/ppermute | solution.py:72
  108.4 2.5 %collective-permute-start.29 = (bf16[4,880,128]{2,1,0:T(8,128)(2,1)S(1)}, bf16[4,880,128]{2,1,0:T(8,128)(2,1)S(1)}, u32[]{:S(2)}, u32[]{:S(2)}) collective-permute-start(bf16[4,880,128]{2,1,0:T(8,128)(2,1)S(1)} %y_regroup.10), channel_id=1, source_target_pairs={{0,96},{1,97},{2,98},{3,99},{4,100},{5,101},{6,102},{7,103},{8,104... | collective-permute-start | bytes 2703368 | tf_op jit(solution)/shard_map/ppermute | solution.py:72
  110.9 1.1 cross.5
  112.1 0.3 collective-permute-start.23
  112.3 2.8 %collective-permute-start.24 = (bf16[2,880,128]{2,1,0:T(8,128)(2,1)S(1)}, bf16[2,880,128]{2,1,0:T(8,128)(2,1)S(1)}, u32[]{:S(2)}, u32[]{:S(2)}) collective-permute-start(bf16[2,880,128]{2,1,0:T(8,128)(2,1)S(1)} %get-tuple-element.246), channel_id=1, source_target_pairs={{0,112},{1,113},{2,114},{3,115},{4,116},{5,117},{6,118},{7,119},{8... | collective-permute-start | bytes 1351688 | tf_op jit(solution)/shard_map/ppermute | solution.py:72
  115.1 4.0 %collective-permute-start.27 = (bf16[4,528,128]{2,1,0:T(8,128)(2,1)S(1)}, bf16[4,528,128]{2,1,0:T(8,128)(2,1)S(1)}, u32[]{:S(2)}, u32[]{:S(2)}) collective-permute-start(bf16[4,528,128]{2,1,0:T(8,128)(2,1)S(1)} %get-tuple-element.251), channel_id=1, source_target_pairs={{0,12},{1,13},{2,14},{3,15},{4,8},{5,9},{6,10},{7,11},{8,4},{9,5},... | collective-permute-start | bytes 1622024 | tf_op jit(solution)/shard_map/ppermute | solution.py:72
  119.2 6.3 %collective-permute-done.23.refs_2_ = bf16[2,880,128]{2,1,0:T(8,128)(2,1)S(1)} collective-permute-done((bf16[2,880,128]{2,1,0:T(8,128)(2,1)S(1)}, bf16[2,880,128]{2,1,0:T(8,128)(2,1)S(1)}, u32[]{:S(2)}, u32[]{:S(2)}) %collective-permute-start.23) | collective-permute-done | bytes 450592 | tf_op jit(solution)/shard_map/ppermute | solution.py:72
  125.4 5.9 %collective-permute-done.24.refs_3_ = bf16[2,880,128]{2,1,0:T(8,128)(2,1)S(1)} collective-permute-done((bf16[2,880,128]{2,1,0:T(8,128)(2,1)S(1)}, bf16[2,880,128]{2,1,0:T(8,128)(2,1)S(1)}, u32[]{:S(2)}, u32[]{:S(2)}) %collective-permute-start.24) | collective-permute-done | bytes 450592 | tf_op jit(solution)/shard_map/ppermute | solution.py:72
  131.4 2.6 %collective-permute-start.25 = (bf16[4,880,128]{2,1,0:T(8,128)(2,1)S(1)}, bf16[4,880,128]{2,1,0:T(8,128)(2,1)S(1)}, u32[]{:S(2)}, u32[]{:S(2)}) collective-permute-start(bf16[4,880,128]{2,1,0:T(8,128)(2,1)S(1)} %y_regroup.11), channel_id=1, source_target_pairs={{0,96},{1,97},{2,98},{3,99},{4,100},{5,101},{6,102},{7,103},{8,104... | collective-permute-start | bytes 2703368 | tf_op jit(solution)/shard_map/ppermute | solution.py:72
  134.0 0.9 spread.4
  134.9 1.3 collective-permute-start.33
  136.1 1.9 collective-permute-start.34
  138.1 0.4 collective-permute-start.35
  138.5 0.5 collective-permute-start.26
  139.0 14.7 %collective-permute-done.26.refs_4_ = bf16[4,528,128]{2,1,0:T(8,128)(2,1)S(1)} collective-permute-done((bf16[4,528,128]{2,1,0:T(8,128)(2,1)S(1)}, bf16[4,528,128]{2,1,0:T(8,128)(2,1)S(1)}, u32[]{:S(2)}, u32[]{:S(2)}) %collective-permute-start.26) | collective-permute-done | bytes 540704 | tf_op jit(solution)/shard_map/ppermute | solution.py:72
  153.7 2.4 %pack.3 = (f32[16,128]{1,0:T(8,128)S(1)}, bf16[1,16,128,2048]{3,2,1,0:T(8,128)(2,1)}) custom-call(s32[144]{0:T(256)S(1)} %copy-done.1, bf16[4,528,128]{2,1,0:T(8,128)(2,1)S(1)} %get-tuple-element.259.refs_0_, bf16[4,528,128]{2,1,0:T(8,128)(2,1)S(1)} %collective-permute-done.11.refs_1_, bf16[4,528,128]{2,1,0:T(8,128)(2,1)S(1)} %collective-permute-done.12.refs_2_, ...), custom_call_target="tpu_custom_call" | custom-call | tf_op jit(solution)/shard_map/pack/pallas_call | solution.py:362
  156.1 0.9 spread.5
  156.9 2.5 %collective-permute-start.30 = (bf16[4,784,128]{2,1,0:T(8,128)(2,1)S(1)}, bf16[4,784,128]{2,1,0:T(8,128)(2,1)S(1)}, u32[]{:S(2)}, u32[]{:S(2)}) collective-permute-start(bf16[4,784,128]{2,1,0:T(8,128)(2,1)S(1)} %get-tuple-element.273), channel_id=1, source_target_pairs={{0,1},{1,0},{2,3},{3,2},{4,5},{5,4},{6,7},{7,6},{8,9},{9,8},{10,11... | collective-permute-start | bytes 2408456 | tf_op jit(solution)/shard_map/ppermute | solution.py:72
  159.4 1.9 collective-permute-start.31
  161.3 1.5 collective-permute-done.35.refs_3_
  163.0 2.6 %collective-permute-start.40 = (bf16[4,784,128]{2,1,0:T(8,128)(2,1)S(1)}, bf16[4,784,128]{2,1,0:T(8,128)(2,1)S(1)}, u32[]{:S(2)}, u32[]{:S(2)}) collective-permute-start(bf16[4,784,128]{2,1,0:T(8,128)(2,1)S(1)} %get-tuple-element.291), channel_id=1, source_target_pairs={{0,12},{1,13},{2,14},{3,15},{4,8},{5,9},{6,10},{7,11},{8,4},{9,5},... | collective-permute-start | bytes 2408456 | tf_op jit(solution)/shard_map/ppermute | solution.py:72
  165.6 0.7 collective-permute-start.41
  166.4 7.3 %collective-permute-done.30.refs_1_ = bf16[4,784,128]{2,1,0:T(8,128)(2,1)S(1)} collective-permute-done((bf16[4,784,128]{2,1,0:T(8,128)(2,1)S(1)}, bf16[4,784,128]{2,1,0:T(8,128)(2,1)S(1)}, u32[]{:S(2)}, u32[]{:S(2)}) %collective-permute-start.30) | collective-permute-done | bytes 802848 | tf_op jit(solution)/shard_map/ppermute | solution.py:72
  173.7 0.6 collective-permute-start.39
  174.2 30.4 %collective-permute-done.31.refs_2_ = bf16[4,784,128]{2,1,0:T(8,128)(2,1)S(1)} collective-permute-done((bf16[4,784,128]{2,1,0:T(8,128)(2,1)S(1)}, bf16[4,784,128]{2,1,0:T(8,128)(2,1)S(1)}, u32[]{:S(2)}, u32[]{:S(2)}) %collective-permute-start.31) | collective-permute-done | bytes 802848 | tf_op jit(solution)/shard_map/ppermute | solution.py:72
  204.8 5.4 %collective-permute-start.37 = (bf16[4,784,128]{2,1,0:T(8,128)(2,1)S(1)}, bf16[4,784,128]{2,1,0:T(8,128)(2,1)S(1)}, u32[]{:S(2)}, u32[]{:S(2)}) collective-permute-start(bf16[4,784,128]{2,1,0:T(8,128)(2,1)S(1)} %get-tuple-element.289), channel_id=1, source_target_pairs={{0,12},{1,13},{2,14},{3,15},{4,8},{5,9},{6,10},{7,11},{8,4},{9,5},... | collective-permute-start | bytes 2408456 | tf_op jit(solution)/shard_map/ppermute | solution.py:72
  210.3 1.6 collective-permute-start.36
  211.8 2.8 %pack.4 = (f32[16,128]{1,0:T(8,128)S(1)}, bf16[1,16,128,2048]{3,2,1,0:T(8,128)(2,1)}) custom-call(s32[144]{0:T(256)S(1)} %copy-done.1, bf16[4,784,128]{2,1,0:T(8,128)(2,1)S(1)} %get-tuple-element.293.refs_0_, bf16[4,784,128]{2,1,0:T(8,128)(2,1)S(1)} %collective-permute-done.33.refs_1_, ...), custom_call_target="tpu_custom_call", output_to_operand_aliasing={{1}: (9, {})} | custom-call | tf_op jit(solution)/shard_map/pack/pallas_call | solution.py:362
  214.6 14.4 %collective-permute-done.37.refs_5_ = bf16[4,784,128]{2,1,0:T(8,128)(2,1)S(1)} collective-permute-done((bf16[4,784,128]{2,1,0:T(8,128)(2,1)S(1)}, bf16[4,784,128]{2,1,0:T(8,128)(2,1)S(1)}, u32[]{:S(2)}, u32[]{:S(2)}) %collective-permute-start.37) | collective-permute-done | bytes 802848 | tf_op jit(solution)/shard_map/ppermute | solution.py:72
  229.0 1.6 collective-permute-done.36.refs_4_
  230.6 3.4 %pack.5 = (f32[16,128]{1,0:T(8,128)}, bf16[1,16,128,2048]{3,2,1,0:T(8,128)(2,1)}) custom-call(s32[144]{0:T(256)S(1)} %copy-done.1, bf16[4,784,128]{2,1,0:T(8,128)(2,1)S(1)} %get-tuple-element.302.refs_0_, bf16[4,784,128]{2,1,0:T(8,128)(2,1)S(1)} %collective-permute-done.30.refs_1_, ...), custom_call_target="tpu_custom_call", output_to_operand_aliasing={{1}: (9, {})} | custom-call | tf_op jit(solution)/shard_map/pack/pallas_call | solution.py:362
  (45 shorter events, 1.4 us)
Async XLA Ops:
  0.6 2.3 copy-start
  3.0 0.8 copy-start.2
  3.7 58.3 %copy-start.1 = (s32[144]{0:T(256)S(1)}, s32[144]{0:T(256)}, u32[]{:S(2)}) copy-start(s32[144]{0:T(256)} %placement_ref.11) | copy-start | bytes 1732
  9.4 3.3 %collective-permute-start = (bf16[2,576,128]{2,1,0:T(8,128)(2,1)S(1)}, bf16[2,576,128]{2,1,0:T(8,128)(2,1)S(1)}, u32[]{:S(2)}, u32[]{:S(2)}) collective-permute-start(bf16[2,576,128]{2,1,0:T(8,128)(2,1)S(1)} %get-tuple-element.158), channel_id=1, source_target_pairs={{0,16},{1,17},{2,18},{3,19},{4,20},{5,21},{6,22},{7,23},{8,24},{9,... | collective-permute-start | bytes 884744 | tf_op jit(solution)/shard_map/ppermute | solution.py:72
  9.5 9.0 %collective-permute-start.1 = (bf16[2,576,128]{2,1,0:T(8,128)(2,1)S(1)}, bf16[2,576,128]{2,1,0:T(8,128)(2,1)S(1)}, u32[]{:S(2)}, u32[]{:S(2)}) collective-permute-start(bf16[2,576,128]{2,1,0:T(8,128)(2,1)S(1)} %get-tuple-element.159), channel_id=1, source_target_pairs={{0,32},{1,33},{2,34},{3,35},{4,36},{5,37},{6,38},{7,39},{8,40},{9,... | collective-permute-start | bytes 884744 | tf_op jit(solution)/shard_map/ppermute | solution.py:72
  11.1 8.3 %collective-permute-start.2 = (bf16[2,576,128]{2,1,0:T(8,128)(2,1)S(1)}, bf16[2,576,128]{2,1,0:T(8,128)(2,1)S(1)}, u32[]{:S(2)}, u32[]{:S(2)}) collective-permute-start(bf16[2,576,128]{2,1,0:T(8,128)(2,1)S(1)} %get-tuple-element.160), channel_id=1, source_target_pairs={{0,112},{1,113},{2,114},{3,115},{4,116},{5,117},{6,118},{7,119},{8... | collective-permute-start | bytes 884744 | tf_op jit(solution)/shard_map/ppermute | solution.py:72
  19.5 15.1 %collective-permute-start.3 = (bf16[4,576,128]{2,1,0:T(8,128)(2,1)S(1)}, bf16[4,576,128]{2,1,0:T(8,128)(2,1)S(1)}, u32[]{:S(2)}, u32[]{:S(2)}) collective-permute-start(bf16[4,576,128]{2,1,0:T(8,128)(2,1)S(1)} %y_regroup.6), channel_id=1, source_target_pairs={{0,96},{1,97},{2,98},{3,99},{4,100},{5,101},{6,102},{7,103},{8,104... | collective-permute-start | bytes 1769480 | tf_op jit(solution)/shard_map/ppermute | solution.py:72
  22.6 12.0 %collective-permute-start.4 = (bf16[2,864,128]{2,1,0:T(8,128)(2,1)S(1)}, bf16[2,864,128]{2,1,0:T(8,128)(2,1)S(1)}, u32[]{:S(2)}, u32[]{:S(2)}) collective-permute-start(bf16[2,864,128]{2,1,0:T(8,128)(2,1)S(1)} %get-tuple-element.167), channel_id=1, source_target_pairs={{0,16},{1,17},{2,18},{3,19},{4,20},{5,21},{6,22},{7,23},{8,24},{9,... | collective-permute-start | bytes 1327112 | tf_op jit(solution)/shard_map/ppermute | solution.py:72
  22.6 13.1 %collective-permute-start.5 = (bf16[2,864,128]{2,1,0:T(8,128)(2,1)S(1)}, bf16[2,864,128]{2,1,0:T(8,128)(2,1)S(1)}, u32[]{:S(2)}, u32[]{:S(2)}) collective-permute-start(bf16[2,864,128]{2,1,0:T(8,128)(2,1)S(1)} %get-tuple-element.168), channel_id=1, source_target_pairs={{0,32},{1,33},{2,34},{3,35},{4,36},{5,37},{6,38},{7,39},{8,40},{9,... | collective-permute-start | bytes 1327112 | tf_op jit(solution)/shard_map/ppermute | solution.py:72
  22.7 16.6 %collective-permute-start.6 = (bf16[2,864,128]{2,1,0:T(8,128)(2,1)S(1)}, bf16[2,864,128]{2,1,0:T(8,128)(2,1)S(1)}, u32[]{:S(2)}, u32[]{:S(2)}) collective-permute-start(bf16[2,864,128]{2,1,0:T(8,128)(2,1)S(1)} %get-tuple-element.169), channel_id=1, source_target_pairs={{0,112},{1,113},{2,114},{3,115},{4,116},{5,117},{6,118},{7,119},{8... | collective-permute-start | bytes 1327112 | tf_op jit(solution)/shard_map/ppermute | solution.py:72
  40.1 3.3 %collective-permute-start.7 = (bf16[2,592,128]{2,1,0:T(8,128)(2,1)S(1)}, bf16[2,592,128]{2,1,0:T(8,128)(2,1)S(1)}, u32[]{:S(2)}, u32[]{:S(2)}) collective-permute-start(bf16[2,592,128]{2,1,0:T(8,128)(2,1)S(1)} %get-tuple-element.176), channel_id=1, source_target_pairs={{0,16},{1,17},{2,18},{3,19},{4,20},{5,21},{6,22},{7,23},{8,24},{9,... | collective-permute-start | bytes 909320 | tf_op jit(solution)/shard_map/ppermute | solution.py:72
  40.8 9.9 %collective-permute-start.8 = (bf16[2,592,128]{2,1,0:T(8,128)(2,1)S(1)}, bf16[2,592,128]{2,1,0:T(8,128)(2,1)S(1)}, u32[]{:S(2)}, u32[]{:S(2)}) collective-permute-start(bf16[2,592,128]{2,1,0:T(8,128)(2,1)S(1)} %get-tuple-element.177), channel_id=1, source_target_pairs={{0,32},{1,33},{2,34},{3,35},{4,36},{5,37},{6,38},{7,39},{8,40},{9,... | collective-permute-start | bytes 909320 | tf_op jit(solution)/shard_map/ppermute | solution.py:72
  41.2 9.5 %collective-permute-start.9 = (bf16[2,592,128]{2,1,0:T(8,128)(2,1)S(1)}, bf16[2,592,128]{2,1,0:T(8,128)(2,1)S(1)}, u32[]{:S(2)}, u32[]{:S(2)}) collective-permute-start(bf16[2,592,128]{2,1,0:T(8,128)(2,1)S(1)} %get-tuple-element.178), channel_id=1, source_target_pairs={{0,112},{1,113},{2,114},{3,115},{4,116},{5,117},{6,118},{7,119},{8... | collective-permute-start | bytes 909320 | tf_op jit(solution)/shard_map/ppermute | solution.py:72
  50.7 11.3 %collective-permute-start.10 = (bf16[4,592,128]{2,1,0:T(8,128)(2,1)S(1)}, bf16[4,592,128]{2,1,0:T(8,128)(2,1)S(1)}, u32[]{:S(2)}, u32[]{:S(2)}) collective-permute-start(bf16[4,592,128]{2,1,0:T(8,128)(2,1)S(1)} %y_regroup.7), channel_id=1, source_target_pairs={{0,96},{1,97},{2,98},{3,99},{4,100},{5,101},{6,102},{7,103},{8,104... | collective-permute-start | bytes 1818632 | tf_op jit(solution)/shard_map/ppermute | solution.py:72
  53.3 18.2 %collective-permute-start.14 = (bf16[4,864,128]{2,1,0:T(8,128)(2,1)S(1)}, bf16[4,864,128]{2,1,0:T(8,128)(2,1)S(1)}, u32[]{:S(2)}, u32[]{:S(2)}) collective-permute-start(bf16[4,864,128]{2,1,0:T(8,128)(2,1)S(1)} %y_regroup.8), channel_id=1, source_target_pairs={{0,96},{1,97},{2,98},{3,99},{4,100},{5,101},{6,102},{7,103},{8,104... | collective-permute-start | bytes 2654216 | tf_op jit(solution)/shard_map/ppermute | solution.py:72
  62.9 9.9 %collective-permute-start.11 = (bf16[4,528,128]{2,1,0:T(8,128)(2,1)S(1)}, bf16[4,528,128]{2,1,0:T(8,128)(2,1)S(1)}, u32[]{:S(2)}, u32[]{:S(2)}) collective-permute-start(bf16[4,528,128]{2,1,0:T(8,128)(2,1)S(1)} %get-tuple-element.197), channel_id=1, source_target_pairs={{0,1},{1,0},{2,3},{3,2},{4,5},{5,4},{6,7},{7,6},{8,9},{9,8},{10,11... | collective-permute-start | bytes 1622024 | tf_op jit(solution)/shard_map/ppermute | solution.py:72
  64.1 14.6 %collective-permute-start.12 = (bf16[4,528,128]{2,1,0:T(8,128)(2,1)S(1)}, bf16[4,528,128]{2,1,0:T(8,128)(2,1)S(1)}, u32[]{:S(2)}, u32[]{:S(2)}) collective-permute-start(bf16[4,528,128]{2,1,0:T(8,128)(2,1)S(1)} %get-tuple-element.198), channel_id=1, source_target_pairs={{0,4},{1,5},{2,6},{3,7},{4,0},{5,1},{6,2},{7,3},{8,12},{9,13},{10,... | collective-permute-start | bytes 1622024 | tf_op jit(solution)/shard_map/ppermute | solution.py:72
  66.0 13.4 %collective-permute-start.13 = (bf16[4,528,128]{2,1,0:T(8,128)(2,1)S(1)}, bf16[4,528,128]{2,1,0:T(8,128)(2,1)S(1)}, u32[]{:S(2)}, u32[]{:S(2)}) collective-permute-start(bf16[4,528,128]{2,1,0:T(8,128)(2,1)S(1)} %get-tuple-element.199), channel_id=1, source_target_pairs={{0,5},{1,4},{2,7},{3,6},{4,1},{5,0},{6,3},{7,2},{8,13},{9,12},{10,... | collective-permute-start | bytes 1622024 | tf_op jit(solution)/shard_map/ppermute | solution.py:72
  72.6 6.8 %collective-permute-start.15 = (bf16[2,864,128]{2,1,0:T(8,128)(2,1)S(1)}, bf16[2,864,128]{2,1,0:T(8,128)(2,1)S(1)}, u32[]{:S(2)}, u32[]{:S(2)}) collective-permute-start(bf16[2,864,128]{2,1,0:T(8,128)(2,1)S(1)} %get-tuple-element.215), channel_id=1, source_target_pairs={{0,16},{1,17},{2,18},{3,19},{4,20},{5,21},{6,22},{7,23},{8,24},{9,... | collective-permute-start | bytes 1327112 | tf_op jit(solution)/shard_map/ppermute | solution.py:72
  72.7 12.6 %collective-permute-start.16 = (bf16[2,864,128]{2,1,0:T(8,128)(2,1)S(1)}, bf16[2,864,128]{2,1,0:T(8,128)(2,1)S(1)}, u32[]{:S(2)}, u32[]{:S(2)}) collective-permute-start(bf16[2,864,128]{2,1,0:T(8,128)(2,1)S(1)} %get-tuple-element.216), channel_id=1, source_target_pairs={{0,32},{1,33},{2,34},{3,35},{4,36},{5,37},{6,38},{7,39},{8,40},{9,... | collective-permute-start | bytes 1327112 | tf_op jit(solution)/shard_map/ppermute | solution.py:72
  72.8 12.5 %collective-permute-start.17 = (bf16[2,864,128]{2,1,0:T(8,128)(2,1)S(1)}, bf16[2,864,128]{2,1,0:T(8,128)(2,1)S(1)}, u32[]{:S(2)}, u32[]{:S(2)}) collective-permute-start(bf16[2,864,128]{2,1,0:T(8,128)(2,1)S(1)} %get-tuple-element.217), channel_id=1, source_target_pairs={{0,112},{1,113},{2,114},{3,115},{4,116},{5,117},{6,118},{7,119},{8... | collective-permute-start | bytes 1327112 | tf_op jit(solution)/shard_map/ppermute | solution.py:72
  85.5 25.4 %collective-permute-start.18 = (bf16[4,864,128]{2,1,0:T(8,128)(2,1)S(1)}, bf16[4,864,128]{2,1,0:T(8,128)(2,1)S(1)}, u32[]{:S(2)}, u32[]{:S(2)}) collective-permute-start(bf16[4,864,128]{2,1,0:T(8,128)(2,1)S(1)} %y_regroup.9), channel_id=1, source_target_pairs={{0,96},{1,97},{2,98},{3,99},{4,100},{5,101},{6,102},{7,103},{8,104... | collective-permute-start | bytes 2654216 | tf_op jit(solution)/shard_map/ppermute | solution.py:72
  88.1 3.1 %collective-permute-start.19 = (bf16[2,880,128]{2,1,0:T(8,128)(2,1)S(1)}, bf16[2,880,128]{2,1,0:T(8,128)(2,1)S(1)}, u32[]{:S(2)}, u32[]{:S(2)}) collective-permute-start(bf16[2,880,128]{2,1,0:T(8,128)(2,1)S(1)} %get-tuple-element.231), channel_id=1, source_target_pairs={{0,16},{1,17},{2,18},{3,19},{4,20},{5,21},{6,22},{7,23},{8,24},{9,... | collective-permute-start | bytes 1351688 | tf_op jit(solution)/shard_map/ppermute | solution.py:72
  88.1 13.3 %collective-permute-start.20 = (bf16[2,880,128]{2,1,0:T(8,128)(2,1)S(1)}, bf16[2,880,128]{2,1,0:T(8,128)(2,1)S(1)}, u32[]{:S(2)}, u32[]{:S(2)}) collective-permute-start(bf16[2,880,128]{2,1,0:T(8,128)(2,1)S(1)} %get-tuple-element.232), channel_id=1, source_target_pairs={{0,32},{1,33},{2,34},{3,35},{4,36},{5,37},{6,38},{7,39},{8,40},{9,... | collective-permute-start | bytes 1351688 | tf_op jit(solution)/shard_map/ppermute | solution.py:72
  88.3 20.0 %collective-permute-start.21 = (bf16[2,880,128]{2,1,0:T(8,128)(2,1)S(1)}, bf16[2,880,128]{2,1,0:T(8,128)(2,1)S(1)}, u32[]{:S(2)}, u32[]{:S(2)}) collective-permute-start(bf16[2,880,128]{2,1,0:T(8,128)(2,1)S(1)} %get-tuple-element.233), channel_id=1, source_target_pairs={{0,112},{1,113},{2,114},{3,115},{4,116},{5,117},{6,118},{7,119},{8... | collective-permute-start | bytes 1351688 | tf_op jit(solution)/shard_map/ppermute | solution.py:72
  108.4 25.6 %collective-permute-start.29 = (bf16[4,880,128]{2,1,0:T(8,128)(2,1)S(1)}, bf16[4,880,128]{2,1,0:T(8,128)(2,1)S(1)}, u32[]{:S(2)}, u32[]{:S(2)}) collective-permute-start(bf16[4,880,128]{2,1,0:T(8,128)(2,1)S(1)} %y_regroup.10), channel_id=1, source_target_pairs={{0,96},{1,97},{2,98},{3,99},{4,100},{5,101},{6,102},{7,103},{8,104... | collective-permute-start | bytes 2703368 | tf_op jit(solution)/shard_map/ppermute | solution.py:72
  112.0 7.1 %collective-permute-start.22 = (bf16[2,880,128]{2,1,0:T(8,128)(2,1)S(1)}, bf16[2,880,128]{2,1,0:T(8,128)(2,1)S(1)}, u32[]{:S(2)}, u32[]{:S(2)}) collective-permute-start(bf16[2,880,128]{2,1,0:T(8,128)(2,1)S(1)} %get-tuple-element.244), channel_id=1, source_target_pairs={{0,16},{1,17},{2,18},{3,19},{4,20},{5,21},{6,22},{7,23},{8,24},{9,... | collective-permute-start | bytes 1351688 | tf_op jit(solution)/shard_map/ppermute | solution.py:72
  112.1 13.4 %collective-permute-start.23 = (bf16[2,880,128]{2,1,0:T(8,128)(2,1)S(1)}, bf16[2,880,128]{2,1,0:T(8,128)(2,1)S(1)}, u32[]{:S(2)}, u32[]{:S(2)}) collective-permute-start(bf16[2,880,128]{2,1,0:T(8,128)(2,1)S(1)} %get-tuple-element.245), channel_id=1, source_target_pairs={{0,32},{1,33},{2,34},{3,35},{4,36},{5,37},{6,38},{7,39},{8,40},{9,... | collective-permute-start | bytes 1351688 | tf_op jit(solution)/shard_map/ppermute | solution.py:72
  112.3 19.0 %collective-permute-start.24 = (bf16[2,880,128]{2,1,0:T(8,128)(2,1)S(1)}, bf16[2,880,128]{2,1,0:T(8,128)(2,1)S(1)}, u32[]{:S(2)}, u32[]{:S(2)}) collective-permute-start(bf16[2,880,128]{2,1,0:T(8,128)(2,1)S(1)} %get-tuple-element.246), channel_id=1, source_target_pairs={{0,112},{1,113},{2,114},{3,115},{4,116},{5,117},{6,118},{7,119},{8... | collective-permute-start | bytes 1351688 | tf_op jit(solution)/shard_map/ppermute | solution.py:72
  115.1 22.9 %collective-permute-start.27 = (bf16[4,528,128]{2,1,0:T(8,128)(2,1)S(1)}, bf16[4,528,128]{2,1,0:T(8,128)(2,1)S(1)}, u32[]{:S(2)}, u32[]{:S(2)}) collective-permute-start(bf16[4,528,128]{2,1,0:T(8,128)(2,1)S(1)} %get-tuple-element.251), channel_id=1, source_target_pairs={{0,12},{1,13},{2,14},{3,15},{4,8},{5,9},{6,10},{7,11},{8,4},{9,5},... | collective-permute-start | bytes 1622024 | tf_op jit(solution)/shard_map/ppermute | solution.py:72
  119.2 19.3 %collective-permute-start.28 = (bf16[4,528,128]{2,1,0:T(8,128)(2,1)S(1)}, bf16[4,528,128]{2,1,0:T(8,128)(2,1)S(1)}, u32[]{:S(2)}, u32[]{:S(2)}) collective-permute-start(bf16[4,528,128]{2,1,0:T(8,128)(2,1)S(1)} %get-tuple-element.252), channel_id=1, source_target_pairs={{0,15},{1,14},{2,13},{3,12},{4,11},{5,10},{6,9},{7,8},{8,7},{9,6},... | collective-permute-start | bytes 1622024 | tf_op jit(solution)/shard_map/ppermute | solution.py:72
  131.4 24.6 %collective-permute-start.25 = (bf16[4,880,128]{2,1,0:T(8,128)(2,1)S(1)}, bf16[4,880,128]{2,1,0:T(8,128)(2,1)S(1)}, u32[]{:S(2)}, u32[]{:S(2)}) collective-permute-start(bf16[4,880,128]{2,1,0:T(8,128)(2,1)S(1)} %y_regroup.11), channel_id=1, source_target_pairs={{0,96},{1,97},{2,98},{3,99},{4,100},{5,101},{6,102},{7,103},{8,104... | collective-permute-start | bytes 2703368 | tf_op jit(solution)/shard_map/ppermute | solution.py:72
  134.9 26.5 %collective-permute-start.33 = (bf16[4,784,128]{2,1,0:T(8,128)(2,1)S(1)}, bf16[4,784,128]{2,1,0:T(8,128)(2,1)S(1)}, u32[]{:S(2)}, u32[]{:S(2)}) collective-permute-start(bf16[4,784,128]{2,1,0:T(8,128)(2,1)S(1)} %get-tuple-element.276), channel_id=1, source_target_pairs={{0,1},{1,0},{2,3},{3,2},{4,5},{5,4},{6,7},{7,6},{8,9},{9,8},{10,11... | collective-permute-start | bytes 2408456 | tf_op jit(solution)/shard_map/ppermute | solution.py:72
  136.1 25.2 %collective-permute-start.34 = (bf16[4,784,128]{2,1,0:T(8,128)(2,1)S(1)}, bf16[4,784,128]{2,1,0:T(8,128)(2,1)S(1)}, u32[]{:S(2)}, u32[]{:S(2)}) collective-permute-start(bf16[4,784,128]{2,1,0:T(8,128)(2,1)S(1)} %get-tuple-element.277), channel_id=1, source_target_pairs={{0,4},{1,5},{2,6},{3,7},{4,0},{5,1},{6,2},{7,3},{8,12},{9,13},{10,... | collective-permute-start | bytes 2408456 | tf_op jit(solution)/shard_map/ppermute | solution.py:72
  138.1 24.8 %collective-permute-start.35 = (bf16[4,784,128]{2,1,0:T(8,128)(2,1)S(1)}, bf16[4,784,128]{2,1,0:T(8,128)(2,1)S(1)}, u32[]{:S(2)}, u32[]{:S(2)}) collective-permute-start(bf16[4,784,128]{2,1,0:T(8,128)(2,1)S(1)} %get-tuple-element.278), channel_id=1, source_target_pairs={{0,5},{1,4},{2,7},{3,6},{4,1},{5,0},{6,3},{7,2},{8,13},{9,12},{10,... | collective-permute-start | bytes 2408456 | tf_op jit(solution)/shard_map/ppermute | solution.py:72
  138.5 15.2 %collective-permute-start.26 = (bf16[4,528,128]{2,1,0:T(8,128)(2,1)S(1)}, bf16[4,528,128]{2,1,0:T(8,128)(2,1)S(1)}, u32[]{:S(2)}, u32[]{:S(2)}) collective-permute-start(bf16[4,528,128]{2,1,0:T(8,128)(2,1)S(1)} %get-tuple-element.226), channel_id=1, source_target_pairs={{0,3},{1,2},{2,1},{3,0},{4,7},{5,6},{6,5},{7,4},{8,11},{9,10},{10,... | collective-permute-start | bytes 1622024 | tf_op jit(solution)/shard_map/ppermute | solution.py:72
  156.9 16.8 %collective-permute-start.30 = (bf16[4,784,128]{2,1,0:T(8,128)(2,1)S(1)}, bf16[4,784,128]{2,1,0:T(8,128)(2,1)S(1)}, u32[]{:S(2)}, u32[]{:S(2)}) collective-permute-start(bf16[4,784,128]{2,1,0:T(8,128)(2,1)S(1)} %get-tuple-element.273), channel_id=1, source_target_pairs={{0,1},{1,0},{2,3},{3,2},{4,5},{5,4},{6,7},{7,6},{8,9},{9,8},{10,11... | collective-permute-start | bytes 2408456 | tf_op jit(solution)/shard_map/ppermute | solution.py:72
  159.4 45.2 %collective-permute-start.31 = (bf16[4,784,128]{2,1,0:T(8,128)(2,1)S(1)}, bf16[4,784,128]{2,1,0:T(8,128)(2,1)S(1)}, u32[]{:S(2)}, u32[]{:S(2)}) collective-permute-start(bf16[4,784,128]{2,1,0:T(8,128)(2,1)S(1)} %get-tuple-element.274), channel_id=1, source_target_pairs={{0,4},{1,5},{2,6},{3,7},{4,0},{5,1},{6,2},{7,3},{8,12},{9,13},{10,... | collective-permute-start | bytes 2408456 | tf_op jit(solution)/shard_map/ppermute | solution.py:72
  161.3 43.3 %collective-permute-start.32 = (bf16[4,784,128]{2,1,0:T(8,128)(2,1)S(1)}, bf16[4,784,128]{2,1,0:T(8,128)(2,1)S(1)}, u32[]{:S(2)}, u32[]{:S(2)}) collective-permute-start(bf16[4,784,128]{2,1,0:T(8,128)(2,1)S(1)} %get-tuple-element.275), channel_id=1, source_target_pairs={{0,5},{1,4},{2,7},{3,6},{4,1},{5,0},{6,3},{7,2},{8,13},{9,12},{10,... | collective-permute-start | bytes 2408456 | tf_op jit(solution)/shard_map/ppermute | solution.py:72
  163.0 47.2 %collective-permute-start.40 = (bf16[4,784,128]{2,1,0:T(8,128)(2,1)S(1)}, bf16[4,784,128]{2,1,0:T(8,128)(2,1)S(1)}, u32[]{:S(2)}, u32[]{:S(2)}) collective-permute-start(bf16[4,784,128]{2,1,0:T(8,128)(2,1)S(1)} %get-tuple-element.291), channel_id=1, source_target_pairs={{0,12},{1,13},{2,14},{3,15},{4,8},{5,9},{6,10},{7,11},{8,4},{9,5},... | collective-permute-start | bytes 2408456 | tf_op jit(solution)/shard_map/ppermute | solution.py:72
  165.6 46.2 %collective-permute-start.41 = (bf16[4,784,128]{2,1,0:T(8,128)(2,1)S(1)}, bf16[4,784,128]{2,1,0:T(8,128)(2,1)S(1)}, u32[]{:S(2)}, u32[]{:S(2)}) collective-permute-start(bf16[4,784,128]{2,1,0:T(8,128)(2,1)S(1)} %get-tuple-element.292), channel_id=1, source_target_pairs={{0,15},{1,14},{2,13},{3,12},{4,11},{5,10},{6,9},{7,8},{8,7},{9,6},... | collective-permute-start | bytes 2408456 | tf_op jit(solution)/shard_map/ppermute | solution.py:72
  173.7 38.1 %collective-permute-start.39 = (bf16[4,784,128]{2,1,0:T(8,128)(2,1)S(1)}, bf16[4,784,128]{2,1,0:T(8,128)(2,1)S(1)}, u32[]{:S(2)}, u32[]{:S(2)}) collective-permute-start(bf16[4,784,128]{2,1,0:T(8,128)(2,1)S(1)} %get-tuple-element.283), channel_id=1, source_target_pairs={{0,3},{1,2},{2,1},{3,0},{4,7},{5,6},{6,5},{7,4},{8,11},{9,10},{10,... | collective-permute-start | bytes 2408456 | tf_op jit(solution)/shard_map/ppermute | solution.py:72
  204.8 24.2 %collective-permute-start.37 = (bf16[4,784,128]{2,1,0:T(8,128)(2,1)S(1)}, bf16[4,784,128]{2,1,0:T(8,128)(2,1)S(1)}, u32[]{:S(2)}, u32[]{:S(2)}) collective-permute-start(bf16[4,784,128]{2,1,0:T(8,128)(2,1)S(1)} %get-tuple-element.289), channel_id=1, source_target_pairs={{0,12},{1,13},{2,14},{3,15},{4,8},{5,9},{6,10},{7,11},{8,4},{9,5},... | collective-permute-start | bytes 2408456 | tf_op jit(solution)/shard_map/ppermute | solution.py:72
  210.2 18.8 %collective-permute-start.38 = (bf16[4,784,128]{2,1,0:T(8,128)(2,1)S(1)}, bf16[4,784,128]{2,1,0:T(8,128)(2,1)S(1)}, u32[]{:S(2)}, u32[]{:S(2)}) collective-permute-start(bf16[4,784,128]{2,1,0:T(8,128)(2,1)S(1)} %get-tuple-element.290), channel_id=1, source_target_pairs={{0,15},{1,14},{2,13},{3,12},{4,11},{5,10},{6,9},{7,8},{8,7},{9,6},... | collective-permute-start | bytes 2408456 | tf_op jit(solution)/shard_map/ppermute | solution.py:72
  210.3 20.3 %collective-permute-start.36 = (bf16[4,784,128]{2,1,0:T(8,128)(2,1)S(1)}, bf16[4,784,128]{2,1,0:T(8,128)(2,1)S(1)}, u32[]{:S(2)}, u32[]{:S(2)}) collective-permute-start(bf16[4,784,128]{2,1,0:T(8,128)(2,1)S(1)} %get-tuple-element.288), channel_id=1, source_target_pairs={{0,3},{1,2},{2,1},{3,0},{4,7},{5,6},{6,5},{7,4},{8,11},{9,10},{10,... | collective-permute-start | bytes 2408456 | tf_op jit(solution)/shard_map/ppermute | solution.py:72

commit v9 on v5

--- a/solution.py
+++ b/solution.py
@@ -1,6 +1,5 @@
 import functools
 
-import numpy as np
 import jax
 import jax.numpy as jnp
 from jax import lax
@@ -39,13 +38,6 @@
 BOTH = ("fsdp", "tp")
 
 
-def hadamard_table(order):
-    matrix = np.ones((1, 1), np.float32)
-    while matrix.shape[0] < order:
-        matrix = np.block([[matrix, matrix], [matrix, -matrix]])
-    return matrix
-
-
 def butterfly(values):
     values = list(values)
     half = 1
@@ -132,13 +124,18 @@
     return (1 - 2 * (both & 1)).astype(jnp.float32)
 
 
-def local_turn_kernel(rows_a, weight_ref, signs_ref, *refs):
+def local_turn_kernel(rows_a, weight_ref, *refs):
     out_refs, turned = refs[:-1], refs[-1]
     group = lax.axis_index("fsdp")
     swap = group & 1 != 0
     flips = [sign_of(group, a >> 1) * (1.0 / HAD) for a in range(rows_a)]
     columns = jnp.concatenate([weight_ref[a * HAD : (a + 1) * HAD, :].T for a in range(rows_a)], axis=0)
-    turned[...] = jnp.dot(columns, signs_ref[...], preferred_element_type=jnp.float32)
+    both = [lax.broadcasted_iota(jnp.int32, (HAD, HAD), dim) for dim in range(2)]
+    both = both[0] & both[1]
+    for shift in (4, 2, 1):
+        both = both ^ (both >> shift)
+    signs = (1 - 2 * (both & 1)).astype(jnp.float32).astype(jnp.bfloat16)
+    turned[...] = jnp.dot(columns, signs, preferred_element_type=jnp.float32)
     for index, (first, chans) in enumerate(CHUNKS):
         for low in range(0, chans, 16):
             outs = []
@@ -242,38 +239,38 @@
         slot_ref[source] = count
         count = count + live
     lane = lax.broadcasted_iota(jnp.int32, (TAIL, HAD), 1)
-    depth = buffer.shape[0]
-    copies = [None] * depth
+    copies = []
     core = group & 1
     pair = jnp.where(core == 0, 2, 6)
     offsets = (0, 1, pair, pair ^ 1, pair ^ 4, pair ^ 5, 4, 5)
+    blocks, rows = [], []
     for origin in range(owners):
         i, j = origin % 4, origin // 4
         in_ref, index = (in_refs[3 + j], i) if j else (in_refs[i], 0)
         source = me ^ pairing_offset(core, 0, i) ^ pairing_offset(core, 1, j)
-        part = origin % depth
-        if copies[part] is not None:
-            copies[part].wait()
         live = live_ref[source] != 0
         slot = jnp.where(live, slot_ref[source], count + source - slot_ref[source])
         tail = in_ref[index, 16 * chans :, :].astype(jnp.float32)
-        row = jnp.where((lane < chans) & live, join_parts(tail, chans), 0.0)[:1, :]
-        scale = jnp.where(live, 1.0 / (row + 1e-06), 0.0)
-        scale = jnp.broadcast_to(scale, (HEAD_DIM, HAD)).T[:chans, :]
-        row = pltpu.roll(jnp.broadcast_to(row, (8, HAD)), first, 1)[:1, :] if first else row
+        row = jnp.where((lane < chans) & live, join_parts(tail, chans), 0.0)
+        rows.append(jnp.where(live, 1.0 / (row[:1, :] + 1e-06), 0.0))
+        row = (pltpu.roll(row, first, 1) if first else row)[:1, :]
         if has_past:
             row = row + past_ref[pl.ds(slot, 1), :]
         peak_ref[pl.ds(slot, 1), :] = row
+        blocks.append((in_ref, index, slot))
+    rows.append(jnp.zeros((HAD - owners, HAD), jnp.float32))
+    scales = jnp.concatenate(rows, axis=0).T
+    for origin, (in_ref, index, slot) in enumerate(blocks):
+        scale = scales[:chans, origin : origin + 1]
         for s in range(8):
             for e in range(2):
                 start = (s * 2 + e) * chans
                 lanes = pl.ds(pl.multiple_of(((group ^ offsets[s]) * 2 + e) * HAD, HAD), HAD)
                 block = in_ref[index, start : start + chans, :]
-                buffer[part, :, lanes] = (block.astype(jnp.float32) * scale).astype(jnp.bfloat16)
-        copies[part] = pltpu.make_async_copy(
-            buffer.at[part], out_ref.at[0, slot, first : first + chans, :], sems.at[part]
-        )
-        copies[part].start()
+                buffer[origin, :, lanes] = (block.astype(jnp.float32) * scale).astype(jnp.bfloat16)
+        rows = out_ref.at[0, slot, first : first + chans, :]
+        copies.append(pltpu.make_async_copy(buffer.at[origin], rows, sems.at[origin]))
+        copies[-1].start()
     for copy in copies:
         copy.wait()
 
@@ -298,21 +295,17 @@
             name=name,
         )(*arrays)
 
-    signs = jnp.asarray(hadamard_table(HAD), jnp.bfloat16)
     widths = [2 * chans for _, chans in CHUNKS for _ in range(4)]
     turned = pl.pallas_call(
         functools.partial(local_turn_kernel, rows_a),
         grid=(heads,),
-        in_specs=[
-            pl.BlockSpec((rows_local, HEAD_DIM), lambda h: (0, h)),
-            pl.BlockSpec((HAD, HAD), lambda h: (0, 0)),
-        ],
+        in_specs=[pl.BlockSpec((rows_local, HEAD_DIM), lambda h: (0, h))],
         out_specs=[pl.BlockSpec((2, width, HAD), lambda h: (0, h, 0)) for width in widths],
         out_shape=[jax.ShapeDtypeStruct((2, heads * width, HAD), jnp.bfloat16) for width in widths],
         scratch_shapes=[pltpu.VMEM((rows_local, HAD), jnp.float32)],
         compiler_params=params,
         name="local_turn",
-    )(qkv_weight, signs)
+    )(qkv_weight)
 
     state = [turned[4 * index : 4 * index + 4] for index in range(len(CHUNKS))]
     token = None
@@ -341,7 +334,7 @@
             kernel = functools.partial(spread_kernel, heads, chans)
             outs = call(kernel, stage, shapes, placement, *arrays, table=True)
             token = outs[0]
-            state[index] = [outs[0]] + owner_hops(outs[1:], 0)
+            state[index] = [token] + owner_hops(outs[1:], 0)
         elif stage == "regroup":
             outs = call(regroup_kernel, stage, [arrays[0].shape[:2]] * 3, *arrays)
             token = outs[0]
@@ -356,8 +349,8 @@
                     jax.ShapeDtypeStruct((1, owners, HEAD_DIM, rows_local), jnp.bfloat16),
                 ],
                 scratch_shapes=[
-                    pltpu.VMEM((3, chans, rows_local), jnp.bfloat16),
-                    pltpu.SemaphoreType.DMA((3,)),
+                    pltpu.VMEM((owners, chans, rows_local), jnp.bfloat16),
+                    pltpu.SemaphoreType.DMA((owners,)),
                     pltpu.SMEM((owners,), jnp.int32),
                     pltpu.SMEM((owners,), jnp.int32),
                 ],

time: 212 us -> 208 us (0.981)
  Pallas kernels: 30 us -> 20.5 us
  waiting for transfers between devices: 122 us -> 127 us
    pallas_call x3, Pallas kernels: 18 us -> 8.52 us  [per_device(): pl.pallas_call(functools.partial(pack_kernel, owners, heads, chunk, bool(...]
    ppermute x42, waiting for transfers between devices: 122 us -> 127 us  [hop(): return lax.ppermute(array, BOTH, pairs)]
  transfers between devices with their start and end apart: 42 -> 42, of which waited for: 21 -> 22; matrix products, arithmetic and copies ran while one was open for 0% -> 0% of each run, Pallas kernels for 8% -> 6%
where the time goes in v9:
time: 208 us; the launch traced here: 206 us
  waiting for transfers between devices  127 us (61%)
  starting transfers between devices  55.6 us (27%)
  Pallas kernels  20.5 us (10%)
  local copies, waits for them, and re-layouts  2.33 us (1%)
    ppermute x42, waiting for transfers between devices, hop(): return lax.ppermute(array, BOTH, pairs)  127 us
    ppermute x42, starting transfers between devices, hop(): return lax.ppermute(array, BOTH, pairs)  55.6 us
    pallas_call x3, Pallas kernels, per_device(): pl.pallas_call(functools.partial(pack_kernel, owners, heads, chunk, bool(...  8.52 us
    pallas_call x15, Pallas kernels, call(): pl.pallas_call(kernel, in_specs=[smem_spec] * table + [vmem_spec] * (len(...  6.35 us
    pallas_call x1, Pallas kernels, per_device(): pl.pallas_call(functools.partial(local_turn_kernel, rows_a), grid=(heads,...  5.61 us
  transfers between devices with their start and end apart: 42, of which 22 were waited for; matrix products, arithmetic and copies ran while one was open for 0% of the time, Pallas kernels for 6%

profile of v9, /device:TPU:0, one launch (start us, length us, event | category | flops | bytes accessed | tf_op | source)
XLA Modules:
  0.0 206.3 jit_solution(17577594017587549563)
XLA Ops:
  0.6 2.3 %copy-done = bf16[2048,1152]{1,0:T(8,128)(2,1)S(1)} copy-done((bf16[2048,1152]{1,0:T(8,128)(2,1)S(1)}, bf16[2048,1152]{1,0:T(8,128)(2,1)}, u32[]{:S(2)}) %copy-start) | copy-done | bytes 4718616
  3.0 5.6 %local_turn.1 = (bf16[2,576,128]{2,1,0:T(8,128)(2,1)S(1)}, bf16[2,576,128]{2,1,0:T(8,128)(2,1)S(1)}, bf16[2,576,128]{2,1,0:T(8,128)(2,1)S(1)}, bf16[2,576,128]{2...) custom-call(bf16[2048,1152]{1,0:T(8,128)(2,1)S(1)} %copy-done), custom_call_target="tpu_custom_call" | custom-call | tf_op jit(solution)/shard_map/local_turn/pallas_call | solution.py:299
  8.7 1.7 collective-permute-start.1
  10.4 1.5 collective-permute-start.2
  12.0 0.6 collective-permute-start.5
  12.6 2.4 %collective-permute-start.6 = (bf16[2,864,128]{2,1,0:T(8,128)(2,1)S(1)}, bf16[2,864,128]{2,1,0:T(8,128)(2,1)S(1)}, u32[]{:S(2)}, u32[]{:S(2)}) collective-permute-start(bf16[2,864,128]{2,1,0:T(8,128)(2,1)S(1)} %get-tuple-element.151), channel_id=1, source_target_pairs={{0,112},{1,113},{2,114},{3,115},{4,116},{5,117},{6,118},{7,119},{8... | collective-permute-start | bytes 1327112 | tf_op jit(solution)/shard_map/ppermute | solution.py:63
  15.0 2.5 %collective-permute-done.1.refs_2_ = bf16[2,576,128]{2,1,0:T(8,128)(2,1)S(1)} collective-permute-done((bf16[2,576,128]{2,1,0:T(8,128)(2,1)S(1)}, bf16[2,576,128]{2,1,0:T(8,128)(2,1)S(1)}, u32[]{:S(2)}, u32[]{:S(2)}) %collective-permute-start.1) | collective-permute-done | bytes 294944 | tf_op jit(solution)/shard_map/ppermute | solution.py:63
  17.5 2.2 %collective-permute-done.2.refs_3_ = bf16[2,576,128]{2,1,0:T(8,128)(2,1)S(1)} collective-permute-done((bf16[2,576,128]{2,1,0:T(8,128)(2,1)S(1)}, bf16[2,576,128]{2,1,0:T(8,128)(2,1)S(1)}, u32[]{:S(2)}, u32[]{:S(2)}) %collective-permute-start.2) | collective-permute-done | bytes 294944 | tf_op jit(solution)/shard_map/ppermute | solution.py:63
  19.8 2.6 %collective-permute-start.3 = (bf16[4,576,128]{2,1,0:T(8,128)(2,1)S(1)}, bf16[4,576,128]{2,1,0:T(8,128)(2,1)S(1)}, u32[]{:S(2)}, u32[]{:S(2)}) collective-permute-start(bf16[4,576,128]{2,1,0:T(8,128)(2,1)S(1)} %y_regroup.6), channel_id=1, source_target_pairs={{0,96},{1,97},{2,98},{3,99},{4,100},{5,101},{6,102},{7,103},{8,104... | collective-permute-start | bytes 1769480 | tf_op jit(solution)/shard_map/ppermute | solution.py:63
  22.4 4.6 %collective-permute-done.5.refs_2_ = bf16[2,864,128]{2,1,0:T(8,128)(2,1)S(1)} collective-permute-done((bf16[2,864,128]{2,1,0:T(8,128)(2,1)S(1)}, bf16[2,864,128]{2,1,0:T(8,128)(2,1)S(1)}, u32[]{:S(2)}, u32[]{:S(2)}) %collective-permute-start.5) | collective-permute-done | bytes 442400 | tf_op jit(solution)/shard_map/ppermute | solution.py:63
  27.0 1.2 collective-permute-done.6.refs_3_
  28.3 3.1 %collective-permute-start.14 = (bf16[4,864,128]{2,1,0:T(8,128)(2,1)S(1)}, bf16[4,864,128]{2,1,0:T(8,128)(2,1)S(1)}, u32[]{:S(2)}, u32[]{:S(2)}) collective-permute-start(bf16[4,864,128]{2,1,0:T(8,128)(2,1)S(1)} %y_regroup.7), channel_id=1, source_target_pairs={{0,96},{1,97},{2,98},{3,99},{4,100},{5,101},{6,102},{7,103},{8,104... | collective-permute-start | bytes 2654216 | tf_op jit(solution)/shard_map/ppermute | solution.py:63
  31.4 3.9 %collective-permute-done.3.refs_4_ = bf16[4,576,128]{2,1,0:T(8,128)(2,1)S(1)} collective-permute-done((bf16[4,576,128]{2,1,0:T(8,128)(2,1)S(1)}, bf16[4,576,128]{2,1,0:T(8,128)(2,1)S(1)}, u32[]{:S(2)}, u32[]{:S(2)}) %collective-permute-start.3) | collective-permute-done | bytes 589856 | tf_op jit(solution)/shard_map/ppermute | solution.py:63
  35.3 0.8 cross.3
  36.1 1.0 collective-permute-start.11
  37.1 2.1 %collective-permute-start.12 = (bf16[2,592,128]{2,1,0:T(8,128)(2,1)S(1)}, bf16[2,592,128]{2,1,0:T(8,128)(2,1)S(1)}, u32[]{:S(2)}, u32[]{:S(2)}) collective-permute-start(bf16[2,592,128]{2,1,0:T(8,128)(2,1)S(1)} %get-tuple-element.168), channel_id=1, source_target_pairs={{0,112},{1,113},{2,114},{3,115},{4,116},{5,117},{6,118},{7,119},{8... | collective-permute-start | bytes 909320 | tf_op jit(solution)/shard_map/ppermute | solution.py:63
  39.3 7.0 %collective-permute-done.11.refs_2_ = bf16[2,592,128]{2,1,0:T(8,128)(2,1)S(1)} collective-permute-done((bf16[2,592,128]{2,1,0:T(8,128)(2,1)S(1)}, bf16[2,592,128]{2,1,0:T(8,128)(2,1)S(1)}, u32[]{:S(2)}, u32[]{:S(2)}) %collective-permute-start.11) | collective-permute-done | bytes 303136 | tf_op jit(solution)/shard_map/ppermute | solution.py:63
  46.3 4.2 %collective-permute-done.12.refs_3_ = bf16[2,592,128]{2,1,0:T(8,128)(2,1)S(1)} collective-permute-done((bf16[2,592,128]{2,1,0:T(8,128)(2,1)S(1)}, bf16[2,592,128]{2,1,0:T(8,128)(2,1)S(1)}, u32[]{:S(2)}, u32[]{:S(2)}) %collective-permute-start.12) | collective-permute-done | bytes 303136 | tf_op jit(solution)/shard_map/ppermute | solution.py:63
  50.5 3.1 %collective-permute-start.13 = (bf16[4,592,128]{2,1,0:T(8,128)(2,1)S(1)}, bf16[4,592,128]{2,1,0:T(8,128)(2,1)S(1)}, u32[]{:S(2)}, u32[]{:S(2)}) collective-permute-start(bf16[4,592,128]{2,1,0:T(8,128)(2,1)S(1)} %y_regroup.8), channel_id=1, source_target_pairs={{0,96},{1,97},{2,98},{3,99},{4,100},{5,101},{6,102},{7,103},{8,104... | collective-permute-start | bytes 1818632 | tf_op jit(solution)/shard_map/ppermute | solution.py:63
  53.7 1.1 cross.4
  55.0 1.9 collective-permute-start.8
  56.9 1.0 collective-permute-start.9
  57.9 8.8 %collective-permute-done.13.refs_4_ = bf16[4,592,128]{2,1,0:T(8,128)(2,1)S(1)} collective-permute-done((bf16[4,592,128]{2,1,0:T(8,128)(2,1)S(1)}, bf16[4,592,128]{2,1,0:T(8,128)(2,1)S(1)}, u32[]{:S(2)}, u32[]{:S(2)}) %collective-permute-start.13) | collective-permute-done | bytes 606240 | tf_op jit(solution)/shard_map/ppermute | solution.py:63
  66.7 0.5 collective-permute-start.21
  67.2 0.8 spread.3
  68.0 9.6 %collective-permute-done.8.refs_2_ = bf16[2,864,128]{2,1,0:T(8,128)(2,1)S(1)} collective-permute-done((bf16[2,864,128]{2,1,0:T(8,128)(2,1)S(1)}, bf16[2,864,128]{2,1,0:T(8,128)(2,1)S(1)}, u32[]{:S(2)}, u32[]{:S(2)}) %collective-permute-start.8) | collective-permute-done | bytes 442400 | tf_op jit(solution)/shard_map/ppermute | solution.py:63
  77.7 0.5 collective-permute-start.15
  78.2 1.5 collective-permute-start.16
  79.7 1.9 collective-permute-start.17
  81.8 2.9 %collective-permute-start.28 = (bf16[4,880,128]{2,1,0:T(8,128)(2,1)S(1)}, bf16[4,880,128]{2,1,0:T(8,128)(2,1)S(1)}, u32[]{:S(2)}, u32[]{:S(2)}) collective-permute-start(bf16[4,880,128]{2,1,0:T(8,128)(2,1)S(1)} %y_regroup.10), channel_id=1, source_target_pairs={{0,96},{1,97},{2,98},{3,99},{4,100},{5,101},{6,102},{7,103},{8,104... | collective-permute-start | bytes 2703368 | tf_op jit(solution)/shard_map/ppermute | solution.py:63
  84.7 2.9 %collective-permute-done.16.refs_1_ = bf16[4,528,128]{2,1,0:T(8,128)(2,1)S(1)} collective-permute-done((bf16[4,528,128]{2,1,0:T(8,128)(2,1)S(1)}, bf16[4,528,128]{2,1,0:T(8,128)(2,1)S(1)}, u32[]{:S(2)}, u32[]{:S(2)}) %collective-permute-start.16) | collective-permute-done | bytes 540704 | tf_op jit(solution)/shard_map/ppermute | solution.py:63
  87.6 7.3 %collective-permute-done.17.refs_2_ = bf16[4,528,128]{2,1,0:T(8,128)(2,1)S(1)} collective-permute-done((bf16[4,528,128]{2,1,0:T(8,128)(2,1)S(1)}, bf16[4,528,128]{2,1,0:T(8,128)(2,1)S(1)}, u32[]{:S(2)}, u32[]{:S(2)}) %collective-permute-start.17) | collective-permute-done | bytes 540704 | tf_op jit(solution)/shard_map/ppermute | solution.py:63
  95.0 4.1 %collective-permute-start.26 = (bf16[4,528,128]{2,1,0:T(8,128)(2,1)S(1)}, bf16[4,528,128]{2,1,0:T(8,128)(2,1)S(1)}, u32[]{:S(2)}, u32[]{:S(2)}) collective-permute-start(bf16[4,528,128]{2,1,0:T(8,128)(2,1)S(1)} %get-tuple-element.213), channel_id=1, source_target_pairs={{0,12},{1,13},{2,14},{3,15},{4,8},{5,9},{6,10},{7,11},{8,4},{9,5},... | collective-permute-start | bytes 1622024 | tf_op jit(solution)/shard_map/ppermute | solution.py:63
  99.1 1.6 collective-permute-start.27
  100.7 1.1 collective-permute-start.25
  101.9 1.1 cross.5
  103.0 0.9 spread.4
  104.2 7.6 %collective-permute-done.26.refs_5_ = bf16[4,528,128]{2,1,0:T(8,128)(2,1)S(1)} collective-permute-done((bf16[4,528,128]{2,1,0:T(8,128)(2,1)S(1)}, bf16[4,528,128]{2,1,0:T(8,128)(2,1)S(1)}, u32[]{:S(2)}, u32[]{:S(2)}) %collective-permute-start.26) | collective-permute-done | bytes 540704 | tf_op jit(solution)/shard_map/ppermute | solution.py:63
  111.8 0.4 collective-permute-start.31
  112.1 0.6 collective-permute-done.27.refs_6_
  112.7 1.5 collective-permute-start.32
  114.2 7.5 %collective-permute-done.25.refs_4_ = bf16[4,528,128]{2,1,0:T(8,128)(2,1)S(1)} collective-permute-done((bf16[4,528,128]{2,1,0:T(8,128)(2,1)S(1)}, bf16[4,528,128]{2,1,0:T(8,128)(2,1)S(1)}, u32[]{:S(2)}, u32[]{:S(2)}) %collective-permute-start.25) | collective-permute-done | bytes 540704 | tf_op jit(solution)/shard_map/ppermute | solution.py:63
  121.7 1.1 collective-permute-start.23
  122.8 2.4 %pack.3 = (f32[16,128]{1,0:T(8,128)S(1)}, bf16[1,16,128,2048]{3,2,1,0:T(8,128)(2,1)}) custom-call(s32[144]{0:T(256)S(1)} %copy-done.1, bf16[4,528,128]{2,1,0:T(8,128)(2,1)S(1)} %get-tuple-element.221.refs_0_, bf16[4,528,128]{2,1,0:T(8,128)(2,1)S(1)} %collective-permute-done.16.refs_1_, bf16[4,528,128]{2,1,0:T(8,128)(2,1)S(1)} %collective-permute-done.17.refs_2_, ...), custom_call_target="tpu_custom_call" | custom-call | tf_op jit(solution)/shard_map/pack/pallas_call | solution.py:343
  125.2 9.2 %collective-permute-done.23.refs_2_ = bf16[2,880,128]{2,1,0:T(8,128)(2,1)S(1)} collective-permute-done((bf16[2,880,128]{2,1,0:T(8,128)(2,1)S(1)}, bf16[2,880,128]{2,1,0:T(8,128)(2,1)S(1)}, u32[]{:S(2)}, u32[]{:S(2)}) %collective-permute-start.23) | collective-permute-done | bytes 450592 | tf_op jit(solution)/shard_map/ppermute | solution.py:63
  134.5 0.5 collective-permute-done.24.refs_3_
  135.0 2.4 %collective-permute-start.29 = (bf16[4,880,128]{2,1,0:T(8,128)(2,1)S(1)}, bf16[4,880,128]{2,1,0:T(8,128)(2,1)S(1)}, u32[]{:S(2)}, u32[]{:S(2)}) collective-permute-start(bf16[4,880,128]{2,1,0:T(8,128)(2,1)S(1)} %y_regroup.11), channel_id=1, source_target_pairs={{0,96},{1,97},{2,98},{3,99},{4,100},{5,101},{6,102},{7,103},{8,104... | collective-permute-start | bytes 2703368 | tf_op jit(solution)/shard_map/ppermute | solution.py:63
  137.5 3.2 %collective-permute-start.37 = (bf16[4,784,128]{2,1,0:T(8,128)(2,1)S(1)}, bf16[4,784,128]{2,1,0:T(8,128)(2,1)S(1)}, u32[]{:S(2)}, u32[]{:S(2)}) collective-permute-start(bf16[4,784,128]{2,1,0:T(8,128)(2,1)S(1)} %get-tuple-element.250), channel_id=1, source_target_pairs={{0,12},{1,13},{2,14},{3,15},{4,8},{5,9},{6,10},{7,11},{8,4},{9,5},... | collective-permute-start | bytes 2408456 | tf_op jit(solution)/shard_map/ppermute | solution.py:63
  140.8 1.6 collective-permute-start.38
  142.4 1.1 collective-permute-start.36
  143.5 6.0 %collective-permute-done.29.refs_4_ = bf16[4,880,128]{2,1,0:T(8,128)(2,1)S(1)} collective-permute-done((bf16[4,880,128]{2,1,0:T(8,128)(2,1)S(1)}, bf16[4,880,128]{2,1,0:T(8,128)(2,1)S(1)}, u32[]{:S(2)}, u32[]{:S(2)}) %collective-permute-start.29) | collective-permute-done | bytes 901152 | tf_op jit(solution)/shard_map/ppermute | solution.py:63
  149.5 0.9 spread.5
  150.4 1.2 collective-permute-start.33
  151.6 12.6 %collective-permute-done.37.refs_5_ = bf16[4,784,128]{2,1,0:T(8,128)(2,1)S(1)} collective-permute-done((bf16[4,784,128]{2,1,0:T(8,128)(2,1)S(1)}, bf16[4,784,128]{2,1,0:T(8,128)(2,1)S(1)}, u32[]{:S(2)}, u32[]{:S(2)}) %collective-permute-start.37) | collective-permute-done | bytes 802848 | tf_op jit(solution)/shard_map/ppermute | solution.py:63
  164.2 0.4 collective-permute-start.35
  164.7 8.9 %collective-permute-done.36.refs_4_ = bf16[4,784,128]{2,1,0:T(8,128)(2,1)S(1)} collective-permute-done((bf16[4,784,128]{2,1,0:T(8,128)(2,1)S(1)}, bf16[4,784,128]{2,1,0:T(8,128)(2,1)S(1)}, u32[]{:S(2)}, u32[]{:S(2)}) %collective-permute-start.36) | collective-permute-done | bytes 802848 | tf_op jit(solution)/shard_map/ppermute | solution.py:63
  173.6 2.8 %pack.4 = (f32[16,128]{1,0:T(8,128)S(1)}, bf16[1,16,128,2048]{3,2,1,0:T(8,128)(2,1)}) custom-call(s32[144]{0:T(256)S(1)} %copy-done.1, bf16[4,784,128]{2,1,0:T(8,128)(2,1)S(1)} %get-tuple-element.252.refs_0_, bf16[4,784,128]{2,1,0:T(8,128)(2,1)S(1)} %collective-permute-done.30.refs_1_, ...), custom_call_target="tpu_custom_call", output_to_operand_aliasing={{1}: (9, {})} | custom-call | tf_op jit(solution)/shard_map/pack/pallas_call | solution.py:343
  176.4 0.9 collective-permute-done.35.refs_3_
  177.5 3.8 %collective-permute-start.40 = (bf16[4,784,128]{2,1,0:T(8,128)(2,1)S(1)}, bf16[4,784,128]{2,1,0:T(8,128)(2,1)S(1)}, u32[]{:S(2)}, u32[]{:S(2)}) collective-permute-start(bf16[4,784,128]{2,1,0:T(8,128)(2,1)S(1)} %get-tuple-element.266), channel_id=1, source_target_pairs={{0,12},{1,13},{2,14},{3,15},{4,8},{5,9},{6,10},{7,11},{8,4},{9,5},... | collective-permute-start | bytes 2408456 | tf_op jit(solution)/shard_map/ppermute | solution.py:63
  181.2 2.1 %collective-permute-start.41 = (bf16[4,784,128]{2,1,0:T(8,128)(2,1)S(1)}, bf16[4,784,128]{2,1,0:T(8,128)(2,1)S(1)}, u32[]{:S(2)}, u32[]{:S(2)}) collective-permute-start(bf16[4,784,128]{2,1,0:T(8,128)(2,1)S(1)} %get-tuple-element.267), channel_id=1, source_target_pairs={{0,15},{1,14},{2,13},{3,12},{4,11},{5,10},{6,9},{7,8},{8,7},{9,6},... | collective-permute-start | bytes 2408456 | tf_op jit(solution)/shard_map/ppermute | solution.py:63
  183.3 0.7 collective-permute-start.39
  184.0 16.0 %collective-permute-done.40.refs_5_ = bf16[4,784,128]{2,1,0:T(8,128)(2,1)S(1)} collective-permute-done((bf16[4,784,128]{2,1,0:T(8,128)(2,1)S(1)}, bf16[4,784,128]{2,1,0:T(8,128)(2,1)S(1)}, u32[]{:S(2)}, u32[]{:S(2)}) %collective-permute-start.40) | collective-permute-done | bytes 802848 | tf_op jit(solution)/shard_map/ppermute | solution.py:63
  200.0 2.8 %collective-permute-done.39.refs_4_ = bf16[4,784,128]{2,1,0:T(8,128)(2,1)S(1)} collective-permute-done((bf16[4,784,128]{2,1,0:T(8,128)(2,1)S(1)}, bf16[4,784,128]{2,1,0:T(8,128)(2,1)S(1)}, u32[]{:S(2)}, u32[]{:S(2)}) %collective-permute-start.39) | collective-permute-done | bytes 802848 | tf_op jit(solution)/shard_map/ppermute | solution.py:63
  202.8 3.4 %pack.5 = (f32[16,128]{1,0:T(8,128)}, bf16[1,16,128,2048]{3,2,1,0:T(8,128)(2,1)}) custom-call(s32[144]{0:T(256)S(1)} %copy-done.1, bf16[4,784,128]{2,1,0:T(8,128)(2,1)S(1)} %get-tuple-element.268.refs_0_, bf16[4,784,128]{2,1,0:T(8,128)(2,1)S(1)} %collective-permute-done.33.refs_1_, ...), custom_call_target="tpu_custom_call", output_to_operand_aliasing={{1}: (9, {})} | custom-call | tf_op jit(solution)/shard_map/pack/pallas_call | solution.py:343
  (43 shorter events, 1.7 us)
Async XLA Ops:
  0.6 2.3 %copy-start = (bf16[2048,1152]{1,0:T(8,128)(2,1)S(1)}, bf16[2048,1152]{1,0:T(8,128)(2,1)}, u32[]{:S(2)}) copy-start(bf16[2048,1152]{1,0:T(8,128)(2,1)} %weight_ref.1) | copy-start | bytes 14155780
  3.0 64.2 %copy-start.1 = (s32[144]{0:T(256)S(1)}, s32[144]{0:T(256)}, u32[]{:S(2)}) copy-start(s32[144]{0:T(256)} %placement_ref.11) | copy-start | bytes 1732
  8.6 4.0 %collective-permute-start = (bf16[2,576,128]{2,1,0:T(8,128)(2,1)S(1)}, bf16[2,576,128]{2,1,0:T(8,128)(2,1)S(1)}, u32[]{:S(2)}, u32[]{:S(2)}) collective-permute-start(bf16[2,576,128]{2,1,0:T(8,128)(2,1)S(1)} %get-tuple-element.145), channel_id=1, source_target_pairs={{0,16},{1,17},{2,18},{3,19},{4,20},{5,21},{6,22},{7,23},{8,24},{9,... | collective-permute-start | bytes 884744 | tf_op jit(solution)/shard_map/ppermute | solution.py:63
  8.7 8.9 %collective-permute-start.1 = (bf16[2,576,128]{2,1,0:T(8,128)(2,1)S(1)}, bf16[2,576,128]{2,1,0:T(8,128)(2,1)S(1)}, u32[]{:S(2)}, u32[]{:S(2)}) collective-permute-start(bf16[2,576,128]{2,1,0:T(8,128)(2,1)S(1)} %get-tuple-element.146), channel_id=1, source_target_pairs={{0,32},{1,33},{2,34},{3,35},{4,36},{5,37},{6,38},{7,39},{8,40},{9,... | collective-permute-start | bytes 884744 | tf_op jit(solution)/shard_map/ppermute | solution.py:63
  10.4 9.3 %collective-permute-start.2 = (bf16[2,576,128]{2,1,0:T(8,128)(2,1)S(1)}, bf16[2,576,128]{2,1,0:T(8,128)(2,1)S(1)}, u32[]{:S(2)}, u32[]{:S(2)}) collective-permute-start(bf16[2,576,128]{2,1,0:T(8,128)(2,1)S(1)} %get-tuple-element.147), channel_id=1, source_target_pairs={{0,112},{1,113},{2,114},{3,115},{4,116},{5,117},{6,118},{7,119},{8... | collective-permute-start | bytes 884744 | tf_op jit(solution)/shard_map/ppermute | solution.py:63
  11.9 10.5 %collective-permute-start.4 = (bf16[2,864,128]{2,1,0:T(8,128)(2,1)S(1)}, bf16[2,864,128]{2,1,0:T(8,128)(2,1)S(1)}, u32[]{:S(2)}, u32[]{:S(2)}) collective-permute-start(bf16[2,864,128]{2,1,0:T(8,128)(2,1)S(1)} %get-tuple-element.149), channel_id=1, source_target_pairs={{0,16},{1,17},{2,18},{3,19},{4,20},{5,21},{6,22},{7,23},{8,24},{9,... | collective-permute-start | bytes 1327112 | tf_op jit(solution)/shard_map/ppermute | solution.py:63
  12.0 15.0 %collective-permute-start.5 = (bf16[2,864,128]{2,1,0:T(8,128)(2,1)S(1)}, bf16[2,864,128]{2,1,0:T(8,128)(2,1)S(1)}, u32[]{:S(2)}, u32[]{:S(2)}) collective-permute-start(bf16[2,864,128]{2,1,0:T(8,128)(2,1)S(1)} %get-tuple-element.150), channel_id=1, source_target_pairs={{0,32},{1,33},{2,34},{3,35},{4,36},{5,37},{6,38},{7,39},{8,40},{9,... | collective-permute-start | bytes 1327112 | tf_op jit(solution)/shard_map/ppermute | solution.py:63
  12.6 15.6 %collective-permute-start.6 = (bf16[2,864,128]{2,1,0:T(8,128)(2,1)S(1)}, bf16[2,864,128]{2,1,0:T(8,128)(2,1)S(1)}, u32[]{:S(2)}, u32[]{:S(2)}) collective-permute-start(bf16[2,864,128]{2,1,0:T(8,128)(2,1)S(1)} %get-tuple-element.151), channel_id=1, source_target_pairs={{0,112},{1,113},{2,114},{3,115},{4,116},{5,117},{6,118},{7,119},{8... | collective-permute-start | bytes 1327112 | tf_op jit(solution)/shard_map/ppermute | solution.py:63
  19.8 15.5 %collective-permute-start.3 = (bf16[4,576,128]{2,1,0:T(8,128)(2,1)S(1)}, bf16[4,576,128]{2,1,0:T(8,128)(2,1)S(1)}, u32[]{:S(2)}, u32[]{:S(2)}) collective-permute-start(bf16[4,576,128]{2,1,0:T(8,128)(2,1)S(1)} %y_regroup.6), channel_id=1, source_target_pairs={{0,96},{1,97},{2,98},{3,99},{4,100},{5,101},{6,102},{7,103},{8,104... | collective-permute-start | bytes 1769480 | tf_op jit(solution)/shard_map/ppermute | solution.py:63
  28.3 25.4 %collective-permute-start.14 = (bf16[4,864,128]{2,1,0:T(8,128)(2,1)S(1)}, bf16[4,864,128]{2,1,0:T(8,128)(2,1)S(1)}, u32[]{:S(2)}, u32[]{:S(2)}) collective-permute-start(bf16[4,864,128]{2,1,0:T(8,128)(2,1)S(1)} %y_regroup.7), channel_id=1, source_target_pairs={{0,96},{1,97},{2,98},{3,99},{4,100},{5,101},{6,102},{7,103},{8,104... | collective-permute-start | bytes 2654216 | tf_op jit(solution)/shard_map/ppermute | solution.py:63
  36.1 3.2 %collective-permute-start.10 = (bf16[2,592,128]{2,1,0:T(8,128)(2,1)S(1)}, bf16[2,592,128]{2,1,0:T(8,128)(2,1)S(1)}, u32[]{:S(2)}, u32[]{:S(2)}) collective-permute-start(bf16[2,592,128]{2,1,0:T(8,128)(2,1)S(1)} %get-tuple-element.166), channel_id=1, source_target_pairs={{0,16},{1,17},{2,18},{3,19},{4,20},{5,21},{6,22},{7,23},{8,24},{9,... | collective-permute-start | bytes 909320 | tf_op jit(solution)/shard_map/ppermute | solution.py:63
  36.1 10.2 %collective-permute-start.11 = (bf16[2,592,128]{2,1,0:T(8,128)(2,1)S(1)}, bf16[2,592,128]{2,1,0:T(8,128)(2,1)S(1)}, u32[]{:S(2)}, u32[]{:S(2)}) collective-permute-start(bf16[2,592,128]{2,1,0:T(8,128)(2,1)S(1)} %get-tuple-element.167), channel_id=1, source_target_pairs={{0,32},{1,33},{2,34},{3,35},{4,36},{5,37},{6,38},{7,39},{8,40},{9,... | collective-permute-start | bytes 909320 | tf_op jit(solution)/shard_map/ppermute | solution.py:63
  37.1 13.4 %collective-permute-start.12 = (bf16[2,592,128]{2,1,0:T(8,128)(2,1)S(1)}, bf16[2,592,128]{2,1,0:T(8,128)(2,1)S(1)}, u32[]{:S(2)}, u32[]{:S(2)}) collective-permute-start(bf16[2,592,128]{2,1,0:T(8,128)(2,1)S(1)} %get-tuple-element.168), channel_id=1, source_target_pairs={{0,112},{1,113},{2,114},{3,115},{4,116},{5,117},{6,118},{7,119},{8... | collective-permute-start | bytes 909320 | tf_op jit(solution)/shard_map/ppermute | solution.py:63
  39.2 17.7 %collective-permute-start.7 = (bf16[2,864,128]{2,1,0:T(8,128)(2,1)S(1)}, bf16[2,864,128]{2,1,0:T(8,128)(2,1)S(1)}, u32[]{:S(2)}, u32[]{:S(2)}) collective-permute-start(bf16[2,864,128]{2,1,0:T(8,128)(2,1)S(1)} %get-tuple-element.163), channel_id=1, source_target_pairs={{0,16},{1,17},{2,18},{3,19},{4,20},{5,21},{6,22},{7,23},{8,24},{9,... | collective-permute-start | bytes 1327112 | tf_op jit(solution)/shard_map/ppermute | solution.py:63
  50.5 16.2 %collective-permute-start.13 = (bf16[4,592,128]{2,1,0:T(8,128)(2,1)S(1)}, bf16[4,592,128]{2,1,0:T(8,128)(2,1)S(1)}, u32[]{:S(2)}, u32[]{:S(2)}) collective-permute-start(bf16[4,592,128]{2,1,0:T(8,128)(2,1)S(1)} %y_regroup.8), channel_id=1, source_target_pairs={{0,96},{1,97},{2,98},{3,99},{4,100},{5,101},{6,102},{7,103},{8,104... | collective-permute-start | bytes 1818632 | tf_op jit(solution)/shard_map/ppermute | solution.py:63
  54.8 24.9 %collective-permute-start.19 = (bf16[2,880,128]{2,1,0:T(8,128)(2,1)S(1)}, bf16[2,880,128]{2,1,0:T(8,128)(2,1)S(1)}, u32[]{:S(2)}, u32[]{:S(2)}) collective-permute-start(bf16[2,880,128]{2,1,0:T(8,128)(2,1)S(1)} %get-tuple-element.192), channel_id=1, source_target_pairs={{0,16},{1,17},{2,18},{3,19},{4,20},{5,21},{6,22},{7,23},{8,24},{9,... | collective-permute-start | bytes 1351688 | tf_op jit(solution)/shard_map/ppermute | solution.py:63
  54.8 26.8 %collective-permute-start.20 = (bf16[2,880,128]{2,1,0:T(8,128)(2,1)S(1)}, bf16[2,880,128]{2,1,0:T(8,128)(2,1)S(1)}, u32[]{:S(2)}, u32[]{:S(2)}) collective-permute-start(bf16[2,880,128]{2,1,0:T(8,128)(2,1)S(1)} %get-tuple-element.193), channel_id=1, source_target_pairs={{0,32},{1,33},{2,34},{3,35},{4,36},{5,37},{6,38},{7,39},{8,40},{9,... | collective-permute-start | bytes 1351688 | tf_op jit(solution)/shard_map/ppermute | solution.py:63
  55.0 22.6 %collective-permute-start.8 = (bf16[2,864,128]{2,1,0:T(8,128)(2,1)S(1)}, bf16[2,864,128]{2,1,0:T(8,128)(2,1)S(1)}, u32[]{:S(2)}, u32[]{:S(2)}) collective-permute-start(bf16[2,864,128]{2,1,0:T(8,128)(2,1)S(1)} %get-tuple-element.164), channel_id=1, source_target_pairs={{0,32},{1,33},{2,34},{3,35},{4,36},{5,37},{6,38},{7,39},{8,40},{9,... | collective-permute-start | bytes 1327112 | tf_op jit(solution)/shard_map/ppermute | solution.py:63
  56.9 20.7 %collective-permute-start.9 = (bf16[2,864,128]{2,1,0:T(8,128)(2,1)S(1)}, bf16[2,864,128]{2,1,0:T(8,128)(2,1)S(1)}, u32[]{:S(2)}, u32[]{:S(2)}) collective-permute-start(bf16[2,864,128]{2,1,0:T(8,128)(2,1)S(1)} %get-tuple-element.165), channel_id=1, source_target_pairs={{0,112},{1,113},{2,114},{3,115},{4,116},{5,117},{6,118},{7,119},{8... | collective-permute-start | bytes 1327112 | tf_op jit(solution)/shard_map/ppermute | solution.py:63
  66.7 15.0 %collective-permute-start.21 = (bf16[2,880,128]{2,1,0:T(8,128)(2,1)S(1)}, bf16[2,880,128]{2,1,0:T(8,128)(2,1)S(1)}, u32[]{:S(2)}, u32[]{:S(2)}) collective-permute-start(bf16[2,880,128]{2,1,0:T(8,128)(2,1)S(1)} %get-tuple-element.194), channel_id=1, source_target_pairs={{0,112},{1,113},{2,114},{3,115},{4,116},{5,117},{6,118},{7,119},{8... | collective-permute-start | bytes 1351688 | tf_op jit(solution)/shard_map/ppermute | solution.py:63
  77.7 24.1 %collective-permute-start.15 = (bf16[4,864,128]{2,1,0:T(8,128)(2,1)S(1)}, bf16[4,864,128]{2,1,0:T(8,128)(2,1)S(1)}, u32[]{:S(2)}, u32[]{:S(2)}) collective-permute-start(bf16[4,864,128]{2,1,0:T(8,128)(2,1)S(1)} %y_regroup.9), channel_id=1, source_target_pairs={{0,96},{1,97},{2,98},{3,99},{4,100},{5,101},{6,102},{7,103},{8,104... | collective-permute-start | bytes 2654216 | tf_op jit(solution)/shard_map/ppermute | solution.py:63
  78.2 9.4 %collective-permute-start.16 = (bf16[4,528,128]{2,1,0:T(8,128)(2,1)S(1)}, bf16[4,528,128]{2,1,0:T(8,128)(2,1)S(1)}, u32[]{:S(2)}, u32[]{:S(2)}) collective-permute-start(bf16[4,528,128]{2,1,0:T(8,128)(2,1)S(1)} %get-tuple-element.189), channel_id=1, source_target_pairs={{0,1},{1,0},{2,3},{3,2},{4,5},{5,4},{6,7},{7,6},{8,9},{9,8},{10,11... | collective-permute-start | bytes 1622024 | tf_op jit(solution)/shard_map/ppermute | solution.py:63
  79.7 15.2 %collective-permute-start.17 = (bf16[4,528,128]{2,1,0:T(8,128)(2,1)S(1)}, bf16[4,528,128]{2,1,0:T(8,128)(2,1)S(1)}, u32[]{:S(2)}, u32[]{:S(2)}) collective-permute-start(bf16[4,528,128]{2,1,0:T(8,128)(2,1)S(1)} %get-tuple-element.190), channel_id=1, source_target_pairs={{0,4},{1,5},{2,6},{3,7},{4,0},{5,1},{6,2},{7,3},{8,12},{9,13},{10,... | collective-permute-start | bytes 1622024 | tf_op jit(solution)/shard_map/ppermute | solution.py:63
  81.6 13.2 %collective-permute-start.18 = (bf16[4,528,128]{2,1,0:T(8,128)(2,1)S(1)}, bf16[4,528,128]{2,1,0:T(8,128)(2,1)S(1)}, u32[]{:S(2)}, u32[]{:S(2)}) collective-permute-start(bf16[4,528,128]{2,1,0:T(8,128)(2,1)S(1)} %get-tuple-element.191), channel_id=1, source_target_pairs={{0,5},{1,4},{2,7},{3,6},{4,1},{5,0},{6,3},{7,2},{8,13},{9,12},{10,... | collective-permute-start | bytes 1622024 | tf_op jit(solution)/shard_map/ppermute | solution.py:63
  81.8 21.2 %collective-permute-start.28 = (bf16[4,880,128]{2,1,0:T(8,128)(2,1)S(1)}, bf16[4,880,128]{2,1,0:T(8,128)(2,1)S(1)}, u32[]{:S(2)}, u32[]{:S(2)}) collective-permute-start(bf16[4,880,128]{2,1,0:T(8,128)(2,1)S(1)} %y_regroup.10), channel_id=1, source_target_pairs={{0,96},{1,97},{2,98},{3,99},{4,100},{5,101},{6,102},{7,103},{8,104... | collective-permute-start | bytes 2703368 | tf_op jit(solution)/shard_map/ppermute | solution.py:63
  95.0 16.8 %collective-permute-start.26 = (bf16[4,528,128]{2,1,0:T(8,128)(2,1)S(1)}, bf16[4,528,128]{2,1,0:T(8,128)(2,1)S(1)}, u32[]{:S(2)}, u32[]{:S(2)}) collective-permute-start(bf16[4,528,128]{2,1,0:T(8,128)(2,1)S(1)} %get-tuple-element.213), channel_id=1, source_target_pairs={{0,12},{1,13},{2,14},{3,15},{4,8},{5,9},{6,10},{7,11},{8,4},{9,5},... | collective-permute-start | bytes 1622024 | tf_op jit(solution)/shard_map/ppermute | solution.py:63
  99.1 13.6 %collective-permute-start.27 = (bf16[4,528,128]{2,1,0:T(8,128)(2,1)S(1)}, bf16[4,528,128]{2,1,0:T(8,128)(2,1)S(1)}, u32[]{:S(2)}, u32[]{:S(2)}) collective-permute-start(bf16[4,528,128]{2,1,0:T(8,128)(2,1)S(1)} %get-tuple-element.214), channel_id=1, source_target_pairs={{0,15},{1,14},{2,13},{3,12},{4,11},{5,10},{6,9},{7,8},{8,7},{9,6},... | collective-permute-start | bytes 1622024 | tf_op jit(solution)/shard_map/ppermute | solution.py:63
  100.7 21.0 %collective-permute-start.25 = (bf16[4,528,128]{2,1,0:T(8,128)(2,1)S(1)}, bf16[4,528,128]{2,1,0:T(8,128)(2,1)S(1)}, u32[]{:S(2)}, u32[]{:S(2)}) collective-permute-start(bf16[4,528,128]{2,1,0:T(8,128)(2,1)S(1)} %get-tuple-element.203), channel_id=1, source_target_pairs={{0,3},{1,2},{2,1},{3,0},{4,7},{5,6},{6,5},{7,4},{8,11},{9,10},{10,... | collective-permute-start | bytes 1622024 | tf_op jit(solution)/shard_map/ppermute | solution.py:63
  103.0 19.8 %collective-permute-start.22 = (bf16[2,880,128]{2,1,0:T(8,128)(2,1)S(1)}, bf16[2,880,128]{2,1,0:T(8,128)(2,1)S(1)}, u32[]{:S(2)}, u32[]{:S(2)}) collective-permute-start(bf16[2,880,128]{2,1,0:T(8,128)(2,1)S(1)} %get-tuple-element.210), channel_id=1, source_target_pairs={{0,16},{1,17},{2,18},{3,19},{4,20},{5,21},{6,22},{7,23},{8,24},{9,... | collective-permute-start | bytes 1351688 | tf_op jit(solution)/shard_map/ppermute | solution.py:63
  103.9 33.5 %collective-permute-start.30 = (bf16[4,784,128]{2,1,0:T(8,128)(2,1)S(1)}, bf16[4,784,128]{2,1,0:T(8,128)(2,1)S(1)}, u32[]{:S(2)}, u32[]{:S(2)}) collective-permute-start(bf16[4,784,128]{2,1,0:T(8,128)(2,1)S(1)} %get-tuple-element.233), channel_id=1, source_target_pairs={{0,1},{1,0},{2,3},{3,2},{4,5},{5,4},{6,7},{7,6},{8,9},{9,8},{10,11... | collective-permute-start | bytes 2408456 | tf_op jit(solution)/shard_map/ppermute | solution.py:63
  111.8 25.6 %collective-permute-start.31 = (bf16[4,784,128]{2,1,0:T(8,128)(2,1)S(1)}, bf16[4,784,128]{2,1,0:T(8,128)(2,1)S(1)}, u32[]{:S(2)}, u32[]{:S(2)}) collective-permute-start(bf16[4,784,128]{2,1,0:T(8,128)(2,1)S(1)} %get-tuple-element.234), channel_id=1, source_target_pairs={{0,4},{1,5},{2,6},{3,7},{4,0},{5,1},{6,2},{7,3},{8,12},{9,13},{10,... | collective-permute-start | bytes 2408456 | tf_op jit(solution)/shard_map/ppermute | solution.py:63
  112.7 24.7 %collective-permute-start.32 = (bf16[4,784,128]{2,1,0:T(8,128)(2,1)S(1)}, bf16[4,784,128]{2,1,0:T(8,128)(2,1)S(1)}, u32[]{:S(2)}, u32[]{:S(2)}) collective-permute-start(bf16[4,784,128]{2,1,0:T(8,128)(2,1)S(1)} %get-tuple-element.235), channel_id=1, source_target_pairs={{0,5},{1,4},{2,7},{3,6},{4,1},{5,0},{6,3},{7,2},{8,13},{9,12},{10,... | collective-permute-start | bytes 2408456 | tf_op jit(solution)/shard_map/ppermute | solution.py:63
  121.7 12.7 %collective-permute-start.23 = (bf16[2,880,128]{2,1,0:T(8,128)(2,1)S(1)}, bf16[2,880,128]{2,1,0:T(8,128)(2,1)S(1)}, u32[]{:S(2)}, u32[]{:S(2)}) collective-permute-start(bf16[2,880,128]{2,1,0:T(8,128)(2,1)S(1)} %get-tuple-element.211), channel_id=1, source_target_pairs={{0,32},{1,33},{2,34},{3,35},{4,36},{5,37},{6,38},{7,39},{8,40},{9,... | collective-permute-start | bytes 1351688 | tf_op jit(solution)/shard_map/ppermute | solution.py:63
  122.8 12.1 %collective-permute-start.24 = (bf16[2,880,128]{2,1,0:T(8,128)(2,1)S(1)}, bf16[2,880,128]{2,1,0:T(8,128)(2,1)S(1)}, u32[]{:S(2)}, u32[]{:S(2)}) collective-permute-start(bf16[2,880,128]{2,1,0:T(8,128)(2,1)S(1)} %get-tuple-element.212), channel_id=1, source_target_pairs={{0,112},{1,113},{2,114},{3,115},{4,116},{5,117},{6,118},{7,119},{8... | collective-permute-start | bytes 1351688 | tf_op jit(solution)/shard_map/ppermute | solution.py:63
  135.0 14.5 %collective-permute-start.29 = (bf16[4,880,128]{2,1,0:T(8,128)(2,1)S(1)}, bf16[4,880,128]{2,1,0:T(8,128)(2,1)S(1)}, u32[]{:S(2)}, u32[]{:S(2)}) collective-permute-start(bf16[4,880,128]{2,1,0:T(8,128)(2,1)S(1)} %y_regroup.11), channel_id=1, source_target_pairs={{0,96},{1,97},{2,98},{3,99},{4,100},{5,101},{6,102},{7,103},{8,104... | collective-permute-start | bytes 2703368 | tf_op jit(solution)/shard_map/ppermute | solution.py:63
  137.5 26.7 %collective-permute-start.37 = (bf16[4,784,128]{2,1,0:T(8,128)(2,1)S(1)}, bf16[4,784,128]{2,1,0:T(8,128)(2,1)S(1)}, u32[]{:S(2)}, u32[]{:S(2)}) collective-permute-start(bf16[4,784,128]{2,1,0:T(8,128)(2,1)S(1)} %get-tuple-element.250), channel_id=1, source_target_pairs={{0,12},{1,13},{2,14},{3,15},{4,8},{5,9},{6,10},{7,11},{8,4},{9,5},... | collective-permute-start | bytes 2408456 | tf_op jit(solution)/shard_map/ppermute | solution.py:63
  140.8 23.9 %collective-permute-start.38 = (bf16[4,784,128]{2,1,0:T(8,128)(2,1)S(1)}, bf16[4,784,128]{2,1,0:T(8,128)(2,1)S(1)}, u32[]{:S(2)}, u32[]{:S(2)}) collective-permute-start(bf16[4,784,128]{2,1,0:T(8,128)(2,1)S(1)} %get-tuple-element.251), channel_id=1, source_target_pairs={{0,15},{1,14},{2,13},{3,12},{4,11},{5,10},{6,9},{7,8},{8,7},{9,6},... | collective-permute-start | bytes 2408456 | tf_op jit(solution)/shard_map/ppermute | solution.py:63
  142.4 31.2 %collective-permute-start.36 = (bf16[4,784,128]{2,1,0:T(8,128)(2,1)S(1)}, bf16[4,784,128]{2,1,0:T(8,128)(2,1)S(1)}, u32[]{:S(2)}, u32[]{:S(2)}) collective-permute-start(bf16[4,784,128]{2,1,0:T(8,128)(2,1)S(1)} %get-tuple-element.240), channel_id=1, source_target_pairs={{0,3},{1,2},{2,1},{3,0},{4,7},{5,6},{6,5},{7,4},{8,11},{9,10},{10,... | collective-permute-start | bytes 2408456 | tf_op jit(solution)/shard_map/ppermute | solution.py:63
  150.4 26.0 %collective-permute-start.33 = (bf16[4,784,128]{2,1,0:T(8,128)(2,1)S(1)}, bf16[4,784,128]{2,1,0:T(8,128)(2,1)S(1)}, u32[]{:S(2)}, u32[]{:S(2)}) collective-permute-start(bf16[4,784,128]{2,1,0:T(8,128)(2,1)S(1)} %get-tuple-element.247), channel_id=1, source_target_pairs={{0,1},{1,0},{2,3},{3,2},{4,5},{5,4},{6,7},{7,6},{8,9},{9,8},{10,11... | collective-permute-start | bytes 2408456 | tf_op jit(solution)/shard_map/ppermute | solution.py:63
  151.6 24.8 %collective-permute-start.34 = (bf16[4,784,128]{2,1,0:T(8,128)(2,1)S(1)}, bf16[4,784,128]{2,1,0:T(8,128)(2,1)S(1)}, u32[]{:S(2)}, u32[]{:S(2)}) collective-permute-start(bf16[4,784,128]{2,1,0:T(8,128)(2,1)S(1)} %get-tuple-element.248), channel_id=1, source_target_pairs={{0,4},{1,5},{2,6},{3,7},{4,0},{5,1},{6,2},{7,3},{8,12},{9,13},{10,... | collective-permute-start | bytes 2408456 | tf_op jit(solution)/shard_map/ppermute | solution.py:63
  164.2 13.1 %collective-permute-start.35 = (bf16[4,784,128]{2,1,0:T(8,128)(2,1)S(1)}, bf16[4,784,128]{2,1,0:T(8,128)(2,1)S(1)}, u32[]{:S(2)}, u32[]{:S(2)}) collective-permute-start(bf16[4,784,128]{2,1,0:T(8,128)(2,1)S(1)} %get-tuple-element.249), channel_id=1, source_target_pairs={{0,5},{1,4},{2,7},{3,6},{4,1},{5,0},{6,3},{7,2},{8,13},{9,12},{10,... | collective-permute-start | bytes 2408456 | tf_op jit(solution)/shard_map/ppermute | solution.py:63
  177.5 22.5 %collective-permute-start.40 = (bf16[4,784,128]{2,1,0:T(8,128)(2,1)S(1)}, bf16[4,784,128]{2,1,0:T(8,128)(2,1)S(1)}, u32[]{:S(2)}, u32[]{:S(2)}) collective-permute-start(bf16[4,784,128]{2,1,0:T(8,128)(2,1)S(1)} %get-tuple-element.266), channel_id=1, source_target_pairs={{0,12},{1,13},{2,14},{3,15},{4,8},{5,9},{6,10},{7,11},{8,4},{9,5},... | collective-permute-start | bytes 2408456 | tf_op jit(solution)/shard_map/ppermute | solution.py:63
  181.2 18.8 %collective-permute-start.41 = (bf16[4,784,128]{2,1,0:T(8,128)(2,1)S(1)}, bf16[4,784,128]{2,1,0:T(8,128)(2,1)S(1)}, u32[]{:S(2)}, u32[]{:S(2)}) collective-permute-start(bf16[4,784,128]{2,1,0:T(8,128)(2,1)S(1)} %get-tuple-element.267), channel_id=1, source_target_pairs={{0,15},{1,14},{2,13},{3,12},{4,11},{5,10},{6,9},{7,8},{8,7},{9,6},... | collective-permute-start | bytes 2408456 | tf_op jit(solution)/shard_map/ppermute | solution.py:63
  183.3 19.4 %collective-permute-start.39 = (bf16[4,784,128]{2,1,0:T(8,128)(2,1)S(1)}, bf16[4,784,128]{2,1,0:T(8,128)(2,1)S(1)}, u32[]{:S(2)}, u32[]{:S(2)}) collective-permute-start(bf16[4,784,128]{2,1,0:T(8,128)(2,1)S(1)} %get-tuple-element.265), channel_id=1, source_target_pairs={{0,3},{1,2},{2,1},{3,0},{4,7},{5,6},{6,5},{7,4},{8,11},{9,10},{10,... | collective-permute-start | bytes 2408456 | tf_op jit(solution)/shard_map/ppermute | solution.py:63

commit v10 on v9

--- a/solution.py
+++ b/solution.py
@@ -16,16 +16,16 @@
     ("y_regroup", 0),
     ("y_regroup", 1),
     ("cross", 0),
-    ("start", 2),
     ("y_regroup", 0),
     ("cross", 1),
     ("spread", 0),
-    ("y_regroup", 2),
+    ("start", 2),
     ("y_regroup", 1),
     ("regroup", 0),
-    ("cross", 2),
     ("spread", 1),
+    ("y_regroup", 2),
     ("pack", 0),
+    ("cross", 2, 1),
     ("y_regroup", 2),
     ("regroup", 1),
     ("spread", 2),
@@ -124,23 +124,24 @@
     return (1 - 2 * (both & 1)).astype(jnp.float32)
 
 
-def local_turn_kernel(rows_a, weight_ref, *refs):
+def local_turn_kernel(rows_a, chunks, weight_ref, *refs):
     out_refs, turned = refs[:-1], refs[-1]
     group = lax.axis_index("fsdp")
     swap = group & 1 != 0
     flips = [sign_of(group, a >> 1) * (1.0 / HAD) for a in range(rows_a)]
-    columns = jnp.concatenate([weight_ref[a * HAD : (a + 1) * HAD, :].T for a in range(rows_a)], axis=0)
+    width = turned.shape[0] // rows_a
+    columns = jnp.concatenate([weight_ref[a * HAD : (a + 1) * HAD, :width].T for a in range(rows_a)], axis=0)
     both = [lax.broadcasted_iota(jnp.int32, (HAD, HAD), dim) for dim in range(2)]
     both = both[0] & both[1]
     for shift in (4, 2, 1):
         both = both ^ (both >> shift)
     signs = (1 - 2 * (both & 1)).astype(jnp.float32).astype(jnp.bfloat16)
     turned[...] = jnp.dot(columns, signs, preferred_element_type=jnp.float32)
-    for index, (first, chans) in enumerate(CHUNKS):
+    for index, (first, chans) in enumerate(chunks):
         for low in range(0, chans, 16):
             outs = []
             for a in range(rows_a):
-                start = a * HEAD_DIM + first + low
+                start = a * width + first + low
                 outs.append(turned[start : start + 16, :] * flips[a])
             outs = butterfly(outs)
             for e in range(2):
@@ -295,18 +296,23 @@
             name=name,
         )(*arrays)
 
-    widths = [2 * chans for _, chans in CHUNKS for _ in range(4)]
-    turned = pl.pallas_call(
-        functools.partial(local_turn_kernel, rows_a),
-        grid=(heads,),
-        in_specs=[pl.BlockSpec((rows_local, HEAD_DIM), lambda h: (0, h))],
-        out_specs=[pl.BlockSpec((2, width, HAD), lambda h: (0, h, 0)) for width in widths],
-        out_shape=[jax.ShapeDtypeStruct((2, heads * width, HAD), jnp.bfloat16) for width in widths],
-        scratch_shapes=[pltpu.VMEM((rows_local, HAD), jnp.float32)],
-        compiler_params=params,
-        name="local_turn",
-    )(qkv_weight)
-
+    def local_turn(weight, chunks):
+        widths = [2 * chans for _, chans in chunks for _ in range(4)]
+        last = sum(chunks[-1])
+        return pl.pallas_call(
+            functools.partial(local_turn_kernel, rows_a, chunks),
+            grid=(heads,),
+            in_specs=[pl.BlockSpec((rows_local, HEAD_DIM), lambda h: (0, h))],
+            out_specs=[pl.BlockSpec((2, width, HAD), lambda h: (0, h, 0)) for width in widths],
+            out_shape=[jax.ShapeDtypeStruct((2, heads * width, HAD), jnp.bfloat16) for width in widths],
+            scratch_shapes=[pltpu.VMEM((rows_a * last, HAD), jnp.float32)],
+            compiler_params=params,
+            name="local_turn",
+        )(weight)
+
+    turned = list(local_turn(qkv_weight, CHUNKS[:1]))
+    qkv_weight, turned = lax.optimization_barrier((qkv_weight, turned))
+    turned += list(local_turn(qkv_weight, CHUNKS[1:]))
     state = [turned[4 * index : 4 * index + 4] for index in range(len(CHUNKS))]
     token = None
     past = []
@@ -316,11 +322,14 @@
             return list(arrays)
         return list(lax.optimization_barrier((list(arrays), token))[0])
 
-    for stage, index in ORDER:
+    for stage, index, *others in ORDER:
         first, chans = chunk = CHUNKS[index]
         arrays = tie(state[index])
+        for other in others:
+            arrays, state[other][3] = lax.optimization_barrier((arrays, state[other][3]))
         if stage == "start":
             state[index] = y_first(arrays)
+            token = turned[4] if index == 0 else token
         elif stage == "y_regroup":
             (token,) = call(y_regroup_kernel, stage, [(4,) + arrays[0].shape[1:2]], *arrays)
             state[index] = arrays + [y_second(token)]

time: 208 us -> 213 us (1.024)
  starting transfers between devices: 55.6 us -> 72.9 us
  waiting for transfers between devices: 127 us -> 112 us
  Pallas kernels: 20.5 us -> 24.1 us
    ppermute x42, starting transfers between devices: 55.6 us -> 72.9 us  [hop(): return lax.ppermute(array, BOTH, pairs)]
    ppermute x42, waiting for transfers between devices: 127 us -> 112 us  [hop(): return lax.ppermute(array, BOTH, pairs)]
    pallas_call x1 -> x2, Pallas kernels: 5.61 us -> 9.28 us  [local_turn(): pl.pallas_call(functools.partial(local_turn_kernel, rows_a, chunks), grid...]
  transfers between devices with their start and end apart: 42 -> 42, of which waited for: 22 -> 18; matrix products, arithmetic and copies ran while one was open for 0% -> 0% of each run, Pallas kernels for 6% -> 8%
where the time goes in v10:
time: 213 us
  waiting for transfers between devices  112 us (53%)
  starting transfers between devices  72.9 us (34%)
  Pallas kernels  24.1 us (11%)
  local copies, waits for them, and re-layouts  2.34 us (1%)
    ppermute x42, waiting for transfers between devices, hop(): return lax.ppermute(array, BOTH, pairs)  112 us
    ppermute x42, starting transfers between devices, hop(): return lax.ppermute(array, BOTH, pairs)  72.9 us
    pallas_call x2, Pallas kernels, local_turn(): pl.pallas_call(functools.partial(local_turn_kernel, rows_a, chunks), grid...  9.28 us
    pallas_call x3, Pallas kernels, per_device(): pl.pallas_call(functools.partial(pack_kernel, owners, heads, chunk, bool(...  8.53 us
    pallas_call x15, Pallas kernels, call(): pl.pallas_call(kernel, in_specs=[smem_spec] * table + [vmem_spec] * (len(...  6.34 us
  transfers between devices with their start and end apart: 42, of which 18 were waited for; matrix products, arithmetic and copies ran while one was open for 0% of the time, Pallas kernels for 8%

profile of v10, /device:TPU:0, one launch (start us, length us, event | category | flops | bytes accessed | tf_op | source)
XLA Modules:
  0.0 212.7 jit_solution(16403187211488285260)
XLA Ops:
  0.6 2.3 %copy-done = bf16[2048,1152]{1,0:T(8,128)(2,1)S(1)} copy-done((bf16[2048,1152]{1,0:T(8,128)(2,1)S(1)}, bf16[2048,1152]{1,0:T(8,128)(2,1)}, u32[]{:S(2)}) %copy-start) | copy-done | bytes 4718616
  3.0 4.1 %local_turn.2 = (bf16[2,576,128]{2,1,0:T(8,128)(2,1)S(1)}, bf16[2,576,128]{2,1,0:T(8,128)(2,1)S(1)}, bf16[2,576,128]{2,1,0:T(8,128)(2,1)S(1)}, bf16[2,576,128]{2,1,0:T(8,128)(2,1)S(1)}) custom-call(bf16[2048,1152]{1,0:T(8,128)(2,1)S(1)} %copy-done), custom_call_target="tpu_custom_call" | custom-call | tf_op jit(solution)/shard_map/local_turn/pallas_call | solution.py:302
  7.2 1.7 collective-permute-start.1
  8.9 1.5 collective-permute-start.2
  10.4 5.2 %local_turn.3 = (bf16[2,864,128]{2,1,0:T(8,128)(2,1)S(1)}, bf16[2,864,128]{2,1,0:T(8,128)(2,1)S(1)}, bf16[2,864,128]{2,1,0:T(8,128)(2,1)S(1)}, bf16[2,864,128]{2...) custom-call(bf16[2048,1152]{1,0:T(8,128)(2,1)S(1)} %copy-done), custom_call_target="tpu_custom_call" | custom-call | tf_op jit(solution)/shard_map/local_turn/pallas_call | solution.py:302
  15.6 0.2 collective-permute-start.4
  15.8 0.6 collective-permute-start.5
  16.3 2.4 %collective-permute-start.6 = (bf16[2,864,128]{2,1,0:T(8,128)(2,1)S(1)}, bf16[2,864,128]{2,1,0:T(8,128)(2,1)S(1)}, u32[]{:S(2)}, u32[]{:S(2)}) collective-permute-start(bf16[2,864,128]{2,1,0:T(8,128)(2,1)S(1)} %get-tuple-element.183), channel_id=1, source_target_pairs={{0,112},{1,113},{2,114},{3,115},{4,116},{5,117},{6,118},{7,119},{8... | collective-permute-start | bytes 1327112 | tf_op jit(solution)/shard_map/ppermute | solution.py:63
  18.8 3.0 %collective-permute-start.3 = (bf16[4,576,128]{2,1,0:T(8,128)(2,1)S(1)}, bf16[4,576,128]{2,1,0:T(8,128)(2,1)S(1)}, u32[]{:S(2)}, u32[]{:S(2)}) collective-permute-start(bf16[4,576,128]{2,1,0:T(8,128)(2,1)S(1)} %y_regroup.6), channel_id=1, source_target_pairs={{0,96},{1,97},{2,98},{3,99},{4,100},{5,101},{6,102},{7,103},{8,104... | collective-permute-start | bytes 1769480 | tf_op jit(solution)/shard_map/ppermute | solution.py:63
  21.8 7.0 %collective-permute-done.5.refs_2_ = bf16[2,864,128]{2,1,0:T(8,128)(2,1)S(1)} collective-permute-done((bf16[2,864,128]{2,1,0:T(8,128)(2,1)S(1)}, bf16[2,864,128]{2,1,0:T(8,128)(2,1)S(1)}, u32[]{:S(2)}, u32[]{:S(2)}) %collective-permute-start.5) | collective-permute-done | bytes 442400 | tf_op jit(solution)/shard_map/ppermute | solution.py:63
  28.9 2.9 %collective-permute-start.11 = (bf16[4,864,128]{2,1,0:T(8,128)(2,1)S(1)}, bf16[4,864,128]{2,1,0:T(8,128)(2,1)S(1)}, u32[]{:S(2)}, u32[]{:S(2)}) collective-permute-start(bf16[4,864,128]{2,1,0:T(8,128)(2,1)S(1)} %y_regroup.7), channel_id=1, source_target_pairs={{0,96},{1,97},{2,98},{3,99},{4,100},{5,101},{6,102},{7,103},{8,104... | collective-permute-start | bytes 2654216 | tf_op jit(solution)/shard_map/ppermute | solution.py:63
  31.8 4.0 %collective-permute-done.3.refs_4_ = bf16[4,576,128]{2,1,0:T(8,128)(2,1)S(1)} collective-permute-done((bf16[4,576,128]{2,1,0:T(8,128)(2,1)S(1)}, bf16[4,576,128]{2,1,0:T(8,128)(2,1)S(1)}, u32[]{:S(2)}, u32[]{:S(2)}) %collective-permute-start.3) | collective-permute-done | bytes 589856 | tf_op jit(solution)/shard_map/ppermute | solution.py:63
  35.8 0.8 cross.3
  36.7 3.0 %collective-permute-start.9 = (bf16[2,592,128]{2,1,0:T(8,128)(2,1)S(1)}, bf16[2,592,128]{2,1,0:T(8,128)(2,1)S(1)}, u32[]{:S(2)}, u32[]{:S(2)}) collective-permute-start(bf16[2,592,128]{2,1,0:T(8,128)(2,1)S(1)} %get-tuple-element.196), channel_id=1, source_target_pairs={{0,112},{1,113},{2,114},{3,115},{4,116},{5,117},{6,118},{7,119},{8... | collective-permute-start | bytes 909320 | tf_op jit(solution)/shard_map/ppermute | solution.py:63
  39.7 7.1 %collective-permute-done.8.refs_2_ = bf16[2,592,128]{2,1,0:T(8,128)(2,1)S(1)} collective-permute-done((bf16[2,592,128]{2,1,0:T(8,128)(2,1)S(1)}, bf16[2,592,128]{2,1,0:T(8,128)(2,1)S(1)}, u32[]{:S(2)}, u32[]{:S(2)}) %collective-permute-start.8) | collective-permute-done | bytes 303136 | tf_op jit(solution)/shard_map/ppermute | solution.py:63
  46.8 4.2 %collective-permute-done.9.refs_3_ = bf16[2,592,128]{2,1,0:T(8,128)(2,1)S(1)} collective-permute-done((bf16[2,592,128]{2,1,0:T(8,128)(2,1)S(1)}, bf16[2,592,128]{2,1,0:T(8,128)(2,1)S(1)}, u32[]{:S(2)}, u32[]{:S(2)}) %collective-permute-start.9) | collective-permute-done | bytes 303136 | tf_op jit(solution)/shard_map/ppermute | solution.py:63
  51.1 2.5 %collective-permute-start.10 = (bf16[4,592,128]{2,1,0:T(8,128)(2,1)S(1)}, bf16[4,592,128]{2,1,0:T(8,128)(2,1)S(1)}, u32[]{:S(2)}, u32[]{:S(2)}) collective-permute-start(bf16[4,592,128]{2,1,0:T(8,128)(2,1)S(1)} %y_regroup.8), channel_id=1, source_target_pairs={{0,96},{1,97},{2,98},{3,99},{4,100},{5,101},{6,102},{7,103},{8,104... | collective-permute-start | bytes 1818632 | tf_op jit(solution)/shard_map/ppermute | solution.py:63
  53.7 1.1 cross.4
  54.9 3.0 %collective-permute-start.17 = (bf16[2,880,128]{2,1,0:T(8,128)(2,1)S(1)}, bf16[2,880,128]{2,1,0:T(8,128)(2,1)S(1)}, u32[]{:S(2)}, u32[]{:S(2)}) collective-permute-start(bf16[2,880,128]{2,1,0:T(8,128)(2,1)S(1)} %get-tuple-element.219), channel_id=1, source_target_pairs={{0,112},{1,113},{2,114},{3,115},{4,116},{5,117},{6,118},{7,119},{8... | collective-permute-start | bytes 1351688 | tf_op jit(solution)/shard_map/ppermute | solution.py:63
  57.9 8.2 %collective-permute-done.10.refs_4_ = bf16[4,592,128]{2,1,0:T(8,128)(2,1)S(1)} collective-permute-done((bf16[4,592,128]{2,1,0:T(8,128)(2,1)S(1)}, bf16[4,592,128]{2,1,0:T(8,128)(2,1)S(1)}, u32[]{:S(2)}, u32[]{:S(2)}) %collective-permute-start.10) | collective-permute-done | bytes 606240 | tf_op jit(solution)/shard_map/ppermute | solution.py:63
  66.1 0.8 spread.3
  66.9 1.6 collective-permute-start.19
  68.5 1.9 collective-permute-start.20
  70.4 0.5 collective-permute-done.17.refs_3_
  71.0 3.3 %collective-permute-start.18 = (bf16[4,880,128]{2,1,0:T(8,128)(2,1)S(1)}, bf16[4,880,128]{2,1,0:T(8,128)(2,1)S(1)}, u32[]{:S(2)}, u32[]{:S(2)}) collective-permute-start(bf16[4,880,128]{2,1,0:T(8,128)(2,1)S(1)} %y_regroup.9), channel_id=1, source_target_pairs={{0,96},{1,97},{2,98},{3,99},{4,100},{5,101},{6,102},{7,103},{8,104... | collective-permute-start | bytes 2703368 | tf_op jit(solution)/shard_map/ppermute | solution.py:63
  74.2 2.1 collective-permute-start.21
  76.4 1.8 collective-permute-start.12
  78.2 1.7 collective-permute-start.13
  79.8 7.1 %collective-permute-start.14 = (bf16[2,864,128]{2,1,0:T(8,128)(2,1)S(1)}, bf16[2,864,128]{2,1,0:T(8,128)(2,1)S(1)}, u32[]{:S(2)}, u32[]{:S(2)}) collective-permute-start(bf16[2,864,128]{2,1,0:T(8,128)(2,1)S(1)} %get-tuple-element.216), channel_id=1, source_target_pairs={{0,112},{1,113},{2,114},{3,115},{4,116},{5,117},{6,118},{7,119},{8... | collective-permute-start | bytes 1327112 | tf_op jit(solution)/shard_map/ppermute | solution.py:63
  87.1 2.1 collective-permute-done.18.refs_4_
  89.2 0.9 spread.4
  90.0 1.2 collective-permute-done.13.refs_2_
  91.3 3.2 %collective-permute-done.14.refs_3_ = bf16[2,864,128]{2,1,0:T(8,128)(2,1)S(1)} collective-permute-done((bf16[2,864,128]{2,1,0:T(8,128)(2,1)S(1)}, bf16[2,864,128]{2,1,0:T(8,128)(2,1)S(1)}, u32[]{:S(2)}, u32[]{:S(2)}) %collective-permute-start.14) | collective-permute-done | bytes 442400 | tf_op jit(solution)/shard_map/ppermute | solution.py:63
  94.5 2.8 %collective-permute-start.22 = (bf16[4,864,128]{2,1,0:T(8,128)(2,1)S(1)}, bf16[4,864,128]{2,1,0:T(8,128)(2,1)S(1)}, u32[]{:S(2)}, u32[]{:S(2)}) collective-permute-start(bf16[4,864,128]{2,1,0:T(8,128)(2,1)S(1)} %y_regroup.10), channel_id=1, source_target_pairs={{0,96},{1,97},{2,98},{3,99},{4,100},{5,101},{6,102},{7,103},{8,104... | collective-permute-start | bytes 2654216 | tf_op jit(solution)/shard_map/ppermute | solution.py:63
  97.3 2.0 collective-permute-start.26
  99.3 2.5 %collective-permute-start.24 = (bf16[4,528,128]{2,1,0:T(8,128)(2,1)S(1)}, bf16[4,528,128]{2,1,0:T(8,128)(2,1)S(1)}, u32[]{:S(2)}, u32[]{:S(2)}) collective-permute-start(bf16[4,528,128]{2,1,0:T(8,128)(2,1)S(1)} %get-tuple-element.242), channel_id=1, source_target_pairs={{0,12},{1,13},{2,14},{3,15},{4,8},{5,9},{6,10},{7,11},{8,4},{9,5},... | collective-permute-start | bytes 1622024 | tf_op jit(solution)/shard_map/ppermute | solution.py:63
  101.8 2.2 %collective-permute-start.25 = (bf16[4,528,128]{2,1,0:T(8,128)(2,1)S(1)}, bf16[4,528,128]{2,1,0:T(8,128)(2,1)S(1)}, u32[]{:S(2)}, u32[]{:S(2)}) collective-permute-start(bf16[4,528,128]{2,1,0:T(8,128)(2,1)S(1)} %get-tuple-element.243), channel_id=1, source_target_pairs={{0,15},{1,14},{2,13},{3,12},{4,11},{5,10},{6,9},{7,8},{8,7},{9,6},... | collective-permute-start | bytes 1622024 | tf_op jit(solution)/shard_map/ppermute | solution.py:63
  104.0 1.1 collective-permute-start.23
  105.2 17.1 %collective-permute-done.24.refs_5_ = bf16[4,528,128]{2,1,0:T(8,128)(2,1)S(1)} collective-permute-done((bf16[4,528,128]{2,1,0:T(8,128)(2,1)S(1)}, bf16[4,528,128]{2,1,0:T(8,128)(2,1)S(1)}, u32[]{:S(2)}, u32[]{:S(2)}) %collective-permute-start.24) | collective-permute-done | bytes 540704 | tf_op jit(solution)/shard_map/ppermute | solution.py:63
  122.3 0.2 collective-permute-start.31
  122.5 2.4 %pack.3 = (f32[16,128]{1,0:T(8,128)S(1)}, bf16[1,16,128,2048]{3,2,1,0:T(8,128)(2,1)}) custom-call(s32[144]{0:T(256)S(1)} %copy-done.1, bf16[4,528,128]{2,1,0:T(8,128)(2,1)S(1)} %get-tuple-element.244.refs_0_, bf16[4,528,128]{2,1,0:T(8,128)(2,1)S(1)} %collective-permute-done.19.refs_1_, bf16[4,528,128]{2,1,0:T(8,128)(2,1)S(1)} %collective-permute-done.20.refs_2_, ...), custom_call_target="tpu_custom_call" | custom-call | tf_op jit(solution)/shard_map/pack/pallas_call | solution.py:352
  124.9 1.1 cross.5
  126.1 1.5 collective-permute-start.27
  127.5 1.8 collective-permute-start.28
  129.4 0.8 collective-permute-start.29
  130.2 9.9 %collective-permute-done.28.refs_2_ = bf16[2,880,128]{2,1,0:T(8,128)(2,1)S(1)} collective-permute-done((bf16[2,880,128]{2,1,0:T(8,128)(2,1)S(1)}, bf16[2,880,128]{2,1,0:T(8,128)(2,1)S(1)}, u32[]{:S(2)}, u32[]{:S(2)}) %collective-permute-start.28) | collective-permute-done | bytes 450592 | tf_op jit(solution)/shard_map/ppermute | solution.py:63
  140.1 0.7 collective-permute-done.29.refs_3_
  140.8 2.8 %collective-permute-start.30 = (bf16[4,880,128]{2,1,0:T(8,128)(2,1)S(1)}, bf16[4,880,128]{2,1,0:T(8,128)(2,1)S(1)}, u32[]{:S(2)}, u32[]{:S(2)}) collective-permute-start(bf16[4,880,128]{2,1,0:T(8,128)(2,1)S(1)} %y_regroup.11), channel_id=1, source_target_pairs={{0,96},{1,97},{2,98},{3,99},{4,100},{5,101},{6,102},{7,103},{8,104... | collective-permute-start | bytes 2703368 | tf_op jit(solution)/shard_map/ppermute | solution.py:63
  143.8 1.1 collective-permute-start.37
  144.9 3.6 %collective-permute-start.38 = (bf16[4,784,128]{2,1,0:T(8,128)(2,1)S(1)}, bf16[4,784,128]{2,1,0:T(8,128)(2,1)S(1)}, u32[]{:S(2)}, u32[]{:S(2)}) collective-permute-start(bf16[4,784,128]{2,1,0:T(8,128)(2,1)S(1)} %get-tuple-element.289), channel_id=1, source_target_pairs={{0,15},{1,14},{2,13},{3,12},{4,11},{5,10},{6,9},{7,8},{8,7},{9,6},... | collective-permute-start | bytes 2408456 | tf_op jit(solution)/shard_map/ppermute | solution.py:63
  148.4 1.4 collective-permute-start.36
  149.8 5.5 %collective-permute-done.30.refs_4_ = bf16[4,880,128]{2,1,0:T(8,128)(2,1)S(1)} collective-permute-done((bf16[4,880,128]{2,1,0:T(8,128)(2,1)S(1)}, bf16[4,880,128]{2,1,0:T(8,128)(2,1)S(1)}, u32[]{:S(2)}, u32[]{:S(2)}) %collective-permute-start.30) | collective-permute-done | bytes 901152 | tf_op jit(solution)/shard_map/ppermute | solution.py:63
  155.3 0.9 spread.5
  156.2 0.5 collective-permute-start.33
  156.7 2.0 collective-permute-start.34
  158.7 12.5 %collective-permute-done.37.refs_5_ = bf16[4,784,128]{2,1,0:T(8,128)(2,1)S(1)} collective-permute-done((bf16[4,784,128]{2,1,0:T(8,128)(2,1)S(1)}, bf16[4,784,128]{2,1,0:T(8,128)(2,1)S(1)}, u32[]{:S(2)}, u32[]{:S(2)}) %collective-permute-start.37) | collective-permute-done | bytes 802848 | tf_op jit(solution)/shard_map/ppermute | solution.py:63
  171.2 7.7 %collective-permute-done.36.refs_4_ = bf16[4,784,128]{2,1,0:T(8,128)(2,1)S(1)} collective-permute-done((bf16[4,784,128]{2,1,0:T(8,128)(2,1)S(1)}, bf16[4,784,128]{2,1,0:T(8,128)(2,1)S(1)}, u32[]{:S(2)}, u32[]{:S(2)}) %collective-permute-start.36) | collective-permute-done | bytes 802848 | tf_op jit(solution)/shard_map/ppermute | solution.py:63
  178.9 2.8 %pack.4 = (f32[16,128]{1,0:T(8,128)S(1)}, bf16[1,16,128,2048]{3,2,1,0:T(8,128)(2,1)}) custom-call(s32[144]{0:T(256)S(1)} %copy-done.1, bf16[4,784,128]{2,1,0:T(8,128)(2,1)S(1)} %get-tuple-element.290.refs_0_, bf16[4,784,128]{2,1,0:T(8,128)(2,1)S(1)} %collective-permute-done.31.refs_1_, ...), custom_call_target="tpu_custom_call", output_to_operand_aliasing={{1}: (9, {})} | custom-call | tf_op jit(solution)/shard_map/pack/pallas_call | solution.py:352
  181.7 2.5 %collective-permute-done.35.refs_3_ = bf16[4,784,128]{2,1,0:T(8,128)(2,1)S(1)} collective-permute-done((bf16[4,784,128]{2,1,0:T(8,128)(2,1)S(1)}, bf16[4,784,128]{2,1,0:T(8,128)(2,1)S(1)}, u32[]{:S(2)}, u32[]{:S(2)}) %collective-permute-start.35) | collective-permute-done | bytes 802848 | tf_op jit(solution)/shard_map/ppermute | solution.py:63
  184.5 4.0 %collective-permute-start.41 = (bf16[4,784,128]{2,1,0:T(8,128)(2,1)S(1)}, bf16[4,784,128]{2,1,0:T(8,128)(2,1)S(1)}, u32[]{:S(2)}, u32[]{:S(2)}) collective-permute-start(bf16[4,784,128]{2,1,0:T(8,128)(2,1)S(1)} %get-tuple-element.305), channel_id=1, source_target_pairs={{0,15},{1,14},{2,13},{3,12},{4,11},{5,10},{6,9},{7,8},{8,7},{9,6},... | collective-permute-start | bytes 2408456 | tf_op jit(solution)/shard_map/ppermute | solution.py:63
  188.5 1.9 collective-permute-start.39
  190.4 16.1 %collective-permute-done.40.refs_5_ = bf16[4,784,128]{2,1,0:T(8,128)(2,1)S(1)} collective-permute-done((bf16[4,784,128]{2,1,0:T(8,128)(2,1)S(1)}, bf16[4,784,128]{2,1,0:T(8,128)(2,1)S(1)}, u32[]{:S(2)}, u32[]{:S(2)}) %collective-permute-start.40) | collective-permute-done | bytes 802848 | tf_op jit(solution)/shard_map/ppermute | solution.py:63
  206.5 2.7 %collective-permute-done.39.refs_4_ = bf16[4,784,128]{2,1,0:T(8,128)(2,1)S(1)} collective-permute-done((bf16[4,784,128]{2,1,0:T(8,128)(2,1)S(1)}, bf16[4,784,128]{2,1,0:T(8,128)(2,1)S(1)}, u32[]{:S(2)}, u32[]{:S(2)}) %collective-permute-start.39) | collective-permute-done | bytes 802848 | tf_op jit(solution)/shard_map/ppermute | solution.py:63
  209.2 3.4 %pack.5 = (f32[16,128]{1,0:T(8,128)}, bf16[1,16,128,2048]{3,2,1,0:T(8,128)(2,1)}) custom-call(s32[144]{0:T(256)S(1)} %copy-done.1, bf16[4,784,128]{2,1,0:T(8,128)(2,1)S(1)} %get-tuple-element.306.refs_0_, bf16[4,784,128]{2,1,0:T(8,128)(2,1)S(1)} %collective-permute-done.33.refs_1_, ...), custom_call_target="tpu_custom_call", output_to_operand_aliasing={{1}: (9, {})} | custom-call | tf_op jit(solution)/shard_map/pack/pallas_call | solution.py:352
  (44 shorter events, 1.2 us)
Async XLA Ops:
  0.6 2.3 %copy-start = (bf16[2048,1152]{1,0:T(8,128)(2,1)S(1)}, bf16[2048,1152]{1,0:T(8,128)(2,1)}, u32[]{:S(2)}) copy-start(bf16[2048,1152]{1,0:T(8,128)(2,1)} %weight_ref.2) | copy-start | bytes 14155780
  7.1 59.0 %copy-start.1 = (s32[144]{0:T(256)S(1)}, s32[144]{0:T(256)}, u32[]{:S(2)}) copy-start(s32[144]{0:T(256)} %placement_ref.11) | copy-start | bytes 1732
  7.1 9.2 %collective-permute-start = (bf16[2,576,128]{2,1,0:T(8,128)(2,1)S(1)}, bf16[2,576,128]{2,1,0:T(8,128)(2,1)S(1)}, u32[]{:S(2)}, u32[]{:S(2)}) collective-permute-start(bf16[2,576,128]{2,1,0:T(8,128)(2,1)S(1)} %get-tuple-element.169), channel_id=1, source_target_pairs={{0,16},{1,17},{2,18},{3,19},{4,20},{5,21},{6,22},{7,23},{8,24},{9,... | collective-permute-start | bytes 884744 | tf_op jit(solution)/shard_map/ppermute | solution.py:63
  7.2 11.6 %collective-permute-start.1 = (bf16[2,576,128]{2,1,0:T(8,128)(2,1)S(1)}, bf16[2,576,128]{2,1,0:T(8,128)(2,1)S(1)}, u32[]{:S(2)}, u32[]{:S(2)}) collective-permute-start(bf16[2,576,128]{2,1,0:T(8,128)(2,1)S(1)} %get-tuple-element.170), channel_id=1, source_target_pairs={{0,32},{1,33},{2,34},{3,35},{4,36},{5,37},{6,38},{7,39},{8,40},{9,... | collective-permute-start | bytes 884744 | tf_op jit(solution)/shard_map/ppermute | solution.py:63
  8.9 9.8 %collective-permute-start.2 = (bf16[2,576,128]{2,1,0:T(8,128)(2,1)S(1)}, bf16[2,576,128]{2,1,0:T(8,128)(2,1)S(1)}, u32[]{:S(2)}, u32[]{:S(2)}) collective-permute-start(bf16[2,576,128]{2,1,0:T(8,128)(2,1)S(1)} %get-tuple-element.171), channel_id=1, source_target_pairs={{0,112},{1,113},{2,114},{3,115},{4,116},{5,117},{6,118},{7,119},{8... | collective-permute-start | bytes 884744 | tf_op jit(solution)/shard_map/ppermute | solution.py:63
  15.6 6.2 %collective-permute-start.4 = (bf16[2,864,128]{2,1,0:T(8,128)(2,1)S(1)}, bf16[2,864,128]{2,1,0:T(8,128)(2,1)S(1)}, u32[]{:S(2)}, u32[]{:S(2)}) collective-permute-start(bf16[2,864,128]{2,1,0:T(8,128)(2,1)S(1)} %get-tuple-element.181), channel_id=1, source_target_pairs={{0,16},{1,17},{2,18},{3,19},{4,20},{5,21},{6,22},{7,23},{8,24},{9,... | collective-permute-start | bytes 1327112 | tf_op jit(solution)/shard_map/ppermute | solution.py:63
  15.8 13.0 %collective-permute-start.5 = (bf16[2,864,128]{2,1,0:T(8,128)(2,1)S(1)}, bf16[2,864,128]{2,1,0:T(8,128)(2,1)S(1)}, u32[]{:S(2)}, u32[]{:S(2)}) collective-permute-start(bf16[2,864,128]{2,1,0:T(8,128)(2,1)S(1)} %get-tuple-element.182), channel_id=1, source_target_pairs={{0,32},{1,33},{2,34},{3,35},{4,36},{5,37},{6,38},{7,39},{8,40},{9,... | collective-permute-start | bytes 1327112 | tf_op jit(solution)/shard_map/ppermute | solution.py:63
  16.3 12.5 %collective-permute-start.6 = (bf16[2,864,128]{2,1,0:T(8,128)(2,1)S(1)}, bf16[2,864,128]{2,1,0:T(8,128)(2,1)S(1)}, u32[]{:S(2)}, u32[]{:S(2)}) collective-permute-start(bf16[2,864,128]{2,1,0:T(8,128)(2,1)S(1)} %get-tuple-element.183), channel_id=1, source_target_pairs={{0,112},{1,113},{2,114},{3,115},{4,116},{5,117},{6,118},{7,119},{8... | collective-permute-start | bytes 1327112 | tf_op jit(solution)/shard_map/ppermute | solution.py:63
  18.8 17.0 %collective-permute-start.3 = (bf16[4,576,128]{2,1,0:T(8,128)(2,1)S(1)}, bf16[4,576,128]{2,1,0:T(8,128)(2,1)S(1)}, u32[]{:S(2)}, u32[]{:S(2)}) collective-permute-start(bf16[4,576,128]{2,1,0:T(8,128)(2,1)S(1)} %y_regroup.6), channel_id=1, source_target_pairs={{0,96},{1,97},{2,98},{3,99},{4,100},{5,101},{6,102},{7,103},{8,104... | collective-permute-start | bytes 1769480 | tf_op jit(solution)/shard_map/ppermute | solution.py:63
  28.9 24.8 %collective-permute-start.11 = (bf16[4,864,128]{2,1,0:T(8,128)(2,1)S(1)}, bf16[4,864,128]{2,1,0:T(8,128)(2,1)S(1)}, u32[]{:S(2)}, u32[]{:S(2)}) collective-permute-start(bf16[4,864,128]{2,1,0:T(8,128)(2,1)S(1)} %y_regroup.7), channel_id=1, source_target_pairs={{0,96},{1,97},{2,98},{3,99},{4,100},{5,101},{6,102},{7,103},{8,104... | collective-permute-start | bytes 2654216 | tf_op jit(solution)/shard_map/ppermute | solution.py:63
  36.6 3.1 %collective-permute-start.7 = (bf16[2,592,128]{2,1,0:T(8,128)(2,1)S(1)}, bf16[2,592,128]{2,1,0:T(8,128)(2,1)S(1)}, u32[]{:S(2)}, u32[]{:S(2)}) collective-permute-start(bf16[2,592,128]{2,1,0:T(8,128)(2,1)S(1)} %get-tuple-element.194), channel_id=1, source_target_pairs={{0,16},{1,17},{2,18},{3,19},{4,20},{5,21},{6,22},{7,23},{8,24},{9,... | collective-permute-start | bytes 909320 | tf_op jit(solution)/shard_map/ppermute | solution.py:63
  36.6 10.2 %collective-permute-start.8 = (bf16[2,592,128]{2,1,0:T(8,128)(2,1)S(1)}, bf16[2,592,128]{2,1,0:T(8,128)(2,1)S(1)}, u32[]{:S(2)}, u32[]{:S(2)}) collective-permute-start(bf16[2,592,128]{2,1,0:T(8,128)(2,1)S(1)} %get-tuple-element.195), channel_id=1, source_target_pairs={{0,32},{1,33},{2,34},{3,35},{4,36},{5,37},{6,38},{7,39},{8,40},{9,... | collective-permute-start | bytes 909320 | tf_op jit(solution)/shard_map/ppermute | solution.py:63
  36.7 14.4 %collective-permute-start.9 = (bf16[2,592,128]{2,1,0:T(8,128)(2,1)S(1)}, bf16[2,592,128]{2,1,0:T(8,128)(2,1)S(1)}, u32[]{:S(2)}, u32[]{:S(2)}) collective-permute-start(bf16[2,592,128]{2,1,0:T(8,128)(2,1)S(1)} %get-tuple-element.196), channel_id=1, source_target_pairs={{0,112},{1,113},{2,114},{3,115},{4,116},{5,117},{6,118},{7,119},{8... | collective-permute-start | bytes 909320 | tf_op jit(solution)/shard_map/ppermute | solution.py:63
  51.1 14.9 %collective-permute-start.10 = (bf16[4,592,128]{2,1,0:T(8,128)(2,1)S(1)}, bf16[4,592,128]{2,1,0:T(8,128)(2,1)S(1)}, u32[]{:S(2)}, u32[]{:S(2)}) collective-permute-start(bf16[4,592,128]{2,1,0:T(8,128)(2,1)S(1)} %y_regroup.8), channel_id=1, source_target_pairs={{0,96},{1,97},{2,98},{3,99},{4,100},{5,101},{6,102},{7,103},{8,104... | collective-permute-start | bytes 1818632 | tf_op jit(solution)/shard_map/ppermute | solution.py:63
  54.8 15.6 %collective-permute-start.15 = (bf16[2,880,128]{2,1,0:T(8,128)(2,1)S(1)}, bf16[2,880,128]{2,1,0:T(8,128)(2,1)S(1)}, u32[]{:S(2)}, u32[]{:S(2)}) collective-permute-start(bf16[2,880,128]{2,1,0:T(8,128)(2,1)S(1)} %get-tuple-element.217), channel_id=1, source_target_pairs={{0,16},{1,17},{2,18},{3,19},{4,20},{5,21},{6,22},{7,23},{8,24},{9,... | collective-permute-start | bytes 1351688 | tf_op jit(solution)/shard_map/ppermute | solution.py:63
  54.8 15.6 %collective-permute-start.16 = (bf16[2,880,128]{2,1,0:T(8,128)(2,1)S(1)}, bf16[2,880,128]{2,1,0:T(8,128)(2,1)S(1)}, u32[]{:S(2)}, u32[]{:S(2)}) collective-permute-start(bf16[2,880,128]{2,1,0:T(8,128)(2,1)S(1)} %get-tuple-element.218), channel_id=1, source_target_pairs={{0,32},{1,33},{2,34},{3,35},{4,36},{5,37},{6,38},{7,39},{8,40},{9,... | collective-permute-start | bytes 1351688 | tf_op jit(solution)/shard_map/ppermute | solution.py:63
  54.9 16.0 %collective-permute-start.17 = (bf16[2,880,128]{2,1,0:T(8,128)(2,1)S(1)}, bf16[2,880,128]{2,1,0:T(8,128)(2,1)S(1)}, u32[]{:S(2)}, u32[]{:S(2)}) collective-permute-start(bf16[2,880,128]{2,1,0:T(8,128)(2,1)S(1)} %get-tuple-element.219), channel_id=1, source_target_pairs={{0,112},{1,113},{2,114},{3,115},{4,116},{5,117},{6,118},{7,119},{8... | collective-permute-start | bytes 1351688 | tf_op jit(solution)/shard_map/ppermute | solution.py:63
  66.9 11.3 %collective-permute-start.19 = (bf16[4,528,128]{2,1,0:T(8,128)(2,1)S(1)}, bf16[4,528,128]{2,1,0:T(8,128)(2,1)S(1)}, u32[]{:S(2)}, u32[]{:S(2)}) collective-permute-start(bf16[4,528,128]{2,1,0:T(8,128)(2,1)S(1)} %get-tuple-element.224), channel_id=1, source_target_pairs={{0,1},{1,0},{2,3},{3,2},{4,5},{5,4},{6,7},{7,6},{8,9},{9,8},{10,11... | collective-permute-start | bytes 1622024 | tf_op jit(solution)/shard_map/ppermute | solution.py:63
  68.5 11.3 %collective-permute-start.20 = (bf16[4,528,128]{2,1,0:T(8,128)(2,1)S(1)}, bf16[4,528,128]{2,1,0:T(8,128)(2,1)S(1)}, u32[]{:S(2)}, u32[]{:S(2)}) collective-permute-start(bf16[4,528,128]{2,1,0:T(8,128)(2,1)S(1)} %get-tuple-element.225), channel_id=1, source_target_pairs={{0,4},{1,5},{2,6},{3,7},{4,0},{5,1},{6,2},{7,3},{8,12},{9,13},{10,... | collective-permute-start | bytes 1622024 | tf_op jit(solution)/shard_map/ppermute | solution.py:63
  71.0 18.2 %collective-permute-start.18 = (bf16[4,880,128]{2,1,0:T(8,128)(2,1)S(1)}, bf16[4,880,128]{2,1,0:T(8,128)(2,1)S(1)}, u32[]{:S(2)}, u32[]{:S(2)}) collective-permute-start(bf16[4,880,128]{2,1,0:T(8,128)(2,1)S(1)} %y_regroup.9), channel_id=1, source_target_pairs={{0,96},{1,97},{2,98},{3,99},{4,100},{5,101},{6,102},{7,103},{8,104... | collective-permute-start | bytes 2703368 | tf_op jit(solution)/shard_map/ppermute | solution.py:63
  74.2 12.7 %collective-permute-start.21 = (bf16[4,528,128]{2,1,0:T(8,128)(2,1)S(1)}, bf16[4,528,128]{2,1,0:T(8,128)(2,1)S(1)}, u32[]{:S(2)}, u32[]{:S(2)}) collective-permute-start(bf16[4,528,128]{2,1,0:T(8,128)(2,1)S(1)} %get-tuple-element.226), channel_id=1, source_target_pairs={{0,5},{1,4},{2,7},{3,6},{4,1},{5,0},{6,3},{7,2},{8,13},{9,12},{10,... | collective-permute-start | bytes 1622024 | tf_op jit(solution)/shard_map/ppermute | solution.py:63
  76.4 13.7 %collective-permute-start.12 = (bf16[2,864,128]{2,1,0:T(8,128)(2,1)S(1)}, bf16[2,864,128]{2,1,0:T(8,128)(2,1)S(1)}, u32[]{:S(2)}, u32[]{:S(2)}) collective-permute-start(bf16[2,864,128]{2,1,0:T(8,128)(2,1)S(1)} %get-tuple-element.214), channel_id=1, source_target_pairs={{0,16},{1,17},{2,18},{3,19},{4,20},{5,21},{6,22},{7,23},{8,24},{9,... | collective-permute-start | bytes 1327112 | tf_op jit(solution)/shard_map/ppermute | solution.py:63
  78.2 13.1 %collective-permute-start.13 = (bf16[2,864,128]{2,1,0:T(8,128)(2,1)S(1)}, bf16[2,864,128]{2,1,0:T(8,128)(2,1)S(1)}, u32[]{:S(2)}, u32[]{:S(2)}) collective-permute-start(bf16[2,864,128]{2,1,0:T(8,128)(2,1)S(1)} %get-tuple-element.215), channel_id=1, source_target_pairs={{0,32},{1,33},{2,34},{3,35},{4,36},{5,37},{6,38},{7,39},{8,40},{9,... | collective-permute-start | bytes 1327112 | tf_op jit(solution)/shard_map/ppermute | solution.py:63
  79.8 14.6 %collective-permute-start.14 = (bf16[2,864,128]{2,1,0:T(8,128)(2,1)S(1)}, bf16[2,864,128]{2,1,0:T(8,128)(2,1)S(1)}, u32[]{:S(2)}, u32[]{:S(2)}) collective-permute-start(bf16[2,864,128]{2,1,0:T(8,128)(2,1)S(1)} %get-tuple-element.216), channel_id=1, source_target_pairs={{0,112},{1,113},{2,114},{3,115},{4,116},{5,117},{6,118},{7,119},{8... | collective-permute-start | bytes 1327112 | tf_op jit(solution)/shard_map/ppermute | solution.py:63
  94.5 30.4 %collective-permute-start.22 = (bf16[4,864,128]{2,1,0:T(8,128)(2,1)S(1)}, bf16[4,864,128]{2,1,0:T(8,128)(2,1)S(1)}, u32[]{:S(2)}, u32[]{:S(2)}) collective-permute-start(bf16[4,864,128]{2,1,0:T(8,128)(2,1)S(1)} %y_regroup.10), channel_id=1, source_target_pairs={{0,96},{1,97},{2,98},{3,99},{4,100},{5,101},{6,102},{7,103},{8,104... | collective-permute-start | bytes 2654216 | tf_op jit(solution)/shard_map/ppermute | solution.py:63
  97.3 27.6 %collective-permute-start.26 = (bf16[4,784,128]{2,1,0:T(8,128)(2,1)S(1)}, bf16[4,784,128]{2,1,0:T(8,128)(2,1)S(1)}, u32[]{:S(2)}, u32[]{:S(2)}) collective-permute-start(bf16[4,784,128]{2,1,0:T(8,128)(2,1)S(1)} %get-tuple-element.257), channel_id=1, source_target_pairs={{0,5},{1,4},{2,7},{3,6},{4,1},{5,0},{6,3},{7,2},{8,13},{9,12},{10,... | collective-permute-start | bytes 2408456 | tf_op jit(solution)/shard_map/ppermute | solution.py:63
  99.3 23.0 %collective-permute-start.24 = (bf16[4,528,128]{2,1,0:T(8,128)(2,1)S(1)}, bf16[4,528,128]{2,1,0:T(8,128)(2,1)S(1)}, u32[]{:S(2)}, u32[]{:S(2)}) collective-permute-start(bf16[4,528,128]{2,1,0:T(8,128)(2,1)S(1)} %get-tuple-element.242), channel_id=1, source_target_pairs={{0,12},{1,13},{2,14},{3,15},{4,8},{5,9},{6,10},{7,11},{8,4},{9,5},... | collective-permute-start | bytes 1622024 | tf_op jit(solution)/shard_map/ppermute | solution.py:63
  101.8 20.7 %collective-permute-start.25 = (bf16[4,528,128]{2,1,0:T(8,128)(2,1)S(1)}, bf16[4,528,128]{2,1,0:T(8,128)(2,1)S(1)}, u32[]{:S(2)}, u32[]{:S(2)}) collective-permute-start(bf16[4,528,128]{2,1,0:T(8,128)(2,1)S(1)} %get-tuple-element.243), channel_id=1, source_target_pairs={{0,15},{1,14},{2,13},{3,12},{4,11},{5,10},{6,9},{7,8},{8,7},{9,6},... | collective-permute-start | bytes 1622024 | tf_op jit(solution)/shard_map/ppermute | solution.py:63
  104.0 18.5 %collective-permute-start.23 = (bf16[4,528,128]{2,1,0:T(8,128)(2,1)S(1)}, bf16[4,528,128]{2,1,0:T(8,128)(2,1)S(1)}, u32[]{:S(2)}, u32[]{:S(2)}) collective-permute-start(bf16[4,528,128]{2,1,0:T(8,128)(2,1)S(1)} %get-tuple-element.231), channel_id=1, source_target_pairs={{0,3},{1,2},{2,1},{3,0},{4,7},{5,6},{6,5},{7,4},{8,11},{9,10},{10,... | collective-permute-start | bytes 1622024 | tf_op jit(solution)/shard_map/ppermute | solution.py:63
  122.3 21.4 %collective-permute-start.31 = (bf16[4,784,128]{2,1,0:T(8,128)(2,1)S(1)}, bf16[4,784,128]{2,1,0:T(8,128)(2,1)S(1)}, u32[]{:S(2)}, u32[]{:S(2)}) collective-permute-start(bf16[4,784,128]{2,1,0:T(8,128)(2,1)S(1)} %get-tuple-element.271), channel_id=1, source_target_pairs={{0,1},{1,0},{2,3},{3,2},{4,5},{5,4},{6,7},{7,6},{8,9},{9,8},{10,11... | collective-permute-start | bytes 2408456 | tf_op jit(solution)/shard_map/ppermute | solution.py:63
  122.5 21.1 %collective-permute-start.32 = (bf16[4,784,128]{2,1,0:T(8,128)(2,1)S(1)}, bf16[4,784,128]{2,1,0:T(8,128)(2,1)S(1)}, u32[]{:S(2)}, u32[]{:S(2)}) collective-permute-start(bf16[4,784,128]{2,1,0:T(8,128)(2,1)S(1)} %get-tuple-element.272), channel_id=1, source_target_pairs={{0,4},{1,5},{2,6},{3,7},{4,0},{5,1},{6,2},{7,3},{8,12},{9,13},{10,... | collective-permute-start | bytes 2408456 | tf_op jit(solution)/shard_map/ppermute | solution.py:63
  126.1 4.1 %collective-permute-start.27 = (bf16[2,880,128]{2,1,0:T(8,128)(2,1)S(1)}, bf16[2,880,128]{2,1,0:T(8,128)(2,1)S(1)}, u32[]{:S(2)}, u32[]{:S(2)}) collective-permute-start(bf16[2,880,128]{2,1,0:T(8,128)(2,1)S(1)} %get-tuple-element.264), channel_id=1, source_target_pairs={{0,16},{1,17},{2,18},{3,19},{4,20},{5,21},{6,22},{7,23},{8,24},{9,... | collective-permute-start | bytes 1351688 | tf_op jit(solution)/shard_map/ppermute | solution.py:63
  127.5 12.5 %collective-permute-start.28 = (bf16[2,880,128]{2,1,0:T(8,128)(2,1)S(1)}, bf16[2,880,128]{2,1,0:T(8,128)(2,1)S(1)}, u32[]{:S(2)}, u32[]{:S(2)}) collective-permute-start(bf16[2,880,128]{2,1,0:T(8,128)(2,1)S(1)} %get-tuple-element.265), channel_id=1, source_target_pairs={{0,32},{1,33},{2,34},{3,35},{4,36},{5,37},{6,38},{7,39},{8,40},{9,... | collective-permute-start | bytes 1351688 | tf_op jit(solution)/shard_map/ppermute | solution.py:63
  129.4 11.4 %collective-permute-start.29 = (bf16[2,880,128]{2,1,0:T(8,128)(2,1)S(1)}, bf16[2,880,128]{2,1,0:T(8,128)(2,1)S(1)}, u32[]{:S(2)}, u32[]{:S(2)}) collective-permute-start(bf16[2,880,128]{2,1,0:T(8,128)(2,1)S(1)} %get-tuple-element.266), channel_id=1, source_target_pairs={{0,112},{1,113},{2,114},{3,115},{4,116},{5,117},{6,118},{7,119},{8... | collective-permute-start | bytes 1351688 | tf_op jit(solution)/shard_map/ppermute | solution.py:63
  140.8 14.5 %collective-permute-start.30 = (bf16[4,880,128]{2,1,0:T(8,128)(2,1)S(1)}, bf16[4,880,128]{2,1,0:T(8,128)(2,1)S(1)}, u32[]{:S(2)}, u32[]{:S(2)}) collective-permute-start(bf16[4,880,128]{2,1,0:T(8,128)(2,1)S(1)} %y_regroup.11), channel_id=1, source_target_pairs={{0,96},{1,97},{2,98},{3,99},{4,100},{5,101},{6,102},{7,103},{8,104... | collective-permute-start | bytes 2703368 | tf_op jit(solution)/shard_map/ppermute | solution.py:63
  143.8 27.4 %collective-permute-start.37 = (bf16[4,784,128]{2,1,0:T(8,128)(2,1)S(1)}, bf16[4,784,128]{2,1,0:T(8,128)(2,1)S(1)}, u32[]{:S(2)}, u32[]{:S(2)}) collective-permute-start(bf16[4,784,128]{2,1,0:T(8,128)(2,1)S(1)} %get-tuple-element.288), channel_id=1, source_target_pairs={{0,12},{1,13},{2,14},{3,15},{4,8},{5,9},{6,10},{7,11},{8,4},{9,5},... | collective-permute-start | bytes 2408456 | tf_op jit(solution)/shard_map/ppermute | solution.py:63
  144.9 26.3 %collective-permute-start.38 = (bf16[4,784,128]{2,1,0:T(8,128)(2,1)S(1)}, bf16[4,784,128]{2,1,0:T(8,128)(2,1)S(1)}, u32[]{:S(2)}, u32[]{:S(2)}) collective-permute-start(bf16[4,784,128]{2,1,0:T(8,128)(2,1)S(1)} %get-tuple-element.289), channel_id=1, source_target_pairs={{0,15},{1,14},{2,13},{3,12},{4,11},{5,10},{6,9},{7,8},{8,7},{9,6},... | collective-permute-start | bytes 2408456 | tf_op jit(solution)/shard_map/ppermute | solution.py:63
  148.4 30.5 %collective-permute-start.36 = (bf16[4,784,128]{2,1,0:T(8,128)(2,1)S(1)}, bf16[4,784,128]{2,1,0:T(8,128)(2,1)S(1)}, u32[]{:S(2)}, u32[]{:S(2)}) collective-permute-start(bf16[4,784,128]{2,1,0:T(8,128)(2,1)S(1)} %get-tuple-element.278), channel_id=1, source_target_pairs={{0,3},{1,2},{2,1},{3,0},{4,7},{5,6},{6,5},{7,4},{8,11},{9,10},{10,... | collective-permute-start | bytes 2408456 | tf_op jit(solution)/shard_map/ppermute | solution.py:63
  156.2 25.5 %collective-permute-start.33 = (bf16[4,784,128]{2,1,0:T(8,128)(2,1)S(1)}, bf16[4,784,128]{2,1,0:T(8,128)(2,1)S(1)}, u32[]{:S(2)}, u32[]{:S(2)}) collective-permute-start(bf16[4,784,128]{2,1,0:T(8,128)(2,1)S(1)} %get-tuple-element.285), channel_id=1, source_target_pairs={{0,1},{1,0},{2,3},{3,2},{4,5},{5,4},{6,7},{7,6},{8,9},{9,8},{10,11... | collective-permute-start | bytes 2408456 | tf_op jit(solution)/shard_map/ppermute | solution.py:63
  156.7 25.0 %collective-permute-start.34 = (bf16[4,784,128]{2,1,0:T(8,128)(2,1)S(1)}, bf16[4,784,128]{2,1,0:T(8,128)(2,1)S(1)}, u32[]{:S(2)}, u32[]{:S(2)}) collective-permute-start(bf16[4,784,128]{2,1,0:T(8,128)(2,1)S(1)} %get-tuple-element.286), channel_id=1, source_target_pairs={{0,4},{1,5},{2,6},{3,7},{4,0},{5,1},{6,2},{7,3},{8,12},{9,13},{10,... | collective-permute-start | bytes 2408456 | tf_op jit(solution)/shard_map/ppermute | solution.py:63
  171.2 13.1 %collective-permute-start.35 = (bf16[4,784,128]{2,1,0:T(8,128)(2,1)S(1)}, bf16[4,784,128]{2,1,0:T(8,128)(2,1)S(1)}, u32[]{:S(2)}, u32[]{:S(2)}) collective-permute-start(bf16[4,784,128]{2,1,0:T(8,128)(2,1)S(1)} %get-tuple-element.287), channel_id=1, source_target_pairs={{0,5},{1,4},{2,7},{3,6},{4,1},{5,0},{6,3},{7,2},{8,13},{9,12},{10,... | collective-permute-start | bytes 2408456 | tf_op jit(solution)/shard_map/ppermute | solution.py:63
  184.4 22.1 %collective-permute-start.40 = (bf16[4,784,128]{2,1,0:T(8,128)(2,1)S(1)}, bf16[4,784,128]{2,1,0:T(8,128)(2,1)S(1)}, u32[]{:S(2)}, u32[]{:S(2)}) collective-permute-start(bf16[4,784,128]{2,1,0:T(8,128)(2,1)S(1)} %get-tuple-element.304), channel_id=1, source_target_pairs={{0,12},{1,13},{2,14},{3,15},{4,8},{5,9},{6,10},{7,11},{8,4},{9,5},... | collective-permute-start | bytes 2408456 | tf_op jit(solution)/shard_map/ppermute | solution.py:63
  184.5 22.0 %collective-permute-start.41 = (bf16[4,784,128]{2,1,0:T(8,128)(2,1)S(1)}, bf16[4,784,128]{2,1,0:T(8,128)(2,1)S(1)}, u32[]{:S(2)}, u32[]{:S(2)}) collective-permute-start(bf16[4,784,128]{2,1,0:T(8,128)(2,1)S(1)} %get-tuple-element.305), channel_id=1, source_target_pairs={{0,15},{1,14},{2,13},{3,12},{4,11},{5,10},{6,9},{7,8},{8,7},{9,6},... | collective-permute-start | bytes 2408456 | tf_op jit(solution)/shard_map/ppermute | solution.py:63
  188.5 20.7 %collective-permute-start.39 = (bf16[4,784,128]{2,1,0:T(8,128)(2,1)S(1)}, bf16[4,784,128]{2,1,0:T(8,128)(2,1)S(1)}, u32[]{:S(2)}, u32[]{:S(2)}) collective-permute-start(bf16[4,784,128]{2,1,0:T(8,128)(2,1)S(1)} %get-tuple-element.303), channel_id=1, source_target_pairs={{0,3},{1,2},{2,1},{3,0},{4,7},{5,6},{6,5},{7,4},{8,11},{9,10},{10,... | collective-permute-start | bytes 2408456 | tf_op jit(solution)/shard_map/ppermute | solution.py:63

commit v11 on v9

--- a/solution.py
+++ b/solution.py
@@ -9,7 +9,7 @@
 
 HEAD_DIM = 128
 HAD = 128
-CHUNKS = ((0, 32), (32, 48), (80, 48))
+CHUNKS = ((0, 48), (48, 48), (96, 32))
 ORDER = (
     ("start", 0),
     ("start", 1),

time: 208 us -> 208 us (level)
  waiting for transfers between devices: 127 us -> 123 us
  starting transfers between devices: 55.6 us -> 59.4 us
    ppermute x42, starting transfers between devices: 55.6 us -> 59.4 us  [hop(): return lax.ppermute(array, BOTH, pairs)]
    ppermute x42, waiting for transfers between devices: 127 us -> 123 us  [hop(): return lax.ppermute(array, BOTH, pairs)]
  transfers between devices with their start and end apart: 42 -> 42, of which waited for: 22 -> 22; matrix products, arithmetic and copies ran while one was open for 0% -> 0% of each run, Pallas kernels for 6% -> 5%
where the time goes in v11:
time: 208 us; the launch traced here: 207 us
  waiting for transfers between devices  123 us (59%)
  starting transfers between devices  59.4 us (29%)
  Pallas kernels  20.5 us (10%)
  local copies, waits for them, and re-layouts  2.33 us (1%)
    ppermute x42, waiting for transfers between devices, hop(): return lax.ppermute(array, BOTH, pairs)  123 us
    ppermute x42, starting transfers between devices, hop(): return lax.ppermute(array, BOTH, pairs)  59.4 us
    pallas_call x3, Pallas kernels, per_device(): pl.pallas_call(functools.partial(pack_kernel, owners, heads, chunk, bool(...  8.52 us
    pallas_call x15, Pallas kernels, call(): pl.pallas_call(kernel, in_specs=[smem_spec] * table + [vmem_spec] * (len(...  6.33 us
    pallas_call x1, Pallas kernels, per_device(): pl.pallas_call(functools.partial(local_turn_kernel, rows_a), grid=(heads,...  5.61 us
  transfers between devices with their start and end apart: 42, of which 22 were waited for; matrix products, arithmetic and copies ran while one was open for 0% of the time, Pallas kernels for 5%

profile of v11, /device:TPU:0, one launch (start us, length us, event | category | flops | bytes accessed | tf_op | source)
XLA Modules:
  0.0 206.5 jit_solution(9869125591262625342)
XLA Ops:
  0.6 2.3 %copy-done = bf16[2048,1152]{1,0:T(8,128)(2,1)S(1)} copy-done((bf16[2048,1152]{1,0:T(8,128)(2,1)S(1)}, bf16[2048,1152]{1,0:T(8,128)(2,1)}, u32[]{:S(2)}) %copy-start) | copy-done | bytes 4718616
  3.0 5.6 %local_turn.1 = (bf16[2,864,128]{2,1,0:T(8,128)(2,1)S(1)}, bf16[2,864,128]{2,1,0:T(8,128)(2,1)S(1)}, bf16[2,864,128]{2,1,0:T(8,128)(2,1)S(1)}, bf16[2,864,128]{2...) custom-call(bf16[2048,1152]{1,0:T(8,128)(2,1)S(1)} %copy-done), custom_call_target="tpu_custom_call" | custom-call | tf_op jit(solution)/shard_map/local_turn/pallas_call | solution.py:299
  8.7 1.7 collective-permute-start.1
  10.4 1.5 collective-permute-start.2
  11.9 8.8 %collective-permute-done.1.refs_2_ = bf16[2,864,128]{2,1,0:T(8,128)(2,1)S(1)} collective-permute-done((bf16[2,864,128]{2,1,0:T(8,128)(2,1)S(1)}, bf16[2,864,128]{2,1,0:T(8,128)(2,1)S(1)}, u32[]{:S(2)}, u32[]{:S(2)}) %collective-permute-start.1) | collective-permute-done | bytes 442400 | tf_op jit(solution)/shard_map/ppermute | solution.py:63
  20.7 1.2 collective-permute-done.2.refs_3_
  21.9 3.1 %collective-permute-start.3 = (bf16[4,864,128]{2,1,0:T(8,128)(2,1)S(1)}, bf16[4,864,128]{2,1,0:T(8,128)(2,1)S(1)}, u32[]{:S(2)}, u32[]{:S(2)}) collective-permute-start(bf16[4,864,128]{2,1,0:T(8,128)(2,1)S(1)} %y_regroup.6), channel_id=1, source_target_pairs={{0,96},{1,97},{2,98},{3,99},{4,100},{5,101},{6,102},{7,103},{8,104... | collective-permute-start | bytes 2654216 | tf_op jit(solution)/shard_map/ppermute | solution.py:63
  25.2 2.9 %collective-permute-start.6 = (bf16[2,864,128]{2,1,0:T(8,128)(2,1)S(1)}, bf16[2,864,128]{2,1,0:T(8,128)(2,1)S(1)}, u32[]{:S(2)}, u32[]{:S(2)}) collective-permute-start(bf16[2,864,128]{2,1,0:T(8,128)(2,1)S(1)} %get-tuple-element.151), channel_id=1, source_target_pairs={{0,112},{1,113},{2,114},{3,115},{4,116},{5,117},{6,118},{7,119},{8... | collective-permute-start | bytes 1327112 | tf_op jit(solution)/shard_map/ppermute | solution.py:63
  28.1 10.0 %collective-permute-done.5.refs_2_ = bf16[2,864,128]{2,1,0:T(8,128)(2,1)S(1)} collective-permute-done((bf16[2,864,128]{2,1,0:T(8,128)(2,1)S(1)}, bf16[2,864,128]{2,1,0:T(8,128)(2,1)S(1)}, u32[]{:S(2)}, u32[]{:S(2)}) %collective-permute-start.5) | collective-permute-done | bytes 442400 | tf_op jit(solution)/shard_map/ppermute | solution.py:63
  38.2 6.8 %collective-permute-done.6.refs_3_ = bf16[2,864,128]{2,1,0:T(8,128)(2,1)S(1)} collective-permute-done((bf16[2,864,128]{2,1,0:T(8,128)(2,1)S(1)}, bf16[2,864,128]{2,1,0:T(8,128)(2,1)S(1)}, u32[]{:S(2)}, u32[]{:S(2)}) %collective-permute-start.6) | collective-permute-done | bytes 442400 | tf_op jit(solution)/shard_map/ppermute | solution.py:63
  45.0 1.1 cross.3
  46.1 0.7 collective-permute-start.10
  46.8 0.4 collective-permute-start.11
  47.2 2.3 %collective-permute-start.12 = (bf16[2,880,128]{2,1,0:T(8,128)(2,1)S(1)}, bf16[2,880,128]{2,1,0:T(8,128)(2,1)S(1)}, u32[]{:S(2)}, u32[]{:S(2)}) collective-permute-start(bf16[2,880,128]{2,1,0:T(8,128)(2,1)S(1)} %get-tuple-element.168), channel_id=1, source_target_pairs={{0,112},{1,113},{2,114},{3,115},{4,116},{5,117},{6,118},{7,119},{8... | collective-permute-start | bytes 1351688 | tf_op jit(solution)/shard_map/ppermute | solution.py:63
  49.4 2.9 %collective-permute-start.14 = (bf16[4,864,128]{2,1,0:T(8,128)(2,1)S(1)}, bf16[4,864,128]{2,1,0:T(8,128)(2,1)S(1)}, u32[]{:S(2)}, u32[]{:S(2)}) collective-permute-start(bf16[4,864,128]{2,1,0:T(8,128)(2,1)S(1)} %y_regroup.7), channel_id=1, source_target_pairs={{0,96},{1,97},{2,98},{3,99},{4,100},{5,101},{6,102},{7,103},{8,104... | collective-permute-start | bytes 2654216 | tf_op jit(solution)/shard_map/ppermute | solution.py:63
  52.3 7.7 %collective-permute-done.11.refs_2_ = bf16[2,880,128]{2,1,0:T(8,128)(2,1)S(1)} collective-permute-done((bf16[2,880,128]{2,1,0:T(8,128)(2,1)S(1)}, bf16[2,880,128]{2,1,0:T(8,128)(2,1)S(1)}, u32[]{:S(2)}, u32[]{:S(2)}) %collective-permute-start.11) | collective-permute-done | bytes 450592 | tf_op jit(solution)/shard_map/ppermute | solution.py:63
  60.1 2.9 %collective-permute-start.13 = (bf16[4,880,128]{2,1,0:T(8,128)(2,1)S(1)}, bf16[4,880,128]{2,1,0:T(8,128)(2,1)S(1)}, u32[]{:S(2)}, u32[]{:S(2)}) collective-permute-start(bf16[4,880,128]{2,1,0:T(8,128)(2,1)S(1)} %y_regroup.8), channel_id=1, source_target_pairs={{0,96},{1,97},{2,98},{3,99},{4,100},{5,101},{6,102},{7,103},{8,104... | collective-permute-start | bytes 2703368 | tf_op jit(solution)/shard_map/ppermute | solution.py:63
  62.9 9.4 %collective-permute-done.14.refs_4_ = bf16[4,864,128]{2,1,0:T(8,128)(2,1)S(1)} collective-permute-done((bf16[4,864,128]{2,1,0:T(8,128)(2,1)S(1)}, bf16[4,864,128]{2,1,0:T(8,128)(2,1)S(1)}, u32[]{:S(2)}, u32[]{:S(2)}) %collective-permute-start.14) | collective-permute-done | bytes 884768 | tf_op jit(solution)/shard_map/ppermute | solution.py:63
  72.3 1.1 cross.4
  73.5 3.6 %collective-permute-start.9 = (bf16[2,576,128]{2,1,0:T(8,128)(2,1)S(1)}, bf16[2,576,128]{2,1,0:T(8,128)(2,1)S(1)}, u32[]{:S(2)}, u32[]{:S(2)}) collective-permute-start(bf16[2,576,128]{2,1,0:T(8,128)(2,1)S(1)} %get-tuple-element.165), channel_id=1, source_target_pairs={{0,112},{1,113},{2,114},{3,115},{4,116},{5,117},{6,118},{7,119},{8... | collective-permute-start | bytes 884744 | tf_op jit(solution)/shard_map/ppermute | solution.py:63
  77.1 5.5 %collective-permute-done.13.refs_4_ = bf16[4,880,128]{2,1,0:T(8,128)(2,1)S(1)} collective-permute-done((bf16[4,880,128]{2,1,0:T(8,128)(2,1)S(1)}, bf16[4,880,128]{2,1,0:T(8,128)(2,1)S(1)}, u32[]{:S(2)}, u32[]{:S(2)}) %collective-permute-start.13) | collective-permute-done | bytes 901152 | tf_op jit(solution)/shard_map/ppermute | solution.py:63
  82.6 0.9 spread.3
  83.5 1.6 collective-permute-start.16
  85.1 1.9 collective-permute-start.17
  87.1 4.9 %collective-permute-start.21 = (bf16[2,880,128]{2,1,0:T(8,128)(2,1)S(1)}, bf16[2,880,128]{2,1,0:T(8,128)(2,1)S(1)}, u32[]{:S(2)}, u32[]{:S(2)}) collective-permute-start(bf16[2,880,128]{2,1,0:T(8,128)(2,1)S(1)} %get-tuple-element.194), channel_id=1, source_target_pairs={{0,112},{1,113},{2,114},{3,115},{4,116},{5,117},{6,118},{7,119},{8... | collective-permute-start | bytes 1351688 | tf_op jit(solution)/shard_map/ppermute | solution.py:63
  92.1 6.6 %collective-permute-done.20.refs_2_ = bf16[2,880,128]{2,1,0:T(8,128)(2,1)S(1)} collective-permute-done((bf16[2,880,128]{2,1,0:T(8,128)(2,1)S(1)}, bf16[2,880,128]{2,1,0:T(8,128)(2,1)S(1)}, u32[]{:S(2)}, u32[]{:S(2)}) %collective-permute-start.20) | collective-permute-done | bytes 450592 | tf_op jit(solution)/shard_map/ppermute | solution.py:63
  98.7 3.1 %collective-permute-done.21.refs_3_ = bf16[2,880,128]{2,1,0:T(8,128)(2,1)S(1)} collective-permute-done((bf16[2,880,128]{2,1,0:T(8,128)(2,1)S(1)}, bf16[2,880,128]{2,1,0:T(8,128)(2,1)S(1)}, u32[]{:S(2)}, u32[]{:S(2)}) %collective-permute-start.21) | collective-permute-done | bytes 450592 | tf_op jit(solution)/shard_map/ppermute | solution.py:63
  101.8 1.2 collective-permute-start.28
  103.0 2.1 %collective-permute-start.15 = (bf16[4,576,128]{2,1,0:T(8,128)(2,1)S(1)}, bf16[4,576,128]{2,1,0:T(8,128)(2,1)S(1)}, u32[]{:S(2)}, u32[]{:S(2)}) collective-permute-start(bf16[4,576,128]{2,1,0:T(8,128)(2,1)S(1)} %y_regroup.9), channel_id=1, source_target_pairs={{0,96},{1,97},{2,98},{3,99},{4,100},{5,101},{6,102},{7,103},{8,104... | collective-permute-start | bytes 1769480 | tf_op jit(solution)/shard_map/ppermute | solution.py:63
  105.2 0.7 collective-permute-done.17.refs_2_
  106.0 4.1 %collective-permute-start.26 = (bf16[4,784,128]{2,1,0:T(8,128)(2,1)S(1)}, bf16[4,784,128]{2,1,0:T(8,128)(2,1)S(1)}, u32[]{:S(2)}, u32[]{:S(2)}) collective-permute-start(bf16[4,784,128]{2,1,0:T(8,128)(2,1)S(1)} %get-tuple-element.213), channel_id=1, source_target_pairs={{0,12},{1,13},{2,14},{3,15},{4,8},{5,9},{6,10},{7,11},{8,4},{9,5},... | collective-permute-start | bytes 2408456 | tf_op jit(solution)/shard_map/ppermute | solution.py:63
  110.1 1.6 collective-permute-start.27
  111.8 1.1 collective-permute-start.25
  112.9 9.8 %collective-permute-done.15.refs_4_ = bf16[4,576,128]{2,1,0:T(8,128)(2,1)S(1)} collective-permute-done((bf16[4,576,128]{2,1,0:T(8,128)(2,1)S(1)}, bf16[4,576,128]{2,1,0:T(8,128)(2,1)S(1)}, u32[]{:S(2)}, u32[]{:S(2)}) %collective-permute-start.15) | collective-permute-done | bytes 589856 | tf_op jit(solution)/shard_map/ppermute | solution.py:63
  122.7 0.8 cross.5
  123.5 0.9 spread.4
  124.4 0.3 collective-permute-start.30
  124.7 0.4 collective-permute-done.22.refs_1_
  125.1 0.8 collective-permute-start.31
  125.9 2.9 %collective-permute-done.26.refs_5_ = bf16[4,784,128]{2,1,0:T(8,128)(2,1)S(1)} collective-permute-done((bf16[4,784,128]{2,1,0:T(8,128)(2,1)S(1)}, bf16[4,784,128]{2,1,0:T(8,128)(2,1)S(1)}, u32[]{:S(2)}, u32[]{:S(2)}) %collective-permute-start.26) | collective-permute-done | bytes 802848 | tf_op jit(solution)/shard_map/ppermute | solution.py:63
  128.9 0.3 collective-permute-start.32
  129.2 5.4 %collective-permute-done.25.refs_4_ = bf16[4,784,128]{2,1,0:T(8,128)(2,1)S(1)} collective-permute-done((bf16[4,784,128]{2,1,0:T(8,128)(2,1)S(1)}, bf16[4,784,128]{2,1,0:T(8,128)(2,1)S(1)}, u32[]{:S(2)}, u32[]{:S(2)}) %collective-permute-start.25) | collective-permute-done | bytes 802848 | tf_op jit(solution)/shard_map/ppermute | solution.py:63
  134.6 2.8 %pack.3 = (f32[16,128]{1,0:T(8,128)S(1)}, bf16[1,16,128,2048]{3,2,1,0:T(8,128)(2,1)}) custom-call(s32[144]{0:T(256)S(1)} %copy-done.1, bf16[4,784,128]{2,1,0:T(8,128)(2,1)S(1)} %get-tuple-element.221.refs_0_, bf16[4,784,128]{2,1,0:T(8,128)(2,1)S(1)} %collective-permute-done.16.refs_1_, bf16[4,784,128]{2,1,0:T(8,128)(2,1)S(1)} %collective-permute-done.17.refs_2_, ...), custom_call_target="tpu_custom_call" | custom-call | tf_op jit(solution)/shard_map/pack/pallas_call | solution.py:343
  137.4 3.4 %collective-permute-done.24.refs_3_ = bf16[2,592,128]{2,1,0:T(8,128)(2,1)S(1)} collective-permute-done((bf16[2,592,128]{2,1,0:T(8,128)(2,1)S(1)}, bf16[2,592,128]{2,1,0:T(8,128)(2,1)S(1)}, u32[]{:S(2)}, u32[]{:S(2)}) %collective-permute-start.24) | collective-permute-done | bytes 303136 | tf_op jit(solution)/shard_map/ppermute | solution.py:63
  140.8 5.0 %collective-permute-done.32.refs_3_ = bf16[4,784,128]{2,1,0:T(8,128)(2,1)S(1)} collective-permute-done((bf16[4,784,128]{2,1,0:T(8,128)(2,1)S(1)}, bf16[4,784,128]{2,1,0:T(8,128)(2,1)S(1)}, u32[]{:S(2)}, u32[]{:S(2)}) %collective-permute-start.32) | collective-permute-done | bytes 802848 | tf_op jit(solution)/shard_map/ppermute | solution.py:63
  146.0 3.3 %collective-permute-start.37 = (bf16[4,784,128]{2,1,0:T(8,128)(2,1)S(1)}, bf16[4,784,128]{2,1,0:T(8,128)(2,1)S(1)}, u32[]{:S(2)}, u32[]{:S(2)}) collective-permute-start(bf16[4,784,128]{2,1,0:T(8,128)(2,1)S(1)} %get-tuple-element.250), channel_id=1, source_target_pairs={{0,12},{1,13},{2,14},{3,15},{4,8},{5,9},{6,10},{7,11},{8,4},{9,5},... | collective-permute-start | bytes 2408456 | tf_op jit(solution)/shard_map/ppermute | solution.py:63
  149.3 2.6 %collective-permute-start.29 = (bf16[4,592,128]{2,1,0:T(8,128)(2,1)S(1)}, bf16[4,592,128]{2,1,0:T(8,128)(2,1)S(1)}, u32[]{:S(2)}, u32[]{:S(2)}) collective-permute-start(bf16[4,592,128]{2,1,0:T(8,128)(2,1)S(1)} %y_regroup.11), channel_id=1, source_target_pairs={{0,96},{1,97},{2,98},{3,99},{4,100},{5,101},{6,102},{7,103},{8,104... | collective-permute-start | bytes 1818632 | tf_op jit(solution)/shard_map/ppermute | solution.py:63
  151.9 2.0 collective-permute-start.38
  153.9 0.7 collective-permute-start.36
  154.7 5.9 %collective-permute-done.29.refs_4_ = bf16[4,592,128]{2,1,0:T(8,128)(2,1)S(1)} collective-permute-done((bf16[4,592,128]{2,1,0:T(8,128)(2,1)S(1)}, bf16[4,592,128]{2,1,0:T(8,128)(2,1)S(1)}, u32[]{:S(2)}, u32[]{:S(2)}) %collective-permute-start.29) | collective-permute-done | bytes 606240 | tf_op jit(solution)/shard_map/ppermute | solution.py:63
  160.6 0.8 spread.5
  161.4 1.1 collective-permute-start.33
  162.5 0.3 collective-permute-start.34
  162.8 8.4 %collective-permute-done.37.refs_5_ = bf16[4,784,128]{2,1,0:T(8,128)(2,1)S(1)} collective-permute-done((bf16[4,784,128]{2,1,0:T(8,128)(2,1)S(1)}, bf16[4,784,128]{2,1,0:T(8,128)(2,1)S(1)}, u32[]{:S(2)}, u32[]{:S(2)}) %collective-permute-start.37) | collective-permute-done | bytes 802848 | tf_op jit(solution)/shard_map/ppermute | solution.py:63
  171.2 1.0 collective-permute-start.35
  172.2 7.1 %collective-permute-done.36.refs_4_ = bf16[4,784,128]{2,1,0:T(8,128)(2,1)S(1)} collective-permute-done((bf16[4,784,128]{2,1,0:T(8,128)(2,1)S(1)}, bf16[4,784,128]{2,1,0:T(8,128)(2,1)S(1)}, u32[]{:S(2)}, u32[]{:S(2)}) %collective-permute-start.36) | collective-permute-done | bytes 802848 | tf_op jit(solution)/shard_map/ppermute | solution.py:63
  179.3 2.8 %pack.4 = (f32[16,128]{1,0:T(8,128)S(1)}, bf16[1,16,128,2048]{3,2,1,0:T(8,128)(2,1)}) custom-call(s32[144]{0:T(256)S(1)} %copy-done.1, bf16[4,784,128]{2,1,0:T(8,128)(2,1)S(1)} %get-tuple-element.252.refs_0_, bf16[4,784,128]{2,1,0:T(8,128)(2,1)S(1)} %collective-permute-done.30.refs_1_, ...), custom_call_target="tpu_custom_call", output_to_operand_aliasing={{1}: (9, {})} | custom-call | tf_op jit(solution)/shard_map/pack/pallas_call | solution.py:343
  182.1 2.1 collective-permute-done.35.refs_3_
  184.2 1.2 collective-permute-start.40
  185.4 3.6 %collective-permute-start.41 = (bf16[4,528,128]{2,1,0:T(8,128)(2,1)S(1)}, bf16[4,528,128]{2,1,0:T(8,128)(2,1)S(1)}, u32[]{:S(2)}, u32[]{:S(2)}) collective-permute-start(bf16[4,528,128]{2,1,0:T(8,128)(2,1)S(1)} %get-tuple-element.267), channel_id=1, source_target_pairs={{0,15},{1,14},{2,13},{3,12},{4,11},{5,10},{6,9},{7,8},{8,7},{9,6},... | collective-permute-start | bytes 1622024 | tf_op jit(solution)/shard_map/ppermute | solution.py:63
  189.0 1.2 collective-permute-start.39
  190.2 10.4 %collective-permute-done.40.refs_5_ = bf16[4,528,128]{2,1,0:T(8,128)(2,1)S(1)} collective-permute-done((bf16[4,528,128]{2,1,0:T(8,128)(2,1)S(1)}, bf16[4,528,128]{2,1,0:T(8,128)(2,1)S(1)}, u32[]{:S(2)}, u32[]{:S(2)}) %collective-permute-start.40) | collective-permute-done | bytes 540704 | tf_op jit(solution)/shard_map/ppermute | solution.py:63
  200.7 2.7 %collective-permute-done.39.refs_4_ = bf16[4,528,128]{2,1,0:T(8,128)(2,1)S(1)} collective-permute-done((bf16[4,528,128]{2,1,0:T(8,128)(2,1)S(1)}, bf16[4,528,128]{2,1,0:T(8,128)(2,1)S(1)}, u32[]{:S(2)}, u32[]{:S(2)}) %collective-permute-start.39) | collective-permute-done | bytes 540704 | tf_op jit(solution)/shard_map/ppermute | solution.py:63
  203.4 3.0 %pack.5 = (f32[16,128]{1,0:T(8,128)}, bf16[1,16,128,2048]{3,2,1,0:T(8,128)(2,1)}) custom-call(s32[144]{0:T(256)S(1)} %copy-done.1, bf16[4,528,128]{2,1,0:T(8,128)(2,1)S(1)} %get-tuple-element.268.refs_0_, bf16[4,528,128]{2,1,0:T(8,128)(2,1)S(1)} %collective-permute-done.33.refs_1_, ...), custom_call_target="tpu_custom_call", output_to_operand_aliasing={{1}: (9, {})} | custom-call | tf_op jit(solution)/shard_map/pack/pallas_call | solution.py:343
  (43 shorter events, 1.2 us)
Async XLA Ops:
  0.6 2.3 %copy-start = (bf16[2048,1152]{1,0:T(8,128)(2,1)S(1)}, bf16[2048,1152]{1,0:T(8,128)(2,1)}, u32[]{:S(2)}) copy-start(bf16[2048,1152]{1,0:T(8,128)(2,1)} %weight_ref.1) | copy-start | bytes 14155780
  3.0 79.7 %copy-start.1 = (s32[144]{0:T(256)S(1)}, s32[144]{0:T(256)}, u32[]{:S(2)}) copy-start(s32[144]{0:T(256)} %placement_ref.11) | copy-start | bytes 1732
  8.6 3.3 %collective-permute-start = (bf16[2,864,128]{2,1,0:T(8,128)(2,1)S(1)}, bf16[2,864,128]{2,1,0:T(8,128)(2,1)S(1)}, u32[]{:S(2)}, u32[]{:S(2)}) collective-permute-start(bf16[2,864,128]{2,1,0:T(8,128)(2,1)S(1)} %get-tuple-element.145), channel_id=1, source_target_pairs={{0,16},{1,17},{2,18},{3,19},{4,20},{5,21},{6,22},{7,23},{8,24},{9,... | collective-permute-start | bytes 1327112 | tf_op jit(solution)/shard_map/ppermute | solution.py:63
  8.7 12.0 %collective-permute-start.1 = (bf16[2,864,128]{2,1,0:T(8,128)(2,1)S(1)}, bf16[2,864,128]{2,1,0:T(8,128)(2,1)S(1)}, u32[]{:S(2)}, u32[]{:S(2)}) collective-permute-start(bf16[2,864,128]{2,1,0:T(8,128)(2,1)S(1)} %get-tuple-element.146), channel_id=1, source_target_pairs={{0,32},{1,33},{2,34},{3,35},{4,36},{5,37},{6,38},{7,39},{8,40},{9,... | collective-permute-start | bytes 1327112 | tf_op jit(solution)/shard_map/ppermute | solution.py:63
  10.4 11.4 %collective-permute-start.2 = (bf16[2,864,128]{2,1,0:T(8,128)(2,1)S(1)}, bf16[2,864,128]{2,1,0:T(8,128)(2,1)S(1)}, u32[]{:S(2)}, u32[]{:S(2)}) collective-permute-start(bf16[2,864,128]{2,1,0:T(8,128)(2,1)S(1)} %get-tuple-element.147), channel_id=1, source_target_pairs={{0,112},{1,113},{2,114},{3,115},{4,116},{5,117},{6,118},{7,119},{8... | collective-permute-start | bytes 1327112 | tf_op jit(solution)/shard_map/ppermute | solution.py:63
  21.9 23.0 %collective-permute-start.3 = (bf16[4,864,128]{2,1,0:T(8,128)(2,1)S(1)}, bf16[4,864,128]{2,1,0:T(8,128)(2,1)S(1)}, u32[]{:S(2)}, u32[]{:S(2)}) collective-permute-start(bf16[4,864,128]{2,1,0:T(8,128)(2,1)S(1)} %y_regroup.6), channel_id=1, source_target_pairs={{0,96},{1,97},{2,98},{3,99},{4,100},{5,101},{6,102},{7,103},{8,104... | collective-permute-start | bytes 2654216 | tf_op jit(solution)/shard_map/ppermute | solution.py:63
  25.0 3.1 %collective-permute-start.4 = (bf16[2,864,128]{2,1,0:T(8,128)(2,1)S(1)}, bf16[2,864,128]{2,1,0:T(8,128)(2,1)S(1)}, u32[]{:S(2)}, u32[]{:S(2)}) collective-permute-start(bf16[2,864,128]{2,1,0:T(8,128)(2,1)S(1)} %get-tuple-element.149), channel_id=1, source_target_pairs={{0,16},{1,17},{2,18},{3,19},{4,20},{5,21},{6,22},{7,23},{8,24},{9,... | collective-permute-start | bytes 1327112 | tf_op jit(solution)/shard_map/ppermute | solution.py:63
  25.0 13.1 %collective-permute-start.5 = (bf16[2,864,128]{2,1,0:T(8,128)(2,1)S(1)}, bf16[2,864,128]{2,1,0:T(8,128)(2,1)S(1)}, u32[]{:S(2)}, u32[]{:S(2)}) collective-permute-start(bf16[2,864,128]{2,1,0:T(8,128)(2,1)S(1)} %get-tuple-element.150), channel_id=1, source_target_pairs={{0,32},{1,33},{2,34},{3,35},{4,36},{5,37},{6,38},{7,39},{8,40},{9,... | collective-permute-start | bytes 1327112 | tf_op jit(solution)/shard_map/ppermute | solution.py:63
  25.2 19.7 %collective-permute-start.6 = (bf16[2,864,128]{2,1,0:T(8,128)(2,1)S(1)}, bf16[2,864,128]{2,1,0:T(8,128)(2,1)S(1)}, u32[]{:S(2)}, u32[]{:S(2)}) collective-permute-start(bf16[2,864,128]{2,1,0:T(8,128)(2,1)S(1)} %get-tuple-element.151), channel_id=1, source_target_pairs={{0,112},{1,113},{2,114},{3,115},{4,116},{5,117},{6,118},{7,119},{8... | collective-permute-start | bytes 1327112 | tf_op jit(solution)/shard_map/ppermute | solution.py:63
  46.1 6.2 %collective-permute-start.10 = (bf16[2,880,128]{2,1,0:T(8,128)(2,1)S(1)}, bf16[2,880,128]{2,1,0:T(8,128)(2,1)S(1)}, u32[]{:S(2)}, u32[]{:S(2)}) collective-permute-start(bf16[2,880,128]{2,1,0:T(8,128)(2,1)S(1)} %get-tuple-element.166), channel_id=1, source_target_pairs={{0,16},{1,17},{2,18},{3,19},{4,20},{5,21},{6,22},{7,23},{8,24},{9,... | collective-permute-start | bytes 1351688 | tf_op jit(solution)/shard_map/ppermute | solution.py:63
  46.8 13.2 %collective-permute-start.11 = (bf16[2,880,128]{2,1,0:T(8,128)(2,1)S(1)}, bf16[2,880,128]{2,1,0:T(8,128)(2,1)S(1)}, u32[]{:S(2)}, u32[]{:S(2)}) collective-permute-start(bf16[2,880,128]{2,1,0:T(8,128)(2,1)S(1)} %get-tuple-element.167), channel_id=1, source_target_pairs={{0,32},{1,33},{2,34},{3,35},{4,36},{5,37},{6,38},{7,39},{8,40},{9,... | collective-permute-start | bytes 1351688 | tf_op jit(solution)/shard_map/ppermute | solution.py:63
  47.2 12.8 %collective-permute-start.12 = (bf16[2,880,128]{2,1,0:T(8,128)(2,1)S(1)}, bf16[2,880,128]{2,1,0:T(8,128)(2,1)S(1)}, u32[]{:S(2)}, u32[]{:S(2)}) collective-permute-start(bf16[2,880,128]{2,1,0:T(8,128)(2,1)S(1)} %get-tuple-element.168), channel_id=1, source_target_pairs={{0,112},{1,113},{2,114},{3,115},{4,116},{5,117},{6,118},{7,119},{8... | collective-permute-start | bytes 1351688 | tf_op jit(solution)/shard_map/ppermute | solution.py:63
  49.4 22.9 %collective-permute-start.14 = (bf16[4,864,128]{2,1,0:T(8,128)(2,1)S(1)}, bf16[4,864,128]{2,1,0:T(8,128)(2,1)S(1)}, u32[]{:S(2)}, u32[]{:S(2)}) collective-permute-start(bf16[4,864,128]{2,1,0:T(8,128)(2,1)S(1)} %y_regroup.7), channel_id=1, source_target_pairs={{0,96},{1,97},{2,98},{3,99},{4,100},{5,101},{6,102},{7,103},{8,104... | collective-permute-start | bytes 2654216 | tf_op jit(solution)/shard_map/ppermute | solution.py:63
  60.1 22.6 %collective-permute-start.13 = (bf16[4,880,128]{2,1,0:T(8,128)(2,1)S(1)}, bf16[4,880,128]{2,1,0:T(8,128)(2,1)S(1)}, u32[]{:S(2)}, u32[]{:S(2)}) collective-permute-start(bf16[4,880,128]{2,1,0:T(8,128)(2,1)S(1)} %y_regroup.8), channel_id=1, source_target_pairs={{0,96},{1,97},{2,98},{3,99},{4,100},{5,101},{6,102},{7,103},{8,104... | collective-permute-start | bytes 2703368 | tf_op jit(solution)/shard_map/ppermute | solution.py:63
  62.9 22.2 %collective-permute-start.7 = (bf16[2,576,128]{2,1,0:T(8,128)(2,1)S(1)}, bf16[2,576,128]{2,1,0:T(8,128)(2,1)S(1)}, u32[]{:S(2)}, u32[]{:S(2)}) collective-permute-start(bf16[2,576,128]{2,1,0:T(8,128)(2,1)S(1)} %get-tuple-element.163), channel_id=1, source_target_pairs={{0,16},{1,17},{2,18},{3,19},{4,20},{5,21},{6,22},{7,23},{8,24},{9,... | collective-permute-start | bytes 884744 | tf_op jit(solution)/shard_map/ppermute | solution.py:63
  62.9 24.1 %collective-permute-start.8 = (bf16[2,576,128]{2,1,0:T(8,128)(2,1)S(1)}, bf16[2,576,128]{2,1,0:T(8,128)(2,1)S(1)}, u32[]{:S(2)}, u32[]{:S(2)}) collective-permute-start(bf16[2,576,128]{2,1,0:T(8,128)(2,1)S(1)} %get-tuple-element.164), channel_id=1, source_target_pairs={{0,32},{1,33},{2,34},{3,35},{4,36},{5,37},{6,38},{7,39},{8,40},{9,... | collective-permute-start | bytes 884744 | tf_op jit(solution)/shard_map/ppermute | solution.py:63
  73.4 13.7 %collective-permute-start.19 = (bf16[2,880,128]{2,1,0:T(8,128)(2,1)S(1)}, bf16[2,880,128]{2,1,0:T(8,128)(2,1)S(1)}, u32[]{:S(2)}, u32[]{:S(2)}) collective-permute-start(bf16[2,880,128]{2,1,0:T(8,128)(2,1)S(1)} %get-tuple-element.192), channel_id=1, source_target_pairs={{0,16},{1,17},{2,18},{3,19},{4,20},{5,21},{6,22},{7,23},{8,24},{9,... | collective-permute-start | bytes 1351688 | tf_op jit(solution)/shard_map/ppermute | solution.py:63
  73.5 13.6 %collective-permute-start.9 = (bf16[2,576,128]{2,1,0:T(8,128)(2,1)S(1)}, bf16[2,576,128]{2,1,0:T(8,128)(2,1)S(1)}, u32[]{:S(2)}, u32[]{:S(2)}) collective-permute-start(bf16[2,576,128]{2,1,0:T(8,128)(2,1)S(1)} %get-tuple-element.165), channel_id=1, source_target_pairs={{0,112},{1,113},{2,114},{3,115},{4,116},{5,117},{6,118},{7,119},{8... | collective-permute-start | bytes 884744 | tf_op jit(solution)/shard_map/ppermute | solution.py:63
  83.5 21.7 %collective-permute-start.16 = (bf16[4,784,128]{2,1,0:T(8,128)(2,1)S(1)}, bf16[4,784,128]{2,1,0:T(8,128)(2,1)S(1)}, u32[]{:S(2)}, u32[]{:S(2)}) collective-permute-start(bf16[4,784,128]{2,1,0:T(8,128)(2,1)S(1)} %get-tuple-element.189), channel_id=1, source_target_pairs={{0,1},{1,0},{2,3},{3,2},{4,5},{5,4},{6,7},{7,6},{8,9},{9,8},{10,11... | collective-permute-start | bytes 2408456 | tf_op jit(solution)/shard_map/ppermute | solution.py:63
  85.1 20.8 %collective-permute-start.17 = (bf16[4,784,128]{2,1,0:T(8,128)(2,1)S(1)}, bf16[4,784,128]{2,1,0:T(8,128)(2,1)S(1)}, u32[]{:S(2)}, u32[]{:S(2)}) collective-permute-start(bf16[4,784,128]{2,1,0:T(8,128)(2,1)S(1)} %get-tuple-element.190), channel_id=1, source_target_pairs={{0,4},{1,5},{2,6},{3,7},{4,0},{5,1},{6,2},{7,3},{8,12},{9,13},{10,... | collective-permute-start | bytes 2408456 | tf_op jit(solution)/shard_map/ppermute | solution.py:63
  87.0 18.9 %collective-permute-start.18 = (bf16[4,784,128]{2,1,0:T(8,128)(2,1)S(1)}, bf16[4,784,128]{2,1,0:T(8,128)(2,1)S(1)}, u32[]{:S(2)}, u32[]{:S(2)}) collective-permute-start(bf16[4,784,128]{2,1,0:T(8,128)(2,1)S(1)} %get-tuple-element.191), channel_id=1, source_target_pairs={{0,5},{1,4},{2,7},{3,6},{4,1},{5,0},{6,3},{7,2},{8,13},{9,12},{10,... | collective-permute-start | bytes 2408456 | tf_op jit(solution)/shard_map/ppermute | solution.py:63
  87.1 11.6 %collective-permute-start.20 = (bf16[2,880,128]{2,1,0:T(8,128)(2,1)S(1)}, bf16[2,880,128]{2,1,0:T(8,128)(2,1)S(1)}, u32[]{:S(2)}, u32[]{:S(2)}) collective-permute-start(bf16[2,880,128]{2,1,0:T(8,128)(2,1)S(1)} %get-tuple-element.193), channel_id=1, source_target_pairs={{0,32},{1,33},{2,34},{3,35},{4,36},{5,37},{6,38},{7,39},{8,40},{9,... | collective-permute-start | bytes 1351688 | tf_op jit(solution)/shard_map/ppermute | solution.py:63
  87.1 14.6 %collective-permute-start.21 = (bf16[2,880,128]{2,1,0:T(8,128)(2,1)S(1)}, bf16[2,880,128]{2,1,0:T(8,128)(2,1)S(1)}, u32[]{:S(2)}, u32[]{:S(2)}) collective-permute-start(bf16[2,880,128]{2,1,0:T(8,128)(2,1)S(1)} %get-tuple-element.194), channel_id=1, source_target_pairs={{0,112},{1,113},{2,114},{3,115},{4,116},{5,117},{6,118},{7,119},{8... | collective-permute-start | bytes 1351688 | tf_op jit(solution)/shard_map/ppermute | solution.py:63
  101.8 21.7 %collective-permute-start.28 = (bf16[4,880,128]{2,1,0:T(8,128)(2,1)S(1)}, bf16[4,880,128]{2,1,0:T(8,128)(2,1)S(1)}, u32[]{:S(2)}, u32[]{:S(2)}) collective-permute-start(bf16[4,880,128]{2,1,0:T(8,128)(2,1)S(1)} %y_regroup.10), channel_id=1, source_target_pairs={{0,96},{1,97},{2,98},{3,99},{4,100},{5,101},{6,102},{7,103},{8,104... | collective-permute-start | bytes 2703368 | tf_op jit(solution)/shard_map/ppermute | solution.py:63
  103.0 19.7 %collective-permute-start.15 = (bf16[4,576,128]{2,1,0:T(8,128)(2,1)S(1)}, bf16[4,576,128]{2,1,0:T(8,128)(2,1)S(1)}, u32[]{:S(2)}, u32[]{:S(2)}) collective-permute-start(bf16[4,576,128]{2,1,0:T(8,128)(2,1)S(1)} %y_regroup.9), channel_id=1, source_target_pairs={{0,96},{1,97},{2,98},{3,99},{4,100},{5,101},{6,102},{7,103},{8,104... | collective-permute-start | bytes 1769480 | tf_op jit(solution)/shard_map/ppermute | solution.py:63
  106.0 22.9 %collective-permute-start.26 = (bf16[4,784,128]{2,1,0:T(8,128)(2,1)S(1)}, bf16[4,784,128]{2,1,0:T(8,128)(2,1)S(1)}, u32[]{:S(2)}, u32[]{:S(2)}) collective-permute-start(bf16[4,784,128]{2,1,0:T(8,128)(2,1)S(1)} %get-tuple-element.213), channel_id=1, source_target_pairs={{0,12},{1,13},{2,14},{3,15},{4,8},{5,9},{6,10},{7,11},{8,4},{9,5},... | collective-permute-start | bytes 2408456 | tf_op jit(solution)/shard_map/ppermute | solution.py:63
  110.1 19.0 %collective-permute-start.27 = (bf16[4,784,128]{2,1,0:T(8,128)(2,1)S(1)}, bf16[4,784,128]{2,1,0:T(8,128)(2,1)S(1)}, u32[]{:S(2)}, u32[]{:S(2)}) collective-permute-start(bf16[4,784,128]{2,1,0:T(8,128)(2,1)S(1)} %get-tuple-element.214), channel_id=1, source_target_pairs={{0,15},{1,14},{2,13},{3,12},{4,11},{5,10},{6,9},{7,8},{8,7},{9,6},... | collective-permute-start | bytes 2408456 | tf_op jit(solution)/shard_map/ppermute | solution.py:63
  111.8 22.8 %collective-permute-start.25 = (bf16[4,784,128]{2,1,0:T(8,128)(2,1)S(1)}, bf16[4,784,128]{2,1,0:T(8,128)(2,1)S(1)}, u32[]{:S(2)}, u32[]{:S(2)}) collective-permute-start(bf16[4,784,128]{2,1,0:T(8,128)(2,1)S(1)} %get-tuple-element.203), channel_id=1, source_target_pairs={{0,3},{1,2},{2,1},{3,0},{4,7},{5,6},{6,5},{7,4},{8,11},{9,10},{10,... | collective-permute-start | bytes 2408456 | tf_op jit(solution)/shard_map/ppermute | solution.py:63
  123.5 1.6 collective-permute-start.22
  124.4 16.4 %collective-permute-start.30 = (bf16[4,784,128]{2,1,0:T(8,128)(2,1)S(1)}, bf16[4,784,128]{2,1,0:T(8,128)(2,1)S(1)}, u32[]{:S(2)}, u32[]{:S(2)}) collective-permute-start(bf16[4,784,128]{2,1,0:T(8,128)(2,1)S(1)} %get-tuple-element.233), channel_id=1, source_target_pairs={{0,1},{1,0},{2,3},{3,2},{4,5},{5,4},{6,7},{7,6},{8,9},{9,8},{10,11... | collective-permute-start | bytes 2408456 | tf_op jit(solution)/shard_map/ppermute | solution.py:63
  125.1 15.7 %collective-permute-start.31 = (bf16[4,784,128]{2,1,0:T(8,128)(2,1)S(1)}, bf16[4,784,128]{2,1,0:T(8,128)(2,1)S(1)}, u32[]{:S(2)}, u32[]{:S(2)}) collective-permute-start(bf16[4,784,128]{2,1,0:T(8,128)(2,1)S(1)} %get-tuple-element.234), channel_id=1, source_target_pairs={{0,4},{1,5},{2,6},{3,7},{4,0},{5,1},{6,2},{7,3},{8,12},{9,13},{10,... | collective-permute-start | bytes 2408456 | tf_op jit(solution)/shard_map/ppermute | solution.py:63
  128.9 17.0 %collective-permute-start.32 = (bf16[4,784,128]{2,1,0:T(8,128)(2,1)S(1)}, bf16[4,784,128]{2,1,0:T(8,128)(2,1)S(1)}, u32[]{:S(2)}, u32[]{:S(2)}) collective-permute-start(bf16[4,784,128]{2,1,0:T(8,128)(2,1)S(1)} %get-tuple-element.235), channel_id=1, source_target_pairs={{0,5},{1,4},{2,7},{3,6},{4,1},{5,0},{6,3},{7,2},{8,13},{9,12},{10,... | collective-permute-start | bytes 2408456 | tf_op jit(solution)/shard_map/ppermute | solution.py:63
  129.2 8.2 %collective-permute-start.23 = (bf16[2,592,128]{2,1,0:T(8,128)(2,1)S(1)}, bf16[2,592,128]{2,1,0:T(8,128)(2,1)S(1)}, u32[]{:S(2)}, u32[]{:S(2)}) collective-permute-start(bf16[2,592,128]{2,1,0:T(8,128)(2,1)S(1)} %get-tuple-element.211), channel_id=1, source_target_pairs={{0,32},{1,33},{2,34},{3,35},{4,36},{5,37},{6,38},{7,39},{8,40},{9,... | collective-permute-start | bytes 909320 | tf_op jit(solution)/shard_map/ppermute | solution.py:63
  134.5 6.2 %collective-permute-start.24 = (bf16[2,592,128]{2,1,0:T(8,128)(2,1)S(1)}, bf16[2,592,128]{2,1,0:T(8,128)(2,1)S(1)}, u32[]{:S(2)}, u32[]{:S(2)}) collective-permute-start(bf16[2,592,128]{2,1,0:T(8,128)(2,1)S(1)} %get-tuple-element.212), channel_id=1, source_target_pairs={{0,112},{1,113},{2,114},{3,115},{4,116},{5,117},{6,118},{7,119},{8... | collective-permute-start | bytes 909320 | tf_op jit(solution)/shard_map/ppermute | solution.py:63
  146.0 25.2 %collective-permute-start.37 = (bf16[4,784,128]{2,1,0:T(8,128)(2,1)S(1)}, bf16[4,784,128]{2,1,0:T(8,128)(2,1)S(1)}, u32[]{:S(2)}, u32[]{:S(2)}) collective-permute-start(bf16[4,784,128]{2,1,0:T(8,128)(2,1)S(1)} %get-tuple-element.250), channel_id=1, source_target_pairs={{0,12},{1,13},{2,14},{3,15},{4,8},{5,9},{6,10},{7,11},{8,4},{9,5},... | collective-permute-start | bytes 2408456 | tf_op jit(solution)/shard_map/ppermute | solution.py:63
  149.3 11.3 %collective-permute-start.29 = (bf16[4,592,128]{2,1,0:T(8,128)(2,1)S(1)}, bf16[4,592,128]{2,1,0:T(8,128)(2,1)S(1)}, u32[]{:S(2)}, u32[]{:S(2)}) collective-permute-start(bf16[4,592,128]{2,1,0:T(8,128)(2,1)S(1)} %y_regroup.11), channel_id=1, source_target_pairs={{0,96},{1,97},{2,98},{3,99},{4,100},{5,101},{6,102},{7,103},{8,104... | collective-permute-start | bytes 1818632 | tf_op jit(solution)/shard_map/ppermute | solution.py:63
  151.9 20.3 %collective-permute-start.38 = (bf16[4,784,128]{2,1,0:T(8,128)(2,1)S(1)}, bf16[4,784,128]{2,1,0:T(8,128)(2,1)S(1)}, u32[]{:S(2)}, u32[]{:S(2)}) collective-permute-start(bf16[4,784,128]{2,1,0:T(8,128)(2,1)S(1)} %get-tuple-element.251), channel_id=1, source_target_pairs={{0,15},{1,14},{2,13},{3,12},{4,11},{5,10},{6,9},{7,8},{8,7},{9,6},... | collective-permute-start | bytes 2408456 | tf_op jit(solution)/shard_map/ppermute | solution.py:63
  153.9 25.3 %collective-permute-start.36 = (bf16[4,784,128]{2,1,0:T(8,128)(2,1)S(1)}, bf16[4,784,128]{2,1,0:T(8,128)(2,1)S(1)}, u32[]{:S(2)}, u32[]{:S(2)}) collective-permute-start(bf16[4,784,128]{2,1,0:T(8,128)(2,1)S(1)} %get-tuple-element.240), channel_id=1, source_target_pairs={{0,3},{1,2},{2,1},{3,0},{4,7},{5,6},{6,5},{7,4},{8,11},{9,10},{10,... | collective-permute-start | bytes 2408456 | tf_op jit(solution)/shard_map/ppermute | solution.py:63
  161.4 20.6 %collective-permute-start.33 = (bf16[4,528,128]{2,1,0:T(8,128)(2,1)S(1)}, bf16[4,528,128]{2,1,0:T(8,128)(2,1)S(1)}, u32[]{:S(2)}, u32[]{:S(2)}) collective-permute-start(bf16[4,528,128]{2,1,0:T(8,128)(2,1)S(1)} %get-tuple-element.247), channel_id=1, source_target_pairs={{0,1},{1,0},{2,3},{3,2},{4,5},{5,4},{6,7},{7,6},{8,9},{9,8},{10,11... | collective-permute-start | bytes 1622024 | tf_op jit(solution)/shard_map/ppermute | solution.py:63
  162.5 19.6 %collective-permute-start.34 = (bf16[4,528,128]{2,1,0:T(8,128)(2,1)S(1)}, bf16[4,528,128]{2,1,0:T(8,128)(2,1)S(1)}, u32[]{:S(2)}, u32[]{:S(2)}) collective-permute-start(bf16[4,528,128]{2,1,0:T(8,128)(2,1)S(1)} %get-tuple-element.248), channel_id=1, source_target_pairs={{0,4},{1,5},{2,6},{3,7},{4,0},{5,1},{6,2},{7,3},{8,12},{9,13},{10,... | collective-permute-start | bytes 1622024 | tf_op jit(solution)/shard_map/ppermute | solution.py:63
  171.2 12.9 %collective-permute-start.35 = (bf16[4,528,128]{2,1,0:T(8,128)(2,1)S(1)}, bf16[4,528,128]{2,1,0:T(8,128)(2,1)S(1)}, u32[]{:S(2)}, u32[]{:S(2)}) collective-permute-start(bf16[4,528,128]{2,1,0:T(8,128)(2,1)S(1)} %get-tuple-element.249), channel_id=1, source_target_pairs={{0,5},{1,4},{2,7},{3,6},{4,1},{5,0},{6,3},{7,2},{8,13},{9,12},{10,... | collective-permute-start | bytes 1622024 | tf_op jit(solution)/shard_map/ppermute | solution.py:63
  184.2 16.4 %collective-permute-start.40 = (bf16[4,528,128]{2,1,0:T(8,128)(2,1)S(1)}, bf16[4,528,128]{2,1,0:T(8,128)(2,1)S(1)}, u32[]{:S(2)}, u32[]{:S(2)}) collective-permute-start(bf16[4,528,128]{2,1,0:T(8,128)(2,1)S(1)} %get-tuple-element.266), channel_id=1, source_target_pairs={{0,12},{1,13},{2,14},{3,15},{4,8},{5,9},{6,10},{7,11},{8,4},{9,5},... | collective-permute-start | bytes 1622024 | tf_op jit(solution)/shard_map/ppermute | solution.py:63
  185.4 15.3 %collective-permute-start.41 = (bf16[4,528,128]{2,1,0:T(8,128)(2,1)S(1)}, bf16[4,528,128]{2,1,0:T(8,128)(2,1)S(1)}, u32[]{:S(2)}, u32[]{:S(2)}) collective-permute-start(bf16[4,528,128]{2,1,0:T(8,128)(2,1)S(1)} %get-tuple-element.267), channel_id=1, source_target_pairs={{0,15},{1,14},{2,13},{3,12},{4,11},{5,10},{6,9},{7,8},{8,7},{9,6},... | collective-permute-start | bytes 1622024 | tf_op jit(solution)/shard_map/ppermute | solution.py:63
  189.0 14.4 %collective-permute-start.39 = (bf16[4,528,128]{2,1,0:T(8,128)(2,1)S(1)}, bf16[4,528,128]{2,1,0:T(8,128)(2,1)S(1)}, u32[]{:S(2)}, u32[]{:S(2)}) collective-permute-start(bf16[4,528,128]{2,1,0:T(8,128)(2,1)S(1)} %get-tuple-element.265), channel_id=1, source_target_pairs={{0,3},{1,2},{2,1},{3,0},{4,7},{5,6},{6,5},{7,4},{8,11},{9,10},{10,... | collective-permute-start | bytes 1622024 | tf_op jit(solution)/shard_map/ppermute | solution.py:63

commit v12 on v9

--- a/solution.py
+++ b/solution.py
@@ -20,11 +20,11 @@
     ("y_regroup", 0),
     ("cross", 1),
     ("spread", 0),
-    ("y_regroup", 2),
     ("y_regroup", 1),
     ("regroup", 0),
+    ("y_regroup", 2),
+    ("spread", 1),
     ("cross", 2),
-    ("spread", 1),
     ("pack", 0),
     ("y_regroup", 2),
     ("regroup", 1),

time: 208 us -> 209 us (level)
  starting transfers between devices: 55.6 us -> 65.1 us
  waiting for transfers between devices: 127 us -> 119 us
    ppermute x42, starting transfers between devices: 55.6 us -> 65.1 us  [hop(): return lax.ppermute(array, BOTH, pairs)]
    ppermute x42, waiting for transfers between devices: 127 us -> 119 us  [hop(): return lax.ppermute(array, BOTH, pairs)]
  transfers between devices with their start and end apart: 42 -> 42, of which waited for: 22 -> 23; matrix products, arithmetic and copies ran while one was open for 0% -> 0% of each run, Pallas kernels for 6% -> 5%
where the time goes in v12:
time: 209 us; the launch traced here: 208 us
  waiting for transfers between devices  119 us (57%)
  starting transfers between devices  65.1 us (31%)
  Pallas kernels  20.5 us (10%)
  local copies, waits for them, and re-layouts  2.33 us (1%)
    ppermute x42, waiting for transfers between devices, hop(): return lax.ppermute(array, BOTH, pairs)  119 us
    ppermute x42, starting transfers between devices, hop(): return lax.ppermute(array, BOTH, pairs)  65.1 us
    pallas_call x3, Pallas kernels, per_device(): pl.pallas_call(functools.partial(pack_kernel, owners, heads, chunk, bool(...  8.52 us
    pallas_call x15, Pallas kernels, call(): pl.pallas_call(kernel, in_specs=[smem_spec] * table + [vmem_spec] * (len(...  6.34 us
    pallas_call x1, Pallas kernels, per_device(): pl.pallas_call(functools.partial(local_turn_kernel, rows_a), grid=(heads,...  5.61 us
  transfers between devices with their start and end apart: 42, of which 23 were waited for; matrix products, arithmetic and copies ran while one was open for 0% of the time, Pallas kernels for 5%

profile of v12, /device:TPU:0, one launch (start us, length us, event | category | flops | bytes accessed | tf_op | source)
XLA Modules:
  0.0 208.0 jit_solution(2280786865769646896)
XLA Ops:
  0.6 2.3 %copy-done = bf16[2048,1152]{1,0:T(8,128)(2,1)S(1)} copy-done((bf16[2048,1152]{1,0:T(8,128)(2,1)S(1)}, bf16[2048,1152]{1,0:T(8,128)(2,1)}, u32[]{:S(2)}) %copy-start) | copy-done | bytes 4718616
  3.0 5.6 %local_turn.1 = (bf16[2,576,128]{2,1,0:T(8,128)(2,1)S(1)}, bf16[2,576,128]{2,1,0:T(8,128)(2,1)S(1)}, bf16[2,576,128]{2,1,0:T(8,128)(2,1)S(1)}, bf16[2,576,128]{2...) custom-call(bf16[2048,1152]{1,0:T(8,128)(2,1)S(1)} %copy-done), custom_call_target="tpu_custom_call" | custom-call | tf_op jit(solution)/shard_map/local_turn/pallas_call | solution.py:299
  8.7 1.7 collective-permute-start.1
  10.4 1.5 collective-permute-start.2
  11.9 5.6 %collective-permute-done.1.refs_2_ = bf16[2,576,128]{2,1,0:T(8,128)(2,1)S(1)} collective-permute-done((bf16[2,576,128]{2,1,0:T(8,128)(2,1)S(1)}, bf16[2,576,128]{2,1,0:T(8,128)(2,1)S(1)}, u32[]{:S(2)}, u32[]{:S(2)}) %collective-permute-start.1) | collective-permute-done | bytes 294944 | tf_op jit(solution)/shard_map/ppermute | solution.py:63
  17.5 1.2 collective-permute-done.2.refs_3_
  18.8 3.1 %collective-permute-start.3 = (bf16[4,576,128]{2,1,0:T(8,128)(2,1)S(1)}, bf16[4,576,128]{2,1,0:T(8,128)(2,1)S(1)}, u32[]{:S(2)}, u32[]{:S(2)}) collective-permute-start(bf16[4,576,128]{2,1,0:T(8,128)(2,1)S(1)} %y_regroup.6), channel_id=1, source_target_pairs={{0,96},{1,97},{2,98},{3,99},{4,100},{5,101},{6,102},{7,103},{8,104... | collective-permute-start | bytes 1769480 | tf_op jit(solution)/shard_map/ppermute | solution.py:63
  22.0 2.9 %collective-permute-start.6 = (bf16[2,864,128]{2,1,0:T(8,128)(2,1)S(1)}, bf16[2,864,128]{2,1,0:T(8,128)(2,1)S(1)}, u32[]{:S(2)}, u32[]{:S(2)}) collective-permute-start(bf16[2,864,128]{2,1,0:T(8,128)(2,1)S(1)} %get-tuple-element.151), channel_id=1, source_target_pairs={{0,112},{1,113},{2,114},{3,115},{4,116},{5,117},{6,118},{7,119},{8... | collective-permute-start | bytes 1327112 | tf_op jit(solution)/shard_map/ppermute | solution.py:63
  24.9 10.0 %collective-permute-done.5.refs_2_ = bf16[2,864,128]{2,1,0:T(8,128)(2,1)S(1)} collective-permute-done((bf16[2,864,128]{2,1,0:T(8,128)(2,1)S(1)}, bf16[2,864,128]{2,1,0:T(8,128)(2,1)S(1)}, u32[]{:S(2)}, u32[]{:S(2)}) %collective-permute-start.5) | collective-permute-done | bytes 442400 | tf_op jit(solution)/shard_map/ppermute | solution.py:63
  35.0 3.6 %collective-permute-done.6.refs_3_ = bf16[2,864,128]{2,1,0:T(8,128)(2,1)S(1)} collective-permute-done((bf16[2,864,128]{2,1,0:T(8,128)(2,1)S(1)}, bf16[2,864,128]{2,1,0:T(8,128)(2,1)S(1)}, u32[]{:S(2)}, u32[]{:S(2)}) %collective-permute-start.6) | collective-permute-done | bytes 442400 | tf_op jit(solution)/shard_map/ppermute | solution.py:63
  38.6 0.8 cross.3
  39.5 0.7 collective-permute-start.10
  40.1 0.4 collective-permute-start.11
  40.5 2.3 %collective-permute-start.12 = (bf16[2,592,128]{2,1,0:T(8,128)(2,1)S(1)}, bf16[2,592,128]{2,1,0:T(8,128)(2,1)S(1)}, u32[]{:S(2)}, u32[]{:S(2)}) collective-permute-start(bf16[2,592,128]{2,1,0:T(8,128)(2,1)S(1)} %get-tuple-element.168), channel_id=1, source_target_pairs={{0,112},{1,113},{2,114},{3,115},{4,116},{5,117},{6,118},{7,119},{8... | collective-permute-start | bytes 909320 | tf_op jit(solution)/shard_map/ppermute | solution.py:63
  42.8 2.9 %collective-permute-start.14 = (bf16[4,864,128]{2,1,0:T(8,128)(2,1)S(1)}, bf16[4,864,128]{2,1,0:T(8,128)(2,1)S(1)}, u32[]{:S(2)}, u32[]{:S(2)}) collective-permute-start(bf16[4,864,128]{2,1,0:T(8,128)(2,1)S(1)} %y_regroup.7), channel_id=1, source_target_pairs={{0,96},{1,97},{2,98},{3,99},{4,100},{5,101},{6,102},{7,103},{8,104... | collective-permute-start | bytes 2654216 | tf_op jit(solution)/shard_map/ppermute | solution.py:63
  45.7 4.5 %collective-permute-done.11.refs_2_ = bf16[2,592,128]{2,1,0:T(8,128)(2,1)S(1)} collective-permute-done((bf16[2,592,128]{2,1,0:T(8,128)(2,1)S(1)}, bf16[2,592,128]{2,1,0:T(8,128)(2,1)S(1)}, u32[]{:S(2)}, u32[]{:S(2)}) %collective-permute-start.11) | collective-permute-done | bytes 303136 | tf_op jit(solution)/shard_map/ppermute | solution.py:63
  50.2 2.9 %collective-permute-start.13 = (bf16[4,592,128]{2,1,0:T(8,128)(2,1)S(1)}, bf16[4,592,128]{2,1,0:T(8,128)(2,1)S(1)}, u32[]{:S(2)}, u32[]{:S(2)}) collective-permute-start(bf16[4,592,128]{2,1,0:T(8,128)(2,1)S(1)} %y_regroup.8), channel_id=1, source_target_pairs={{0,96},{1,97},{2,98},{3,99},{4,100},{5,101},{6,102},{7,103},{8,104... | collective-permute-start | bytes 1818632 | tf_op jit(solution)/shard_map/ppermute | solution.py:63
  53.1 6.9 %collective-permute-done.14.refs_4_ = bf16[4,864,128]{2,1,0:T(8,128)(2,1)S(1)} collective-permute-done((bf16[4,864,128]{2,1,0:T(8,128)(2,1)S(1)}, bf16[4,864,128]{2,1,0:T(8,128)(2,1)S(1)}, u32[]{:S(2)}, u32[]{:S(2)}) %collective-permute-start.14) | collective-permute-done | bytes 884768 | tf_op jit(solution)/shard_map/ppermute | solution.py:63
  60.0 1.1 cross.4
  61.2 5.3 %collective-permute-done.13.refs_4_ = bf16[4,592,128]{2,1,0:T(8,128)(2,1)S(1)} collective-permute-done((bf16[4,592,128]{2,1,0:T(8,128)(2,1)S(1)}, bf16[4,592,128]{2,1,0:T(8,128)(2,1)S(1)}, u32[]{:S(2)}, u32[]{:S(2)}) %collective-permute-start.13) | collective-permute-done | bytes 606240 | tf_op jit(solution)/shard_map/ppermute | solution.py:63
  66.5 0.8 spread.3
  67.3 1.6 collective-permute-start.15
  68.9 3.1 %collective-permute-start.20 = (bf16[2,880,128]{2,1,0:T(8,128)(2,1)S(1)}, bf16[2,880,128]{2,1,0:T(8,128)(2,1)S(1)}, u32[]{:S(2)}, u32[]{:S(2)}) collective-permute-start(bf16[2,880,128]{2,1,0:T(8,128)(2,1)S(1)} %get-tuple-element.190), channel_id=1, source_target_pairs={{0,112},{1,113},{2,114},{3,115},{4,116},{5,117},{6,118},{7,119},{8... | collective-permute-start | bytes 1351688 | tf_op jit(solution)/shard_map/ppermute | solution.py:63
  72.0 1.9 collective-permute-start.16
  74.0 7.9 %collective-permute-done.19.refs_2_ = bf16[2,880,128]{2,1,0:T(8,128)(2,1)S(1)} collective-permute-done((bf16[2,880,128]{2,1,0:T(8,128)(2,1)S(1)}, bf16[2,880,128]{2,1,0:T(8,128)(2,1)S(1)}, u32[]{:S(2)}, u32[]{:S(2)}) %collective-permute-start.19) | collective-permute-done | bytes 450592 | tf_op jit(solution)/shard_map/ppermute | solution.py:63
  81.9 0.3 collective-permute-start.8
  82.1 3.3 %collective-permute-start.9 = (bf16[2,864,128]{2,1,0:T(8,128)(2,1)S(1)}, bf16[2,864,128]{2,1,0:T(8,128)(2,1)S(1)}, u32[]{:S(2)}, u32[]{:S(2)}) collective-permute-start(bf16[2,864,128]{2,1,0:T(8,128)(2,1)S(1)} %get-tuple-element.165), channel_id=1, source_target_pairs={{0,112},{1,113},{2,114},{3,115},{4,116},{5,117},{6,118},{7,119},{8... | collective-permute-start | bytes 1327112 | tf_op jit(solution)/shard_map/ppermute | solution.py:63
  85.5 1.7 collective-permute-done.16.refs_2_
  87.2 2.5 %collective-permute-start.22 = (bf16[4,880,128]{2,1,0:T(8,128)(2,1)S(1)}, bf16[4,880,128]{2,1,0:T(8,128)(2,1)S(1)}, u32[]{:S(2)}, u32[]{:S(2)}) collective-permute-start(bf16[4,880,128]{2,1,0:T(8,128)(2,1)S(1)} %y_regroup.9), channel_id=1, source_target_pairs={{0,96},{1,97},{2,98},{3,99},{4,100},{5,101},{6,102},{7,103},{8,104... | collective-permute-start | bytes 2703368 | tf_op jit(solution)/shard_map/ppermute | solution.py:63
  89.8 5.1 %collective-permute-done.8.refs_2_ = bf16[2,864,128]{2,1,0:T(8,128)(2,1)S(1)} collective-permute-done((bf16[2,864,128]{2,1,0:T(8,128)(2,1)S(1)}, bf16[2,864,128]{2,1,0:T(8,128)(2,1)S(1)}, u32[]{:S(2)}, u32[]{:S(2)}) %collective-permute-start.8) | collective-permute-done | bytes 442400 | tf_op jit(solution)/shard_map/ppermute | solution.py:63
  95.1 2.6 %collective-permute-start.21 = (bf16[4,864,128]{2,1,0:T(8,128)(2,1)S(1)}, bf16[4,864,128]{2,1,0:T(8,128)(2,1)S(1)}, u32[]{:S(2)}, u32[]{:S(2)}) collective-permute-start(bf16[4,864,128]{2,1,0:T(8,128)(2,1)S(1)} %y_regroup.10), channel_id=1, source_target_pairs={{0,96},{1,97},{2,98},{3,99},{4,100},{5,101},{6,102},{7,103},{8,104... | collective-permute-start | bytes 2654216 | tf_op jit(solution)/shard_map/ppermute | solution.py:63
  97.6 4.0 %collective-permute-start.27 = (bf16[4,528,128]{2,1,0:T(8,128)(2,1)S(1)}, bf16[4,528,128]{2,1,0:T(8,128)(2,1)S(1)}, u32[]{:S(2)}, u32[]{:S(2)}) collective-permute-start(bf16[4,528,128]{2,1,0:T(8,128)(2,1)S(1)} %get-tuple-element.219), channel_id=1, source_target_pairs={{0,12},{1,13},{2,14},{3,15},{4,8},{5,9},{6,10},{7,11},{8,4},{9,5},... | collective-permute-start | bytes 1622024 | tf_op jit(solution)/shard_map/ppermute | solution.py:63
  101.7 1.5 collective-permute-start.28
  103.2 1.1 collective-permute-start.26
  104.3 1.5 collective-permute-done.22.refs_4_
  105.8 0.9 spread.4
  106.7 8.6 %collective-permute-done.21.refs_4_ = bf16[4,864,128]{2,1,0:T(8,128)(2,1)S(1)} collective-permute-done((bf16[4,864,128]{2,1,0:T(8,128)(2,1)S(1)}, bf16[4,864,128]{2,1,0:T(8,128)(2,1)S(1)}, u32[]{:S(2)}, u32[]{:S(2)}) %collective-permute-start.21) | collective-permute-done | bytes 884768 | tf_op jit(solution)/shard_map/ppermute | solution.py:63
  115.3 1.1 cross.5
  116.5 0.3 collective-permute-start.30
  116.8 1.9 collective-permute-start.31
  118.7 1.3 collective-permute-start.32
  120.1 5.7 %collective-permute-start.25 = (bf16[2,880,128]{2,1,0:T(8,128)(2,1)S(1)}, bf16[2,880,128]{2,1,0:T(8,128)(2,1)S(1)}, u32[]{:S(2)}, u32[]{:S(2)}) collective-permute-start(bf16[2,880,128]{2,1,0:T(8,128)(2,1)S(1)} %get-tuple-element.218), channel_id=1, source_target_pairs={{0,112},{1,113},{2,114},{3,115},{4,116},{5,117},{6,118},{7,119},{8... | collective-permute-start | bytes 1351688 | tf_op jit(solution)/shard_map/ppermute | solution.py:63
  125.8 2.4 %pack.3 = (f32[16,128]{1,0:T(8,128)S(1)}, bf16[1,16,128,2048]{3,2,1,0:T(8,128)(2,1)}) custom-call(s32[144]{0:T(256)S(1)} %copy-done.1, bf16[4,528,128]{2,1,0:T(8,128)(2,1)S(1)} %get-tuple-element.221.refs_0_, bf16[4,528,128]{2,1,0:T(8,128)(2,1)S(1)} %collective-permute-done.15.refs_1_, bf16[4,528,128]{2,1,0:T(8,128)(2,1)S(1)} %collective-permute-done.16.refs_2_, ...), custom_call_target="tpu_custom_call" | custom-call | tf_op jit(solution)/shard_map/pack/pallas_call | solution.py:343
  128.2 4.0 %collective-permute-done.24.refs_2_ = bf16[2,880,128]{2,1,0:T(8,128)(2,1)S(1)} collective-permute-done((bf16[2,880,128]{2,1,0:T(8,128)(2,1)S(1)}, bf16[2,880,128]{2,1,0:T(8,128)(2,1)S(1)}, u32[]{:S(2)}, u32[]{:S(2)}) %collective-permute-start.24) | collective-permute-done | bytes 450592 | tf_op jit(solution)/shard_map/ppermute | solution.py:63
  132.2 3.3 %collective-permute-done.25.refs_3_ = bf16[2,880,128]{2,1,0:T(8,128)(2,1)S(1)} collective-permute-done((bf16[2,880,128]{2,1,0:T(8,128)(2,1)S(1)}, bf16[2,880,128]{2,1,0:T(8,128)(2,1)S(1)}, u32[]{:S(2)}, u32[]{:S(2)}) %collective-permute-start.25) | collective-permute-done | bytes 450592 | tf_op jit(solution)/shard_map/ppermute | solution.py:63
  135.6 0.8 collective-permute-start.29
  136.4 0.7 collective-permute-done.31.refs_2_
  137.0 1.5 collective-permute-done.32.refs_3_
  138.7 3.1 %collective-permute-start.37 = (bf16[4,784,128]{2,1,0:T(8,128)(2,1)S(1)}, bf16[4,784,128]{2,1,0:T(8,128)(2,1)S(1)}, u32[]{:S(2)}, u32[]{:S(2)}) collective-permute-start(bf16[4,784,128]{2,1,0:T(8,128)(2,1)S(1)} %get-tuple-element.250), channel_id=1, source_target_pairs={{0,12},{1,13},{2,14},{3,15},{4,8},{5,9},{6,10},{7,11},{8,4},{9,5},... | collective-permute-start | bytes 2408456 | tf_op jit(solution)/shard_map/ppermute | solution.py:63
  141.8 1.8 collective-permute-start.38
  143.7 1.0 collective-permute-start.36
  144.7 5.4 %collective-permute-done.29.refs_4_ = bf16[4,880,128]{2,1,0:T(8,128)(2,1)S(1)} collective-permute-done((bf16[4,880,128]{2,1,0:T(8,128)(2,1)S(1)}, bf16[4,880,128]{2,1,0:T(8,128)(2,1)S(1)}, u32[]{:S(2)}, u32[]{:S(2)}) %collective-permute-start.29) | collective-permute-done | bytes 901152 | tf_op jit(solution)/shard_map/ppermute | solution.py:63
  150.1 0.9 spread.5
  151.1 14.6 %collective-permute-done.37.refs_5_ = bf16[4,784,128]{2,1,0:T(8,128)(2,1)S(1)} collective-permute-done((bf16[4,784,128]{2,1,0:T(8,128)(2,1)S(1)}, bf16[4,784,128]{2,1,0:T(8,128)(2,1)S(1)}, u32[]{:S(2)}, u32[]{:S(2)}) %collective-permute-start.37) | collective-permute-done | bytes 802848 | tf_op jit(solution)/shard_map/ppermute | solution.py:63
  165.7 2.3 %collective-permute-start.35 = (bf16[4,784,128]{2,1,0:T(8,128)(2,1)S(1)}, bf16[4,784,128]{2,1,0:T(8,128)(2,1)S(1)}, u32[]{:S(2)}, u32[]{:S(2)}) collective-permute-start(bf16[4,784,128]{2,1,0:T(8,128)(2,1)S(1)} %get-tuple-element.249), channel_id=1, source_target_pairs={{0,5},{1,4},{2,7},{3,6},{4,1},{5,0},{6,3},{7,2},{8,13},{9,12},{10,... | collective-permute-start | bytes 2408456 | tf_op jit(solution)/shard_map/ppermute | solution.py:63
  168.0 4.5 %collective-permute-done.36.refs_4_ = bf16[4,784,128]{2,1,0:T(8,128)(2,1)S(1)} collective-permute-done((bf16[4,784,128]{2,1,0:T(8,128)(2,1)S(1)}, bf16[4,784,128]{2,1,0:T(8,128)(2,1)S(1)}, u32[]{:S(2)}, u32[]{:S(2)}) %collective-permute-start.36) | collective-permute-done | bytes 802848 | tf_op jit(solution)/shard_map/ppermute | solution.py:63
  172.5 2.8 %pack.4 = (f32[16,128]{1,0:T(8,128)S(1)}, bf16[1,16,128,2048]{3,2,1,0:T(8,128)(2,1)}) custom-call(s32[144]{0:T(256)S(1)} %copy-done.1, bf16[4,784,128]{2,1,0:T(8,128)(2,1)S(1)} %get-tuple-element.252.refs_0_, bf16[4,784,128]{2,1,0:T(8,128)(2,1)S(1)} %collective-permute-done.30.refs_1_, ...), custom_call_target="tpu_custom_call", output_to_operand_aliasing={{1}: (9, {})} | custom-call | tf_op jit(solution)/shard_map/pack/pallas_call | solution.py:343
  175.3 4.2 %collective-permute-done.35.refs_3_ = bf16[4,784,128]{2,1,0:T(8,128)(2,1)S(1)} collective-permute-done((bf16[4,784,128]{2,1,0:T(8,128)(2,1)S(1)}, bf16[4,784,128]{2,1,0:T(8,128)(2,1)S(1)}, u32[]{:S(2)}, u32[]{:S(2)}) %collective-permute-start.35) | collective-permute-done | bytes 802848 | tf_op jit(solution)/shard_map/ppermute | solution.py:63
  179.7 3.0 %collective-permute-start.40 = (bf16[4,784,128]{2,1,0:T(8,128)(2,1)S(1)}, bf16[4,784,128]{2,1,0:T(8,128)(2,1)S(1)}, u32[]{:S(2)}, u32[]{:S(2)}) collective-permute-start(bf16[4,784,128]{2,1,0:T(8,128)(2,1)S(1)} %get-tuple-element.266), channel_id=1, source_target_pairs={{0,12},{1,13},{2,14},{3,15},{4,8},{5,9},{6,10},{7,11},{8,4},{9,5},... | collective-permute-start | bytes 2408456 | tf_op jit(solution)/shard_map/ppermute | solution.py:63
  182.7 1.6 collective-permute-start.41
  184.3 1.3 collective-permute-start.39
  185.7 16.1 %collective-permute-done.40.refs_5_ = bf16[4,784,128]{2,1,0:T(8,128)(2,1)S(1)} collective-permute-done((bf16[4,784,128]{2,1,0:T(8,128)(2,1)S(1)}, bf16[4,784,128]{2,1,0:T(8,128)(2,1)S(1)}, u32[]{:S(2)}, u32[]{:S(2)}) %collective-permute-start.40) | collective-permute-done | bytes 802848 | tf_op jit(solution)/shard_map/ppermute | solution.py:63
  201.8 2.7 %collective-permute-done.39.refs_4_ = bf16[4,784,128]{2,1,0:T(8,128)(2,1)S(1)} collective-permute-done((bf16[4,784,128]{2,1,0:T(8,128)(2,1)S(1)}, bf16[4,784,128]{2,1,0:T(8,128)(2,1)S(1)}, u32[]{:S(2)}, u32[]{:S(2)}) %collective-permute-start.39) | collective-permute-done | bytes 802848 | tf_op jit(solution)/shard_map/ppermute | solution.py:63
  204.5 3.4 %pack.5 = (f32[16,128]{1,0:T(8,128)}, bf16[1,16,128,2048]{3,2,1,0:T(8,128)(2,1)}) custom-call(s32[144]{0:T(256)S(1)} %copy-done.1, bf16[4,784,128]{2,1,0:T(8,128)(2,1)S(1)} %get-tuple-element.268.refs_0_, bf16[4,784,128]{2,1,0:T(8,128)(2,1)S(1)} %collective-permute-done.33.refs_1_, ...), custom_call_target="tpu_custom_call", output_to_operand_aliasing={{1}: (9, {})} | custom-call | tf_op jit(solution)/shard_map/pack/pallas_call | solution.py:343
  (43 shorter events, 1.3 us)
Async XLA Ops:
  0.6 2.3 %copy-start = (bf16[2048,1152]{1,0:T(8,128)(2,1)S(1)}, bf16[2048,1152]{1,0:T(8,128)(2,1)}, u32[]{:S(2)}) copy-start(bf16[2048,1152]{1,0:T(8,128)(2,1)} %weight_ref.1) | copy-start | bytes 14155780
  3.0 63.5 %copy-start.1 = (s32[144]{0:T(256)S(1)}, s32[144]{0:T(256)}, u32[]{:S(2)}) copy-start(s32[144]{0:T(256)} %placement_ref.11) | copy-start | bytes 1732
  8.6 3.3 %collective-permute-start = (bf16[2,576,128]{2,1,0:T(8,128)(2,1)S(1)}, bf16[2,576,128]{2,1,0:T(8,128)(2,1)S(1)}, u32[]{:S(2)}, u32[]{:S(2)}) collective-permute-start(bf16[2,576,128]{2,1,0:T(8,128)(2,1)S(1)} %get-tuple-element.145), channel_id=1, source_target_pairs={{0,16},{1,17},{2,18},{3,19},{4,20},{5,21},{6,22},{7,23},{8,24},{9,... | collective-permute-start | bytes 884744 | tf_op jit(solution)/shard_map/ppermute | solution.py:63
  8.7 8.9 %collective-permute-start.1 = (bf16[2,576,128]{2,1,0:T(8,128)(2,1)S(1)}, bf16[2,576,128]{2,1,0:T(8,128)(2,1)S(1)}, u32[]{:S(2)}, u32[]{:S(2)}) collective-permute-start(bf16[2,576,128]{2,1,0:T(8,128)(2,1)S(1)} %get-tuple-element.146), channel_id=1, source_target_pairs={{0,32},{1,33},{2,34},{3,35},{4,36},{5,37},{6,38},{7,39},{8,40},{9,... | collective-permute-start | bytes 884744 | tf_op jit(solution)/shard_map/ppermute | solution.py:63
  10.4 8.3 %collective-permute-start.2 = (bf16[2,576,128]{2,1,0:T(8,128)(2,1)S(1)}, bf16[2,576,128]{2,1,0:T(8,128)(2,1)S(1)}, u32[]{:S(2)}, u32[]{:S(2)}) collective-permute-start(bf16[2,576,128]{2,1,0:T(8,128)(2,1)S(1)} %get-tuple-element.147), channel_id=1, source_target_pairs={{0,112},{1,113},{2,114},{3,115},{4,116},{5,117},{6,118},{7,119},{8... | collective-permute-start | bytes 884744 | tf_op jit(solution)/shard_map/ppermute | solution.py:63
  18.8 19.9 %collective-permute-start.3 = (bf16[4,576,128]{2,1,0:T(8,128)(2,1)S(1)}, bf16[4,576,128]{2,1,0:T(8,128)(2,1)S(1)}, u32[]{:S(2)}, u32[]{:S(2)}) collective-permute-start(bf16[4,576,128]{2,1,0:T(8,128)(2,1)S(1)} %y_regroup.6), channel_id=1, source_target_pairs={{0,96},{1,97},{2,98},{3,99},{4,100},{5,101},{6,102},{7,103},{8,104... | collective-permute-start | bytes 1769480 | tf_op jit(solution)/shard_map/ppermute | solution.py:63
  21.9 3.1 %collective-permute-start.4 = (bf16[2,864,128]{2,1,0:T(8,128)(2,1)S(1)}, bf16[2,864,128]{2,1,0:T(8,128)(2,1)S(1)}, u32[]{:S(2)}, u32[]{:S(2)}) collective-permute-start(bf16[2,864,128]{2,1,0:T(8,128)(2,1)S(1)} %get-tuple-element.149), channel_id=1, source_target_pairs={{0,16},{1,17},{2,18},{3,19},{4,20},{5,21},{6,22},{7,23},{8,24},{9,... | collective-permute-start | bytes 1327112 | tf_op jit(solution)/shard_map/ppermute | solution.py:63
  21.9 13.1 %collective-permute-start.5 = (bf16[2,864,128]{2,1,0:T(8,128)(2,1)S(1)}, bf16[2,864,128]{2,1,0:T(8,128)(2,1)S(1)}, u32[]{:S(2)}, u32[]{:S(2)}) collective-permute-start(bf16[2,864,128]{2,1,0:T(8,128)(2,1)S(1)} %get-tuple-element.150), channel_id=1, source_target_pairs={{0,32},{1,33},{2,34},{3,35},{4,36},{5,37},{6,38},{7,39},{8,40},{9,... | collective-permute-start | bytes 1327112 | tf_op jit(solution)/shard_map/ppermute | solution.py:63
  22.0 16.6 %collective-permute-start.6 = (bf16[2,864,128]{2,1,0:T(8,128)(2,1)S(1)}, bf16[2,864,128]{2,1,0:T(8,128)(2,1)S(1)}, u32[]{:S(2)}, u32[]{:S(2)}) collective-permute-start(bf16[2,864,128]{2,1,0:T(8,128)(2,1)S(1)} %get-tuple-element.151), channel_id=1, source_target_pairs={{0,112},{1,113},{2,114},{3,115},{4,116},{5,117},{6,118},{7,119},{8... | collective-permute-start | bytes 1327112 | tf_op jit(solution)/shard_map/ppermute | solution.py:63
  39.5 6.2 %collective-permute-start.10 = (bf16[2,592,128]{2,1,0:T(8,128)(2,1)S(1)}, bf16[2,592,128]{2,1,0:T(8,128)(2,1)S(1)}, u32[]{:S(2)}, u32[]{:S(2)}) collective-permute-start(bf16[2,592,128]{2,1,0:T(8,128)(2,1)S(1)} %get-tuple-element.166), channel_id=1, source_target_pairs={{0,16},{1,17},{2,18},{3,19},{4,20},{5,21},{6,22},{7,23},{8,24},{9,... | collective-permute-start | bytes 909320 | tf_op jit(solution)/shard_map/ppermute | solution.py:63
  40.1 10.1 %collective-permute-start.11 = (bf16[2,592,128]{2,1,0:T(8,128)(2,1)S(1)}, bf16[2,592,128]{2,1,0:T(8,128)(2,1)S(1)}, u32[]{:S(2)}, u32[]{:S(2)}) collective-permute-start(bf16[2,592,128]{2,1,0:T(8,128)(2,1)S(1)} %get-tuple-element.167), channel_id=1, source_target_pairs={{0,32},{1,33},{2,34},{3,35},{4,36},{5,37},{6,38},{7,39},{8,40},{9,... | collective-permute-start | bytes 909320 | tf_op jit(solution)/shard_map/ppermute | solution.py:63
  40.5 9.7 %collective-permute-start.12 = (bf16[2,592,128]{2,1,0:T(8,128)(2,1)S(1)}, bf16[2,592,128]{2,1,0:T(8,128)(2,1)S(1)}, u32[]{:S(2)}, u32[]{:S(2)}) collective-permute-start(bf16[2,592,128]{2,1,0:T(8,128)(2,1)S(1)} %get-tuple-element.168), channel_id=1, source_target_pairs={{0,112},{1,113},{2,114},{3,115},{4,116},{5,117},{6,118},{7,119},{8... | collective-permute-start | bytes 909320 | tf_op jit(solution)/shard_map/ppermute | solution.py:63
  42.8 17.2 %collective-permute-start.14 = (bf16[4,864,128]{2,1,0:T(8,128)(2,1)S(1)}, bf16[4,864,128]{2,1,0:T(8,128)(2,1)S(1)}, u32[]{:S(2)}, u32[]{:S(2)}) collective-permute-start(bf16[4,864,128]{2,1,0:T(8,128)(2,1)S(1)} %y_regroup.7), channel_id=1, source_target_pairs={{0,96},{1,97},{2,98},{3,99},{4,100},{5,101},{6,102},{7,103},{8,104... | collective-permute-start | bytes 2654216 | tf_op jit(solution)/shard_map/ppermute | solution.py:63
  50.2 16.3 %collective-permute-start.13 = (bf16[4,592,128]{2,1,0:T(8,128)(2,1)S(1)}, bf16[4,592,128]{2,1,0:T(8,128)(2,1)S(1)}, u32[]{:S(2)}, u32[]{:S(2)}) collective-permute-start(bf16[4,592,128]{2,1,0:T(8,128)(2,1)S(1)} %y_regroup.8), channel_id=1, source_target_pairs={{0,96},{1,97},{2,98},{3,99},{4,100},{5,101},{6,102},{7,103},{8,104... | collective-permute-start | bytes 1818632 | tf_op jit(solution)/shard_map/ppermute | solution.py:63
  61.1 12.8 %collective-permute-start.18 = (bf16[2,880,128]{2,1,0:T(8,128)(2,1)S(1)}, bf16[2,880,128]{2,1,0:T(8,128)(2,1)S(1)}, u32[]{:S(2)}, u32[]{:S(2)}) collective-permute-start(bf16[2,880,128]{2,1,0:T(8,128)(2,1)S(1)} %get-tuple-element.188), channel_id=1, source_target_pairs={{0,16},{1,17},{2,18},{3,19},{4,20},{5,21},{6,22},{7,23},{8,24},{9,... | collective-permute-start | bytes 1351688 | tf_op jit(solution)/shard_map/ppermute | solution.py:63
  67.3 14.8 %collective-permute-start.15 = (bf16[4,528,128]{2,1,0:T(8,128)(2,1)S(1)}, bf16[4,528,128]{2,1,0:T(8,128)(2,1)S(1)}, u32[]{:S(2)}, u32[]{:S(2)}) collective-permute-start(bf16[4,528,128]{2,1,0:T(8,128)(2,1)S(1)} %get-tuple-element.185), channel_id=1, source_target_pairs={{0,1},{1,0},{2,3},{3,2},{4,5},{5,4},{6,7},{7,6},{8,9},{9,8},{10,11... | collective-permute-start | bytes 1622024 | tf_op jit(solution)/shard_map/ppermute | solution.py:63
  68.9 12.9 %collective-permute-start.19 = (bf16[2,880,128]{2,1,0:T(8,128)(2,1)S(1)}, bf16[2,880,128]{2,1,0:T(8,128)(2,1)S(1)}, u32[]{:S(2)}, u32[]{:S(2)}) collective-permute-start(bf16[2,880,128]{2,1,0:T(8,128)(2,1)S(1)} %get-tuple-element.189), channel_id=1, source_target_pairs={{0,32},{1,33},{2,34},{3,35},{4,36},{5,37},{6,38},{7,39},{8,40},{9,... | collective-permute-start | bytes 1351688 | tf_op jit(solution)/shard_map/ppermute | solution.py:63
  68.9 12.9 %collective-permute-start.20 = (bf16[2,880,128]{2,1,0:T(8,128)(2,1)S(1)}, bf16[2,880,128]{2,1,0:T(8,128)(2,1)S(1)}, u32[]{:S(2)}, u32[]{:S(2)}) collective-permute-start(bf16[2,880,128]{2,1,0:T(8,128)(2,1)S(1)} %get-tuple-element.190), channel_id=1, source_target_pairs={{0,112},{1,113},{2,114},{3,115},{4,116},{5,117},{6,118},{7,119},{8... | collective-permute-start | bytes 1351688 | tf_op jit(solution)/shard_map/ppermute | solution.py:63
  72.0 15.2 %collective-permute-start.16 = (bf16[4,528,128]{2,1,0:T(8,128)(2,1)S(1)}, bf16[4,528,128]{2,1,0:T(8,128)(2,1)S(1)}, u32[]{:S(2)}, u32[]{:S(2)}) collective-permute-start(bf16[4,528,128]{2,1,0:T(8,128)(2,1)S(1)} %get-tuple-element.186), channel_id=1, source_target_pairs={{0,4},{1,5},{2,6},{3,7},{4,0},{5,1},{6,2},{7,3},{8,12},{9,13},{10,... | collective-permute-start | bytes 1622024 | tf_op jit(solution)/shard_map/ppermute | solution.py:63
  74.0 15.7 %collective-permute-start.17 = (bf16[4,528,128]{2,1,0:T(8,128)(2,1)S(1)}, bf16[4,528,128]{2,1,0:T(8,128)(2,1)S(1)}, u32[]{:S(2)}, u32[]{:S(2)}) collective-permute-start(bf16[4,528,128]{2,1,0:T(8,128)(2,1)S(1)} %get-tuple-element.187), channel_id=1, source_target_pairs={{0,5},{1,4},{2,7},{3,6},{4,1},{5,0},{6,3},{7,2},{8,13},{9,12},{10,... | collective-permute-start | bytes 1622024 | tf_op jit(solution)/shard_map/ppermute | solution.py:63
  81.9 8.0 %collective-permute-start.7 = (bf16[2,864,128]{2,1,0:T(8,128)(2,1)S(1)}, bf16[2,864,128]{2,1,0:T(8,128)(2,1)S(1)}, u32[]{:S(2)}, u32[]{:S(2)}) collective-permute-start(bf16[2,864,128]{2,1,0:T(8,128)(2,1)S(1)} %get-tuple-element.163), channel_id=1, source_target_pairs={{0,16},{1,17},{2,18},{3,19},{4,20},{5,21},{6,22},{7,23},{8,24},{9,... | collective-permute-start | bytes 1327112 | tf_op jit(solution)/shard_map/ppermute | solution.py:63
  81.9 13.0 %collective-permute-start.8 = (bf16[2,864,128]{2,1,0:T(8,128)(2,1)S(1)}, bf16[2,864,128]{2,1,0:T(8,128)(2,1)S(1)}, u32[]{:S(2)}, u32[]{:S(2)}) collective-permute-start(bf16[2,864,128]{2,1,0:T(8,128)(2,1)S(1)} %get-tuple-element.164), channel_id=1, source_target_pairs={{0,32},{1,33},{2,34},{3,35},{4,36},{5,37},{6,38},{7,39},{8,40},{9,... | collective-permute-start | bytes 1327112 | tf_op jit(solution)/shard_map/ppermute | solution.py:63
  82.1 12.9 %collective-permute-start.9 = (bf16[2,864,128]{2,1,0:T(8,128)(2,1)S(1)}, bf16[2,864,128]{2,1,0:T(8,128)(2,1)S(1)}, u32[]{:S(2)}, u32[]{:S(2)}) collective-permute-start(bf16[2,864,128]{2,1,0:T(8,128)(2,1)S(1)} %get-tuple-element.165), channel_id=1, source_target_pairs={{0,112},{1,113},{2,114},{3,115},{4,116},{5,117},{6,118},{7,119},{8... | collective-permute-start | bytes 1327112 | tf_op jit(solution)/shard_map/ppermute | solution.py:63
  87.2 18.6 %collective-permute-start.22 = (bf16[4,880,128]{2,1,0:T(8,128)(2,1)S(1)}, bf16[4,880,128]{2,1,0:T(8,128)(2,1)S(1)}, u32[]{:S(2)}, u32[]{:S(2)}) collective-permute-start(bf16[4,880,128]{2,1,0:T(8,128)(2,1)S(1)} %y_regroup.9), channel_id=1, source_target_pairs={{0,96},{1,97},{2,98},{3,99},{4,100},{5,101},{6,102},{7,103},{8,104... | collective-permute-start | bytes 2703368 | tf_op jit(solution)/shard_map/ppermute | solution.py:63
  95.1 20.3 %collective-permute-start.21 = (bf16[4,864,128]{2,1,0:T(8,128)(2,1)S(1)}, bf16[4,864,128]{2,1,0:T(8,128)(2,1)S(1)}, u32[]{:S(2)}, u32[]{:S(2)}) collective-permute-start(bf16[4,864,128]{2,1,0:T(8,128)(2,1)S(1)} %y_regroup.10), channel_id=1, source_target_pairs={{0,96},{1,97},{2,98},{3,99},{4,100},{5,101},{6,102},{7,103},{8,104... | collective-permute-start | bytes 2654216 | tf_op jit(solution)/shard_map/ppermute | solution.py:63
  97.6 19.2 %collective-permute-start.27 = (bf16[4,528,128]{2,1,0:T(8,128)(2,1)S(1)}, bf16[4,528,128]{2,1,0:T(8,128)(2,1)S(1)}, u32[]{:S(2)}, u32[]{:S(2)}) collective-permute-start(bf16[4,528,128]{2,1,0:T(8,128)(2,1)S(1)} %get-tuple-element.219), channel_id=1, source_target_pairs={{0,12},{1,13},{2,14},{3,15},{4,8},{5,9},{6,10},{7,11},{8,4},{9,5},... | collective-permute-start | bytes 1622024 | tf_op jit(solution)/shard_map/ppermute | solution.py:63
  101.7 17.1 %collective-permute-start.28 = (bf16[4,528,128]{2,1,0:T(8,128)(2,1)S(1)}, bf16[4,528,128]{2,1,0:T(8,128)(2,1)S(1)}, u32[]{:S(2)}, u32[]{:S(2)}) collective-permute-start(bf16[4,528,128]{2,1,0:T(8,128)(2,1)S(1)} %get-tuple-element.220), channel_id=1, source_target_pairs={{0,15},{1,14},{2,13},{3,12},{4,11},{5,10},{6,9},{7,8},{8,7},{9,6},... | collective-permute-start | bytes 1622024 | tf_op jit(solution)/shard_map/ppermute | solution.py:63
  103.2 16.9 %collective-permute-start.26 = (bf16[4,528,128]{2,1,0:T(8,128)(2,1)S(1)}, bf16[4,528,128]{2,1,0:T(8,128)(2,1)S(1)}, u32[]{:S(2)}, u32[]{:S(2)}) collective-permute-start(bf16[4,528,128]{2,1,0:T(8,128)(2,1)S(1)} %get-tuple-element.199), channel_id=1, source_target_pairs={{0,3},{1,2},{2,1},{3,0},{4,7},{5,6},{6,5},{7,4},{8,11},{9,10},{10,... | collective-permute-start | bytes 1622024 | tf_op jit(solution)/shard_map/ppermute | solution.py:63
  116.5 3.6 %collective-permute-start.23 = (bf16[2,880,128]{2,1,0:T(8,128)(2,1)S(1)}, bf16[2,880,128]{2,1,0:T(8,128)(2,1)S(1)}, u32[]{:S(2)}, u32[]{:S(2)}) collective-permute-start(bf16[2,880,128]{2,1,0:T(8,128)(2,1)S(1)} %get-tuple-element.216), channel_id=1, source_target_pairs={{0,16},{1,17},{2,18},{3,19},{4,20},{5,21},{6,22},{7,23},{8,24},{9,... | collective-permute-start | bytes 1351688 | tf_op jit(solution)/shard_map/ppermute | solution.py:63
  116.5 19.9 %collective-permute-start.30 = (bf16[4,784,128]{2,1,0:T(8,128)(2,1)S(1)}, bf16[4,784,128]{2,1,0:T(8,128)(2,1)S(1)}, u32[]{:S(2)}, u32[]{:S(2)}) collective-permute-start(bf16[4,784,128]{2,1,0:T(8,128)(2,1)S(1)} %get-tuple-element.233), channel_id=1, source_target_pairs={{0,1},{1,0},{2,3},{3,2},{4,5},{5,4},{6,7},{7,6},{8,9},{9,8},{10,11... | collective-permute-start | bytes 2408456 | tf_op jit(solution)/shard_map/ppermute | solution.py:63
  116.8 20.2 %collective-permute-start.31 = (bf16[4,784,128]{2,1,0:T(8,128)(2,1)S(1)}, bf16[4,784,128]{2,1,0:T(8,128)(2,1)S(1)}, u32[]{:S(2)}, u32[]{:S(2)}) collective-permute-start(bf16[4,784,128]{2,1,0:T(8,128)(2,1)S(1)} %get-tuple-element.234), channel_id=1, source_target_pairs={{0,4},{1,5},{2,6},{3,7},{4,0},{5,1},{6,2},{7,3},{8,12},{9,13},{10,... | collective-permute-start | bytes 2408456 | tf_op jit(solution)/shard_map/ppermute | solution.py:63
  118.7 19.8 %collective-permute-start.32 = (bf16[4,784,128]{2,1,0:T(8,128)(2,1)S(1)}, bf16[4,784,128]{2,1,0:T(8,128)(2,1)S(1)}, u32[]{:S(2)}, u32[]{:S(2)}) collective-permute-start(bf16[4,784,128]{2,1,0:T(8,128)(2,1)S(1)} %get-tuple-element.235), channel_id=1, source_target_pairs={{0,5},{1,4},{2,7},{3,6},{4,1},{5,0},{6,3},{7,2},{8,13},{9,12},{10,... | collective-permute-start | bytes 2408456 | tf_op jit(solution)/shard_map/ppermute | solution.py:63
  120.1 12.1 %collective-permute-start.24 = (bf16[2,880,128]{2,1,0:T(8,128)(2,1)S(1)}, bf16[2,880,128]{2,1,0:T(8,128)(2,1)S(1)}, u32[]{:S(2)}, u32[]{:S(2)}) collective-permute-start(bf16[2,880,128]{2,1,0:T(8,128)(2,1)S(1)} %get-tuple-element.217), channel_id=1, source_target_pairs={{0,32},{1,33},{2,34},{3,35},{4,36},{5,37},{6,38},{7,39},{8,40},{9,... | collective-permute-start | bytes 1351688 | tf_op jit(solution)/shard_map/ppermute | solution.py:63
  120.1 15.4 %collective-permute-start.25 = (bf16[2,880,128]{2,1,0:T(8,128)(2,1)S(1)}, bf16[2,880,128]{2,1,0:T(8,128)(2,1)S(1)}, u32[]{:S(2)}, u32[]{:S(2)}) collective-permute-start(bf16[2,880,128]{2,1,0:T(8,128)(2,1)S(1)} %get-tuple-element.218), channel_id=1, source_target_pairs={{0,112},{1,113},{2,114},{3,115},{4,116},{5,117},{6,118},{7,119},{8... | collective-permute-start | bytes 1351688 | tf_op jit(solution)/shard_map/ppermute | solution.py:63
  135.6 14.5 %collective-permute-start.29 = (bf16[4,880,128]{2,1,0:T(8,128)(2,1)S(1)}, bf16[4,880,128]{2,1,0:T(8,128)(2,1)S(1)}, u32[]{:S(2)}, u32[]{:S(2)}) collective-permute-start(bf16[4,880,128]{2,1,0:T(8,128)(2,1)S(1)} %y_regroup.11), channel_id=1, source_target_pairs={{0,96},{1,97},{2,98},{3,99},{4,100},{5,101},{6,102},{7,103},{8,104... | collective-permute-start | bytes 2703368 | tf_op jit(solution)/shard_map/ppermute | solution.py:63
  138.7 27.0 %collective-permute-start.37 = (bf16[4,784,128]{2,1,0:T(8,128)(2,1)S(1)}, bf16[4,784,128]{2,1,0:T(8,128)(2,1)S(1)}, u32[]{:S(2)}, u32[]{:S(2)}) collective-permute-start(bf16[4,784,128]{2,1,0:T(8,128)(2,1)S(1)} %get-tuple-element.250), channel_id=1, source_target_pairs={{0,12},{1,13},{2,14},{3,15},{4,8},{5,9},{6,10},{7,11},{8,4},{9,5},... | collective-permute-start | bytes 2408456 | tf_op jit(solution)/shard_map/ppermute | solution.py:63
  141.8 26.2 %collective-permute-start.38 = (bf16[4,784,128]{2,1,0:T(8,128)(2,1)S(1)}, bf16[4,784,128]{2,1,0:T(8,128)(2,1)S(1)}, u32[]{:S(2)}, u32[]{:S(2)}) collective-permute-start(bf16[4,784,128]{2,1,0:T(8,128)(2,1)S(1)} %get-tuple-element.251), channel_id=1, source_target_pairs={{0,15},{1,14},{2,13},{3,12},{4,11},{5,10},{6,9},{7,8},{8,7},{9,6},... | collective-permute-start | bytes 2408456 | tf_op jit(solution)/shard_map/ppermute | solution.py:63
  143.7 28.9 %collective-permute-start.36 = (bf16[4,784,128]{2,1,0:T(8,128)(2,1)S(1)}, bf16[4,784,128]{2,1,0:T(8,128)(2,1)S(1)}, u32[]{:S(2)}, u32[]{:S(2)}) collective-permute-start(bf16[4,784,128]{2,1,0:T(8,128)(2,1)S(1)} %get-tuple-element.240), channel_id=1, source_target_pairs={{0,3},{1,2},{2,1},{3,0},{4,7},{5,6},{6,5},{7,4},{8,11},{9,10},{10,... | collective-permute-start | bytes 2408456 | tf_op jit(solution)/shard_map/ppermute | solution.py:63
  150.9 24.4 %collective-permute-start.33 = (bf16[4,784,128]{2,1,0:T(8,128)(2,1)S(1)}, bf16[4,784,128]{2,1,0:T(8,128)(2,1)S(1)}, u32[]{:S(2)}, u32[]{:S(2)}) collective-permute-start(bf16[4,784,128]{2,1,0:T(8,128)(2,1)S(1)} %get-tuple-element.247), channel_id=1, source_target_pairs={{0,1},{1,0},{2,3},{3,2},{4,5},{5,4},{6,7},{7,6},{8,9},{9,8},{10,11... | collective-permute-start | bytes 2408456 | tf_op jit(solution)/shard_map/ppermute | solution.py:63
  151.0 24.3 %collective-permute-start.34 = (bf16[4,784,128]{2,1,0:T(8,128)(2,1)S(1)}, bf16[4,784,128]{2,1,0:T(8,128)(2,1)S(1)}, u32[]{:S(2)}, u32[]{:S(2)}) collective-permute-start(bf16[4,784,128]{2,1,0:T(8,128)(2,1)S(1)} %get-tuple-element.248), channel_id=1, source_target_pairs={{0,4},{1,5},{2,6},{3,7},{4,0},{5,1},{6,2},{7,3},{8,12},{9,13},{10,... | collective-permute-start | bytes 2408456 | tf_op jit(solution)/shard_map/ppermute | solution.py:63
  165.7 13.8 %collective-permute-start.35 = (bf16[4,784,128]{2,1,0:T(8,128)(2,1)S(1)}, bf16[4,784,128]{2,1,0:T(8,128)(2,1)S(1)}, u32[]{:S(2)}, u32[]{:S(2)}) collective-permute-start(bf16[4,784,128]{2,1,0:T(8,128)(2,1)S(1)} %get-tuple-element.249), channel_id=1, source_target_pairs={{0,5},{1,4},{2,7},{3,6},{4,1},{5,0},{6,3},{7,2},{8,13},{9,12},{10,... | collective-permute-start | bytes 2408456 | tf_op jit(solution)/shard_map/ppermute | solution.py:63
  179.7 22.1 %collective-permute-start.40 = (bf16[4,784,128]{2,1,0:T(8,128)(2,1)S(1)}, bf16[4,784,128]{2,1,0:T(8,128)(2,1)S(1)}, u32[]{:S(2)}, u32[]{:S(2)}) collective-permute-start(bf16[4,784,128]{2,1,0:T(8,128)(2,1)S(1)} %get-tuple-element.266), channel_id=1, source_target_pairs={{0,12},{1,13},{2,14},{3,15},{4,8},{5,9},{6,10},{7,11},{8,4},{9,5},... | collective-permute-start | bytes 2408456 | tf_op jit(solution)/shard_map/ppermute | solution.py:63
  182.7 19.0 %collective-permute-start.41 = (bf16[4,784,128]{2,1,0:T(8,128)(2,1)S(1)}, bf16[4,784,128]{2,1,0:T(8,128)(2,1)S(1)}, u32[]{:S(2)}, u32[]{:S(2)}) collective-permute-start(bf16[4,784,128]{2,1,0:T(8,128)(2,1)S(1)} %get-tuple-element.267), channel_id=1, source_target_pairs={{0,15},{1,14},{2,13},{3,12},{4,11},{5,10},{6,9},{7,8},{8,7},{9,6},... | collective-permute-start | bytes 2408456 | tf_op jit(solution)/shard_map/ppermute | solution.py:63
  184.3 20.1 %collective-permute-start.39 = (bf16[4,784,128]{2,1,0:T(8,128)(2,1)S(1)}, bf16[4,784,128]{2,1,0:T(8,128)(2,1)S(1)}, u32[]{:S(2)}, u32[]{:S(2)}) collective-permute-start(bf16[4,784,128]{2,1,0:T(8,128)(2,1)S(1)} %get-tuple-element.265), channel_id=1, source_target_pairs={{0,3},{1,2},{2,1},{3,0},{4,7},{5,6},{6,5},{7,4},{8,11},{9,10},{10,... | collective-permute-start | bytes 2408456 | tf_op jit(solution)/shard_map/ppermute | solution.py:63

commit v13 on v11

--- a/solution.py
+++ b/solution.py
@@ -9,7 +9,7 @@
 
 HEAD_DIM = 128
 HAD = 128
-CHUNKS = ((0, 48), (48, 48), (96, 32))
+CHUNKS = ((0, 32), (32, 64), (96, 32))
 ORDER = (
     ("start", 0),
     ("start", 1),

time: 208 us -> 226 us (1.087)
  waiting for transfers between devices: 123 us -> 144 us
    ppermute x42, waiting for transfers between devices: 123 us -> 144 us  [hop(): return lax.ppermute(array, BOTH, pairs)]
  transfers between devices with their start and end apart: 42 -> 42, of which waited for: 22 -> 19; matrix products, arithmetic and copies ran while one was open for 0% -> 0% of each run, Pallas kernels for 5% -> 5%
where the time goes in v13:
time: 226 us
  waiting for transfers between devices  144 us (64%)
  starting transfers between devices  57.9 us (26%)
  Pallas kernels  20.6 us (9%)
  local copies, waits for them, and re-layouts  2.34 us (1%)
    ppermute x42, waiting for transfers between devices, hop(): return lax.ppermute(array, BOTH, pairs)  144 us
    ppermute x42, starting transfers between devices, hop(): return lax.ppermute(array, BOTH, pairs)  57.9 us
    pallas_call x3, Pallas kernels, per_device(): pl.pallas_call(functools.partial(pack_kernel, owners, heads, chunk, bool(...  8.62 us
    pallas_call x15, Pallas kernels, call(): pl.pallas_call(kernel, in_specs=[smem_spec] * table + [vmem_spec] * (len(...  6.36 us
    pallas_call x1, Pallas kernels, per_device(): pl.pallas_call(functools.partial(local_turn_kernel, rows_a), grid=(heads,...  5.65 us
  transfers between devices with their start and end apart: 42, of which 19 were waited for; matrix products, arithmetic and copies ran while one was open for 0% of the time, Pallas kernels for 5%

profile of v13, /device:TPU:0, one launch (start us, length us, event | category | flops | bytes accessed | tf_op | source)
XLA Modules:
  0.0 225.8 jit_solution(15464124502867316794)
XLA Ops:
  0.6 2.3 %copy-done = bf16[2048,1152]{1,0:T(8,128)(2,1)S(1)} copy-done((bf16[2048,1152]{1,0:T(8,128)(2,1)S(1)}, bf16[2048,1152]{1,0:T(8,128)(2,1)}, u32[]{:S(2)}) %copy-start) | copy-done | bytes 4718616
  3.0 5.6 %local_turn.1 = (bf16[2,576,128]{2,1,0:T(8,128)(2,1)S(1)}, bf16[2,576,128]{2,1,0:T(8,128)(2,1)S(1)}, bf16[2,576,128]{2,1,0:T(8,128)(2,1)S(1)}, bf16[2,576,128]{2...) custom-call(bf16[2048,1152]{1,0:T(8,128)(2,1)S(1)} %copy-done), custom_call_target="tpu_custom_call" | custom-call | tf_op jit(solution)/shard_map/local_turn/pallas_call | solution.py:299
  8.7 0.5 collective-permute-start.4
  9.2 1.7 collective-permute-start.5
  10.9 1.2 collective-permute-start.6
  12.0 0.3 collective-permute-start.1
  12.3 2.4 %collective-permute-start.2 = (bf16[2,576,128]{2,1,0:T(8,128)(2,1)S(1)}, bf16[2,576,128]{2,1,0:T(8,128)(2,1)S(1)}, u32[]{:S(2)}, u32[]{:S(2)}) collective-permute-start(bf16[2,576,128]{2,1,0:T(8,128)(2,1)S(1)} %get-tuple-element.147), channel_id=1, source_target_pairs={{0,112},{1,113},{2,114},{3,115},{4,116},{5,117},{6,118},{7,119},{8... | collective-permute-start | bytes 884744 | tf_op jit(solution)/shard_map/ppermute | solution.py:63
  14.7 15.9 %collective-permute-done.1.refs_2_ = bf16[2,576,128]{2,1,0:T(8,128)(2,1)S(1)} collective-permute-done((bf16[2,576,128]{2,1,0:T(8,128)(2,1)S(1)}, bf16[2,576,128]{2,1,0:T(8,128)(2,1)S(1)}, u32[]{:S(2)}, u32[]{:S(2)}) %collective-permute-start.1) | collective-permute-done | bytes 294944 | tf_op jit(solution)/shard_map/ppermute | solution.py:63
  30.6 1.1 collective-permute-done.2.refs_3_
  31.8 3.2 %collective-permute-start.3 = (bf16[4,576,128]{2,1,0:T(8,128)(2,1)S(1)}, bf16[4,576,128]{2,1,0:T(8,128)(2,1)S(1)}, u32[]{:S(2)}, u32[]{:S(2)}) collective-permute-start(bf16[4,576,128]{2,1,0:T(8,128)(2,1)S(1)} %y_regroup.6), channel_id=1, source_target_pairs={{0,96},{1,97},{2,98},{3,99},{4,100},{5,101},{6,102},{7,103},{8,104... | collective-permute-start | bytes 1769480 | tf_op jit(solution)/shard_map/ppermute | solution.py:63
  35.1 0.2 collective-permute-start.14
  35.3 7.7 %collective-permute-done.3.refs_4_ = bf16[4,576,128]{2,1,0:T(8,128)(2,1)S(1)} collective-permute-done((bf16[4,576,128]{2,1,0:T(8,128)(2,1)S(1)}, bf16[4,576,128]{2,1,0:T(8,128)(2,1)S(1)}, u32[]{:S(2)}, u32[]{:S(2)}) %collective-permute-start.3) | collective-permute-done | bytes 589856 | tf_op jit(solution)/shard_map/ppermute | solution.py:63
  43.0 0.8 cross.3
  43.8 0.5 collective-permute-start.11
  44.3 2.7 %collective-permute-start.12 = (bf16[2,592,128]{2,1,0:T(8,128)(2,1)S(1)}, bf16[2,592,128]{2,1,0:T(8,128)(2,1)S(1)}, u32[]{:S(2)}, u32[]{:S(2)}) collective-permute-start(bf16[2,592,128]{2,1,0:T(8,128)(2,1)S(1)} %get-tuple-element.168), channel_id=1, source_target_pairs={{0,112},{1,113},{2,114},{3,115},{4,116},{5,117},{6,118},{7,119},{8... | collective-permute-start | bytes 909320 | tf_op jit(solution)/shard_map/ppermute | solution.py:63
  47.0 7.0 %collective-permute-done.11.refs_2_ = bf16[2,592,128]{2,1,0:T(8,128)(2,1)S(1)} collective-permute-done((bf16[2,592,128]{2,1,0:T(8,128)(2,1)S(1)}, bf16[2,592,128]{2,1,0:T(8,128)(2,1)S(1)}, u32[]{:S(2)}, u32[]{:S(2)}) %collective-permute-start.11) | collective-permute-done | bytes 303136 | tf_op jit(solution)/shard_map/ppermute | solution.py:63
  54.0 7.5 %collective-permute-done.12.refs_3_ = bf16[2,592,128]{2,1,0:T(8,128)(2,1)S(1)} collective-permute-done((bf16[2,592,128]{2,1,0:T(8,128)(2,1)S(1)}, bf16[2,592,128]{2,1,0:T(8,128)(2,1)S(1)}, u32[]{:S(2)}, u32[]{:S(2)}) %collective-permute-start.12) | collective-permute-done | bytes 303136 | tf_op jit(solution)/shard_map/ppermute | solution.py:63
  61.6 1.7 collective-permute-start.13
  63.3 1.4 cross.4
  64.8 0.5 collective-permute-start.20
  65.2 2.6 %collective-permute-start.21 = (bf16[2,1168,128]{2,1,0:T(8,128)(2,1)S(1)}, bf16[2,1168,128]{2,1,0:T(8,128)(2,1)S(1)}, u32[]{:S(2)}, u32[]{:S(2)}) collective-permute-start(bf16[2,1168,128]{2,1,0:T(8,128)(2,1)S(1)} %get-tuple-element.194), channel_id=1, source_target_pairs={{0,112},{1,113},{2,114},{3,115},{4,116},{5,117},{6,118},{7,119},{8... | collective-permute-start | bytes 1794056 | tf_op jit(solution)/shard_map/ppermute | solution.py:63
  67.8 1.6 collective-permute-done.7.refs_1_
  69.4 7.3 %collective-permute-done.13.refs_4_ = bf16[4,592,128]{2,1,0:T(8,128)(2,1)S(1)} collective-permute-done((bf16[4,592,128]{2,1,0:T(8,128)(2,1)S(1)}, bf16[4,592,128]{2,1,0:T(8,128)(2,1)S(1)}, u32[]{:S(2)}, u32[]{:S(2)}) %collective-permute-start.13) | collective-permute-done | bytes 606240 | tf_op jit(solution)/shard_map/ppermute | solution.py:63
  76.7 1.3 collective-permute-start.9
  77.9 0.8 spread.3
  78.8 8.8 %collective-permute-done.8.refs_2_ = bf16[2,576,128]{2,1,0:T(8,128)(2,1)S(1)} collective-permute-done((bf16[2,576,128]{2,1,0:T(8,128)(2,1)S(1)}, bf16[2,576,128]{2,1,0:T(8,128)(2,1)S(1)}, u32[]{:S(2)}, u32[]{:S(2)}) %collective-permute-start.8) | collective-permute-done | bytes 294944 | tf_op jit(solution)/shard_map/ppermute | solution.py:63
  87.6 2.7 %collective-permute-done.9.refs_3_ = bf16[2,576,128]{2,1,0:T(8,128)(2,1)S(1)} collective-permute-done((bf16[2,576,128]{2,1,0:T(8,128)(2,1)S(1)}, bf16[2,576,128]{2,1,0:T(8,128)(2,1)S(1)}, u32[]{:S(2)}, u32[]{:S(2)}) %collective-permute-start.9) | collective-permute-done | bytes 294944 | tf_op jit(solution)/shard_map/ppermute | solution.py:63
  90.4 3.2 %collective-permute-start.28 = (bf16[4,1168,128]{2,1,0:T(8,128)(2,1)S(1)}, bf16[4,1168,128]{2,1,0:T(8,128)(2,1)S(1)}, u32[]{:S(2)}, u32[]{:S(2)}) collective-permute-start(bf16[4,1168,128]{2,1,0:T(8,128)(2,1)S(1)} %y_regroup.10), channel_id=1, source_target_pairs={{0,96},{1,97},{2,98},{3,99},{4,100},{5,101},{6,102},{7,103},{8,104... | collective-permute-start | bytes 3588104 | tf_op jit(solution)/shard_map/ppermute | solution.py:63
  93.6 1.5 collective-permute-start.16
  95.1 1.9 collective-permute-start.17
  97.1 0.1 collective-permute-start.15
  97.2 5.7 %collective-permute-done.16.refs_1_ = bf16[4,528,128]{2,1,0:T(8,128)(2,1)S(1)} collective-permute-done((bf16[4,528,128]{2,1,0:T(8,128)(2,1)S(1)}, bf16[4,528,128]{2,1,0:T(8,128)(2,1)S(1)}, u32[]{:S(2)}, u32[]{:S(2)}) %collective-permute-start.16) | collective-permute-done | bytes 540704 | tf_op jit(solution)/shard_map/ppermute | solution.py:63
  103.0 7.3 %collective-permute-done.17.refs_2_ = bf16[4,528,128]{2,1,0:T(8,128)(2,1)S(1)} collective-permute-done((bf16[4,528,128]{2,1,0:T(8,128)(2,1)S(1)}, bf16[4,528,128]{2,1,0:T(8,128)(2,1)S(1)}, u32[]{:S(2)}, u32[]{:S(2)}) %collective-permute-start.17) | collective-permute-done | bytes 540704 | tf_op jit(solution)/shard_map/ppermute | solution.py:63
  110.3 0.1 regroup.3
  110.4 4.1 %collective-permute-start.26 = (bf16[4,528,128]{2,1,0:T(8,128)(2,1)S(1)}, bf16[4,528,128]{2,1,0:T(8,128)(2,1)S(1)}, u32[]{:S(2)}, u32[]{:S(2)}) collective-permute-start(bf16[4,528,128]{2,1,0:T(8,128)(2,1)S(1)} %get-tuple-element.213), channel_id=1, source_target_pairs={{0,12},{1,13},{2,14},{3,15},{4,8},{5,9},{6,10},{7,11},{8,4},{9,5},... | collective-permute-start | bytes 1622024 | tf_op jit(solution)/shard_map/ppermute | solution.py:63
  114.5 0.8 cross.5
  115.3 0.2 collective-permute-start.22
  115.5 0.9 spread.4
  116.5 1.6 collective-permute-start.30
  118.1 1.9 collective-permute-start.31
  120.0 6.3 %collective-permute-start.27 = (bf16[4,528,128]{2,1,0:T(8,128)(2,1)S(1)}, bf16[4,528,128]{2,1,0:T(8,128)(2,1)S(1)}, u32[]{:S(2)}, u32[]{:S(2)}) collective-permute-start(bf16[4,528,128]{2,1,0:T(8,128)(2,1)S(1)} %get-tuple-element.214), channel_id=1, source_target_pairs={{0,15},{1,14},{2,13},{3,12},{4,11},{5,10},{6,9},{7,8},{8,7},{9,6},... | collective-permute-start | bytes 1622024 | tf_op jit(solution)/shard_map/ppermute | solution.py:63
  126.3 0.5 collective-permute-start.25
  126.8 12.7 %collective-permute-done.27.refs_6_ = bf16[4,528,128]{2,1,0:T(8,128)(2,1)S(1)} collective-permute-done((bf16[4,528,128]{2,1,0:T(8,128)(2,1)S(1)}, bf16[4,528,128]{2,1,0:T(8,128)(2,1)S(1)}, u32[]{:S(2)}, u32[]{:S(2)}) %collective-permute-start.27) | collective-permute-done | bytes 540704 | tf_op jit(solution)/shard_map/ppermute | solution.py:63
  139.5 12.1 %collective-permute-done.25.refs_4_ = bf16[4,528,128]{2,1,0:T(8,128)(2,1)S(1)} collective-permute-done((bf16[4,528,128]{2,1,0:T(8,128)(2,1)S(1)}, bf16[4,528,128]{2,1,0:T(8,128)(2,1)S(1)}, u32[]{:S(2)}, u32[]{:S(2)}) %collective-permute-start.25) | collective-permute-done | bytes 540704 | tf_op jit(solution)/shard_map/ppermute | solution.py:63
  151.6 2.4 %pack.3 = (f32[16,128]{1,0:T(8,128)S(1)}, bf16[1,16,128,2048]{3,2,1,0:T(8,128)(2,1)}) custom-call(s32[144]{0:T(256)S(1)} %copy-done.1, bf16[4,528,128]{2,1,0:T(8,128)(2,1)S(1)} %get-tuple-element.221.refs_0_, bf16[4,528,128]{2,1,0:T(8,128)(2,1)S(1)} %collective-permute-done.16.refs_1_, bf16[4,528,128]{2,1,0:T(8,128)(2,1)S(1)} %collective-permute-done.17.refs_2_, ...), custom_call_target="tpu_custom_call" | custom-call | tf_op jit(solution)/shard_map/pack/pallas_call | solution.py:343
  154.0 3.8 %collective-permute-done.24.refs_3_ = bf16[2,592,128]{2,1,0:T(8,128)(2,1)S(1)} collective-permute-done((bf16[2,592,128]{2,1,0:T(8,128)(2,1)S(1)}, bf16[2,592,128]{2,1,0:T(8,128)(2,1)S(1)}, u32[]{:S(2)}, u32[]{:S(2)}) %collective-permute-start.24) | collective-permute-done | bytes 303136 | tf_op jit(solution)/shard_map/ppermute | solution.py:63
  157.9 0.2 regroup.4
  158.1 0.6 collective-permute-start.37
  158.7 3.0 %collective-permute-start.29 = (bf16[4,592,128]{2,1,0:T(8,128)(2,1)S(1)}, bf16[4,592,128]{2,1,0:T(8,128)(2,1)S(1)}, u32[]{:S(2)}, u32[]{:S(2)}) collective-permute-start(bf16[4,592,128]{2,1,0:T(8,128)(2,1)S(1)} %y_regroup.11), channel_id=1, source_target_pairs={{0,96},{1,97},{2,98},{3,99},{4,100},{5,101},{6,102},{7,103},{8,104... | collective-permute-start | bytes 1818632 | tf_op jit(solution)/shard_map/ppermute | solution.py:63
  161.7 4.9 %collective-permute-start.38 = (bf16[4,1040,128]{2,1,0:T(8,128)(2,1)S(1)}, bf16[4,1040,128]{2,1,0:T(8,128)(2,1)S(1)}, u32[]{:S(2)}, u32[]{:S(2)}) collective-permute-start(bf16[4,1040,128]{2,1,0:T(8,128)(2,1)S(1)} %get-tuple-element.251), channel_id=1, source_target_pairs={{0,15},{1,14},{2,13},{3,12},{4,11},{5,10},{6,9},{7,8},{8,7},{9,6},... | collective-permute-start | bytes 3194888 | tf_op jit(solution)/shard_map/ppermute | solution.py:63
  166.7 0.5 collective-permute-start.36
  167.1 2.9 %collective-permute-done.29.refs_4_ = bf16[4,592,128]{2,1,0:T(8,128)(2,1)S(1)} collective-permute-done((bf16[4,592,128]{2,1,0:T(8,128)(2,1)S(1)}, bf16[4,592,128]{2,1,0:T(8,128)(2,1)S(1)}, u32[]{:S(2)}, u32[]{:S(2)}) %collective-permute-start.29) | collective-permute-done | bytes 606240 | tf_op jit(solution)/shard_map/ppermute | solution.py:63
  170.0 0.8 spread.5
  170.8 1.6 collective-permute-start.33
  172.4 1.0 collective-permute-start.34
  173.4 17.3 %collective-permute-done.37.refs_5_ = bf16[4,1040,128]{2,1,0:T(8,128)(2,1)S(1)} collective-permute-done((bf16[4,1040,128]{2,1,0:T(8,128)(2,1)S(1)}, bf16[4,1040,128]{2,1,0:T(8,128)(2,1)S(1)}, u32[]{:S(2)}, u32[]{:S(2)}) %collective-permute-start.37) | collective-permute-done | bytes 1064992 | tf_op jit(solution)/shard_map/ppermute | solution.py:63
  190.7 9.4 %collective-permute-done.36.refs_4_ = bf16[4,1040,128]{2,1,0:T(8,128)(2,1)S(1)} collective-permute-done((bf16[4,1040,128]{2,1,0:T(8,128)(2,1)S(1)}, bf16[4,1040,128]{2,1,0:T(8,128)(2,1)S(1)}, u32[]{:S(2)}, u32[]{:S(2)}) %collective-permute-start.36) | collective-permute-done | bytes 1064992 | tf_op jit(solution)/shard_map/ppermute | solution.py:63
  200.1 3.3 %pack.4 = (f32[16,128]{1,0:T(8,128)S(1)}, bf16[1,16,128,2048]{3,2,1,0:T(8,128)(2,1)}) custom-call(s32[144]{0:T(256)S(1)} %copy-done.1, bf16[4,1040,128]{2,1,0:T(8,128)(2,1)S(1)} %get-tuple-element.252.refs_0_, bf16[4,1040,128]{2,1,0:T(8,128)(2,1)S(1)} %collective-permute-done.30.refs_1_, ...), custom_call_target="tpu_custom_call", output_to_operand_aliasing={{1}: (9, {})} | custom-call | tf_op jit(solution)/shard_map/pack/pallas_call | solution.py:343
  203.4 0.1 regroup.5
  203.6 5.7 %collective-permute-start.41 = (bf16[4,528,128]{2,1,0:T(8,128)(2,1)S(1)}, bf16[4,528,128]{2,1,0:T(8,128)(2,1)S(1)}, u32[]{:S(2)}, u32[]{:S(2)}) collective-permute-start(bf16[4,528,128]{2,1,0:T(8,128)(2,1)S(1)} %get-tuple-element.267), channel_id=1, source_target_pairs={{0,15},{1,14},{2,13},{3,12},{4,11},{5,10},{6,9},{7,8},{8,7},{9,6},... | collective-permute-start | bytes 1622024 | tf_op jit(solution)/shard_map/ppermute | solution.py:63
  209.3 0.2 collective-permute-start.39
  209.5 10.4 %collective-permute-done.40.refs_5_ = bf16[4,528,128]{2,1,0:T(8,128)(2,1)S(1)} collective-permute-done((bf16[4,528,128]{2,1,0:T(8,128)(2,1)S(1)}, bf16[4,528,128]{2,1,0:T(8,128)(2,1)S(1)}, u32[]{:S(2)}, u32[]{:S(2)}) %collective-permute-start.40) | collective-permute-done | bytes 540704 | tf_op jit(solution)/shard_map/ppermute | solution.py:63
  219.9 2.7 %collective-permute-done.39.refs_4_ = bf16[4,528,128]{2,1,0:T(8,128)(2,1)S(1)} collective-permute-done((bf16[4,528,128]{2,1,0:T(8,128)(2,1)S(1)}, bf16[4,528,128]{2,1,0:T(8,128)(2,1)S(1)}, u32[]{:S(2)}, u32[]{:S(2)}) %collective-permute-start.39) | collective-permute-done | bytes 540704 | tf_op jit(solution)/shard_map/ppermute | solution.py:63
  222.6 3.0 %pack.5 = (f32[16,128]{1,0:T(8,128)}, bf16[1,16,128,2048]{3,2,1,0:T(8,128)(2,1)}) custom-call(s32[144]{0:T(256)S(1)} %copy-done.1, bf16[4,528,128]{2,1,0:T(8,128)(2,1)S(1)} %get-tuple-element.268.refs_0_, bf16[4,528,128]{2,1,0:T(8,128)(2,1)S(1)} %collective-permute-done.33.refs_1_, ...), custom_call_target="tpu_custom_call", output_to_operand_aliasing={{1}: (9, {})} | custom-call | tf_op jit(solution)/shard_map/pack/pallas_call | solution.py:343
  (43 shorter events, 0.8 us)
Async XLA Ops:
  0.6 2.3 %copy-start = (bf16[2048,1152]{1,0:T(8,128)(2,1)S(1)}, bf16[2048,1152]{1,0:T(8,128)(2,1)}, u32[]{:S(2)}) copy-start(bf16[2048,1152]{1,0:T(8,128)(2,1)} %weight_ref.1) | copy-start | bytes 14155780
  8.6 3.7 %collective-permute-start = (bf16[2,576,128]{2,1,0:T(8,128)(2,1)S(1)}, bf16[2,576,128]{2,1,0:T(8,128)(2,1)S(1)}, u32[]{:S(2)}, u32[]{:S(2)}) collective-permute-start(bf16[2,576,128]{2,1,0:T(8,128)(2,1)S(1)} %get-tuple-element.145), channel_id=1, source_target_pairs={{0,16},{1,17},{2,18},{3,19},{4,20},{5,21},{6,22},{7,23},{8,24},{9,... | collective-permute-start | bytes 884744 | tf_op jit(solution)/shard_map/ppermute | solution.py:63
  8.7 26.2 %collective-permute-start.4 = (bf16[2,1152,128]{2,1,0:T(8,128)(2,1)S(1)}, bf16[2,1152,128]{2,1,0:T(8,128)(2,1)S(1)}, u32[]{:S(2)}, u32[]{:S(2)}) collective-permute-start(bf16[2,1152,128]{2,1,0:T(8,128)(2,1)S(1)} %get-tuple-element.149), channel_id=1, source_target_pairs={{0,16},{1,17},{2,18},{3,19},{4,20},{5,21},{6,22},{7,23},{8,24},{9,... | collective-permute-start | bytes 1769480 | tf_op jit(solution)/shard_map/ppermute | solution.py:63
  9.2 25.8 %collective-permute-start.5 = (bf16[2,1152,128]{2,1,0:T(8,128)(2,1)S(1)}, bf16[2,1152,128]{2,1,0:T(8,128)(2,1)S(1)}, u32[]{:S(2)}, u32[]{:S(2)}) collective-permute-start(bf16[2,1152,128]{2,1,0:T(8,128)(2,1)S(1)} %get-tuple-element.150), channel_id=1, source_target_pairs={{0,32},{1,33},{2,34},{3,35},{4,36},{5,37},{6,38},{7,39},{8,40},{9,... | collective-permute-start | bytes 1769480 | tf_op jit(solution)/shard_map/ppermute | solution.py:63
  10.9 24.1 %collective-permute-start.6 = (bf16[2,1152,128]{2,1,0:T(8,128)(2,1)S(1)}, bf16[2,1152,128]{2,1,0:T(8,128)(2,1)S(1)}, u32[]{:S(2)}, u32[]{:S(2)}) collective-permute-start(bf16[2,1152,128]{2,1,0:T(8,128)(2,1)S(1)} %get-tuple-element.151), channel_id=1, source_target_pairs={{0,112},{1,113},{2,114},{3,115},{4,116},{5,117},{6,118},{7,119},{8... | collective-permute-start | bytes 1769480 | tf_op jit(solution)/shard_map/ppermute | solution.py:63
  12.0 18.6 %collective-permute-start.1 = (bf16[2,576,128]{2,1,0:T(8,128)(2,1)S(1)}, bf16[2,576,128]{2,1,0:T(8,128)(2,1)S(1)}, u32[]{:S(2)}, u32[]{:S(2)}) collective-permute-start(bf16[2,576,128]{2,1,0:T(8,128)(2,1)S(1)} %get-tuple-element.146), channel_id=1, source_target_pairs={{0,32},{1,33},{2,34},{3,35},{4,36},{5,37},{6,38},{7,39},{8,40},{9,... | collective-permute-start | bytes 884744 | tf_op jit(solution)/shard_map/ppermute | solution.py:63
  12.3 19.4 %collective-permute-start.2 = (bf16[2,576,128]{2,1,0:T(8,128)(2,1)S(1)}, bf16[2,576,128]{2,1,0:T(8,128)(2,1)S(1)}, u32[]{:S(2)}, u32[]{:S(2)}) collective-permute-start(bf16[2,576,128]{2,1,0:T(8,128)(2,1)S(1)} %get-tuple-element.147), channel_id=1, source_target_pairs={{0,112},{1,113},{2,114},{3,115},{4,116},{5,117},{6,118},{7,119},{8... | collective-permute-start | bytes 884744 | tf_op jit(solution)/shard_map/ppermute | solution.py:63
  31.8 11.2 %collective-permute-start.3 = (bf16[4,576,128]{2,1,0:T(8,128)(2,1)S(1)}, bf16[4,576,128]{2,1,0:T(8,128)(2,1)S(1)}, u32[]{:S(2)}, u32[]{:S(2)}) collective-permute-start(bf16[4,576,128]{2,1,0:T(8,128)(2,1)S(1)} %y_regroup.6), channel_id=1, source_target_pairs={{0,96},{1,97},{2,98},{3,99},{4,100},{5,101},{6,102},{7,103},{8,104... | collective-permute-start | bytes 1769480 | tf_op jit(solution)/shard_map/ppermute | solution.py:63
  35.1 28.2 %collective-permute-start.14 = (bf16[4,1152,128]{2,1,0:T(8,128)(2,1)S(1)}, bf16[4,1152,128]{2,1,0:T(8,128)(2,1)S(1)}, u32[]{:S(2)}, u32[]{:S(2)}) collective-permute-start(bf16[4,1152,128]{2,1,0:T(8,128)(2,1)S(1)} %y_regroup.7), channel_id=1, source_target_pairs={{0,96},{1,97},{2,98},{3,99},{4,100},{5,101},{6,102},{7,103},{8,104... | collective-permute-start | bytes 3538952 | tf_op jit(solution)/shard_map/ppermute | solution.py:63
  43.8 3.3 %collective-permute-start.10 = (bf16[2,592,128]{2,1,0:T(8,128)(2,1)S(1)}, bf16[2,592,128]{2,1,0:T(8,128)(2,1)S(1)}, u32[]{:S(2)}, u32[]{:S(2)}) collective-permute-start(bf16[2,592,128]{2,1,0:T(8,128)(2,1)S(1)} %get-tuple-element.166), channel_id=1, source_target_pairs={{0,16},{1,17},{2,18},{3,19},{4,20},{5,21},{6,22},{7,23},{8,24},{9,... | collective-permute-start | bytes 909320 | tf_op jit(solution)/shard_map/ppermute | solution.py:63
  43.8 10.2 %collective-permute-start.11 = (bf16[2,592,128]{2,1,0:T(8,128)(2,1)S(1)}, bf16[2,592,128]{2,1,0:T(8,128)(2,1)S(1)}, u32[]{:S(2)}, u32[]{:S(2)}) collective-permute-start(bf16[2,592,128]{2,1,0:T(8,128)(2,1)S(1)} %get-tuple-element.167), channel_id=1, source_target_pairs={{0,32},{1,33},{2,34},{3,35},{4,36},{5,37},{6,38},{7,39},{8,40},{9,... | collective-permute-start | bytes 909320 | tf_op jit(solution)/shard_map/ppermute | solution.py:63
  44.3 17.2 %collective-permute-start.12 = (bf16[2,592,128]{2,1,0:T(8,128)(2,1)S(1)}, bf16[2,592,128]{2,1,0:T(8,128)(2,1)S(1)}, u32[]{:S(2)}, u32[]{:S(2)}) collective-permute-start(bf16[2,592,128]{2,1,0:T(8,128)(2,1)S(1)} %get-tuple-element.168), channel_id=1, source_target_pairs={{0,112},{1,113},{2,114},{3,115},{4,116},{5,117},{6,118},{7,119},{8... | collective-permute-start | bytes 909320 | tf_op jit(solution)/shard_map/ppermute | solution.py:63
  61.5 16.4 %copy-start.1 = (s32[144]{0:T(256)S(1)}, s32[144]{0:T(256)}, u32[]{:S(2)}) copy-start(s32[144]{0:T(256)} %placement_ref.11) | copy-start | bytes 1732
  61.6 15.1 %collective-permute-start.13 = (bf16[4,592,128]{2,1,0:T(8,128)(2,1)S(1)}, bf16[4,592,128]{2,1,0:T(8,128)(2,1)S(1)}, u32[]{:S(2)}, u32[]{:S(2)}) collective-permute-start(bf16[4,592,128]{2,1,0:T(8,128)(2,1)S(1)} %y_regroup.8), channel_id=1, source_target_pairs={{0,96},{1,97},{2,98},{3,99},{4,100},{5,101},{6,102},{7,103},{8,104... | collective-permute-start | bytes 1818632 | tf_op jit(solution)/shard_map/ppermute | solution.py:63
  64.7 25.6 %collective-permute-start.19 = (bf16[2,1168,128]{2,1,0:T(8,128)(2,1)S(1)}, bf16[2,1168,128]{2,1,0:T(8,128)(2,1)S(1)}, u32[]{:S(2)}, u32[]{:S(2)}) collective-permute-start(bf16[2,1168,128]{2,1,0:T(8,128)(2,1)S(1)} %get-tuple-element.192), channel_id=1, source_target_pairs={{0,16},{1,17},{2,18},{3,19},{4,20},{5,21},{6,22},{7,23},{8,24},{9,... | collective-permute-start | bytes 1794056 | tf_op jit(solution)/shard_map/ppermute | solution.py:63
  64.8 25.6 %collective-permute-start.20 = (bf16[2,1168,128]{2,1,0:T(8,128)(2,1)S(1)}, bf16[2,1168,128]{2,1,0:T(8,128)(2,1)S(1)}, u32[]{:S(2)}, u32[]{:S(2)}) collective-permute-start(bf16[2,1168,128]{2,1,0:T(8,128)(2,1)S(1)} %get-tuple-element.193), channel_id=1, source_target_pairs={{0,32},{1,33},{2,34},{3,35},{4,36},{5,37},{6,38},{7,39},{8,40},{9,... | collective-permute-start | bytes 1794056 | tf_op jit(solution)/shard_map/ppermute | solution.py:63
  65.2 25.1 %collective-permute-start.21 = (bf16[2,1168,128]{2,1,0:T(8,128)(2,1)S(1)}, bf16[2,1168,128]{2,1,0:T(8,128)(2,1)S(1)}, u32[]{:S(2)}, u32[]{:S(2)}) collective-permute-start(bf16[2,1168,128]{2,1,0:T(8,128)(2,1)S(1)} %get-tuple-element.194), channel_id=1, source_target_pairs={{0,112},{1,113},{2,114},{3,115},{4,116},{5,117},{6,118},{7,119},{8... | collective-permute-start | bytes 1794056 | tf_op jit(solution)/shard_map/ppermute | solution.py:63
  67.8 1.6 collective-permute-start.7
  69.4 18.2 %collective-permute-start.8 = (bf16[2,576,128]{2,1,0:T(8,128)(2,1)S(1)}, bf16[2,576,128]{2,1,0:T(8,128)(2,1)S(1)}, u32[]{:S(2)}, u32[]{:S(2)}) collective-permute-start(bf16[2,576,128]{2,1,0:T(8,128)(2,1)S(1)} %get-tuple-element.164), channel_id=1, source_target_pairs={{0,32},{1,33},{2,34},{3,35},{4,36},{5,37},{6,38},{7,39},{8,40},{9,... | collective-permute-start | bytes 884744 | tf_op jit(solution)/shard_map/ppermute | solution.py:63
  76.7 13.6 %collective-permute-start.9 = (bf16[2,576,128]{2,1,0:T(8,128)(2,1)S(1)}, bf16[2,576,128]{2,1,0:T(8,128)(2,1)S(1)}, u32[]{:S(2)}, u32[]{:S(2)}) collective-permute-start(bf16[2,576,128]{2,1,0:T(8,128)(2,1)S(1)} %get-tuple-element.165), channel_id=1, source_target_pairs={{0,112},{1,113},{2,114},{3,115},{4,116},{5,117},{6,118},{7,119},{8... | collective-permute-start | bytes 884744 | tf_op jit(solution)/shard_map/ppermute | solution.py:63
  90.4 25.1 %collective-permute-start.28 = (bf16[4,1168,128]{2,1,0:T(8,128)(2,1)S(1)}, bf16[4,1168,128]{2,1,0:T(8,128)(2,1)S(1)}, u32[]{:S(2)}, u32[]{:S(2)}) collective-permute-start(bf16[4,1168,128]{2,1,0:T(8,128)(2,1)S(1)} %y_regroup.10), channel_id=1, source_target_pairs={{0,96},{1,97},{2,98},{3,99},{4,100},{5,101},{6,102},{7,103},{8,104... | collective-permute-start | bytes 3588104 | tf_op jit(solution)/shard_map/ppermute | solution.py:63
  93.6 9.4 %collective-permute-start.16 = (bf16[4,528,128]{2,1,0:T(8,128)(2,1)S(1)}, bf16[4,528,128]{2,1,0:T(8,128)(2,1)S(1)}, u32[]{:S(2)}, u32[]{:S(2)}) collective-permute-start(bf16[4,528,128]{2,1,0:T(8,128)(2,1)S(1)} %get-tuple-element.189), channel_id=1, source_target_pairs={{0,1},{1,0},{2,3},{3,2},{4,5},{5,4},{6,7},{7,6},{8,9},{9,8},{10,11... | collective-permute-start | bytes 1622024 | tf_op jit(solution)/shard_map/ppermute | solution.py:63
  95.1 15.2 %collective-permute-start.17 = (bf16[4,528,128]{2,1,0:T(8,128)(2,1)S(1)}, bf16[4,528,128]{2,1,0:T(8,128)(2,1)S(1)}, u32[]{:S(2)}, u32[]{:S(2)}) collective-permute-start(bf16[4,528,128]{2,1,0:T(8,128)(2,1)S(1)} %get-tuple-element.190), channel_id=1, source_target_pairs={{0,4},{1,5},{2,6},{3,7},{4,0},{5,1},{6,2},{7,3},{8,12},{9,13},{10,... | collective-permute-start | bytes 1622024 | tf_op jit(solution)/shard_map/ppermute | solution.py:63
  97.0 13.2 %collective-permute-start.18 = (bf16[4,528,128]{2,1,0:T(8,128)(2,1)S(1)}, bf16[4,528,128]{2,1,0:T(8,128)(2,1)S(1)}, u32[]{:S(2)}, u32[]{:S(2)}) collective-permute-start(bf16[4,528,128]{2,1,0:T(8,128)(2,1)S(1)} %get-tuple-element.191), channel_id=1, source_target_pairs={{0,5},{1,4},{2,7},{3,6},{4,1},{5,0},{6,3},{7,2},{8,13},{9,12},{10,... | collective-permute-start | bytes 1622024 | tf_op jit(solution)/shard_map/ppermute | solution.py:63
  97.1 17.4 %collective-permute-start.15 = (bf16[4,576,128]{2,1,0:T(8,128)(2,1)S(1)}, bf16[4,576,128]{2,1,0:T(8,128)(2,1)S(1)}, u32[]{:S(2)}, u32[]{:S(2)}) collective-permute-start(bf16[4,576,128]{2,1,0:T(8,128)(2,1)S(1)} %y_regroup.9), channel_id=1, source_target_pairs={{0,96},{1,97},{2,98},{3,99},{4,100},{5,101},{6,102},{7,103},{8,104... | collective-permute-start | bytes 1769480 | tf_op jit(solution)/shard_map/ppermute | solution.py:63
  110.4 15.9 %collective-permute-start.26 = (bf16[4,528,128]{2,1,0:T(8,128)(2,1)S(1)}, bf16[4,528,128]{2,1,0:T(8,128)(2,1)S(1)}, u32[]{:S(2)}, u32[]{:S(2)}) collective-permute-start(bf16[4,528,128]{2,1,0:T(8,128)(2,1)S(1)} %get-tuple-element.213), channel_id=1, source_target_pairs={{0,12},{1,13},{2,14},{3,15},{4,8},{5,9},{6,10},{7,11},{8,4},{9,5},... | collective-permute-start | bytes 1622024 | tf_op jit(solution)/shard_map/ppermute | solution.py:63
  115.3 4.7 %collective-permute-start.22 = (bf16[2,592,128]{2,1,0:T(8,128)(2,1)S(1)}, bf16[2,592,128]{2,1,0:T(8,128)(2,1)S(1)}, u32[]{:S(2)}, u32[]{:S(2)}) collective-permute-start(bf16[2,592,128]{2,1,0:T(8,128)(2,1)S(1)} %get-tuple-element.210), channel_id=1, source_target_pairs={{0,16},{1,17},{2,18},{3,19},{4,20},{5,21},{6,22},{7,23},{8,24},{9,... | collective-permute-start | bytes 909320 | tf_op jit(solution)/shard_map/ppermute | solution.py:63
  116.5 41.4 %collective-permute-start.30 = (bf16[4,1040,128]{2,1,0:T(8,128)(2,1)S(1)}, bf16[4,1040,128]{2,1,0:T(8,128)(2,1)S(1)}, u32[]{:S(2)}, u32[]{:S(2)}) collective-permute-start(bf16[4,1040,128]{2,1,0:T(8,128)(2,1)S(1)} %get-tuple-element.233), channel_id=1, source_target_pairs={{0,1},{1,0},{2,3},{3,2},{4,5},{5,4},{6,7},{7,6},{8,9},{9,8},{10,11... | collective-permute-start | bytes 3194888 | tf_op jit(solution)/shard_map/ppermute | solution.py:63
  118.1 39.8 %collective-permute-start.31 = (bf16[4,1040,128]{2,1,0:T(8,128)(2,1)S(1)}, bf16[4,1040,128]{2,1,0:T(8,128)(2,1)S(1)}, u32[]{:S(2)}, u32[]{:S(2)}) collective-permute-start(bf16[4,1040,128]{2,1,0:T(8,128)(2,1)S(1)} %get-tuple-element.234), channel_id=1, source_target_pairs={{0,4},{1,5},{2,6},{3,7},{4,0},{5,1},{6,2},{7,3},{8,12},{9,13},{10,... | collective-permute-start | bytes 3194888 | tf_op jit(solution)/shard_map/ppermute | solution.py:63
  120.0 37.9 %collective-permute-start.32 = (bf16[4,1040,128]{2,1,0:T(8,128)(2,1)S(1)}, bf16[4,1040,128]{2,1,0:T(8,128)(2,1)S(1)}, u32[]{:S(2)}, u32[]{:S(2)}) collective-permute-start(bf16[4,1040,128]{2,1,0:T(8,128)(2,1)S(1)} %get-tuple-element.235), channel_id=1, source_target_pairs={{0,5},{1,4},{2,7},{3,6},{4,1},{5,0},{6,3},{7,2},{8,13},{9,12},{10,... | collective-permute-start | bytes 3194888 | tf_op jit(solution)/shard_map/ppermute | solution.py:63
  120.0 19.4 %collective-permute-start.27 = (bf16[4,528,128]{2,1,0:T(8,128)(2,1)S(1)}, bf16[4,528,128]{2,1,0:T(8,128)(2,1)S(1)}, u32[]{:S(2)}, u32[]{:S(2)}) collective-permute-start(bf16[4,528,128]{2,1,0:T(8,128)(2,1)S(1)} %get-tuple-element.214), channel_id=1, source_target_pairs={{0,15},{1,14},{2,13},{3,12},{4,11},{5,10},{6,9},{7,8},{8,7},{9,6},... | collective-permute-start | bytes 1622024 | tf_op jit(solution)/shard_map/ppermute | solution.py:63
  126.3 25.3 %collective-permute-start.25 = (bf16[4,528,128]{2,1,0:T(8,128)(2,1)S(1)}, bf16[4,528,128]{2,1,0:T(8,128)(2,1)S(1)}, u32[]{:S(2)}, u32[]{:S(2)}) collective-permute-start(bf16[4,528,128]{2,1,0:T(8,128)(2,1)S(1)} %get-tuple-element.203), channel_id=1, source_target_pairs={{0,3},{1,2},{2,1},{3,0},{4,7},{5,6},{6,5},{7,4},{8,11},{9,10},{10,... | collective-permute-start | bytes 1622024 | tf_op jit(solution)/shard_map/ppermute | solution.py:63
  139.5 14.5 %collective-permute-start.23 = (bf16[2,592,128]{2,1,0:T(8,128)(2,1)S(1)}, bf16[2,592,128]{2,1,0:T(8,128)(2,1)S(1)}, u32[]{:S(2)}, u32[]{:S(2)}) collective-permute-start(bf16[2,592,128]{2,1,0:T(8,128)(2,1)S(1)} %get-tuple-element.211), channel_id=1, source_target_pairs={{0,32},{1,33},{2,34},{3,35},{4,36},{5,37},{6,38},{7,39},{8,40},{9,... | collective-permute-start | bytes 909320 | tf_op jit(solution)/shard_map/ppermute | solution.py:63
  151.6 6.2 %collective-permute-start.24 = (bf16[2,592,128]{2,1,0:T(8,128)(2,1)S(1)}, bf16[2,592,128]{2,1,0:T(8,128)(2,1)S(1)}, u32[]{:S(2)}, u32[]{:S(2)}) collective-permute-start(bf16[2,592,128]{2,1,0:T(8,128)(2,1)S(1)} %get-tuple-element.212), channel_id=1, source_target_pairs={{0,112},{1,113},{2,114},{3,115},{4,116},{5,117},{6,118},{7,119},{8... | collective-permute-start | bytes 909320 | tf_op jit(solution)/shard_map/ppermute | solution.py:63
  158.1 32.6 %collective-permute-start.37 = (bf16[4,1040,128]{2,1,0:T(8,128)(2,1)S(1)}, bf16[4,1040,128]{2,1,0:T(8,128)(2,1)S(1)}, u32[]{:S(2)}, u32[]{:S(2)}) collective-permute-start(bf16[4,1040,128]{2,1,0:T(8,128)(2,1)S(1)} %get-tuple-element.250), channel_id=1, source_target_pairs={{0,12},{1,13},{2,14},{3,15},{4,8},{5,9},{6,10},{7,11},{8,4},{9,5},... | collective-permute-start | bytes 3194888 | tf_op jit(solution)/shard_map/ppermute | solution.py:63
  158.7 11.3 %collective-permute-start.29 = (bf16[4,592,128]{2,1,0:T(8,128)(2,1)S(1)}, bf16[4,592,128]{2,1,0:T(8,128)(2,1)S(1)}, u32[]{:S(2)}, u32[]{:S(2)}) collective-permute-start(bf16[4,592,128]{2,1,0:T(8,128)(2,1)S(1)} %y_regroup.11), channel_id=1, source_target_pairs={{0,96},{1,97},{2,98},{3,99},{4,100},{5,101},{6,102},{7,103},{8,104... | collective-permute-start | bytes 1818632 | tf_op jit(solution)/shard_map/ppermute | solution.py:63
  161.7 29.0 %collective-permute-start.38 = (bf16[4,1040,128]{2,1,0:T(8,128)(2,1)S(1)}, bf16[4,1040,128]{2,1,0:T(8,128)(2,1)S(1)}, u32[]{:S(2)}, u32[]{:S(2)}) collective-permute-start(bf16[4,1040,128]{2,1,0:T(8,128)(2,1)S(1)} %get-tuple-element.251), channel_id=1, source_target_pairs={{0,15},{1,14},{2,13},{3,12},{4,11},{5,10},{6,9},{7,8},{8,7},{9,6},... | collective-permute-start | bytes 3194888 | tf_op jit(solution)/shard_map/ppermute | solution.py:63
  166.7 33.4 %collective-permute-start.36 = (bf16[4,1040,128]{2,1,0:T(8,128)(2,1)S(1)}, bf16[4,1040,128]{2,1,0:T(8,128)(2,1)S(1)}, u32[]{:S(2)}, u32[]{:S(2)}) collective-permute-start(bf16[4,1040,128]{2,1,0:T(8,128)(2,1)S(1)} %get-tuple-element.240), channel_id=1, source_target_pairs={{0,3},{1,2},{2,1},{3,0},{4,7},{5,6},{6,5},{7,4},{8,11},{9,10},{10,... | collective-permute-start | bytes 3194888 | tf_op jit(solution)/shard_map/ppermute | solution.py:63
  170.8 32.5 %collective-permute-start.33 = (bf16[4,528,128]{2,1,0:T(8,128)(2,1)S(1)}, bf16[4,528,128]{2,1,0:T(8,128)(2,1)S(1)}, u32[]{:S(2)}, u32[]{:S(2)}) collective-permute-start(bf16[4,528,128]{2,1,0:T(8,128)(2,1)S(1)} %get-tuple-element.247), channel_id=1, source_target_pairs={{0,1},{1,0},{2,3},{3,2},{4,5},{5,4},{6,7},{7,6},{8,9},{9,8},{10,11... | collective-permute-start | bytes 1622024 | tf_op jit(solution)/shard_map/ppermute | solution.py:63
  172.4 31.0 %collective-permute-start.34 = (bf16[4,528,128]{2,1,0:T(8,128)(2,1)S(1)}, bf16[4,528,128]{2,1,0:T(8,128)(2,1)S(1)}, u32[]{:S(2)}, u32[]{:S(2)}) collective-permute-start(bf16[4,528,128]{2,1,0:T(8,128)(2,1)S(1)} %get-tuple-element.248), channel_id=1, source_target_pairs={{0,4},{1,5},{2,6},{3,7},{4,0},{5,1},{6,2},{7,3},{8,12},{9,13},{10,... | collective-permute-start | bytes 1622024 | tf_op jit(solution)/shard_map/ppermute | solution.py:63
  190.7 12.7 %collective-permute-start.35 = (bf16[4,528,128]{2,1,0:T(8,128)(2,1)S(1)}, bf16[4,528,128]{2,1,0:T(8,128)(2,1)S(1)}, u32[]{:S(2)}, u32[]{:S(2)}) collective-permute-start(bf16[4,528,128]{2,1,0:T(8,128)(2,1)S(1)} %get-tuple-element.249), channel_id=1, source_target_pairs={{0,5},{1,4},{2,7},{3,6},{4,1},{5,0},{6,3},{7,2},{8,13},{9,12},{10,... | collective-permute-start | bytes 1622024 | tf_op jit(solution)/shard_map/ppermute | solution.py:63
  203.5 16.4 %collective-permute-start.40 = (bf16[4,528,128]{2,1,0:T(8,128)(2,1)S(1)}, bf16[4,528,128]{2,1,0:T(8,128)(2,1)S(1)}, u32[]{:S(2)}, u32[]{:S(2)}) collective-permute-start(bf16[4,528,128]{2,1,0:T(8,128)(2,1)S(1)} %get-tuple-element.266), channel_id=1, source_target_pairs={{0,12},{1,13},{2,14},{3,15},{4,8},{5,9},{6,10},{7,11},{8,4},{9,5},... | collective-permute-start | bytes 1622024 | tf_op jit(solution)/shard_map/ppermute | solution.py:63
  203.6 16.4 %collective-permute-start.41 = (bf16[4,528,128]{2,1,0:T(8,128)(2,1)S(1)}, bf16[4,528,128]{2,1,0:T(8,128)(2,1)S(1)}, u32[]{:S(2)}, u32[]{:S(2)}) collective-permute-start(bf16[4,528,128]{2,1,0:T(8,128)(2,1)S(1)} %get-tuple-element.267), channel_id=1, source_target_pairs={{0,15},{1,14},{2,13},{3,12},{4,11},{5,10},{6,9},{7,8},{8,7},{9,6},... | collective-permute-start | bytes 1622024 | tf_op jit(solution)/shard_map/ppermute | solution.py:63
  209.3 13.3 %collective-permute-start.39 = (bf16[4,528,128]{2,1,0:T(8,128)(2,1)S(1)}, bf16[4,528,128]{2,1,0:T(8,128)(2,1)S(1)}, u32[]{:S(2)}, u32[]{:S(2)}) collective-permute-start(bf16[4,528,128]{2,1,0:T(8,128)(2,1)S(1)} %get-tuple-element.265), channel_id=1, source_target_pairs={{0,3},{1,2},{2,1},{3,0},{4,7},{5,6},{6,5},{7,4},{8,11},{9,10},{10,... | collective-permute-start | bytes 1622024 | tf_op jit(solution)/shard_map/ppermute | solution.py:63
